TPU v7x, 32 devices: a whole 2x2x4 slice. The times are simulated.
32 devices in a mesh: seg: 4 (over y, x), slab: 8 (over z, core).
Axes of the slice: x: 2, y: 2, z: 4, core: 2. Of those that a mesh axis runs over, the one named last changes fastest.
Arguments:
- states: float32 [4, 4, 256, 64, 128], P('seg', None, 'slab'), may hold values from -6 to 6
- viscosity: float32 [256, 64, 128], P('slab'), may hold values from 0.2 to 2
- inverse: float32 [4, 256, 256], replicated, may hold values from -0.375 to 0.375
Outputs:
- residual: float32 [4, 4, 256, 64, 128], P('seg', None, 'slab')
- gradient: float32 [4, 4, 256, 64, 128], P('seg', None, 'slab')
All inputs are finite; a program needn't handle non-finite values.
Results may differ from a plain program's by a relative error of at most 0.000075.
Values sent between devices are 32-bit elements; how exact they have to be, the bound alone decides.
No kernel may reach another device: no remote copies, remote signals or barrier semaphores. Data moves between devices by JAX's collectives and lax.ppermute only.
A program may use at most 128 MiB of HBM per device.

v0:
```python
import jax
import jax.numpy as jnp
from jax import lax
from jax.sharding import PartitionSpec as P

time_step = 0.1
buoyancy = 1.0


def padded_2(block, sides, width):
    for axis, dim in sides:
        count = lax.axis_size(axis)
        forward = [(i, i + 1) for i in range(count - 1)]
        backward = [(target, source) for source, target in forward]
        low = lax.ppermute(
            lax.slice_in_dim(block, block.shape[dim] - width, None, axis=dim), axis, forward
        )
        high = lax.ppermute(lax.slice_in_dim(block, 0, width, axis=dim), axis, backward)
        block = jnp.concatenate([low, block, high], axis=dim)
    return block


def from_behind(value, axis, steps):
    count = lax.axis_size(axis)
    pairs = [(source, (source + steps) % count) for source in range(count)]
    return lax.ppermute(value, axis, pairs)


def neighbours(field_now):
    north_side, south_side = (jnp.roll(field_now, -1, axis=2), jnp.roll(field_now, 1, axis=2))
    return (north_side, south_side, jnp.roll(field_now, -1, axis=3), jnp.roll(field_now, 1, axis=3))


def vertical(field_now):
    padded = padded_2(field_now, (("slab", 1),), 1)
    return padded[:, 2:] - padded[:, :-2]


def apply_columns(matrices, field_now):
    return jnp.einsum("fzk,fkyx->fzyx", matrices, field_now, precision=lax.Precision.HIGHEST)


def line_solve(field_now, matrices):
    product = apply_columns(
        matrices, lax.all_to_all(field_now, "slab", split_axis=2, concat_axis=1, tiled=True)
    )
    return lax.all_to_all(product, "slab", split_axis=1, concat_axis=2, tiled=True)


def face_values(viscous):
    north_side, south_side, east_side, west_side = neighbours(viscous)
    along_x = 0.5 * (viscous + east_side)
    back_x = 0.5 * (west_side + viscous)
    along_y = 0.5 * (viscous + north_side)
    back_y = 0.5 * (viscous + south_side)
    return (along_x, back_x, along_y, back_y)


def horizontal(field_now, face_visc):
    along_x, back_x, along_y, back_y = face_visc
    north_side, south_side, east_side, west_side = neighbours(field_now)
    return (
        along_x * (east_side - field_now)
        - back_x * (field_now - west_side)
        + along_y * (north_side - field_now)
        - back_y * (field_now - south_side)
    )


def forcing(state_now):
    zero_plane = jnp.zeros_like(state_now[0])
    return jnp.stack([zero_plane, zero_plane, state_now[3], state_now[2]])


def advance(state_now, face_visc, matrices):
    slopes = vertical(state_now)
    explicit = state_now + time_step * (
        horizontal(state_now, face_visc) - state_now[2] * slopes + buoyancy * forcing(state_now)
    )
    return (line_solve(explicit, matrices), slopes)


def retreat(state_now, slopes, cotangent, face_visc, transposed):
    pulled = line_solve(cotangent, transposed)
    scaled = time_step * pulled
    zero_plane = jnp.zeros_like(scaled[0])
    coupling = buoyancy * scaled[3] - jnp.sum(scaled * slopes, axis=0)
    coupled_terms = jnp.stack([zero_plane, zero_plane, coupling, buoyancy * scaled[2]])
    return pulled + horizontal(scaled, face_visc) + vertical(state_now[2] * scaled) + coupled_terms


def local(states, viscosity, inverse):
    start_state = states[0]
    target = from_behind(start_state, "seg", -1)
    viscous = viscosity[None]
    face_visc = face_values(viscous)
    transposed = jnp.swapaxes(inverse, 1, 2)
    first_state, slopes_start = advance(start_state, face_visc, inverse)
    second_state, slopes_first = advance(first_state, face_visc, inverse)
    residual = second_state - target
    carried = retreat(first_state, slopes_first, residual, face_visc, transposed)
    prior = from_behind(residual, "seg", 1)
    gradient = retreat(start_state, slopes_start, carried, face_visc, transposed) - prior
    return (residual[None], gradient[None])


def solution(mesh):
    in_specs = (P("seg", None, "slab", None, None), P("slab", None, None), P())
    out_specs = (P("seg", None, "slab", None, None), P("seg", None, "slab", None, None))
    return jax.shard_map(local, mesh=mesh, in_specs=in_specs, out_specs=out_specs, check_vma=False)
```

profile of v0, /device:TPU:9, one launch (start us, length us, event | category | flops | bytes accessed | tf_op | source)
XLA Modules:
  0.0 1058.2 jit_solution(14915748097671172243)
XLA Ops:
  16.0 4.8 fusion.95
  20.8 4.7 fusion.96
  29.7 16.8 %fusion.17 = f32[4,32,64,128]{3,2,1,0:T(8,128)} fusion(f32[4,32,64,128]{3,2,1,0:T(8,128)} %bitcast.128, f32[4,32,64,1]{3,2,1,0:T(8,128)} %get-tuple-element.54, f32[4,32,64,127]{3,2,1,0:T(8,128)} %get-tuple-element.56, f32[4,32,64,127]{3,2,1,0:T(8,128)} %get-tuple-element.55, f32[4,32,64,1]{3,2,1,0:T(8,128)} %get-tuple-element.53, ...), kind=kLoop, calls=%fused_computation.26 | loop fusion | flops 26214400 | bytes 32768016 | tf_op jit(solution)/shard_map/add | solution.py:77
  51.1 95.2 %all_to_all.144 = f32[4,32,64,128]{3,1,0,2:T(8,128)S(1)} all-to-all(f32[4,32,64,128]{3,1,0,2:T(8,128)S(1)} %copy.119), channel_id=1, replica_groups=mesh['seg'=4,'slab'=8] {'slab'}, dimensions={2} | all-to-all | bytes 8388608 | tf_op jit(solution)/shard_map/all_to_all | solution.py:45
  150.1 8.2 fusion.56
  158.4 5.4 copy.123
  163.8 98.0 %all_to_all.145 = f32[4,256,8,128]{3,2,0,1:T(8,128)S(1)} all-to-all(f32[4,256,8,128]{3,2,0,1:T(8,128)} %copy.123), channel_id=1, replica_groups=mesh['seg'=4,'slab'=8] {'slab'}, dimensions={1} | all-to-all | bytes 8388608 | tf_op jit(solution)/shard_map/all_to_all | solution.py:47
  267.0 4.7 fusion.90
  271.8 4.7 fusion.91
  286.7 20.2 %fusion.28 = f32[4,32,64,128]{3,2,1,0:T(8,128)} fusion(f32[4,32,64,128]{3,2,1,0:T(8,128)} %bitcast.125, f32[4,32,64,1]{3,2,1,0:T(8,128)} %get-tuple-element.41, f32[4,32,64,127]{3,2,1,0:T(8,128)} %get-tuple-element.43, f32[4,32,64,127]{3,2,1,0:T(8,128)} %get-tuple-element.42, f32[4,32,64,1]{3,2,1,0:T(8,128)} %get-tuple-element.40, ...), kind=kLoop, calls=%fused_computation.41 | loop fusion | flops 26214400 | bytes 32768016 | tf_op jit(solution)/shard_map/add | solution.py:77
  311.6 97.3 %all_to_all.146 = f32[4,32,64,128]{3,1,0,2:T(8,128)S(1)} all-to-all(f32[4,32,64,128]{3,1,0,2:T(8,128)S(1)} %copy.129), channel_id=1, replica_groups=mesh['seg'=4,'slab'=8] {'slab'}, dimensions={2} | all-to-all | bytes 8388608 | tf_op jit(solution)/shard_map/all_to_all | solution.py:45
  412.7 8.2 fusion.59
  420.9 5.5 copy.133
  426.4 7.6 all-to-all-start.3
  436.1 89.9 %collective-permute-done.4 = f32[4,32,64,128]{3,2,1,0:T(8,128)} collective-permute-done((f32[4,32,64,128]{3,2,1,0:T(8,128)}, f32[4,32,64,128]{3,2,1,0:T(8,128)}, u32[]{:S(2)}, u32[]{:S(2)}) %collective-permute-start.4) | collective-permute-done | bytes 4194336 | tf_op jit(solution)/shard_map/ppermute | solution.py:26
  532.6 96.9 %all_to_all.147 = f32[4,32,64,128]{3,1,0,2:T(8,128)S(1)} all-to-all(f32[4,32,64,128]{3,1,0,2:T(8,128)S(1)} %copy.136), channel_id=1, replica_groups=mesh['seg'=4,'slab'=8] {'slab'}, dimensions={2} | all-to-all | bytes 8388608 | tf_op jit(solution)/shard_map/all_to_all | solution.py:45
  633.3 8.2 fusion.62
  641.5 5.5 copy.140
  647.0 8.0 all-to-all-start.5
  657.4 88.0 %all-to-all-done.5 = f32[4,256,8,128]{3,2,0,1:T(8,128)} async-done(((f32[4,256,8,128]{3,2,0,1:T(8,128)}), f32[4,256,8,128]{3,2,0,1:T(8,128)}, u32[]{:S(2)}, u32[]{:S(2)}) %all-to-all-start.5) | async-done | bytes 4194336 | tf_op jit(solution)/shard_map/all_to_all | solution.py:47
  745.5 5.8 multiply_reduce_fusion.1
  751.2 4.7 fusion.82
  755.9 4.7 fusion.83
  774.8 17.5 %fusion.7 = f32[4,32,64,128]{3,2,1,0:T(8,128)} fusion(f32[4,32,64,128]{3,2,1,0:T(8,128)} %copy-done.6, f32[4,1,64,128]{3,2,1,0:T(8,128)S(1)} %collective-permute-done.6, f32[4,1,64,128]{3,2,1,0:T(8,128)S(1)} %collective-permute-done.5, f32[4,32,64,1]{3,2,1,0:T(8,128)} %get-tuple-element.27, f32[4,32,64,127]{3,2,1,0:T(8,128)} %get-tuple-element.29, ...), kind=kLoop, calls=%fused_computation.10 | loop fusion | flops 25165824 | bytes 35913744 | tf_op jit(solution)/shard_map/add | solution.py:89
  796.9 97.4 %all_to_all.148 = f32[4,32,64,128]{3,1,0,2:T(8,128)S(1)} all-to-all(f32[4,32,64,128]{3,1,0,2:T(8,128)S(1)} %copy.143), channel_id=1, replica_groups=mesh['seg'=4,'slab'=8] {'slab'}, dimensions={2} | all-to-all | bytes 8388608 | tf_op jit(solution)/shard_map/all_to_all | solution.py:45
  898.1 8.2 fusion.65
  906.3 5.5 copy.147
  911.8 7.6 all-to-all-start.7
  923.8 86.0 %all-to-all-done.7 = f32[4,256,8,128]{3,2,0,1:T(8,128)} async-done(((f32[4,256,8,128]{3,2,0,1:T(8,128)}), f32[4,256,8,128]{3,2,0,1:T(8,128)}, u32[]{:S(2)}, u32[]{:S(2)}) %all-to-all-start.7) | async-done | bytes 4194336 | tf_op jit(solution)/shard_map/all_to_all | solution.py:47
  1009.8 5.6 multiply_reduce_fusion
  1034.1 4.7 fusion.79
  1038.8 19.1 %fusion.4 = f32[1,4,32,64,128]{4,3,2,1,0:T(8,128)} fusion(f32[4,32,64,128]{3,2,1,0:T(8,128)} %collective-permute-done.9, f32[4,32,64,128]{3,2,1,0:T(8,128)} %copy-done.5, f32[4,1,64,128]{3,2,1,0:T(8,128)S(1)} %collective-permute-done.8, f32[4,1,64,128]{3,2,1,0:T(8,128)S(1)} %collective-permute-done.7, f32[4,32,64,1]{3,2,1,0:T(8,128)} %get-tuple-element.12, ...), kind=kLoop, calls=%fused_computation.5 | loop fusion | flops 26214400 | bytes 40108048 | tf_op jit(solution)/shard_map/broadcast_in_dim | solution.py:104
  (77 shorter events, 112.1 us)
Async XLA Ops:
  0.6 149.5 %copy-start = (f32[4,256,256]{2,1,0:T(8,128)S(1)}, f32[4,256,256]{2,1,0:T(8,128)}, u32[]{:S(2)}) copy-start(f32[4,256,256]{2,1,0:T(8,128)} %param.5) | copy-start | bytes 3145732
  0.6 8.8 copy-start.3
  1.8 27.9 %collective-permute-start = (f32[4,1,64,128]{3,2,1,0:T(8,128)S(1)}, f32[4,1,64,128]{3,2,1,0:T(8,128)S(1)}, u32[]{:S(2)}, u32[]{:S(2)}) collective-permute-start(f32[4,1,64,128]{3,2,1,0:T(8,128)S(1)} %get-tuple-element.47), channel_id=1, source_target_pairs={{1,0},{2,1},{3,2},{4,3},{5,4},{6,5},{7,6},{9,8},{10,9},{11,10},{12... | collective-permute-start | bytes 393224 | tf_op jit(solution)/shard_map/ppermute | solution.py:18
  4.4 25.3 %collective-permute-start.1 = (f32[4,1,64,128]{3,2,1,0:T(8,128)S(1)}, f32[4,1,64,128]{3,2,1,0:T(8,128)S(1)}, u32[]{:S(2)}, u32[]{:S(2)}) collective-permute-start(f32[4,1,64,128]{3,2,1,0:T(8,128)S(1)} %get-tuple-element.48), channel_id=1, source_target_pairs={{0,1},{1,2},{2,3},{3,4},{4,5},{5,6},{6,7},{8,9},{9,10},{10,11},{11... | collective-permute-start | bytes 393224 | tf_op jit(solution)/shard_map/ppermute | solution.py:15
  9.5 2.2 copy-start.2
  262.4 22.4 %copy-start.1 = (f32[4,32,8,8,128]{4,3,2,1,0:T(8,128)}, f32[4,32,8,8,128]{4,3,2,1,0:T(8,128)S(1)}, u32[]{:S(2)}) copy-start(f32[4,32,8,8,128]{4,3,2,1,0:T(8,128)S(1)} %copy.196) | copy-start | bytes 12582916
  276.9 8.7 copy-start.8
  279.2 6.3 collective-permute-start.2
  282.2 4.5 collective-permute-start.3
  426.4 99.7 %all-to-all-start.3 = ((f32[4,256,8,128]{3,2,0,1:T(8,128)}), f32[4,256,8,128]{3,2,0,1:T(8,128)}, u32[]{:S(2)}, u32[]{:S(2)}) async-start(f32[4,256,8,128]{3,2,0,1:T(8,128)} %copy.133), calls=%async_computation.3 | async-start | bytes 8388608 | tf_op jit(solution)/shard_map/all_to_all | solution.py:47
  434.0 92.1 %collective-permute-start.4 = (f32[4,32,64,128]{3,2,1,0:T(8,128)}, f32[4,32,64,128]{3,2,1,0:T(8,128)}, u32[]{:S(2)}, u32[]{:S(2)}) collective-permute-start(f32[4,32,64,128]{3,2,1,0:T(8,128)} %bitcast.129), channel_id=1, source_target_pairs={{0,24},{8,0},{16,8},{24,16},{1,25},{9,1},{17,9},{25,17},{2,26},{10... | collective-permute-start | bytes 12582920 | tf_op jit(solution)/shard_map/ppermute | solution.py:26
  530.1 2.5 copy-start.7
  647.0 98.4 %all-to-all-start.5 = ((f32[4,256,8,128]{3,2,0,1:T(8,128)}), f32[4,256,8,128]{3,2,0,1:T(8,128)}, u32[]{:S(2)}, u32[]{:S(2)}) async-start(f32[4,256,8,128]{3,2,0,1:T(8,128)} %copy.140), calls=%async_computation.5 | async-start | bytes 8388608 | tf_op jit(solution)/shard_map/all_to_all | solution.py:47
  751.2 15.6 %copy-start.6 = (f32[4,32,64,128]{3,2,1,0:T(8,128)}, f32[4,32,64,128]{3,2,1,0:T(8,128)S(1)}, u32[]{:S(2)}) copy-start(f32[4,32,64,128]{3,2,1,0:T(8,128)S(1)} %get-tuple-element.20) | copy-start | bytes 12582916
  765.2 9.5 copy-start.4
  766.8 6.3 collective-permute-start.5
  769.2 5.6 collective-permute-start.6
  911.8 98.0 %all-to-all-start.7 = ((f32[4,256,8,128]{3,2,0,1:T(8,128)}), f32[4,256,8,128]{3,2,0,1:T(8,128)}, u32[]{:S(2)}, u32[]{:S(2)}) async-start(f32[4,256,8,128]{3,2,0,1:T(8,128)} %copy.147), calls=%async_computation.7 | async-start | bytes 8388608 | tf_op jit(solution)/shard_map/all_to_all | solution.py:47
  919.4 119.5 %collective-permute-start.9 = (f32[4,32,64,128]{3,2,1,0:T(8,128)}, f32[4,32,64,128]{3,2,1,0:T(8,128)}, u32[]{:S(2)}, u32[]{:S(2)}) collective-permute-start(f32[4,32,64,128]{3,2,1,0:T(8,128)} %copy-done.7), channel_id=1, source_target_pairs={{0,8},{8,16},{16,24},{24,0},{1,9},{9,17},{17,25},{25,1},{2,10},{10... | collective-permute-start | bytes 12582920 | tf_op jit(solution)/shard_map/ppermute | solution.py:26
  1015.4 2.1 copy-start.5
  1017.5 21.3 %collective-permute-start.7 = (f32[4,1,64,128]{3,2,1,0:T(8,128)S(1)}, f32[4,1,64,128]{3,2,1,0:T(8,128)S(1)}, u32[]{:S(2)}, u32[]{:S(2)}) collective-permute-start(f32[4,1,64,128]{3,2,1,0:T(8,128)S(1)} %get-tuple-element.15), channel_id=1, source_target_pairs={{1,0},{2,1},{3,2},{4,3},{5,4},{6,5},{7,6},{9,8},{10,9},{11,10},{12... | collective-permute-start | bytes 393224 | tf_op jit(solution)/shard_map/ppermute | solution.py:18
  1019.9 19.0 %collective-permute-start.8 = (f32[4,1,64,128]{3,2,1,0:T(8,128)S(1)}, f32[4,1,64,128]{3,2,1,0:T(8,128)S(1)}, u32[]{:S(2)}, u32[]{:S(2)}) collective-permute-start(f32[4,1,64,128]{3,2,1,0:T(8,128)S(1)} %get-tuple-element.16), channel_id=1, source_target_pairs={{0,1},{1,2},{2,3},{3,4},{4,5},{5,6},{6,7},{8,9},{9,10},{10,11},{11... | collective-permute-start | bytes 393224 | tf_op jit(solution)/shard_map/ppermute | solution.py:15
where the time goes:
time: 1070 us; the launch traced here: 1060 us
  blocking collectives  485 us (45%)
  waiting for transfers between devices  267 us (25%)
  local copies, waits for them, and re-layouts  123 us (11%)
  other arithmetic  99.1 us (9%)
  starting transfers between devices  50 us (5%)
  matrix products  33 us (3%)
    all_to_all x4, blocking collectives, line_solve(): lax.all_to_all(field_now, 'slab', split_axis=2, concat_axis=1, tiled=True)  387 us
    all_to_all x3, waiting for transfers between devices, line_solve(): lax.all_to_all(product, 'slab', split_axis=1, concat_axis=2, tiled=True)  174 us
    all_to_all x1, blocking collectives, line_solve(): lax.all_to_all(product, 'slab', split_axis=1, concat_axis=2, tiled=True)  98 us
    ppermute x2, waiting for transfers between devices, from_behind(): return lax.ppermute(value, axis, pairs)  89.9 us
    slice x8, local copies, waits for them, and re-layouts, neighbours(): jnp.roll(field_now, 1, axis=3)  37.5 us
    add x2, other arithmetic, advance(): state_now + time_step * (horizontal(state_now, face_visc) - state_now[2]...  37 us
    dot_general x4, matrix products, apply_columns(): jnp.einsum('fzk,fkyx->fzyx', matrices, field_now, precision=lax.Precision...  33 us
    all_to_all x3, starting transfers between devices, line_solve(): lax.all_to_all(product, 'slab', split_axis=1, concat_axis=2, tiled=True)  23.2 us
  transfers between devices with their start and end apart: 13, of which 6 were waited for; matrix products, arithmetic and copies ran while one was open for 4% of the time, Pallas kernels for 0%

commit v1 on v0

v1 whole, which is shorter than its diff:
```python
import functools

import jax
import jax.numpy as jnp
from jax import lax
from jax.experimental import pallas as pl
from jax.experimental.pallas import tpu as pltpu
from jax.sharding import PartitionSpec as P

time_step = 0.1
vmem_bytes = 56 * 1024 * 1024
f32, bf16 = jnp.float32, jnp.bfloat16
U, V, W, T = range(4)
fields = 4


def whole():
    return pl.BlockSpec(memory_space=pltpu.VMEM)


def anywhere():
    return pl.BlockSpec(memory_space=pl.ANY)


def params():
    return pltpu.CompilerParams(vmem_limit_bytes=vmem_bytes)


def cost(flops, moved):
    return pl.CostEstimate(flops=flops, bytes_accessed=moved, transcendentals=0)


def east(value):
    return pltpu.roll(value, value.shape[1] - 1, 1)


def west(value):
    return pltpu.roll(value, 1, 1)


def slope(value, before, after):
    count = value.shape[0]
    row = lax.broadcasted_iota(jnp.int32, value.shape, 0)
    above = jnp.where(row == count - 1, after, pltpu.roll(value, count - 1, 0))
    below = jnp.where(row == 0, before, pltpu.roll(value, 1, 0))
    return above - below


def parts_of(value):
    high = value.astype(bf16)
    return high, (value - high.astype(f32)).astype(bf16)


def product(matrix_high, matrix_low, high, low):
    dot = functools.partial(jnp.dot, preferred_element_type=f32)
    return dot(matrix_high, high) + (dot(matrix_high, low) + dot(matrix_low, high))


def to_rows_kernel(x_ref, o_ref):
    depth, rows, _ = x_ref.shape
    for z in range(depth):
        o_ref[pl.ds(z, rows, stride=depth), :] = x_ref[z]


def to_rows(states, field):
    _, depth, rows, width = states.shape
    return pl.pallas_call(
        to_rows_kernel,
        grid=(1,),
        in_specs=[pl.BlockSpec((None, depth, rows, width), lambda i: (field, 0, 0, 0))],
        out_specs=pl.BlockSpec((rows * depth, width), lambda i: (0, 0)),
        out_shape=jax.ShapeDtypeStruct((rows * depth, width), f32),
        compiler_params=params(),
        cost_estimate=cost(0, 8 * rows * depth * width),
        name="to_rows",
    )(states)


def visc_rows_kernel(depth, rows, block, share, own_ref, x_ref, o_ref, send_ref):
    for z in range(depth):
        o_ref[pl.ds(z, rows, stride=depth), :] = x_ref[z]
    own = own_ref[0]
    for target in range(rows // block):
        for i in range(share):
            row = lax.rem(target * block - 2 + share * own + i + rows, rows)
            send_ref[target, i] = o_ref[pl.ds(pl.multiple_of(row * depth, depth), depth), :]


def visc_rows(viscosity, slabs, share):
    depth, rows, width = viscosity.shape
    own = jnp.full((1,), lax.axis_index("seg"), jnp.int32)
    return pl.pallas_call(
        functools.partial(visc_rows_kernel, depth, rows, rows // slabs, share),
        in_specs=[pl.BlockSpec(memory_space=pltpu.SMEM), whole()],
        out_specs=(whole(), whole()),
        out_shape=(
            jax.ShapeDtypeStruct((rows * depth, width), f32),
            jax.ShapeDtypeStruct((slabs, share, depth, width), f32),
        ),
        compiler_params=params(),
        cost_estimate=cost(0, 8 * rows * depth * width),
        name="visc_rows",
    )(own, viscosity)


def to_planes_kernel(*refs):
    o_ref = refs[-1]
    _, depth, rows, _ = o_ref.shape
    for f in range(fields):
        for z in range(depth):
            o_ref[f, z] = refs[f][pl.ds(z, rows, stride=depth), :]


def to_planes(parts, depth):
    total, width = parts[0].shape
    return pl.pallas_call(
        to_planes_kernel,
        in_specs=[whole()] * fields,
        out_specs=whole(),
        out_shape=jax.ShapeDtypeStruct((fields, depth, total // depth, width), f32),
        compiler_params=params(),
        cost_estimate=cost(0, 8 * fields * total * width),
        name="to_planes",
    )(*parts)


def advance_rows(state, visc, shift, mat_high, mat_low, carry, high, low, count, finish):
    slabs, _, depth, width = state.shape[1:]
    edge = jnp.zeros((1, width), f32)
    for p in range(slabs):
        along_y = 0.5 * (visc[p, shift] + visc[p, shift + 1])
        for f in range(fields):
            carry[f, p] = along_y * (state[f, p, 1] - state[f, p, 0])

    def pair(k, _):
        for half in range(2):
            j = 2 * k + half + 1
            for p in range(slabs):
                here = visc[p, j + shift]
                along_x = 0.5 * (here + east(here))
                along_y = 0.5 * (here + visc[p, j + shift + 1])
                speed = state[W, p, j]
                for f in range(fields):
                    value = state[f, p, j]
                    flux_x = along_x * (east(value) - value)
                    flux_y = along_y * (state[f, p, j + 1] - value)
                    spread = flux_x - west(flux_x) + (flux_y - carry[f, p])
                    carry[f, p] = flux_y
                    before = state[f, p - 1, j, depth - 1 : depth] if p > 0 else edge
                    after = state[f, p + 1, j, 0:1] if p < slabs - 1 else edge
                    rate = spread - speed * slope(value, before, after)
                    if f == W:
                        rate = rate + state[T, p, j]
                    if f == T:
                        rate = rate + speed
                    a, b = parts_of(value + time_step * rate)
                    high[f, p * depth : (p + 1) * depth, half * width : (half + 1) * width] = a
                    low[f, p * depth : (p + 1) * depth, half * width : (half + 1) * width] = b
        for f in range(fields):
            out = product(mat_high[f], mat_low[f], high[f], low[f])
            for half in range(2):
                piece = out[:, half * width : (half + 1) * width]
                finish(f, 2 * k + half, piece.reshape(slabs, depth, width))
        return 0

    lax.fori_loop(0, count // 2, pair, 0)


def first_kernel(share, *refs):
    mains, lows, highs = refs[0:4], refs[4:8], refs[8:12]
    visc_in, mat_high, mat_low, first, visc, state, carry, high, low, sem = refs[12:]
    block = mains[0].shape[1]
    copies = []
    for s in range(visc_in.shape[0]):
        copies.append((visc_in.at[s], visc.at[:, pl.ds(share * s, share)]))
    for f in range(fields):
        copies.append((lows[f], state.at[f, :, pl.ds(0, 2)]))
        copies.append((mains[f], state.at[f, :, pl.ds(2, block)]))
        copies.append((highs[f], state.at[f, :, pl.ds(block + 2, 2)]))
    copies = [
        pltpu.make_async_copy(source, target, sem.at[i])
        for i, (source, target) in enumerate(copies)
    ]
    for copy in copies:
        copy.start()
    for copy in copies:
        copy.wait()

    def finish(f, row, piece):
        first[f, :, row] = piece

    advance_rows(
        state, visc, 0, mat_high, mat_low, carry, high, low, first.shape[2], finish
    )


def first_step(mains, lows, highs, visc_in, mat_high, mat_low):
    slabs, block, depth, width = mains[0].shape
    segs, _, share = visc_in.shape[:3]
    order = slabs * depth
    volume = fields * (block + 2) * order * width
    return pl.pallas_call(
        functools.partial(first_kernel, share),
        in_specs=[anywhere()] * 13 + [whole()] * 2,
        out_specs=(whole(), whole()),
        out_shape=(
            jax.ShapeDtypeStruct((fields, slabs, block + 2, depth, width), f32),
            jax.ShapeDtypeStruct((slabs, segs * share, depth, width), f32),
        ),
        scratch_shapes=[
            pltpu.VMEM((fields, slabs, block + 4, depth, width), f32),
            pltpu.VMEM((fields, slabs, depth, width), f32),
            pltpu.VMEM((fields, order, 2 * width), bf16),
            pltpu.VMEM((fields, order, 2 * width), bf16),
            pltpu.SemaphoreType.DMA((segs + 12,)),
        ],
        compiler_params=params(),
        cost_estimate=cost(6 * order * volume, 12 * volume),
        name="first_step",
    )(*mains, *lows, *highs, visc_in, mat_high, mat_low)


def second_kernel(*refs):
    first, visc, mat_high, mat_low = refs[0:4]
    targets, outs = refs[4:8], refs[8:12]
    low_edge, high_edge, carry, high, low = refs[12:]
    block = outs[0].shape[1]

    def finish(f, row, piece):
        outs[f][:, row] = piece - targets[f][:, row]

    advance_rows(first, visc, 1, mat_high, mat_low, carry, high, low, block, finish)
    for f in range(fields):
        low_edge[f] = outs[f][:, 0]
        high_edge[f] = outs[f][:, block - 1]


def second_step(first, visc, mat_high, mat_low, targets):
    slabs, block, depth, width = targets[0].shape
    order = slabs * depth
    volume = fields * block * order * width
    one = jax.ShapeDtypeStruct(targets[0].shape, f32)
    edge = jax.ShapeDtypeStruct((fields, slabs, depth, width), f32)
    out = pl.pallas_call(
        second_kernel,
        in_specs=[whole()] * 8,
        out_specs=(whole(),) * 6,
        out_shape=(one,) * 4 + (edge,) * 2,
        scratch_shapes=[
            pltpu.VMEM((fields, slabs, depth, width), f32),
            pltpu.VMEM((fields, order, 2 * width), bf16),
            pltpu.VMEM((fields, order, 2 * width), bf16),
        ],
        compiler_params=params(),
        cost_estimate=cost(6 * order * volume, 12 * volume),
        name="second_step",
    )(first, visc, mat_high, mat_low, *targets)
    return out[:4], out[4], out[5]


def adjoint_kernel(*refs):
    parts = refs[0:4]
    low_edge, high_edge, first, visc, mat_high, mat_low = refs[4:10]
    outs = refs[10:14]
    cot, pulled, carry, high, low, sem = refs[14:]
    slabs, block, depth, width = outs[0].shape
    copies = []
    for f in range(fields):
        copies.append((low_edge.at[f], cot.at[f, :, 0]))
        copies.append((parts[f], cot.at[f, :, pl.ds(1, block)]))
        copies.append((high_edge.at[f], cot.at[f, :, block + 1]))
    copies = [
        pltpu.make_async_copy(source, target, sem.at[i])
        for i, (source, target) in enumerate(copies)
    ]
    for copy in copies:
        copy.start()
    for copy in copies:
        copy.wait()

    def pull(k, _):
        for f in range(fields):
            pair = [cot[f, :, 2 * k + half].reshape(slabs * depth, width) for half in range(2)]
            a, b = parts_of(jnp.concatenate(pair, axis=1))
            out = product(mat_high[f], mat_low[f], a, b)
            for half in range(2):
                piece = out[:, half * width : (half + 1) * width]
                pulled[f, :, 2 * k + half] = piece.reshape(slabs, depth, width)
        return 0

    lax.fori_loop(0, (block + 2) // 2, pull, 0)
    edge = jnp.zeros((1, width), f32)
    for p in range(slabs):
        along_y = 0.5 * (visc[p, 1] + visc[p, 2])
        for f in range(fields):
            carry[f, p] = along_y * (pulled[f, p, 1] - pulled[f, p, 0])

    def rows(k, _):
        for half in range(2):
            j = 2 * k + half + 1
            for p in range(slabs):
                here = visc[p, j + 1]
                along_x = 0.5 * (here + east(here))
                along_y = 0.5 * (here + visc[p, j + 2])
                speed = first[W, p, j]
                speed_before = first[W, p - 1, j, depth - 1 : depth] if p > 0 else edge
                speed_after = first[W, p + 1, j, 0:1] if p < slabs - 1 else edge
                coupling = pulled[T, p, j]
                for f in (U, V, T, W):
                    value = pulled[f, p, j]
                    flux_x = along_x * (east(value) - value)
                    flux_y = along_y * (pulled[f, p, j + 1] - value)
                    rate = flux_x - west(flux_x) + (flux_y - carry[f, p])
                    carry[f, p] = flux_y
                    before, after = edge, edge
                    q_before, q_after = edge, edge
                    if p > 0:
                        before = speed_before * pulled[f, p - 1, j, depth - 1 : depth]
                        q_before = first[f, p - 1, j, depth - 1 : depth]
                    if p < slabs - 1:
                        after = speed_after * pulled[f, p + 1, j, 0:1]
                        q_after = first[f, p + 1, j, 0:1]
                    rate = rate + slope(speed * value, before, after)
                    coupling = coupling - value * slope(first[f, p, j], q_before, q_after)
                    if f == T:
                        rate = rate + pulled[W, p, j]
                    if f == W:
                        rate = rate + coupling
                    a, b = parts_of(value + time_step * rate)
                    high[f, p * depth : (p + 1) * depth, half * width : (half + 1) * width] = a
                    low[f, p * depth : (p + 1) * depth, half * width : (half + 1) * width] = b
        for f in range(fields):
            out = product(mat_high[f], mat_low[f], high[f], low[f])
            for half in range(2):
                piece = out[:, half * width : (half + 1) * width]
                outs[f][:, 2 * k + half] = piece.reshape(slabs, depth, width)
        return 0

    lax.fori_loop(0, block // 2, rows, 0)


def adjoint_step(parts, low_edge, high_edge, first, visc, mat_high, mat_low):
    slabs, block, depth, width = parts[0].shape
    order = slabs * depth
    volume = fields * (block + 1) * order * width
    return pl.pallas_call(
        adjoint_kernel,
        in_specs=[anywhere()] * 6 + [whole()] * 4,
        out_specs=(whole(),) * 4,
        out_shape=(jax.ShapeDtypeStruct(parts[0].shape, f32),) * 4,
        scratch_shapes=[
            pltpu.VMEM((fields, slabs, block + 2, depth, width), f32),
            pltpu.VMEM((fields, slabs, block + 2, depth, width), f32),
            pltpu.VMEM((fields, slabs, depth, width), f32),
            pltpu.VMEM((fields, order, 2 * width), bf16),
            pltpu.VMEM((fields, order, 2 * width), bf16),
            pltpu.SemaphoreType.DMA((12,)),
        ],
        compiler_params=params(),
        cost_estimate=cost(12 * order * volume, 16 * volume),
        name="adjoint_step",
    )(*parts, low_edge, high_edge, first, visc, mat_high, mat_low)


def last_kernel(*refs):
    pulled, state, prior = refs[0:4], refs[4:8], refs[8:12]
    visc, pulled_before, pulled_after, state_before, state_after, out, carry = refs[12:]
    depth = out.shape[0] // fields // pulled_before.shape[1]
    rows = pulled_before.shape[1]

    def row_of(ref, y):
        return ref[pl.ds(pl.multiple_of(y * depth, depth), depth), :]

    along_y = 0.5 * (row_of(visc, rows - 1) + row_of(visc, 0))
    for f in range(fields):
        carry[f] = along_y * (row_of(pulled[f], 0) - row_of(pulled[f], rows - 1))

    def row(y, _):
        north = lax.rem(y + 1, rows)
        here = row_of(visc, y)
        along_x = 0.5 * (here + east(here))
        along_y = 0.5 * (here + row_of(visc, north))
        speed = row_of(state[W], y)
        one = pl.ds(y, 1)
        coupling = row_of(pulled[T], y)
        for f in (U, V, T, W):
            value = row_of(pulled[f], y)
            flux_x = along_x * (east(value) - value)
            flux_y = along_y * (row_of(pulled[f], north) - value)
            rate = flux_x - west(flux_x) + (flux_y - carry[f])
            carry[f] = flux_y
            before = state_before[W, one] * pulled_before[f, one]
            after = state_after[W, one] * pulled_after[f, one]
            rate = rate + slope(speed * value, before, after)
            q_slope = slope(row_of(state[f], y), state_before[f, one], state_after[f, one])
            coupling = coupling - value * q_slope
            if f == T:
                rate = rate + row_of(pulled[W], y)
            if f == W:
                rate = rate + coupling
            result = value + time_step * rate - row_of(prior[f], y)
            out[pl.ds(f * depth * rows + y, depth, stride=rows), :] = result
        return 0

    lax.fori_loop(0, rows, row, 0)


def last_step(pulled, state, prior, visc, edges, depth):
    total, width = visc.shape
    return pl.pallas_call(
        last_kernel,
        in_specs=[whole()] * 17,
        out_specs=whole(),
        out_shape=jax.ShapeDtypeStruct((fields * total, width), f32),
        scratch_shapes=[pltpu.VMEM((fields, depth, width), f32)],
        compiler_params=params(),
        cost_estimate=cost(30 * fields * total * width, 20 * fields * total * width),
        name="last_step",
    )(*pulled, *state, *prior, visc, *edges)


def exchange(value):
    return lax.all_to_all(value, "slab", split_axis=0, concat_axis=0, tiled=True)


def around(value, axis, steps):
    count = lax.axis_size(axis)
    return lax.ppermute(value, axis, [(i, (i + steps) % count) for i in range(count)])


def up_and_down(first_plane, last_plane):
    count = lax.axis_size("slab")
    forward = [(i, i + 1) for i in range(count - 1)]
    backward = [(target, source) for source, target in forward]
    return lax.ppermute(last_plane, "slab", forward), lax.ppermute(first_plane, "slab", backward)


def local(states, viscosity, inverse):
    start = states[0]
    _, depth, rows, width = start.shape
    slabs, segs = lax.axis_size("slab"), lax.axis_size("seg")
    block = rows // slabs
    share = -(-(block + 4) // segs)
    columns = (slabs, block, depth, width)

    visc, visc_send = visc_rows(viscosity, slabs, share)
    visc_in = lax.all_gather(exchange(visc_send), "seg", axis=0)
    state = [to_rows(start, f) for f in range(fields)]
    state_edges = up_and_down(start[:, 0], start[:, depth - 1])

    high = lax.reduce_precision(inverse, 8, 7)
    mat_high, mat_low = high.astype(bf16), (inverse - high).astype(bf16)
    adj_high, adj_low = jnp.swapaxes(mat_high, 1, 2), jnp.swapaxes(mat_low, 1, 2)

    mains = [exchange(part.reshape(columns)) for part in state]
    lows = [around(part[:, block - 2 :], "slab", 1) for part in mains]
    highs = [around(part[:, :2], "slab", -1) for part in mains]
    targets = [around(part, "seg", -1) for part in mains]

    first, frame = first_step(mains, lows, highs, visc_in, mat_high, mat_low)
    residual, low_edge, high_edge = second_step(first, frame, mat_high, mat_low, targets)
    before = around(high_edge, "slab", 1)
    after = around(low_edge, "slab", -1)
    residual_rows = [exchange(part).reshape(rows * depth, width) for part in residual]
    priors = [around(part, "seg", 1) for part in residual_rows]
    residual_out = to_planes(residual_rows, depth)

    pulled = adjoint_step(residual, before, after, first, frame, adj_high, adj_low)
    pulled = [exchange(part).reshape(rows, depth, width) for part in pulled]
    pulled_edges = up_and_down(
        jnp.stack([part[:, 0] for part in pulled]), jnp.stack([part[:, depth - 1] for part in pulled])
    )
    gradient = last_step(
        [part.reshape(rows * depth, width) for part in pulled],
        state,
        priors,
        visc,
        (*pulled_edges, *state_edges),
        depth,
    )
    return (residual_out[None], gradient.reshape(1, fields, depth, rows, width))


def solution(mesh):
    in_specs = (P("seg", None, "slab", None, None), P("slab", None, None), P())
    out_specs = (P("seg", None, "slab", None, None), P("seg", None, "slab", None, None))
    return jax.shard_map(local, mesh=mesh, in_specs=in_specs, out_specs=out_specs, check_vma=False)
```

time: 1070 us -> 639 us (0.60)
  blocking collectives: 485 us -> 179 us
  local copies, waits for them, and re-layouts: 123 us -> 20.6 us
  other arithmetic: 99.1 us -> 2.4 us
  Pallas kernels: 0 us -> 89.2 us
  starting transfers between devices: 50 us -> 83.8 us
  matrix products: 33 us -> 0 us
  waiting for transfers between devices: 267 us -> 248 us
  between operations: 1.25 us -> 14.3 us
    all_to_all x5 -> x6, blocking collectives: 485 us -> 179 us  [exchange(): lax.all_to_all(value, 'slab', split_axis=0, concat_axis=0, tiled=True)]
    pallas_call x0 -> x10, Pallas kernels: none -> 89.2 us  [the longest x1 21 us: last_step(): pl.pallas_call(last_kernel, in_specs=[whole()] * 17, out_specs=whole(), o...]
    all_to_all x3 -> x7, waiting for transfers between devices: 174 us -> 91.8 us  [exchange(): lax.all_to_all(value, 'slab', split_axis=0, concat_axis=0, tiled=True)]
    ppermute x10 -> x22, waiting for transfers between devices: 93.4 us -> 155 us  [the longest x18 147 us: around(): lax.ppermute(value, axis, [(i, (i + steps) % count) for i in range(count)])]
    slice x23 -> x4, local copies, waits for them, and re-layouts: 60.3 us -> 4.37 us  [local(): highs = [around(part[:, :2], 'slab', -1) for part in mains]]
    add x3 -> x0, other arithmetic: 54.6 us -> none  [the longest x2 37 us: advance(): state_now + time_step * (horizontal(state_now, face_visc) - state_now[2]...]
    dot_general x4 -> x0, matrix products: 33 us -> none  [apply_columns(): jnp.einsum('fzk,fkyx->fzyx', matrices, field_now, precision=lax.Precision...]
    all_to_all x3 -> x7, starting transfers between devices: 23.2 us -> 48.5 us  [exchange(): lax.all_to_all(value, 'slab', split_axis=0, concat_axis=0, tiled=True)]
  transfers between devices with their start and end apart: 13 -> 30, of which waited for: 6 -> 19; matrix products, arithmetic and copies ran while one was open for 4% -> 3% of each run, Pallas kernels for 0% -> 8%
where the time goes in v1:
time: 639 us; the launch traced here: 637 us
  waiting for transfers between devices  248 us (39%)
  blocking collectives  179 us (28%)
  Pallas kernels  89.2 us (14%)
  starting transfers between devices  83.8 us (13%)
  local copies, waits for them, and re-layouts  20.6 us (3%)
  between operations  14.3 us (2%)
    all_to_all x6, blocking collectives, exchange(): lax.all_to_all(value, 'slab', split_axis=0, concat_axis=0, tiled=True)  179 us
    ppermute x18, waiting for transfers between devices, around(): lax.ppermute(value, axis, [(i, (i + steps) % count) for i in range(count)])  147 us
    all_to_all x7, waiting for transfers between devices, exchange(): lax.all_to_all(value, 'slab', split_axis=0, concat_axis=0, tiled=True)  91.8 us
    all_to_all x7, starting transfers between devices, exchange(): lax.all_to_all(value, 'slab', split_axis=0, concat_axis=0, tiled=True)  48.5 us
    ppermute x18, starting transfers between devices, around(): lax.ppermute(value, axis, [(i, (i + steps) % count) for i in range(count)])  24.7 us
    pallas_call x1, Pallas kernels, last_step(): pl.pallas_call(last_kernel, in_specs=[whole()] * 17, out_specs=whole(), o...  21 us
    pallas_call x1, Pallas kernels, adjoint_step(): pl.pallas_call(adjoint_kernel, in_specs=[anywhere()] * 6 + [whole()] * 4,...  17.9 us
    pallas_call x1, Pallas kernels, first_step(): pl.pallas_call(functools.partial(first_kernel, share), in_specs=[anywhere...  14.6 us
  transfers between devices with their start and end apart: 30, of which 19 were waited for; matrix products, arithmetic and copies ran while one was open for 3% of the time, Pallas kernels for 8%

profile of v1, /device:TPU:9, one launch (start us, length us, event | category | flops | bytes accessed | tf_op | source)
XLA Modules:
  0.0 637.1 jit_solution(8847513916132395289)
XLA Ops:
  10.6 5.6 all-to-all-start.4
  19.5 6.1 all-to-all-done.4
  25.7 6.6 %all-to-all-start = ((f32[8,8,32,128]{3,2,1,0:T(8,128)}), f32[8,8,32,128]{3,2,1,0:T(8,128)S(1)}, u32[]{:S(2)}, u32[]{:S(2)}) async-start(f32[8,8,32,128]{3,2,1,0:T(8,128)} %bitcast.58), calls=%async_computation | async-start | bytes 2097152 | tf_op jit(solution)/shard_map/all_to_all | solution.py:423
  35.5 19.8 %all-to-all-done.refs_0_ = f32[8,8,32,128]{3,2,1,0:T(8,128)S(1)} async-done(((f32[8,8,32,128]{3,2,1,0:T(8,128)}), f32[8,8,32,128]{3,2,1,0:T(8,128)S(1)}, u32[]{:S(2)}, u32[]{:S(2)}) %all-to-all-start) | async-done | bytes 1048608 | tf_op jit(solution)/shard_map/all_to_all | solution.py:423
  55.3 7.0 %all-to-all-start.1 = ((f32[8,8,32,128]{3,2,1,0:T(8,128)}), f32[8,8,32,128]{3,2,1,0:T(8,128)S(1)}, u32[]{:S(2)}, u32[]{:S(2)}) async-start(f32[8,8,32,128]{3,2,1,0:T(8,128)} %bitcast.59), calls=%async_computation.1 | async-start | bytes 2097152 | tf_op jit(solution)/shard_map/all_to_all | solution.py:423
  65.6 19.8 %all-to-all-done.1.refs_1_ = f32[8,8,32,128]{3,2,1,0:T(8,128)S(1)} async-done(((f32[8,8,32,128]{3,2,1,0:T(8,128)}), f32[8,8,32,128]{3,2,1,0:T(8,128)S(1)}, u32[]{:S(2)}, u32[]{:S(2)}) %all-to-all-start.1) | async-done | bytes 1048608 | tf_op jit(solution)/shard_map/all_to_all | solution.py:423
  85.4 7.0 %all-to-all-start.2 = ((f32[8,8,32,128]{3,2,1,0:T(8,128)}), f32[8,8,32,128]{3,2,1,0:T(8,128)S(1)}, u32[]{:S(2)}, u32[]{:S(2)}) async-start(f32[8,8,32,128]{3,2,1,0:T(8,128)} %bitcast.60), calls=%async_computation.2 | async-start | bytes 2097152 | tf_op jit(solution)/shard_map/all_to_all | solution.py:423
  95.7 19.7 %all-to-all-done.2.refs_2_ = f32[8,8,32,128]{3,2,1,0:T(8,128)S(1)} async-done(((f32[8,8,32,128]{3,2,1,0:T(8,128)}), f32[8,8,32,128]{3,2,1,0:T(8,128)S(1)}, u32[]{:S(2)}, u32[]{:S(2)}) %all-to-all-start.2) | async-done | bytes 1048608 | tf_op jit(solution)/shard_map/all_to_all | solution.py:423
  115.4 7.7 %all-to-all-start.3 = ((f32[8,8,32,128]{3,2,1,0:T(8,128)}), f32[8,8,32,128]{3,2,1,0:T(8,128)}, u32[]{:S(2)}, u32[]{:S(2)}) async-start(f32[8,8,32,128]{3,2,1,0:T(8,128)} %bitcast.61), calls=%async_computation.3 | async-start | bytes 2097152 | tf_op jit(solution)/shard_map/all_to_all | solution.py:423
  129.5 16.8 %all-to-all-done.3.refs_3_ = f32[8,8,32,128]{3,2,1,0:T(8,128)} async-done(((f32[8,8,32,128]{3,2,1,0:T(8,128)}), f32[8,8,32,128]{3,2,1,0:T(8,128)}, u32[]{:S(2)}, u32[]{:S(2)}) %all-to-all-start.3) | async-done | bytes 1048608 | tf_op jit(solution)/shard_map/all_to_all | solution.py:423
  148.0 10.1 %collective-permute-start.3 = (f32[8,2,32,128]{3,2,1,0:T(8,128)S(1)}, f32[8,2,32,128]{3,2,1,0:T(8,128)S(1)}, u32[]{:S(2)}, u32[]{:S(2)}) collective-permute-start(f32[8,2,32,128]{3,2,1,0:T(8,128)S(1)} %get-tuple-element.43), channel_id=1, source_target_pairs={{0,1},{1,2},{2,3},{3,4},{4,5},{5,6},{6,7},{7,0},{8,9},{9,10},{10,1... | collective-permute-start | bytes 786440 | tf_op jit(solution)/shard_map/ppermute | solution.py:428
  168.1 6.4 %collective-permute-done.5.refs_9_ = f32[8,2,32,128]{3,2,1,0:T(8,128)} collective-permute-done((f32[8,2,32,128]{3,2,1,0:T(8,128)}, f32[8,2,32,128]{3,2,1,0:T(8,128)}, u32[]{:S(2)}, u32[]{:S(2)}) %collective-permute-start.5) | collective-permute-done | bytes 262176 | tf_op jit(solution)/shard_map/ppermute | solution.py:428
  187.4 14.6 %first_step.1 = (f32[4,8,10,32,128]{4,3,2,1,0:T(8,128)}, f32[8,12,32,128]{3,2,1,0:T(8,128)}) custom-call(f32[8,8,32,128]{3,2,1,0:T(8,128)} %copy-done.3, f32[8,8,32,128]{3,2,1,0:T(8,128)} %copy-done.4, f32[8,8,32,128]{3,2,1,0:T(8,128)} %copy-done.5, f32[8,8,32,128]{3,2,1,0:T(8,128)} %all-to-all-done.3.refs_3_, f32[8,2,32,128]{3,2,1,0:T(8,128)} %copy-done.9, ...), custom_call_target="tpu_custom_call" | custom-call | flops 2013265920 | bytes 15728640 | tf_op jit(solution)/shard_map/first_step/pallas_call | solution.py:202
  203.9 22.5 %collective-permute-done.8.refs_4_ = f32[8,8,32,128]{3,2,1,0:T(8,128)} collective-permute-done((f32[8,8,32,128]{3,2,1,0:T(8,128)S(1)}, f32[8,8,32,128]{3,2,1,0:T(8,128)}, u32[]{:S(2)}, u32[]{:S(2)}) %collective-permute-start.8) | collective-permute-done | bytes 1048608 | tf_op jit(solution)/shard_map/ppermute | solution.py:428
  226.4 22.5 %collective-permute-done.9.refs_5_ = f32[8,8,32,128]{3,2,1,0:T(8,128)} collective-permute-done((f32[8,8,32,128]{3,2,1,0:T(8,128)S(1)}, f32[8,8,32,128]{3,2,1,0:T(8,128)}, u32[]{:S(2)}, u32[]{:S(2)}) %collective-permute-start.9) | collective-permute-done | bytes 1048608 | tf_op jit(solution)/shard_map/ppermute | solution.py:428
  248.9 12.7 %second_step.1 = (f32[8,8,32,128]{3,2,1,0:T(8,128)}, f32[8,8,32,128]{3,2,1,0:T(8,128)}, f32[8,8,32,128]{3,2,1,0:T(8,128)}, f32[8,8,32,128]{3,2,1,0:T(8,128)}, f3...) custom-call(f32[4,8,10,32,128]{4,3,2,1,0:T(8,128)} %get-tuple-element.17.refs_0_.refs_6_, ...), custom_call_target="tpu_custom_call" | custom-call | flops 1610612736 | bytes 12582912 | tf_op jit(solution)/shard_map/second_step/pallas_call | solution.py:244
  261.6 32.2 %all_to_all.65 = f32[8,8,32,128]{3,2,1,0:T(8,128)} all-to-all(f32[8,8,32,128]{3,2,1,0:T(8,128)} %get-tuple-element.19.refs_0_), channel_id=1, replica_groups=mesh['seg'=4,'slab'=8] {'slab'}, dimensions={0} | all-to-all | bytes 2097152 | tf_op jit(solution)/shard_map/all_to_all | solution.py:423
  293.7 30.8 %all_to_all.66 = f32[8,8,32,128]{3,2,1,0:T(8,128)} all-to-all(f32[8,8,32,128]{3,2,1,0:T(8,128)} %get-tuple-element.20.refs_1_), channel_id=1, replica_groups=mesh['seg'=4,'slab'=8] {'slab'}, dimensions={0} | all-to-all | bytes 2097152 | tf_op jit(solution)/shard_map/all_to_all | solution.py:423
  324.6 29.7 %all_to_all.67 = f32[8,8,32,128]{3,2,1,0:T(8,128)} all-to-all(f32[8,8,32,128]{3,2,1,0:T(8,128)S(1)} %copy-done.7), channel_id=1, replica_groups=mesh['seg'=4,'slab'=8] {'slab'}, dimensions={0} | all-to-all | bytes 2097152 | tf_op jit(solution)/shard_map/all_to_all | solution.py:423
  354.2 7.3 %all-to-all-start.8 = ((f32[8,8,32,128]{3,2,1,0:T(8,128)}), f32[8,8,32,128]{3,2,1,0:T(8,128)}, u32[]{:S(2)}, u32[]{:S(2)}) async-start(f32[8,8,32,128]{3,2,1,0:T(8,128)} %get-tuple-element.22.refs_3_), calls=%async_computation.8 | async-start | bytes 2097152 | tf_op jit(solution)/shard_map/all_to_all | solution.py:423
  363.0 32.8 %collective-permute-done.12.refs_4_ = f32[4,8,32,128]{3,2,1,0:T(8,128)S(1)} collective-permute-done((f32[4,8,32,128]{3,2,1,0:T(8,128)S(1)}, f32[4,8,32,128]{3,2,1,0:T(8,128)S(1)}, u32[]{:S(2)}, u32[]{:S(2)}) %collective-permute-start.12) | collective-permute-done | bytes 524320 | tf_op jit(solution)/shard_map/ppermute | solution.py:428
  398.4 17.9 %adjoint_step.1 = (f32[8,8,32,128]{3,2,1,0:T(8,128)}, f32[8,8,32,128]{3,2,1,0:T(8,128)}, f32[8,8,32,128]{3,2,1,0:T(8,128)}, f32[8,8,32,128]{3,2,1,0:T(8,128)}) custom-call(f32[8,8,32,128]{3,2,1,0:T(8,128)} %get-tuple-element.19.refs_0_, f32[8,8,32,128]{3,2,1,0:T(8,128)} %get-tuple-element.20.refs_1_, f32[8,8,32,128]{3,2,1,0:T(8,128)} %get-tuple-element.21.refs_2_, ...), custom_call_target="tpu_custom_call" | custom-call | flops 3623878656 | bytes 18874368 | tf_op jit(solution)/shard_map/adjoint_step/pallas_call | solution.py:346
  416.3 27.2 %all_to_all.68 = f32[8,8,32,128]{3,2,1,0:T(8,128)S(1)} all-to-all(f32[8,8,32,128]{3,2,1,0:T(8,128)} %get-tuple-element.25), channel_id=1, replica_groups=mesh['seg'=4,'slab'=8] {'slab'}, dimensions={0} | all-to-all | bytes 2097152 | tf_op jit(solution)/shard_map/all_to_all | solution.py:423
  443.5 30.1 %all_to_all.69 = f32[8,8,32,128]{3,2,1,0:T(8,128)S(1)} all-to-all(f32[8,8,32,128]{3,2,1,0:T(8,128)} %get-tuple-element.26), channel_id=1, replica_groups=mesh['seg'=4,'slab'=8] {'slab'}, dimensions={0} | all-to-all | bytes 2097152 | tf_op jit(solution)/shard_map/all_to_all | solution.py:423
  473.5 29.0 %all_to_all.70 = f32[8,8,32,128]{3,2,1,0:T(8,128)S(1)} all-to-all(f32[8,8,32,128]{3,2,1,0:T(8,128)S(1)} %copy-done.8), channel_id=1, replica_groups=mesh['seg'=4,'slab'=8] {'slab'}, dimensions={0} | all-to-all | bytes 2097152 | tf_op jit(solution)/shard_map/all_to_all | solution.py:423
  502.5 7.3 %all-to-all-start.12 = ((f32[8,8,32,128]{3,2,1,0:T(8,128)}), f32[8,8,32,128]{3,2,1,0:T(8,128)}, u32[]{:S(2)}, u32[]{:S(2)}) async-start(f32[8,8,32,128]{3,2,1,0:T(8,128)} %get-tuple-element.28), calls=%async_computation.12 | async-start | bytes 2097152 | tf_op jit(solution)/shard_map/all_to_all | solution.py:423
  523.2 9.7 %all-to-all-done.12 = f32[8,8,32,128]{3,2,1,0:T(8,128)} async-done(((f32[8,8,32,128]{3,2,1,0:T(8,128)}), f32[8,8,32,128]{3,2,1,0:T(8,128)}, u32[]{:S(2)}, u32[]{:S(2)}) %all-to-all-start.12) | async-done | bytes 1048608 | tf_op jit(solution)/shard_map/all_to_all | solution.py:423
  550.8 6.6 %to_planes.1 = f32[4,32,64,128]{3,2,1,0:T(8,128)} custom-call(f32[2048,128]{1,0:T(8,128)} %bitcast.8.refs_0_, f32[2048,128]{1,0:T(8,128)} %bitcast.9.refs_1_, f32[2048,128]{1,0:T(8,128)} %bitcast.10.refs_2_, f32[2048,128]{1,0:T(8,128)} %bitcast.11.refs_3_), custom_call_target="tpu_custom_call" | custom-call | bytes 8388608 | tf_op jit(solution)/shard_map/to_planes/pallas_call | solution.py:116
  557.4 7.9 %collective-permute-done.15.refs_9_ = f32[2048,128]{1,0:T(8,128)} collective-permute-done((f32[2048,128]{1,0:T(8,128)}, f32[2048,128]{1,0:T(8,128)}, u32[]{:S(2)}, u32[]{:S(2)}) %collective-permute-start.15) | collective-permute-done | bytes 1048608 | tf_op jit(solution)/shard_map/ppermute | solution.py:428
  565.3 22.5 %collective-permute-done.16.refs_10_ = f32[2048,128]{1,0:T(8,128)} collective-permute-done((f32[2048,128]{1,0:T(8,128)}, f32[2048,128]{1,0:T(8,128)}, u32[]{:S(2)}, u32[]{:S(2)}) %collective-permute-start.16) | collective-permute-done | bytes 1048608 | tf_op jit(solution)/shard_map/ppermute | solution.py:428
  587.8 21.5 %collective-permute-done.17.refs_11_ = f32[2048,128]{1,0:T(8,128)} collective-permute-done((f32[2048,128]{1,0:T(8,128)}, f32[2048,128]{1,0:T(8,128)}, u32[]{:S(2)}, u32[]{:S(2)}) %collective-permute-start.17) | collective-permute-done | bytes 1048608 | tf_op jit(solution)/shard_map/ppermute | solution.py:428
  609.2 21.0 %last_step.1 = f32[8192,128]{1,0:T(8,128)} custom-call(f32[2048,128]{1,0:T(8,128)} %bitcast.62, f32[2048,128]{1,0:T(8,128)} %bitcast.63, f32[2048,128]{1,0:T(8,128)} %bitcast.64, f32[2048,128]{1,0:T(8,128)} %bitcast.18.refs_3_, f32[2048,128]{1,0:T(8,128)} %to_rows.4.refs_4_, f32[2048,128]{1,0:T(8,128)} %to_rows.5.refs_5_, f32[2048,128]{1,0:T(8,128)} %to_rows.6.refs_6_, ...), custom_call_target="tpu_custom_call" | custom-call | flops 31457280 | bytes 20971520 | tf_op jit(solution)/shard_map/last_step/pallas_call | solution.py:410
  (105 shorter events, 84.8 us)
Async XLA Ops:
  10.6 15.1 %all-to-all-start.4 = ((f32[8,3,32,128]{3,2,1,0:T(8,128)}), f32[8,3,32,128]{3,2,1,0:T(8,128)S(1)}, u32[]{:S(2)}, u32[]{:S(2)}) async-start(f32[8,3,32,128]{3,2,1,0:T(8,128)} %get-tuple-element.16), calls=%async_computation.4 | async-start | bytes 786432 | tf_op jit(solution)/shard_map/all_to_all | solution.py:423
  25.7 29.6 %all-to-all-start = ((f32[8,8,32,128]{3,2,1,0:T(8,128)}), f32[8,8,32,128]{3,2,1,0:T(8,128)S(1)}, u32[]{:S(2)}, u32[]{:S(2)}) async-start(f32[8,8,32,128]{3,2,1,0:T(8,128)} %bitcast.58), calls=%async_computation | async-start | bytes 2097152 | tf_op jit(solution)/shard_map/all_to_all | solution.py:423
  55.3 105.4 %copy-start.3 = (f32[8,8,32,128]{3,2,1,0:T(8,128)}, f32[8,8,32,128]{3,2,1,0:T(8,128)S(1)}, u32[]{:S(2)}) copy-start(f32[8,8,32,128]{3,2,1,0:T(8,128)S(1)} %all-to-all-done.refs_0_) | copy-start | bytes 3145732
  55.3 30.1 %all-to-all-start.1 = ((f32[8,8,32,128]{3,2,1,0:T(8,128)}), f32[8,8,32,128]{3,2,1,0:T(8,128)S(1)}, u32[]{:S(2)}, u32[]{:S(2)}) async-start(f32[8,8,32,128]{3,2,1,0:T(8,128)} %bitcast.59), calls=%async_computation.1 | async-start | bytes 2097152 | tf_op jit(solution)/shard_map/all_to_all | solution.py:423
  85.4 30.1 %all-to-all-start.2 = ((f32[8,8,32,128]{3,2,1,0:T(8,128)}), f32[8,8,32,128]{3,2,1,0:T(8,128)S(1)}, u32[]{:S(2)}, u32[]{:S(2)}) async-start(f32[8,8,32,128]{3,2,1,0:T(8,128)} %bitcast.60), calls=%async_computation.2 | async-start | bytes 2097152 | tf_op jit(solution)/shard_map/all_to_all | solution.py:423
  115.4 30.8 %all-to-all-start.3 = ((f32[8,8,32,128]{3,2,1,0:T(8,128)}), f32[8,8,32,128]{3,2,1,0:T(8,128)}, u32[]{:S(2)}, u32[]{:S(2)}) async-start(f32[8,8,32,128]{3,2,1,0:T(8,128)} %bitcast.61), calls=%async_computation.3 | async-start | bytes 2097152 | tf_op jit(solution)/shard_map/all_to_all | solution.py:423
  123.2 64.2 %all-gather.3.cloned.1.call-start = ((), (), s32[]{:S(2)}) async-start(), calls=%async_computation.13 | async-start | bytes 1966080 | tf_op jit(solution)/shard_map/all_gather | solution.py:447
  124.7 33.4 %collective-permute-start = (f32[8,2,32,128]{3,2,1,0:T(8,128)}, f32[8,2,32,128]{3,2,1,0:T(8,128)S(1)}, u32[]{:S(2)}, u32[]{:S(2)}) collective-permute-start(f32[8,2,32,128]{3,2,1,0:T(8,128)} %get-tuple-element.49), channel_id=1, source_target_pairs={{0,1},{1,2},{2,3},{3,4},{4,5},{5,6},{6,7},{7,0},{8,9},{9,10},{10,1... | collective-permute-start | bytes 786440 | tf_op jit(solution)/shard_map/ppermute | solution.py:428
  127.0 33.4 %collective-permute-start.1 = (f32[8,2,32,128]{3,2,1,0:T(8,128)}, f32[8,2,32,128]{3,2,1,0:T(8,128)}, u32[]{:S(2)}, u32[]{:S(2)}) collective-permute-start(f32[8,2,32,128]{3,2,1,0:T(8,128)} %get-tuple-element.47), channel_id=1, source_target_pairs={{0,1},{1,2},{2,3},{3,4},{4,5},{5,6},{6,7},{7,0},{8,9},{9,10},{10,1... | collective-permute-start | bytes 786440 | tf_op jit(solution)/shard_map/ppermute | solution.py:428
  128.0 32.6 %collective-permute-start.2 = (f32[8,2,32,128]{3,2,1,0:T(8,128)}, f32[8,2,32,128]{3,2,1,0:T(8,128)}, u32[]{:S(2)}, u32[]{:S(2)}) collective-permute-start(f32[8,2,32,128]{3,2,1,0:T(8,128)} %get-tuple-element.45), channel_id=1, source_target_pairs={{0,1},{1,2},{2,3},{3,4},{4,5},{5,6},{6,7},{7,0},{8,9},{9,10},{10,1... | collective-permute-start | bytes 786440 | tf_op jit(solution)/shard_map/ppermute | solution.py:428
  148.0 13.8 %collective-permute-start.3 = (f32[8,2,32,128]{3,2,1,0:T(8,128)S(1)}, f32[8,2,32,128]{3,2,1,0:T(8,128)S(1)}, u32[]{:S(2)}, u32[]{:S(2)}) collective-permute-start(f32[8,2,32,128]{3,2,1,0:T(8,128)S(1)} %get-tuple-element.43), channel_id=1, source_target_pairs={{0,1},{1,2},{2,3},{3,4},{4,5},{5,6},{6,7},{7,0},{8,9},{9,10},{10,1... | collective-permute-start | bytes 786440 | tf_op jit(solution)/shard_map/ppermute | solution.py:428
  158.2 9.2 %collective-permute-start.4 = (f32[8,2,32,128]{3,2,1,0:T(8,128)}, f32[8,2,32,128]{3,2,1,0:T(8,128)S(1)}, u32[]{:S(2)}, u32[]{:S(2)}) collective-permute-start(f32[8,2,32,128]{3,2,1,0:T(8,128)} %get-tuple-element.48), channel_id=1, source_target_pairs={{0,7},{1,0},{2,1},{3,2},{4,3},{5,4},{6,5},{7,6},{8,15},{9,8},{10,9... | collective-permute-start | bytes 786440 | tf_op jit(solution)/shard_map/ppermute | solution.py:428
  158.2 43.8 %collective-permute-start.10 = (f32[8,8,32,128]{3,2,1,0:T(8,128)S(1)}, f32[8,8,32,128]{3,2,1,0:T(8,128)}, u32[]{:S(2)}, u32[]{:S(2)}) collective-permute-start(f32[8,8,32,128]{3,2,1,0:T(8,128)S(1)} %all-to-all-done.2.refs_2_), channel_id=1, source_target_pairs={{0,24},{8,0},{16,8},{24,16},{1,25},{9,1},{17,9},{25,17},{2,26},{10... | collective-permute-start | bytes 3145736 | tf_op jit(solution)/shard_map/ppermute | solution.py:428
  160.4 43.6 %collective-permute-start.11 = (f32[8,8,32,128]{3,2,1,0:T(8,128)}, f32[8,8,32,128]{3,2,1,0:T(8,128)}, u32[]{:S(2)}, u32[]{:S(2)}) collective-permute-start(f32[8,8,32,128]{3,2,1,0:T(8,128)} %all-to-all-done.3.refs_3_), channel_id=1, source_target_pairs={{0,24},{8,0},{16,8},{24,16},{1,25},{9,1},{17,9},{25,17},{2,26},{10... | collective-permute-start | bytes 3145736 | tf_op jit(solution)/shard_map/ppermute | solution.py:428
  160.6 65.8 %collective-permute-start.8 = (f32[8,8,32,128]{3,2,1,0:T(8,128)S(1)}, f32[8,8,32,128]{3,2,1,0:T(8,128)}, u32[]{:S(2)}, u32[]{:S(2)}) collective-permute-start(f32[8,8,32,128]{3,2,1,0:T(8,128)S(1)} %all-to-all-done.refs_0_), channel_id=1, source_target_pairs={{0,24},{8,0},{16,8},{24,16},{1,25},{9,1},{17,9},{25,17},{2,26},{10... | collective-permute-start | bytes 3145736 | tf_op jit(solution)/shard_map/ppermute | solution.py:428
  161.8 87.1 %collective-permute-start.9 = (f32[8,8,32,128]{3,2,1,0:T(8,128)S(1)}, f32[8,8,32,128]{3,2,1,0:T(8,128)}, u32[]{:S(2)}, u32[]{:S(2)}) collective-permute-start(f32[8,8,32,128]{3,2,1,0:T(8,128)S(1)} %all-to-all-done.1.refs_1_), channel_id=1, source_target_pairs={{0,24},{8,0},{16,8},{24,16},{1,25},{9,1},{17,9},{25,17},{2,26},{10... | collective-permute-start | bytes 3145736 | tf_op jit(solution)/shard_map/ppermute | solution.py:428
  168.1 6.4 %collective-permute-start.5 = (f32[8,2,32,128]{3,2,1,0:T(8,128)}, f32[8,2,32,128]{3,2,1,0:T(8,128)}, u32[]{:S(2)}, u32[]{:S(2)}) collective-permute-start(f32[8,2,32,128]{3,2,1,0:T(8,128)} %get-tuple-element.46), channel_id=1, source_target_pairs={{0,7},{1,0},{2,1},{3,2},{4,3},{5,4},{6,5},{7,6},{8,15},{9,8},{10,9... | collective-permute-start | bytes 786440 | tf_op jit(solution)/shard_map/ppermute | solution.py:428
  174.5 6.4 %collective-permute-start.6 = (f32[8,2,32,128]{3,2,1,0:T(8,128)}, f32[8,2,32,128]{3,2,1,0:T(8,128)}, u32[]{:S(2)}, u32[]{:S(2)}) collective-permute-start(f32[8,2,32,128]{3,2,1,0:T(8,128)} %get-tuple-element.44), channel_id=1, source_target_pairs={{0,7},{1,0},{2,1},{3,2},{4,3},{5,4},{6,5},{7,6},{8,15},{9,8},{10,9... | collective-permute-start | bytes 786440 | tf_op jit(solution)/shard_map/ppermute | solution.py:428
  180.9 6.5 %collective-permute-start.7 = (f32[8,2,32,128]{3,2,1,0:T(8,128)}, f32[8,2,32,128]{3,2,1,0:T(8,128)}, u32[]{:S(2)}, u32[]{:S(2)}) collective-permute-start(f32[8,2,32,128]{3,2,1,0:T(8,128)} %get-tuple-element.42), channel_id=1, source_target_pairs={{0,7},{1,0},{2,1},{3,2},{4,3},{5,4},{6,5},{7,6},{8,15},{9,8},{10,9... | collective-permute-start | bytes 786440 | tf_op jit(solution)/shard_map/ppermute | solution.py:428
  261.6 101.4 %copy-start.16 = (f32[4,8,32,128]{3,2,1,0:T(8,128)S(1)}, f32[4,8,32,128]{3,2,1,0:T(8,128)}, u32[]{:S(2)}) copy-start(f32[4,8,32,128]{3,2,1,0:T(8,128)} %get-tuple-element.24) | copy-start | bytes 1572868
  354.2 62.0 %all-to-all-start.8 = ((f32[8,8,32,128]{3,2,1,0:T(8,128)}), f32[8,8,32,128]{3,2,1,0:T(8,128)}, u32[]{:S(2)}, u32[]{:S(2)}) async-start(f32[8,8,32,128]{3,2,1,0:T(8,128)} %get-tuple-element.22.refs_3_), calls=%async_computation.8 | async-start | bytes 2097152 | tf_op jit(solution)/shard_map/all_to_all | solution.py:423
  361.5 34.2 %collective-permute-start.12 = (f32[4,8,32,128]{3,2,1,0:T(8,128)S(1)}, f32[4,8,32,128]{3,2,1,0:T(8,128)S(1)}, u32[]{:S(2)}, u32[]{:S(2)}) collective-permute-start(f32[4,8,32,128]{3,2,1,0:T(8,128)S(1)} %copy-done.17), channel_id=1, source_target_pairs={{0,1},{1,2},{2,3},{3,4},{4,5},{5,6},{6,7},{7,0},{8,9},{9,10},{10,1... | collective-permute-start | bytes 1572872 | tf_op jit(solution)/shard_map/ppermute | solution.py:428
  363.0 34.6 %collective-permute-start.13 = (f32[4,8,32,128]{3,2,1,0:T(8,128)S(1)}, f32[4,8,32,128]{3,2,1,0:T(8,128)S(1)}, u32[]{:S(2)}, u32[]{:S(2)}) collective-permute-start(f32[4,8,32,128]{3,2,1,0:T(8,128)S(1)} %copy-done.16), channel_id=1, source_target_pairs={{0,7},{1,0},{2,1},{3,2},{4,3},{5,4},{6,5},{7,6},{8,15},{9,8},{10,9... | collective-permute-start | bytes 1572872 | tf_op jit(solution)/shard_map/ppermute | solution.py:428
  502.5 30.3 %all-to-all-start.12 = ((f32[8,8,32,128]{3,2,1,0:T(8,128)}), f32[8,8,32,128]{3,2,1,0:T(8,128)}, u32[]{:S(2)}, u32[]{:S(2)}) async-start(f32[8,8,32,128]{3,2,1,0:T(8,128)} %get-tuple-element.28), calls=%async_computation.12 | async-start | bytes 2097152 | tf_op jit(solution)/shard_map/all_to_all | solution.py:423
  512.3 23.1 %collective-permute-start.20 = (f32[4,64,128]{2,1,0:T(8,128)S(1)}, f32[4,64,128]{2,1,0:T(8,128)S(1)}, u32[]{:S(2)}, u32[]{:S(2)}) collective-permute-start(f32[4,64,128]{2,1,0:T(8,128)S(1)} %get-tuple-element.31), channel_id=1, source_target_pairs={{0,1},{1,2},{2,3},{3,4},{4,5},{5,6},{6,7},{8,9},{9,10},{10,11},{11... | collective-permute-start | bytes 393224 | tf_op jit(solution)/shard_map/ppermute | solution.py:435
  515.7 41.7 %collective-permute-start.14 = (f32[2048,128]{1,0:T(8,128)}, f32[2048,128]{1,0:T(8,128)}, u32[]{:S(2)}, u32[]{:S(2)}) collective-permute-start(f32[2048,128]{1,0:T(8,128)} %bitcast.8.refs_0_), channel_id=1, source_target_pairs={{0,8},{8,16},{16,24},{24,0},{1,9},{9,17},{17,25},{25,1},{2,10},{10... | collective-permute-start | bytes 3145736 | tf_op jit(solution)/shard_map/ppermute | solution.py:428
  517.8 47.4 %collective-permute-start.15 = (f32[2048,128]{1,0:T(8,128)}, f32[2048,128]{1,0:T(8,128)}, u32[]{:S(2)}, u32[]{:S(2)}) collective-permute-start(f32[2048,128]{1,0:T(8,128)} %bitcast.9.refs_1_), channel_id=1, source_target_pairs={{0,8},{8,16},{16,24},{24,0},{1,9},{9,17},{17,25},{25,1},{2,10},{10... | collective-permute-start | bytes 3145736 | tf_op jit(solution)/shard_map/ppermute | solution.py:428
  518.2 69.6 %collective-permute-start.16 = (f32[2048,128]{1,0:T(8,128)}, f32[2048,128]{1,0:T(8,128)}, u32[]{:S(2)}, u32[]{:S(2)}) collective-permute-start(f32[2048,128]{1,0:T(8,128)} %bitcast.10.refs_2_), channel_id=1, source_target_pairs={{0,8},{8,16},{16,24},{24,0},{1,9},{9,17},{17,25},{25,1},{2,10},{10... | collective-permute-start | bytes 3145736 | tf_op jit(solution)/shard_map/ppermute | solution.py:428
  520.3 88.9 %collective-permute-start.17 = (f32[2048,128]{1,0:T(8,128)}, f32[2048,128]{1,0:T(8,128)}, u32[]{:S(2)}, u32[]{:S(2)}) collective-permute-start(f32[2048,128]{1,0:T(8,128)} %bitcast.11.refs_3_), channel_id=1, source_target_pairs={{0,8},{8,16},{16,24},{24,0},{1,9},{9,17},{17,25},{25,1},{2,10},{10... | collective-permute-start | bytes 3145736 | tf_op jit(solution)/shard_map/ppermute | solution.py:428
  535.5 6.7 %collective-permute-start.21 = (f32[4,64,128]{2,1,0:T(8,128)S(1)}, f32[4,64,128]{2,1,0:T(8,128)S(1)}, u32[]{:S(2)}, u32[]{:S(2)}) collective-permute-start(f32[4,64,128]{2,1,0:T(8,128)S(1)} %get-tuple-element.30), channel_id=1, source_target_pairs={{1,0},{2,1},{3,2},{4,3},{5,4},{6,5},{7,6},{9,8},{10,9},{11,10},{12... | collective-permute-start | bytes 393224 | tf_op jit(solution)/shard_map/ppermute | solution.py:435
  542.2 6.7 %collective-permute-start.19 = (f32[4,64,128]{2,1,0:T(8,128)S(1)}, f32[4,64,128]{2,1,0:T(8,128)S(1)}, u32[]{:S(2)}, u32[]{:S(2)}) collective-permute-start(f32[4,64,128]{2,1,0:T(8,128)S(1)} %pad_maximum_fusion.1), channel_id=1, source_target_pairs={{1,0},{2,1},{3,2},{4,3},{5,4},{6,5},{7,6},{9,8},{10,9},{11,10},{12... | collective-permute-start | bytes 393224 | tf_op jit(solution)/shard_map/ppermute | solution.py:435
  548.9 8.5 %collective-permute-start.18 = (f32[4,64,128]{2,1,0:T(8,128)S(1)}, f32[4,64,128]{2,1,0:T(8,128)S(1)}, u32[]{:S(2)}, u32[]{:S(2)}) collective-permute-start(f32[4,64,128]{2,1,0:T(8,128)S(1)} %pad_maximum_fusion), channel_id=1, source_target_pairs={{0,1},{1,2},{2,3},{3,4},{4,5},{5,6},{6,7},{8,9},{9,10},{10,11},{11... | collective-permute-start | bytes 393224 | tf_op jit(solution)/shard_map/ppermute | solution.py:435
  (18 other events, 664.0 us)
Sparse Core Ops, SparseCore 0:
  125.8 31.6 all-gather.2

commit v2 on v0

v2 whole, which is shorter than its diff:
```python
import functools

import jax
import jax.numpy as jnp
from jax import lax
from jax.experimental import pallas as pl
from jax.experimental.pallas import tpu as pltpu
from jax.sharding import PartitionSpec as P

time_step = 0.1
vmem_bytes = 56 * 1024 * 1024
f32, bf16 = jnp.float32, jnp.bfloat16
U, V, W, T = range(4)
fields = 4
pad = 8
tall = 32


def whole():
    return pl.BlockSpec(memory_space=pltpu.VMEM)


def anywhere():
    return pl.BlockSpec(memory_space=pl.ANY)


def scalars():
    return pl.BlockSpec(memory_space=pltpu.SMEM)


def vmem(*shape):
    return pltpu.VMEM(shape, f32)


def dmas(count):
    return pltpu.SemaphoreType.DMA((count,))


def call(kernel, ins, outs, scratch, flops, name, kind=f32):
    moved = sum(4 * x.size for x, _ in ins)
    return pl.pallas_call(
        kernel,
        in_specs=[spec for _, spec in ins],
        out_specs=tuple(spec for _, spec in outs),
        out_shape=tuple(jax.ShapeDtypeStruct(shape, kind) for shape, _ in outs),
        scratch_shapes=scratch,
        compiler_params=pltpu.CompilerParams(vmem_limit_bytes=vmem_bytes),
        cost_estimate=pl.CostEstimate(flops=flops, bytes_accessed=moved, transcendentals=0),
        name=name,
    )(*[x for x, _ in ins])


def start_all(pairs, sem):
    copies = [
        pltpu.make_async_copy(source, target, sem.at[i])
        for i, (source, target) in enumerate(pairs)
    ]
    for copy in copies:
        copy.start()
    return copies


def wait_all(copies):
    for copy in copies:
        copy.wait()


def east(value):
    return pltpu.roll(value, value.shape[1] - 1, 1)


def west(value):
    return pltpu.roll(value, 1, 1)


def parts_of(value):
    high = value.astype(bf16)
    return high, (value - high.astype(f32)).astype(bf16)


def product(matrix_high, matrix_low, high, low):
    dot = functools.partial(jnp.dot, preferred_element_type=f32)
    return dot(matrix_high, high) + (dot(matrix_high, low) + dot(matrix_low, high))


def split_kernel(x_ref, high, low, adj_high, adj_low):
    for f in range(fields):
        high[f], low[f] = parts_of(x_ref[f])
        adj_high[f], adj_low[f] = parts_of(x_ref[f].T)


def split(inverse):
    return call(
        split_kernel,
        [(inverse, whole())],
        [(inverse.shape, whole())] * 4,
        [],
        0,
        "split",
        bf16,
    )


def chunks_kernel(own, x_ref, visc_in, send, visc, edges, planes, held, extra, flat, sem):
    slabs, block = held.shape[1:3]
    rows, depth, _ = visc.shape
    share = extra.shape[1]
    visc_copy = pltpu.make_async_copy(visc_in, flat, sem.at[2 * fields])
    visc_copy.start()
    copies = start_all([(x_ref.at[f], planes.at[f]) for f in range(fields)], sem)
    visc_copy.wait()
    for y in range(rows):
        visc[y] = flat[pl.ds(y, depth, stride=rows), :]
    for p in range(slabs):
        for i in range(share):
            row = lax.rem(p * block - 2 + share * own[0] + i + rows, rows)
            extra[p, i] = visc[row]
    leaving = [
        pltpu.make_async_copy(extra, send.at[:, pl.ds(fields * block, share)], sem.at[2 * fields])
    ]
    leaving[0].start()
    for f in range(fields):
        copies[f].wait()
        for y in range(rows):
            held[f, y // block, y % block] = planes[f, pl.ds(y, depth, stride=rows), :]
        leaving.append(
            pltpu.make_async_copy(
                held.at[f], send.at[:, pl.ds(f * block, block)], sem.at[fields + f]
            )
        )
        leaving[-1].start()
        edges[0, f] = planes[f, pl.ds(0, rows), :]
        edges[1, f] = planes[f, pl.ds((depth - 1) * rows, rows), :]
    wait_all(leaving)


def to_chunks(states, viscosity, slabs, share):
    _, depth, rows, width = states.shape
    block = rows // slabs
    own = jnp.full((1,), lax.axis_index("seg"), jnp.int32)
    return call(
        chunks_kernel,
        [
            (own, scalars()),
            (states.reshape(fields, -1, width), anywhere()),
            (viscosity.reshape(-1, width), anywhere()),
        ],
        [
            ((slabs, fields * block + share, depth, width), anywhere()),
            ((rows, depth, width), whole()),
            ((2, fields, rows, width), whole()),
        ],
        [
            vmem(fields, depth * rows, width),
            vmem(fields, slabs, block, depth, width),
            vmem(slabs, share, depth, width),
            vmem(depth * rows, width),
            dmas(2 * fields + 1),
        ],
        0,
        "to_chunks",
    )


def planes_kernel(half, other, target, _, o_ref, held, sem):
    slabs, _, block, depth, _ = half.shape
    rows = slabs * block
    pairs = []
    for p in range(slabs):
        place = pl.ds(p * block, block)
        pairs.append((half.at[p], held.at[pl.ds(0, 2), place]))
        pairs.append((other.at[p], held.at[pl.ds(2, 2), place]))
    wait_all(start_all(pairs, sem))

    def row(y, _):
        for f in range(fields):
            where = pl.ds(f * depth * rows + y, depth, stride=rows)
            o_ref[where, :] = held[f, y] - target[where, :]
        return 0

    lax.fori_loop(0, rows, row, 0, unroll=4)


def residual_planes(halves, target, later):
    slabs, _, block, depth, width = halves[0].shape
    return call(
        planes_kernel,
        [(halves[0], anywhere()), (halves[1], anywhere())]
        + [(target.reshape(-1, width), whole()), (later, anywhere())],
        [((fields * depth * slabs * block, width), whole())],
        [vmem(fields, slabs * block, depth, width), dmas(2 * slabs)],
        0,
        "residual_planes",
    )[0]


def clear_pads(ref):
    edge = jnp.zeros(ref.shape[1:2] + (pad, ref.shape[3]), f32)
    for f in range(fields):
        ref[f, :, 0:pad] = edge
        ref[f, :, ref.shape[2] - pad :] = edge


def first_fluxes(state, visc, shift, carry):
    order = visc.shape[1]
    for z in range(0, order, tall):
        here, pads = pl.ds(z, tall), pl.ds(z + pad, tall)
        along_y = 0.5 * (visc[shift, here] + visc[shift + 1, here])
        for f in range(fields):
            carry[f, here] = along_y * (state[f, 1, pads] - state[f, 0, pads])


def spread_of(state, f, j, value, here, pads, along_x, along_y, carry):
    flux_x = along_x * (east(value) - value)
    flux_y = along_y * (state[f, j + 1, pads] - value)
    spread = flux_x - west(flux_x) + (flux_y - carry[f, here])
    carry[f, here] = flux_y
    return spread


def advance_rows(state, visc, shift, mat_high, mat_low, carry, high, low, count, finish):
    order, width = visc.shape[1:]
    first_fluxes(state, visc, shift, carry)

    def pair(k, _):
        for half in range(2):
            j = 2 * k + half + 1
            side = slice(half * width, (half + 1) * width)
            for z in range(0, order, tall):
                here, pads = pl.ds(z, tall), pl.ds(z + pad, tall)
                above, below = pl.ds(z + pad + 1, tall), pl.ds(z + pad - 1, tall)
                own = visc[j + shift, here]
                along_x = 0.5 * (own + east(own))
                along_y = 0.5 * (own + visc[j + shift + 1, here])
                speed = state[W, j, pads]
                for f in range(fields):
                    value = state[f, j, pads]
                    rate = spread_of(state, f, j, value, here, pads, along_x, along_y, carry)
                    rate = rate - speed * (state[f, j, above] - state[f, j, below])
                    if f == W:
                        rate = rate + state[T, j, pads]
                    if f == T:
                        rate = rate + speed
                    high[f, here, side], low[f, here, side] = parts_of(value + time_step * rate)
        for f in range(fields):
            out = product(mat_high[f], mat_low[f], high[f], low[f])
            finish(f, 2 * k, out[:, :width])
            finish(f, 2 * k + 1, out[:, width:])
        return 0

    lax.fori_loop(0, count // 2, pair, 0)


def step_scratch(order, width):
    return [
        vmem(fields, order, width),
        pltpu.VMEM((fields, order, 2 * width), bf16),
        pltpu.VMEM((fields, order, 2 * width), bf16),
    ]


def first_kernel(chunks, low_in, high_in, visc_in, mat_high, mat_low, first, visc, *scratch):
    state, carry, high, low, sem = scratch
    slabs, _, _, depth, _ = low_in.shape
    segs, _, share = visc_in.shape[:3]
    block = first.shape[1] - 2
    order = visc.shape[1]
    pairs = []
    for p in range(slabs):
        planes, padded = pl.ds(p * depth, depth), pl.ds(p * depth + pad, depth)
        for f in range(fields):
            source = chunks.at[p, pl.ds(f * block, block)]
            pairs.append((source, state.at[f, pl.ds(2, block), padded]))
        pairs.append((low_in.at[p], state.at[:, pl.ds(0, 2), padded]))
        pairs.append((high_in.at[p], state.at[:, pl.ds(block + 2, 2), padded]))
        for s in range(segs):
            pairs.append((visc_in.at[s, p], visc.at[pl.ds(share * s, share), planes]))
    copies = start_all(pairs, sem)
    clear_pads(state)
    clear_pads(first)
    wait_all(copies)

    def finish(f, row, piece):
        first[f, row, pl.ds(pad, order)] = piece

    advance_rows(state, visc, 0, mat_high, mat_low, carry, high, low, block + 2, finish)


def first_step(chunks, low_in, high_in, visc_in, mat_high, mat_low):
    slabs, _, depth, width = chunks.shape
    segs, _, share = visc_in.shape[:3]
    block = (chunks.shape[1] - share) // fields
    order = slabs * depth
    volume = fields * (block + 2) * order * width
    return call(
        first_kernel,
        [(x, anywhere()) for x in (chunks, low_in, high_in, visc_in)]
        + [(mat_high, whole()), (mat_low, whole())],
        [
            ((fields, block + 2, order + 2 * pad, width), whole()),
            ((segs * share, order, width), whole()),
        ],
        [vmem(fields, block + 4, order + 2 * pad, width)]
        + step_scratch(order, width)
        + [dmas(slabs * (fields + 2 + segs))],
        6 * order * volume,
        "first_step",
    )


def second_kernel(first, visc, mat_high, mat_low, half, other, carry, high, low, held, sem):
    slabs, _, block, depth, _ = half.shape

    def finish(f, row, piece):
        held[f, row] = piece

    advance_rows(first, visc, 1, mat_high, mat_low, carry, high, low, block, finish)
    pairs = []
    for p in range(slabs):
        planes = pl.ds(p * depth, depth)
        pairs.append((held.at[pl.ds(0, 2), :, planes], half.at[p]))
        pairs.append((held.at[pl.ds(2, 2), :, planes], other.at[p]))
    wait_all(start_all(pairs, sem))


def second_step(first, visc, mat_high, mat_low, slabs):
    _, block, _, width = first.shape
    block, order = block - 2, visc.shape[1]
    return call(
        second_kernel,
        [(x, whole()) for x in (first, visc, mat_high, mat_low)],
        [((slabs, 2, block, order // slabs, width), anywhere())] * 2,
        step_scratch(order, width) + [vmem(fields, block, order, width), dmas(2 * slabs)],
        6 * order * fields * block * order * width,
        "second_step",
    )


def outer_kernel(chunks, _, low_rows, high_rows, visc, sem):
    share = visc.shape[1]
    block = (chunks.shape[1] - share) // fields
    pairs = []
    for f in range(fields):
        pairs.append((chunks.at[:, pl.ds((f + 1) * block - 2, 2)], high_rows.at[:, f]))
        pairs.append((chunks.at[:, pl.ds(f * block, 2)], low_rows.at[:, f]))
    pairs.append((chunks.at[:, pl.ds(fields * block, share)], visc))
    wait_all(start_all(pairs, sem))


def outer_rows(chunks, share, later):
    slabs, _, depth, width = chunks.shape
    rows = ((slabs, fields, 2, depth, width), anywhere())
    return call(
        outer_kernel,
        [(chunks, anywhere()), (later, anywhere())],
        [rows, rows, ((slabs, share, depth, width), anywhere())],
        [dmas(2 * fields + 1)],
        0,
        "outer_rows",
    )


def edge_kernel(half, other, target, _, low_edge, high_edge, ours, theirs, sem):
    block = half.shape[2]
    pairs = []
    for side, row in ((0, 0), (1, block - 1)):
        for f in range(fields):
            source = (half, other)[f // 2]
            pairs.append((source.at[:, f % 2, row], ours.at[side, f]))
            pairs.append((target.at[:, f * block + row], theirs.at[side, f]))
    wait_all(start_all(pairs, sem))
    for f in range(fields):
        low_edge[:, f] = ours[0, f] - theirs[0, f]
        high_edge[:, f] = ours[1, f] - theirs[1, f]


def edge_rows(halves, target, later):
    slabs, _, _, depth, width = halves[0].shape
    edge = ((slabs, fields, depth, width), whole())
    both = vmem(2, fields, slabs, depth, width)
    return call(
        edge_kernel,
        [(x, anywhere()) for x in (*halves, target, later)],
        [edge, edge],
        [both, both, dmas(4 * fields)],
        0,
        "edge_rows",
    )


def adjoint_kernel(half, other, target, low_edge, high_edge, *refs):
    first, visc, mat_high, mat_low = refs[:4]
    out, cot, less, pulled, ends, carry, high, low, sem = refs[4:]
    slabs, _, block, depth, width = half.shape
    order = slabs * depth
    main = pl.ds(1, block)
    pairs = []
    for p in range(slabs):
        planes = pl.ds(p * depth, depth)
        pairs.append((half.at[p], cot.at[pl.ds(0, 2), main, planes]))
        pairs.append((other.at[p], cot.at[pl.ds(2, 2), main, planes]))
        for f in range(fields):
            source = target.at[p, pl.ds(f * block, block)]
            pairs.append((source, less.at[f, main, planes]))
        pairs.append((low_edge.at[p], cot.at[:, 0, planes]))
        pairs.append((high_edge.at[p], cot.at[:, block + 1, planes]))
    copies = start_all(pairs, sem)
    clear_pads(pulled)
    for f in range(fields):
        less[f, 0] = jnp.zeros((order, width), f32)
        less[f, block + 1] = jnp.zeros((order, width), f32)
    wait_all(copies)

    def pull(k, _):
        for f in range(fields):
            pair = [cot[f, 2 * k + i] - less[f, 2 * k + i] for i in range(2)]
            pair = jnp.concatenate(pair, axis=1)
            out = product(mat_high[f], mat_low[f], *parts_of(pair))
            pulled[f, 2 * k, pl.ds(pad, order)] = out[:, :width]
            pulled[f, 2 * k + 1, pl.ds(pad, order)] = out[:, width:]
        return 0

    lax.fori_loop(0, (block + 2) // 2, pull, 0)
    first_fluxes(pulled, visc, 1, carry)

    def rows(k, _):
        for half in range(2):
            j = 2 * k + half + 1
            side = slice(half * width, (half + 1) * width)
            for z in range(0, order, tall):
                here, pads = pl.ds(z, tall), pl.ds(z + pad, tall)
                above, below = pl.ds(z + pad + 1, tall), pl.ds(z + pad - 1, tall)
                own = visc[j + 1, here]
                along_x = 0.5 * (own + east(own))
                along_y = 0.5 * (own + visc[j + 2, here])
                speed_above, speed_below = first[W, j, above], first[W, j, below]
                coupling = pulled[T, j, pads]
                for f in (U, V, T, W):
                    value = pulled[f, j, pads]
                    rate = spread_of(pulled, f, j, value, here, pads, along_x, along_y, carry)
                    up, down = pulled[f, j, above], pulled[f, j, below]
                    rate = rate + (speed_above * up - speed_below * down)
                    if f == W:
                        slope = speed_above - speed_below
                    else:
                        slope = first[f, j, above] - first[f, j, below]
                    coupling = coupling - value * slope
                    if f == T:
                        rate = rate + pulled[W, j, pads]
                    if f == W:
                        rate = rate + coupling
                    high[f, here, side], low[f, here, side] = parts_of(value + time_step * rate)
        for f in range(fields):
            out = product(mat_high[f], mat_low[f], high[f], low[f])
            cot[f, 2 * k + 1] = out[:, :width]
            cot[f, 2 * k + 2] = out[:, width:]
        return 0

    lax.fori_loop(0, block // 2, rows, 0)
    pairs = []
    for p in range(slabs):
        for f in range(fields):
            source = cot.at[f, main, pl.ds(p * depth, depth)]
            pairs.append((source, out.at[p, pl.ds(f * block, block)]))
    copies = start_all(pairs, sem)
    for p in range(slabs):
        for f in range(fields):
            for y in range(block):
                for side, z in ((0, p * depth - 1), (1, (p + 1) * depth)):
                    to = slice(f * block + y, f * block + y + 1)
                    if 0 <= z < order:
                        ends[p, side, to] = cot[f, y + 1, z : z + 1]
                    else:
                        ends[p, side, to] = jnp.zeros((1, width), f32)
    ends_copy = pltpu.make_async_copy(
        ends, out.at[:, pl.ds(fields * block, 2)], sem.at[len(pairs)]
    )
    ends_copy.start()
    wait_all(copies)
    ends_copy.wait()


def adjoint_step(halves, target, low_edge, high_edge, first, visc, mat_high, mat_low):
    slabs, _, block, depth, width = halves[0].shape
    order = slabs * depth
    volume = fields * (block + 1) * order * width
    return call(
        adjoint_kernel,
        [(x, anywhere()) for x in (*halves, target, low_edge, high_edge)]
        + [(x, whole()) for x in (first, visc, mat_high, mat_low)],
        [((slabs, fields * block + 2, depth, width), anywhere())],
        [
            vmem(fields, block + 2, order, width),
            vmem(fields, block + 2, order, width),
            vmem(fields, block + 2, order + 2 * pad, width),
            vmem(slabs, 2, depth, width),
        ]
        + step_scratch(order, width)
        + [dmas(slabs * (fields + 4))],
        12 * order * volume,
        "adjoint_step",
    )[0]


def last_kernel(visc, edges_below, edges_above, prior, chunks, states, out, *scratch):
    pulled, state, ends, carry, sem = scratch
    slabs = chunks.shape[0]
    rows, depth, width = visc.shape
    block = rows // slabs
    pairs = []
    for p in range(slabs):
        for f in range(fields):
            source, place = pl.ds(f * block, block), pl.ds(p * block, block)
            pairs.append((chunks.at[p, source], pulled.at[f, place, pl.ds(pad, depth)]))
            pairs.append((states.at[p, source], state.at[f, place, pl.ds(pad, depth)]))
    pairs.append((chunks.at[:, pl.ds(fields * block, 2)], ends))
    copies = start_all(pairs, sem)
    first, last = slice(pad - 1, pad), slice(pad + depth, pad + depth + 1)
    for f in range(fields):
        for y in range(rows):
            state[f, y, first] = edges_below[f, y : y + 1]
            state[f, y, last] = edges_above[f, y : y + 1]
    wait_all(copies)
    for f in range(fields):
        for y in range(rows):
            row = f * block + y % block
            pulled[f, y, first] = ends[y // block, 0, row : row + 1]
            pulled[f, y, last] = ends[y // block, 1, row : row + 1]
    here = pl.ds(pad, depth)
    above, below = pl.ds(pad + 1, depth), pl.ds(pad - 1, depth)
    along_y = 0.5 * (visc[rows - 1] + visc[0])
    for f in range(fields):
        carry[f] = along_y * (pulled[f, 0, here] - pulled[f, rows - 1, here])

    def row(y, _):
        north = lax.rem(y + 1, rows)
        own = visc[y]
        along_x = 0.5 * (own + east(own))
        along_y = 0.5 * (own + visc[north])
        speed_above, speed_below = state[W, y, above], state[W, y, below]
        coupling = pulled[T, y, here]
        for f in (U, V, T, W):
            value = pulled[f, y, here]
            flux_x = along_x * (east(value) - value)
            flux_y = along_y * (pulled[f, north, here] - value)
            rate = flux_x - west(flux_x) + (flux_y - carry[f])
            carry[f] = flux_y
            up, down = pulled[f, y, above], pulled[f, y, below]
            rate = rate + (speed_above * up - speed_below * down)
            if f == W:
                slope = speed_above - speed_below
            else:
                slope = state[f, y, above] - state[f, y, below]
            coupling = coupling - value * slope
            if f == T:
                rate = rate + pulled[W, y, here]
            if f == W:
                rate = rate + coupling
            where = pl.ds(f * depth * rows + y, depth, stride=rows)
            out[where, :] = value + time_step * rate - prior[where, :]
        return 0

    lax.fori_loop(0, rows, row, 0, unroll=4)


def last_step(visc, below, above, prior, chunks, states):
    rows, depth, width = visc.shape
    slabs = chunks.shape[0]
    return call(
        last_kernel,
        [(x, whole()) for x in (visc, below, above, prior)]
        + [(chunks, anywhere()), (states, anywhere())],
        [((fields * depth * rows, width), whole())],
        [
            vmem(fields, rows, depth + 2 * pad, width),
            vmem(fields, rows, depth + 2 * pad, width),
            vmem(slabs, 2, depth, width),
            vmem(fields, depth, width),
            dmas(2 * fields * slabs + 1),
        ],
        30 * fields * rows * depth * width,
        "last_step",
    )[0]


def exchange(chunks):
    return lax.all_to_all(chunks, "slab", split_axis=0, concat_axis=0, tiled=True)


def around(value, axis, steps):
    count = lax.axis_size(axis)
    return lax.ppermute(value, axis, [(i, (i + steps) % count) for i in range(count)])


def local(states, viscosity, inverse):
    start = states[0]
    _, depth, rows, width = start.shape
    slabs, segs = lax.axis_size("slab"), lax.axis_size("seg")
    block = rows // slabs
    share = -(-(block + 4) // segs)

    send, visc, ends = to_chunks(start, viscosity, slabs, share)
    target_planes = around(start, "seg", -1)
    chunks = exchange(send)
    forward = [(i, i + 1) for i in range(slabs - 1)]
    below = lax.ppermute(ends[1], "slab", forward)
    above = lax.ppermute(ends[0], "slab", [(i, j) for j, i in forward])
    mat_high, mat_low, adj_high, adj_low = split(inverse)

    low_rows, high_rows, visc_rows = outer_rows(chunks, share, target_planes)
    low_in = around(high_rows, "slab", 1)
    high_in = around(low_rows, "slab", -1)
    visc_in = lax.all_gather(visc_rows, "seg", axis=0)
    target = around(chunks, "seg", -1)

    first, frame = first_step(chunks, low_in, high_in, visc_in, mat_high, mat_low)
    halves = second_step(first, frame, mat_high, mat_low, slabs)
    half = exchange(halves[0])
    low_edge, high_edge = edge_rows(halves, target, half)
    low_edge, high_edge = around(high_edge, "slab", 1), around(low_edge, "slab", -1)
    pulled = adjoint_step(halves, target, low_edge, high_edge, first, frame, adj_high, adj_low)
    other = exchange(halves[1])
    residual = residual_planes((half, other), target_planes, pulled)
    prior = around(residual, "seg", 1)
    gradient = last_step(visc, below, above, prior, exchange(pulled), send)
    shape = (1, fields, depth, rows, width)
    return (residual.reshape(shape), gradient.reshape(shape))


def solution(mesh):
    in_specs = (P("seg", None, "slab", None, None), P("slab", None, None), P())
    out_specs = (P("seg", None, "slab", None, None), P("seg", None, "slab", None, None))
    return jax.shard_map(local, mesh=mesh, in_specs=in_specs, out_specs=out_specs, check_vma=False)
```

time: 1070 us -> 540 us (0.50)
  blocking collectives: 485 us -> 0 us
  Pallas kernels: 0 us -> 169 us
  local copies, waits for them, and re-layouts: 123 us -> 0.84 us
  other arithmetic: 99.1 us -> 0 us
  waiting for transfers between devices: 267 us -> 315 us
  matrix products: 33 us -> 0 us
  between operations: 1.25 us -> 14.2 us
  starting transfers between devices: 50 us -> 38.5 us
    all_to_all x5 -> x0, blocking collectives: 485 us -> none  [the longest x4 387 us: line_solve(): lax.all_to_all(field_now, 'slab', split_axis=2, concat_axis=1, tiled=True)]
    pallas_call x0 -> x9, Pallas kernels: none -> 169 us  [call(): pl.pallas_call(kernel, in_specs=[spec for _, spec in ins], out_specs=tupl...]
    ppermute x10 -> x9, waiting for transfers between devices: 93.4 us -> 257 us  [the longest x7 180 us: around(): lax.ppermute(value, axis, [(i, (i + steps) % count) for i in range(count)])]
    all_to_all x3 -> x4, waiting for transfers between devices: 174 us -> 51.1 us  [exchange(): lax.all_to_all(chunks, 'slab', split_axis=0, concat_axis=0, tiled=True)]
    slice x23 -> x0, local copies, waits for them, and re-layouts: 60.3 us -> none  [the longest x8 37.5 us: neighbours(): jnp.roll(field_now, 1, axis=3)]
    add x3 -> x0, other arithmetic: 54.6 us -> none  [the longest x2 37 us: advance(): state_now + time_step * (horizontal(state_now, face_visc) - state_now[2]...]
    dot_general x4 -> x0, matrix products: 33 us -> none  [apply_columns(): jnp.einsum('fzk,fkyx->fzyx', matrices, field_now, precision=lax.Precision...]
    dot_general x4 -> x0, local copies, waits for them, and re-layouts: 21.9 us -> none  [apply_columns(): jnp.einsum('fzk,fkyx->fzyx', matrices, field_now, precision=lax.Precision...]
  transfers between devices with their start and end apart: 13 -> 14, of which waited for: 6 -> 12; matrix products, arithmetic and copies ran while one was open for 4% -> 0% of each run, Pallas kernels for 0% -> 7%
where the time goes in v2:
time: 540 us; the launch traced here: 538 us
  waiting for transfers between devices  315 us (58%)
  Pallas kernels  169 us (31%)
  starting transfers between devices  38.5 us (7%)
  between operations  14.2 us (3%)
    ppermute x7, waiting for transfers between devices, around(): lax.ppermute(value, axis, [(i, (i + steps) % count) for i in range(count)])  180 us
    pallas_call x9, Pallas kernels, call(): pl.pallas_call(kernel, in_specs=[spec for _, spec in ins], out_specs=tupl...  169 us
    ppermute x1, waiting for transfers between devices, local(): below = lax.ppermute(ends[1], 'slab', forward)  75.4 us
    all_to_all x4, waiting for transfers between devices, exchange(): lax.all_to_all(chunks, 'slab', split_axis=0, concat_axis=0, tiled=True)  51.1 us
    all_to_all x4, starting transfers between devices, exchange(): lax.all_to_all(chunks, 'slab', split_axis=0, concat_axis=0, tiled=True)  23.5 us
  transfers between devices with their start and end apart: 14, of which 12 were waited for; matrix products, arithmetic and copies ran while one was open for 0% of the time, Pallas kernels for 7%

profile of v2, /device:TPU:9, one launch (start us, length us, event | category | flops | bytes accessed | tf_op | source)
XLA Modules:
  0.0 538.1 jit_solution(7793647039115537083)
XLA Ops:
  7.2 6.5 %to_chunks.1 = (f32[8,35,32,128]{3,2,1,0:T(8,128)}, f32[64,32,128]{2,1,0:T(8,128)}, f32[2,4,64,128]{3,2,1,0:T(8,128)}) custom-call(s32[1]{0:T(128)} %bitcast.own, f32[4,2048,128]{2,1,0:T(8,128)} %bitcast.12, f32[2048,128]{1,0:T(8,128)} %bitcast.17), custom_call_target="tpu_custom_call" | custom-call | bytes 5242884 | tf_op jit(solution)/shard_map/to_chunks/pallas_call | solution.py:41
  13.6 5.6 %all-to-all-start = ((f32[8,35,32,128]{3,2,1,0:T(8,128)}), f32[8,35,32,128]{3,2,1,0:T(8,128)}, u32[]{:S(2)}, u32[]{:S(2)}) async-start(f32[8,35,32,128]{3,2,1,0:T(8,128)} %get-tuple-element.18.states), calls=%async_computation | async-start | bytes 9175040 | tf_op jit(solution)/shard_map/all_to_all | solution.py:587
  19.3 2.2 collective-permute-start
  21.4 89.9 %collective-permute-done._ = f32[4,32,64,128]{3,2,1,0:T(8,128)} collective-permute-done((f32[4,32,64,128]{3,2,1,0:T(8,128)}, f32[4,32,64,128]{3,2,1,0:T(8,128)}, u32[]{:S(2)}, u32[]{:S(2)}) %collective-permute-start) | collective-permute-done | bytes 4194336 | tf_op jit(solution)/shard_map/ppermute | solution.py:592
  111.4 6.8 %all-to-all-done.chunks = f32[8,35,32,128]{3,2,1,0:T(8,128)} async-done(((f32[8,35,32,128]{3,2,1,0:T(8,128)}), f32[8,35,32,128]{3,2,1,0:T(8,128)}, u32[]{:S(2)}, u32[]{:S(2)}) %all-to-all-start) | async-done | bytes 4587552 | tf_op jit(solution)/shard_map/all_to_all | solution.py:587
  118.2 76.6 %outer_rows.1 = (f32[8,4,2,32,128]{4,3,2,1,0:T(8,128)}, f32[8,4,2,32,128]{4,3,2,1,0:T(8,128)}, f32[8,3,32,128]{3,2,1,0:T(8,128)}) custom-call(f32[8,35,32,128]{3,2,1,0:T(8,128)} %all-to-all-done.chunks, f32[4,32,64,128]{3,2,1,0:T(8,128)} %collective-permute-done._), custom_call_target="tpu_custom_call" | custom-call | bytes 8781824 | tf_op jit(solution)/shard_map/outer_rows/pallas_call | solution.py:41
  194.8 1.8 collective-permute-start.1
  196.6 3.0 split.1
  199.6 14.6 %collective-permute-done.1.low_in = f32[8,4,2,32,128]{4,3,2,1,0:T(8,128)S(1)} collective-permute-done((f32[8,4,2,32,128]{4,3,2,1,0:T(8,128)}, f32[8,4,2,32,128]{4,3,2,1,0:T(8,128)S(1)}, u32[]{:S(2)}, u32[]{:S(2)}) %collective-permute-start.1) | collective-permute-done | bytes 1048608 | tf_op jit(solution)/shard_map/ppermute | solution.py:592
  214.2 6.5 %collective-permute-done.2.high_in = f32[8,4,2,32,128]{4,3,2,1,0:T(8,128)S(1)} collective-permute-done((f32[8,4,2,32,128]{4,3,2,1,0:T(8,128)}, f32[8,4,2,32,128]{4,3,2,1,0:T(8,128)S(1)}, u32[]{:S(2)}, u32[]{:S(2)}) %collective-permute-start.2) | collective-permute-done | bytes 1048608 | tf_op jit(solution)/shard_map/ppermute | solution.py:592
  220.7 7.0 %all-gather.3.cloned.1.call-done = f32[32,3,32,128]{3,2,1,0:T(8,128)} async-done(((f32[8,3,32,128]{3,2,1,0:T(8,128)}), f32[32,3,32,128]{3,2,1,0:T(8,128)}) %all-gather.3.cloned.1.call-update) | async-done | bytes 1572880 | tf_op jit(solution)/shard_map/all_gather | solution.py:613
  227.7 15.0 %first_step.1 = (f32[4,10,272,128]{3,2,1,0:T(8,128)}, f32[12,256,128]{2,1,0:T(8,128)}) custom-call(f32[8,35,32,128]{3,2,1,0:T(8,128)} %all-to-all-done.chunks, f32[8,4,2,32,128]{4,3,2,1,0:T(8,128)} %copy-done.1, f32[8,4,2,32,128]{4,3,2,1,0:T(8,128)} %copy-done.2, f32[4,8,3,32,128]{4,3,2,1,0:T(8,128)} %bitcast.16, ...), custom_call_target="tpu_custom_call" | custom-call | flops 2013265920 | bytes 10354688 | tf_op jit(solution)/shard_map/first_step/pallas_call | solution.py:41
  242.6 11.3 %second_step.1 = (f32[8,2,8,32,128]{4,3,2,1,0:T(8,128)}, f32[8,2,8,32,128]{4,3,2,1,0:T(8,128)}) custom-call(f32[4,10,272,128]{3,2,1,0:T(8,128)} %get-tuple-element.24.first.refs_0_, f32[12,256,128]{2,1,0:T(8,128)} %get-tuple-element.25.visc.refs_1_, bf16[4,256,256]{2,1,0:T(8,128)(2,1)} %get-tuple-element.22.mat_high, ...), custom_call_target="tpu_custom_call" | custom-call | flops 1610612736 | bytes 9240576 | tf_op jit(solution)/shard_map/second_step/pallas_call | solution.py:41
  254.0 5.5 %all-to-all-start.1 = ((f32[8,2,8,32,128]{4,3,2,1,0:T(8,128)}), f32[8,2,8,32,128]{4,3,2,1,0:T(8,128)S(1)}, u32[]{:S(2)}, u32[]{:S(2)}) async-start(f32[8,2,8,32,128]{4,3,2,1,0:T(8,128)} %get-tuple-element.26.half), calls=%async_computation.1 | async-start | bytes 4194304 | tf_op jit(solution)/shard_map/all_to_all | solution.py:587
  259.4 1.2 collective-permute-start.3
  260.6 44.3 %all-to-all-done.1._.half = f32[8,2,8,32,128]{4,3,2,1,0:T(8,128)S(1)} async-done(((f32[8,2,8,32,128]{4,3,2,1,0:T(8,128)}), f32[8,2,8,32,128]{4,3,2,1,0:T(8,128)S(1)}, u32[]{:S(2)}, u32[]{:S(2)}) %all-to-all-start.1) | async-done | bytes 2097184 | tf_op jit(solution)/shard_map/all_to_all | solution.py:587
  305.0 7.8 %all-to-all-start.2 = ((f32[8,2,8,32,128]{4,3,2,1,0:T(8,128)}), f32[8,2,8,32,128]{4,3,2,1,0:T(8,128)}, u32[]{:S(2)}, u32[]{:S(2)}) async-start(f32[8,2,8,32,128]{4,3,2,1,0:T(8,128)} %get-tuple-element.27.other), calls=%async_computation.2 | async-start | bytes 4194304 | tf_op jit(solution)/shard_map/all_to_all | solution.py:587
  312.8 47.2 %collective-permute-done.3.target = f32[8,35,32,128]{3,2,1,0:T(8,128)} collective-permute-done((f32[8,35,32,128]{3,2,1,0:T(8,128)}, f32[8,35,32,128]{3,2,1,0:T(8,128)}, u32[]{:S(2)}, u32[]{:S(2)}) %collective-permute-start.3) | collective-permute-done | bytes 4587552 | tf_op jit(solution)/shard_map/ppermute | solution.py:592
  360.0 2.8 edge_rows.1
  362.8 2.3 collective-permute-start.4
  365.1 9.4 %collective-permute-done.4.low_edge = f32[8,4,32,128]{3,2,1,0:T(8,128)S(1)} collective-permute-done((f32[8,4,32,128]{3,2,1,0:T(8,128)}, f32[8,4,32,128]{3,2,1,0:T(8,128)S(1)}, u32[]{:S(2)}, u32[]{:S(2)}) %collective-permute-start.4) | collective-permute-done | bytes 524320 | tf_op jit(solution)/shard_map/ppermute | solution.py:592
  374.5 4.0 collective-permute-done.5.high_edge
  379.3 19.2 %adjoint_step.1._ = f32[8,34,32,128]{3,2,1,0:T(8,128)} custom-call(f32[8,2,8,32,128]{4,3,2,1,0:T(8,128)} %get-tuple-element.26.half, f32[8,2,8,32,128]{4,3,2,1,0:T(8,128)} %get-tuple-element.27.other, f32[8,35,32,128]{3,2,1,0:T(8,128)} %collective-permute-done.3.target, f32[8,4,32,128]{3,2,1,0:T(8,128)} %copy-done.3, f32[8,4,32,128]{3,2,1,0:T(8,128)} %copy-done.4, ...), custom_call_target="tpu_custom_call" | custom-call | flops 3623878656 | bytes 19070976 | tf_op jit(solution)/shard_map/adjoint_step/pallas_call | solution.py:41
  398.5 4.5 all-to-all-start.3
  403.1 14.5 %residual_planes.1 = f32[8192,128]{1,0:T(8,128)} custom-call(f32[8,2,8,32,128]{4,3,2,1,0:T(8,128)} %copy-done, f32[8,2,8,32,128]{4,3,2,1,0:T(8,128)} %all-to-all-done.2.other, f32[8192,128]{1,0:T(8,128)} %bitcast.5.target, f32[8,34,32,128]{3,2,1,0:T(8,128)} %adjoint_step.1._), custom_call_target="tpu_custom_call" | custom-call | bytes 12845056 | tf_op jit(solution)/shard_map/residual_planes/pallas_call | solution.py:41
  417.5 2.2 collective-permute-start.8
  419.7 3.5 collective-permute-start.6
  423.2 1.9 collective-permute-start.7
  425.2 75.4 %collective-permute-done.6.edges_below = f32[4,64,128]{2,1,0:T(8,128)S(1)} collective-permute-done((f32[4,64,128]{2,1,0:T(8,128)S(1)}, f32[4,64,128]{2,1,0:T(8,128)S(1)}, u32[]{:S(2)}, u32[]{:S(2)}) %collective-permute-start.6) | collective-permute-done | bytes 131104 | tf_op jit(solution)/shard_map/ppermute | solution.py:606
  500.6 2.0 collective-permute-done.7.edges_above
  502.6 8.0 %collective-permute-done.8.prior = f32[8192,128]{1,0:T(8,128)} collective-permute-done((f32[8192,128]{1,0:T(8,128)}, f32[8192,128]{1,0:T(8,128)}, u32[]{:S(2)}, u32[]{:S(2)}) %collective-permute-start.8) | collective-permute-done | bytes 4194336 | tf_op jit(solution)/shard_map/ppermute | solution.py:592
  510.7 20.6 %last_step.1 = f32[8192,128]{1,0:T(8,128)} custom-call(f32[64,32,128]{2,1,0:T(8,128)} %get-tuple-element.32.visc, f32[4,64,128]{2,1,0:T(8,128)} %copy-done.6, f32[4,64,128]{2,1,0:T(8,128)} %copy-done.7, f32[8192,128]{1,0:T(8,128)} %collective-permute-done.8.prior, f32[8,34,32,128]{3,2,1,0:T(8,128)} %all-to-all-done.3.chunks, ...), custom_call_target="tpu_custom_call" | custom-call | flops 31457280 | bytes 14548992 | tf_op jit(solution)/shard_map/last_step/pallas_call | solution.py:41
  (23 shorter events, 0.9 us)
Async XLA Ops:
  13.6 104.5 %all-to-all-start = ((f32[8,35,32,128]{3,2,1,0:T(8,128)}), f32[8,35,32,128]{3,2,1,0:T(8,128)}, u32[]{:S(2)}, u32[]{:S(2)}) async-start(f32[8,35,32,128]{3,2,1,0:T(8,128)} %get-tuple-element.18.states), calls=%async_computation | async-start | bytes 9175040 | tf_op jit(solution)/shard_map/all_to_all | solution.py:587
  19.3 208.4 %all-gather.3.cloned.1.call-start = ((), (), s32[]{:S(2)}) async-start(), calls=%async_computation.4 | async-start | bytes 1966080 | tf_op jit(solution)/shard_map/all_gather | solution.py:613
  19.3 92.1 %collective-permute-start = (f32[4,32,64,128]{3,2,1,0:T(8,128)}, f32[4,32,64,128]{3,2,1,0:T(8,128)}, u32[]{:S(2)}, u32[]{:S(2)}) collective-permute-start(f32[4,32,64,128]{3,2,1,0:T(8,128)} %bitcast.13), channel_id=1, source_target_pairs={{0,24},{8,0},{16,8},{24,16},{1,25},{9,1},{17,9},{25,17},{2,26},{10... | collective-permute-start | bytes 12582920 | tf_op jit(solution)/shard_map/ppermute | solution.py:592
  194.8 19.4 %collective-permute-start.1 = (f32[8,4,2,32,128]{4,3,2,1,0:T(8,128)}, f32[8,4,2,32,128]{4,3,2,1,0:T(8,128)S(1)}, u32[]{:S(2)}, u32[]{:S(2)}) collective-permute-start(f32[8,4,2,32,128]{4,3,2,1,0:T(8,128)} %get-tuple-element.19), channel_id=1, source_target_pairs={{0,1},{1,2},{2,3},{3,4},{4,5},{5,6},{6,7},{7,0},{8,9},{9,10},{10,1... | collective-permute-start | bytes 3145736 | tf_op jit(solution)/shard_map/ppermute | solution.py:592
  196.6 24.1 %collective-permute-start.2 = (f32[8,4,2,32,128]{4,3,2,1,0:T(8,128)}, f32[8,4,2,32,128]{4,3,2,1,0:T(8,128)S(1)}, u32[]{:S(2)}, u32[]{:S(2)}) collective-permute-start(f32[8,4,2,32,128]{4,3,2,1,0:T(8,128)} %get-tuple-element.20), channel_id=1, source_target_pairs={{0,7},{1,0},{2,1},{3,2},{4,3},{5,4},{6,5},{7,6},{8,15},{9,8},{10,9... | collective-permute-start | bytes 3145736 | tf_op jit(solution)/shard_map/ppermute | solution.py:592
  214.2 13.5 %copy-start.1 = (f32[8,4,2,32,128]{4,3,2,1,0:T(8,128)}, f32[8,4,2,32,128]{4,3,2,1,0:T(8,128)S(1)}, u32[]{:S(2)}) copy-start(f32[8,4,2,32,128]{4,3,2,1,0:T(8,128)S(1)} %collective-permute-done.1.low_in) | copy-start | bytes 3145732
  220.7 7.0 %copy-start.2 = (f32[8,4,2,32,128]{4,3,2,1,0:T(8,128)}, f32[8,4,2,32,128]{4,3,2,1,0:T(8,128)S(1)}, u32[]{:S(2)}) copy-start(f32[8,4,2,32,128]{4,3,2,1,0:T(8,128)S(1)} %collective-permute-done.2.high_in) | copy-start | bytes 3145732
  254.0 51.0 %all-to-all-start.1 = ((f32[8,2,8,32,128]{4,3,2,1,0:T(8,128)}), f32[8,2,8,32,128]{4,3,2,1,0:T(8,128)S(1)}, u32[]{:S(2)}, u32[]{:S(2)}) async-start(f32[8,2,8,32,128]{4,3,2,1,0:T(8,128)} %get-tuple-element.26.half), calls=%async_computation.1 | async-start | bytes 4194304 | tf_op jit(solution)/shard_map/all_to_all | solution.py:587
  259.4 100.5 %collective-permute-start.3 = (f32[8,35,32,128]{3,2,1,0:T(8,128)}, f32[8,35,32,128]{3,2,1,0:T(8,128)}, u32[]{:S(2)}, u32[]{:S(2)}) collective-permute-start(f32[8,35,32,128]{3,2,1,0:T(8,128)} %all-to-all-done.chunks), channel_id=1, source_target_pairs={{0,24},{8,0},{16,8},{24,16},{1,25},{9,1},{17,9},{25,17},{2,26},{10... | collective-permute-start | bytes 13762568 | tf_op jit(solution)/shard_map/ppermute | solution.py:592
  305.0 55.0 %copy-start = (f32[8,2,8,32,128]{4,3,2,1,0:T(8,128)}, f32[8,2,8,32,128]{4,3,2,1,0:T(8,128)S(1)}, u32[]{:S(2)}) copy-start(f32[8,2,8,32,128]{4,3,2,1,0:T(8,128)S(1)} %all-to-all-done.1._.half) | copy-start | bytes 6291460
  305.0 93.5 %all-to-all-start.2 = ((f32[8,2,8,32,128]{4,3,2,1,0:T(8,128)}), f32[8,2,8,32,128]{4,3,2,1,0:T(8,128)}, u32[]{:S(2)}, u32[]{:S(2)}) async-start(f32[8,2,8,32,128]{4,3,2,1,0:T(8,128)} %get-tuple-element.27.other), calls=%async_computation.2 | async-start | bytes 4194304 | tf_op jit(solution)/shard_map/all_to_all | solution.py:587
  362.8 11.7 %collective-permute-start.4 = (f32[8,4,32,128]{3,2,1,0:T(8,128)}, f32[8,4,32,128]{3,2,1,0:T(8,128)S(1)}, u32[]{:S(2)}, u32[]{:S(2)}) collective-permute-start(f32[8,4,32,128]{3,2,1,0:T(8,128)} %get-tuple-element.28), channel_id=1, source_target_pairs={{0,1},{1,2},{2,3},{3,4},{4,5},{5,6},{6,7},{7,0},{8,9},{9,10},{10,1... | collective-permute-start | bytes 1572872 | tf_op jit(solution)/shard_map/ppermute | solution.py:592
  365.1 13.4 %collective-permute-start.5 = (f32[8,4,32,128]{3,2,1,0:T(8,128)}, f32[8,4,32,128]{3,2,1,0:T(8,128)S(1)}, u32[]{:S(2)}, u32[]{:S(2)}) collective-permute-start(f32[8,4,32,128]{3,2,1,0:T(8,128)} %get-tuple-element.29), channel_id=1, source_target_pairs={{0,7},{1,0},{2,1},{3,2},{4,3},{5,4},{6,5},{7,6},{8,15},{9,8},{10,9... | collective-permute-start | bytes 1572872 | tf_op jit(solution)/shard_map/ppermute | solution.py:592
  374.5 4.0 copy-start.3
  378.5 0.8 copy-start.4
  398.5 112.2 %all-to-all-start.3 = ((f32[8,34,32,128]{3,2,1,0:T(8,128)}), f32[8,34,32,128]{3,2,1,0:T(8,128)}, u32[]{:S(2)}, u32[]{:S(2)}) async-start(f32[8,34,32,128]{3,2,1,0:T(8,128)} %adjoint_step.1._), calls=%async_computation.3 | async-start | bytes 8912896 | tf_op jit(solution)/shard_map/all_to_all | solution.py:587
  403.0 16.6 %copy-start.5 = (f32[2,4,64,128]{3,2,1,0:T(8,128)S(1)}, f32[2,4,64,128]{3,2,1,0:T(8,128)}, u32[]{:S(2)}) copy-start(f32[2,4,64,128]{3,2,1,0:T(8,128)} %get-tuple-element.33) | copy-start | bytes 786436
  417.5 93.1 %collective-permute-start.8 = (f32[8192,128]{1,0:T(8,128)}, f32[8192,128]{1,0:T(8,128)}, u32[]{:S(2)}, u32[]{:S(2)}) collective-permute-start(f32[8192,128]{1,0:T(8,128)} %residual_planes.1), channel_id=1, source_target_pairs={{0,8},{8,16},{16,24},{24,0},{1,9},{9,17},{17,25},{25,1},{2,10},{10... | collective-permute-start | bytes 12582920 | tf_op jit(solution)/shard_map/ppermute | solution.py:592
  419.7 80.9 %collective-permute-start.6 = (f32[4,64,128]{2,1,0:T(8,128)S(1)}, f32[4,64,128]{2,1,0:T(8,128)S(1)}, u32[]{:S(2)}, u32[]{:S(2)}) collective-permute-start(f32[4,64,128]{2,1,0:T(8,128)S(1)} %get-tuple-element.35), channel_id=1, source_target_pairs={{0,1},{1,2},{2,3},{3,4},{4,5},{5,6},{6,7},{8,9},{9,10},{10,11},{11... | collective-permute-start | bytes 393224 | tf_op jit(solution)/shard_map/ppermute | solution.py:606
  423.2 79.4 %collective-permute-start.7 = (f32[4,64,128]{2,1,0:T(8,128)S(1)}, f32[4,64,128]{2,1,0:T(8,128)S(1)}, u32[]{:S(2)}, u32[]{:S(2)}) collective-permute-start(f32[4,64,128]{2,1,0:T(8,128)S(1)} %get-tuple-element.34), channel_id=1, source_target_pairs={{1,0},{2,1},{3,2},{4,3},{5,4},{6,5},{7,6},{9,8},{10,9},{11,10},{12... | collective-permute-start | bytes 393224 | tf_op jit(solution)/shard_map/ppermute | solution.py:607
  500.6 10.1 %copy-start.6 = (f32[4,64,128]{2,1,0:T(8,128)}, f32[4,64,128]{2,1,0:T(8,128)S(1)}, u32[]{:S(2)}) copy-start(f32[4,64,128]{2,1,0:T(8,128)S(1)} %collective-permute-done.6.edges_below) | copy-start | bytes 393220
  502.6 8.0 %copy-start.7 = (f32[4,64,128]{2,1,0:T(8,128)}, f32[4,64,128]{2,1,0:T(8,128)S(1)}, u32[]{:S(2)}) copy-start(f32[4,64,128]{2,1,0:T(8,128)S(1)} %collective-permute-done.7.edges_above) | copy-start | bytes 393220
Sparse Core Ops, SparseCore 0:
  194.9 32.6 all-gather.2

commit v3 on v2

--- a/solution.py
+++ b/solution.py
@@ -65,6 +65,13 @@
         copy.wait()
 
 
+def spans(parts):
+    start = 0
+    for part in parts:
+        yield part, pl.ds(start, part.shape[1])
+        start += part.shape[1]
+
+
 def east(value):
     return pltpu.roll(value, value.shape[1] - 1, 1)
 
@@ -101,68 +108,72 @@
     )
 
 
-def chunks_kernel(own, x_ref, visc_in, send, visc, edges, planes, held, extra, flat, sem):
-    slabs, block = held.shape[1:3]
+def visc_kernel(own, x_ref, visc, send):
+    slabs, share = send.shape[:2]
     rows, depth, _ = visc.shape
-    share = extra.shape[1]
-    visc_copy = pltpu.make_async_copy(visc_in, flat, sem.at[2 * fields])
-    visc_copy.start()
-    copies = start_all([(x_ref.at[f], planes.at[f]) for f in range(fields)], sem)
-    visc_copy.wait()
+    block = rows // slabs
     for y in range(rows):
-        visc[y] = flat[pl.ds(y, depth, stride=rows), :]
+        visc[y] = x_ref[pl.ds(y, depth, stride=rows), :]
     for p in range(slabs):
         for i in range(share):
-            row = lax.rem(p * block - 2 + share * own[0] + i + rows, rows)
-            extra[p, i] = visc[row]
-    leaving = [
-        pltpu.make_async_copy(extra, send.at[:, pl.ds(fields * block, share)], sem.at[2 * fields])
+            send[p, i] = visc[lax.rem(p * block - 2 + share * own[0] + i + rows, rows)]
+
+
+def visc_chunks(viscosity, slabs, share):
+    depth, rows, width = viscosity.shape
+    own = jnp.full((1,), lax.axis_index("seg"), jnp.int32)
+    return call(
+        visc_kernel,
+        [(own, scalars()), (viscosity.reshape(-1, width), whole())],
+        [((rows, depth, width), whole()), ((slabs, share, depth, width), whole())],
+        [],
+        0,
+        "visc_chunks",
+    )
+
+
+def chunks_kernel(start, x_ref, _, send, edges, planes, held, sem):
+    count, slabs, block, depth, _ = held.shape
+    rows = slabs * block
+    copies = start_all([(x_ref.at[start + f], planes.at[f]) for f in range(count)], sem)
+    ends = [
+        pltpu.make_async_copy(x_ref.at[:, pl.ds(z * rows, rows)], edges.at[i], sem.at[count + i])
+        for i, z in enumerate((0, depth - 1))
     ]
-    leaving[0].start()
-    for f in range(fields):
+    for copy in ends:
+        copy.start()
+    leaving = []
+    for f in range(count):
         copies[f].wait()
         for y in range(rows):
             held[f, y // block, y % block] = planes[f, pl.ds(y, depth, stride=rows), :]
-        leaving.append(
-            pltpu.make_async_copy(
-                held.at[f], send.at[:, pl.ds(f * block, block)], sem.at[fields + f]
-            )
-        )
-        leaving[-1].start()
-        edges[0, f] = planes[f, pl.ds(0, rows), :]
-        edges[1, f] = planes[f, pl.ds((depth - 1) * rows, rows), :]
-    wait_all(leaving)
-
-
-def to_chunks(states, viscosity, slabs, share):
+        copy = pltpu.make_async_copy(held.at[f], send.at[:, f], sem.at[f])
+        copy.start()
+        leaving.append(copy)
+    wait_all(leaving + ends)
+
+
+def to_chunks(states, slabs, start, count, later):
     _, depth, rows, width = states.shape
     block = rows // slabs
-    own = jnp.full((1,), lax.axis_index("seg"), jnp.int32)
-    return call(
-        chunks_kernel,
+    return call(
+        functools.partial(chunks_kernel, start),
+        [(states.reshape(fields, -1, width), anywhere()), (later, anywhere())],
         [
-            (own, scalars()),
-            (states.reshape(fields, -1, width), anywhere()),
-            (viscosity.reshape(-1, width), anywhere()),
-        ],
-        [
-            ((slabs, fields * block + share, depth, width), anywhere()),
-            ((rows, depth, width), whole()),
+            ((slabs, count, block, depth, width), anywhere()),
             ((2, fields, rows, width), whole()),
         ],
         [
-            vmem(fields, depth * rows, width),
-            vmem(fields, slabs, block, depth, width),
-            vmem(slabs, share, depth, width),
-            vmem(depth * rows, width),
-            dmas(2 * fields + 1),
+            vmem(count, depth * rows, width),
+            vmem(count, slabs, block, depth, width),
+            dmas(count + 2),
         ],
         0,
         "to_chunks",
     )
 
 
-def planes_kernel(half, other, target, _, o_ref, held, sem):
+def planes_kernel(half, other, target, _, o_ref, again, held, sem):
     slabs, _, block, depth, _ = half.shape
     rows = slabs * block
     pairs = []
@@ -178,7 +189,10 @@
             o_ref[where, :] = held[f, y] - target[where, :]
         return 0
 
+    places = [held.at[pl.ds(2, 2), pl.ds(p * block, block)] for p in range(slabs)]
+    copies = start_all([(places[p], again.at[p]) for p in range(slabs)], sem)
     lax.fori_loop(0, rows, row, 0, unroll=4)
+    wait_all(copies)
 
 
 def residual_planes(halves, target, later):
@@ -187,11 +201,14 @@
         planes_kernel,
         [(halves[0], anywhere()), (halves[1], anywhere())]
         + [(target.reshape(-1, width), whole()), (later, anywhere())],
-        [((fields * depth * slabs * block, width), whole())],
+        [
+            ((fields * depth * slabs * block, width), whole()),
+            (halves[1].shape, anywhere()),
+        ],
         [vmem(fields, slabs * block, depth, width), dmas(2 * slabs)],
         0,
         "residual_planes",
-    )[0]
+    )
 
 
 def clear_pads(ref):
@@ -259,20 +276,18 @@
     ]
 
 
-def first_kernel(chunks, low_in, high_in, visc_in, mat_high, mat_low, first, visc, *scratch):
-    state, carry, high, low, sem = scratch
-    slabs, _, _, depth, _ = low_in.shape
+def first_kernel(*refs):
+    visc_in, mat_high, mat_low, first, visc, state, carry, high, low, sem = refs[-10:]
+    halves, low_in, high_in = refs[0:2], refs[2:4], refs[4:6]
+    slabs, _, block, depth, _ = halves[0].shape
     segs, _, share = visc_in.shape[:3]
-    block = first.shape[1] - 2
     order = visc.shape[1]
     pairs = []
     for p in range(slabs):
         planes, padded = pl.ds(p * depth, depth), pl.ds(p * depth + pad, depth)
-        for f in range(fields):
-            source = chunks.at[p, pl.ds(f * block, block)]
-            pairs.append((source, state.at[f, pl.ds(2, block), padded]))
-        pairs.append((low_in.at[p], state.at[:, pl.ds(0, 2), padded]))
-        pairs.append((high_in.at[p], state.at[:, pl.ds(block + 2, 2), padded]))
+        for row, count, parts in ((0, 2, low_in), (2, block, halves), (block + 2, 2, high_in)):
+            for part, span in spans(parts):
+                pairs.append((part.at[p], state.at[span, pl.ds(row, count), padded]))
         for s in range(segs):
             pairs.append((visc_in.at[s, p], visc.at[pl.ds(share * s, share), planes]))
     copies = start_all(pairs, sem)
@@ -286,15 +301,14 @@
     advance_rows(state, visc, 0, mat_high, mat_low, carry, high, low, block + 2, finish)
 
 
-def first_step(chunks, low_in, high_in, visc_in, mat_high, mat_low):
-    slabs, _, depth, width = chunks.shape
+def first_step(halves, low_in, high_in, later, visc_in, mat_high, mat_low):
+    slabs, _, block, depth, width = halves[0].shape
     segs, _, share = visc_in.shape[:3]
-    block = (chunks.shape[1] - share) // fields
     order = slabs * depth
     volume = fields * (block + 2) * order * width
     return call(
         first_kernel,
-        [(x, anywhere()) for x in (chunks, low_in, high_in, visc_in)]
+        [(x, anywhere()) for x in (*halves, *low_in, *high_in, later, visc_in)]
         + [(mat_high, whole()), (mat_low, whole())],
         [
             ((fields, block + 2, order + 2 * pad, width), whole()),
@@ -302,13 +316,13 @@
         ],
         [vmem(fields, block + 4, order + 2 * pad, width)]
         + step_scratch(order, width)
-        + [dmas(slabs * (fields + 2 + segs))],
+        + [dmas(slabs * (6 + segs))],
         6 * order * volume,
         "first_step",
     )
 
 
-def second_kernel(first, visc, mat_high, mat_low, half, other, carry, high, low, held, sem):
+def second_kernel(first, visc, mat_high, mat_low, _, half, other, carry, high, low, held, sem):
     slabs, _, block, depth, _ = half.shape
 
     def finish(f, row, piece):
@@ -323,12 +337,12 @@
     wait_all(start_all(pairs, sem))
 
 
-def second_step(first, visc, mat_high, mat_low, slabs):
+def second_step(first, visc, mat_high, mat_low, slabs, later):
     _, block, _, width = first.shape
     block, order = block - 2, visc.shape[1]
     return call(
         second_kernel,
-        [(x, whole()) for x in (first, visc, mat_high, mat_low)],
+        [(x, whole()) for x in (first, visc, mat_high, mat_low)] + [(later, anywhere())],
         [((slabs, 2, block, order // slabs, width), anywhere())] * 2,
         step_scratch(order, width) + [vmem(fields, block, order, width), dmas(2 * slabs)],
         6 * order * fields * block * order * width,
@@ -336,51 +350,46 @@
     )
 
 
-def outer_kernel(chunks, _, low_rows, high_rows, visc, sem):
-    share = visc.shape[1]
-    block = (chunks.shape[1] - share) // fields
-    pairs = []
-    for f in range(fields):
-        pairs.append((chunks.at[:, pl.ds((f + 1) * block - 2, 2)], high_rows.at[:, f]))
-        pairs.append((chunks.at[:, pl.ds(f * block, 2)], low_rows.at[:, f]))
-    pairs.append((chunks.at[:, pl.ds(fields * block, share)], visc))
-    wait_all(start_all(pairs, sem))
-
-
-def outer_rows(chunks, share, later):
-    slabs, _, depth, width = chunks.shape
-    rows = ((slabs, fields, 2, depth, width), anywhere())
+def outer_kernel(chunks, _, low_rows, high_rows, sem):
+    block = chunks.shape[2]
+    low, high = chunks.at[:, :, pl.ds(0, 2)], chunks.at[:, :, pl.ds(block - 2, 2)]
+    wait_all(start_all([(high, high_rows), (low, low_rows)], sem))
+
+
+def outer_rows(chunks, later):
+    slabs, _, _, depth, width = chunks.shape
+    rows = ((slabs, chunks.shape[1], 2, depth, width), whole())
     return call(
         outer_kernel,
         [(chunks, anywhere()), (later, anywhere())],
-        [rows, rows, ((slabs, share, depth, width), anywhere())],
-        [dmas(2 * fields + 1)],
+        [rows, rows],
+        [dmas(2)],
         0,
         "outer_rows",
     )
 
 
-def edge_kernel(half, other, target, _, low_edge, high_edge, ours, theirs, sem):
+def edge_kernel(*refs):
+    half, other, *targets, _, low_edge, high_edge, ours, theirs, sem = refs
     block = half.shape[2]
     pairs = []
     for side, row in ((0, 0), (1, block - 1)):
-        for f in range(fields):
-            source = (half, other)[f // 2]
-            pairs.append((source.at[:, f % 2, row], ours.at[side, f]))
-            pairs.append((target.at[:, f * block + row], theirs.at[side, f]))
+        for source, span in spans((half, other)):
+            pairs.append((source.at[:, :, row], ours.at[side, :, span]))
+        for source, span in spans(targets):
+            pairs.append((source.at[:, :, row], theirs.at[side, :, span]))
     wait_all(start_all(pairs, sem))
-    for f in range(fields):
-        low_edge[:, f] = ours[0, f] - theirs[0, f]
-        high_edge[:, f] = ours[1, f] - theirs[1, f]
-
-
-def edge_rows(halves, target, later):
+    low_edge[...] = ours[0] - theirs[0]
+    high_edge[...] = ours[1] - theirs[1]
+
+
+def edge_rows(halves, targets, later):
     slabs, _, _, depth, width = halves[0].shape
     edge = ((slabs, fields, depth, width), whole())
-    both = vmem(2, fields, slabs, depth, width)
+    both = vmem(2, slabs, fields, depth, width)
     return call(
         edge_kernel,
-        [(x, anywhere()) for x in (*halves, target, later)],
+        [(x, anywhere()) for x in (*halves, *targets, later)],
         [edge, edge],
         [both, both, dmas(4 * fields)],
         0,
@@ -388,20 +397,20 @@
     )
 
 
-def adjoint_kernel(half, other, target, low_edge, high_edge, *refs):
-    first, visc, mat_high, mat_low = refs[:4]
-    out, cot, less, pulled, ends, carry, high, low, sem = refs[4:]
+def adjoint_kernel(*refs):
+    half, other, *targets, low_edge, high_edge = refs[:-13]
+    first, visc, mat_high, mat_low = refs[-13:-9]
+    out, cot, less, pulled, ends, carry, high, low, sem = refs[-9:]
     slabs, _, block, depth, width = half.shape
     order = slabs * depth
     main = pl.ds(1, block)
     pairs = []
     for p in range(slabs):
         planes = pl.ds(p * depth, depth)
-        pairs.append((half.at[p], cot.at[pl.ds(0, 2), main, planes]))
-        pairs.append((other.at[p], cot.at[pl.ds(2, 2), main, planes]))
-        for f in range(fields):
-            source = target.at[p, pl.ds(f * block, block)]
-            pairs.append((source, less.at[f, main, planes]))
+        for source, span in spans((half, other)):
+            pairs.append((source.at[p], cot.at[span, main, planes]))
+        for source, span in spans(targets):
+            pairs.append((source.at[p], less.at[span, main, planes]))
         pairs.append((low_edge.at[p], cot.at[:, 0, planes]))
         pairs.append((high_edge.at[p], cot.at[:, block + 1, planes]))
     copies = start_all(pairs, sem)
@@ -480,13 +489,13 @@
     ends_copy.wait()
 
 
-def adjoint_step(halves, target, low_edge, high_edge, first, visc, mat_high, mat_low):
+def adjoint_step(halves, targets, low_edge, high_edge, first, visc, mat_high, mat_low):
     slabs, _, block, depth, width = halves[0].shape
     order = slabs * depth
     volume = fields * (block + 1) * order * width
     return call(
         adjoint_kernel,
-        [(x, anywhere()) for x in (*halves, target, low_edge, high_edge)]
+        [(x, anywhere()) for x in (*halves, *targets, low_edge, high_edge)]
         + [(x, whole()) for x in (first, visc, mat_high, mat_low)],
         [((slabs, fields * block + 2, depth, width), anywhere())],
         [
@@ -496,87 +505,119 @@
             vmem(slabs, 2, depth, width),
         ]
         + step_scratch(order, width)
-        + [dmas(slabs * (fields + 4))],
+        + [dmas(slabs * (fields + 6))],
         12 * order * volume,
         "adjoint_step",
     )[0]
 
 
-def last_kernel(visc, edges_below, edges_above, prior, chunks, states, out, *scratch):
-    pulled, state, ends, carry, sem = scratch
+def last_kernel(*refs):
+    visc, edges_below, edges_above, chunks, *states, half, other, out = refs[:9]
+    pulled, state, prior, planes, coupling, ends, carry, sem = refs[9:]
     slabs = chunks.shape[0]
     rows, depth, width = visc.shape
     block = rows // slabs
-    pairs = []
-    for p in range(slabs):
-        for f in range(fields):
-            source, place = pl.ds(f * block, block), pl.ds(p * block, block)
-            pairs.append((chunks.at[p, source], pulled.at[f, place, pl.ds(pad, depth)]))
-            pairs.append((states.at[p, source], state.at[f, place, pl.ds(pad, depth)]))
-    pairs.append((chunks.at[:, pl.ds(fields * block, 2)], ends))
-    copies = start_all(pairs, sem)
+    main = pl.ds(pad, depth)
+    above, below = pl.ds(pad + 1, depth), pl.ds(pad - 1, depth)
     first, last = slice(pad - 1, pad), slice(pad + depth, pad + depth + 1)
+
+    def arrive(f, which):
+        pairs = []
+        for p in range(slabs):
+            place, rest = pl.ds(p * block, block), pl.ds(f * block, block)
+            if which == "pulled":
+                pairs.append((chunks.at[p, rest], pulled.at[f, place, main]))
+            if which == "state":
+                pairs.append((states[f // 2].at[p, f % 2], state.at[f, place, main]))
+            if which == "prior":
+                pairs.append(((half, other)[f // 2].at[p, f % 2], prior.at[f, place]))
+        return [pltpu.make_async_copy(a, b, sem.at[f, which_of[which]]) for a, b in pairs]
+
+    which_of = {"pulled": 0, "state": 1, "prior": 2}
+    ends_copy = pltpu.make_async_copy(
+        chunks.at[:, pl.ds(fields * block, 2)], ends, sem.at[fields, 0]
+    )
+    copies = {}
+    for f, which in [(W, "state"), (U, "pulled"), (U, "state"), (U, "prior")] + [
+        (f, which) for f in (V, T, W) for which in which_of if (f, which) != (W, "state")
+    ]:
+        copies[f, which] = arrive(f, which)
+        for copy in copies[f, which]:
+            copy.start()
+        if (f, which) == (U, "pulled"):
+            ends_copy.start()
     for f in range(fields):
         for y in range(rows):
             state[f, y, first] = edges_below[f, y : y + 1]
             state[f, y, last] = edges_above[f, y : y + 1]
-    wait_all(copies)
+    ends_copy.wait()
     for f in range(fields):
         for y in range(rows):
             row = f * block + y % block
             pulled[f, y, first] = ends[y // block, 0, row : row + 1]
             pulled[f, y, last] = ends[y // block, 1, row : row + 1]
-    here = pl.ds(pad, depth)
-    above, below = pl.ds(pad + 1, depth), pl.ds(pad - 1, depth)
-    along_y = 0.5 * (visc[rows - 1] + visc[0])
-    for f in range(fields):
-        carry[f] = along_y * (pulled[f, 0, here] - pulled[f, rows - 1, here])
-
-    def row(y, _):
-        north = lax.rem(y + 1, rows)
-        own = visc[y]
-        along_x = 0.5 * (own + east(own))
-        along_y = 0.5 * (own + visc[north])
-        speed_above, speed_below = state[W, y, above], state[W, y, below]
-        coupling = pulled[T, y, here]
-        for f in (U, V, T, W):
-            value = pulled[f, y, here]
+    wait_all(copies[W, "state"])
+    leaving = []
+    for f in (U, V, T, W):
+        for which in which_of:
+            if (f, which) != (W, "state"):
+                wait_all(copies[f, which])
+        if f == T:
+            wait_all(copies[W, "pulled"])
+            copies[W, "pulled"] = []
+        along_y = 0.5 * (visc[rows - 1] + visc[0])
+        carry[...] = along_y * (pulled[f, 0, main] - pulled[f, rows - 1, main])
+
+        def row(y, _):
+            north = lax.rem(y + 1, rows)
+            own = visc[y]
+            along_x = 0.5 * (own + east(own))
+            along_y = 0.5 * (own + visc[north])
+            value = pulled[f, y, main]
             flux_x = along_x * (east(value) - value)
-            flux_y = along_y * (pulled[f, north, here] - value)
-            rate = flux_x - west(flux_x) + (flux_y - carry[f])
-            carry[f] = flux_y
-            up, down = pulled[f, y, above], pulled[f, y, below]
-            rate = rate + (speed_above * up - speed_below * down)
-            if f == W:
-                slope = speed_above - speed_below
+            flux_y = along_y * (pulled[f, north, main] - value)
+            rate = flux_x - west(flux_x) + (flux_y - carry[...])
+            carry[...] = flux_y
+            flow = state[W, y, above] * pulled[f, y, above]
+            rate = rate + (flow - state[W, y, below] * pulled[f, y, below])
+            lost = value * (state[f, y, above] - state[f, y, below])
+            if f == U:
+                coupling[y] = lost
+            elif f == V:
+                coupling[y] = coupling[y] + lost
+            elif f == T:
+                coupling[y] = value - (coupling[y] + lost)
+                rate = rate + pulled[W, y, main]
             else:
-                slope = state[f, y, above] - state[f, y, below]
-            coupling = coupling - value * slope
-            if f == T:
-                rate = rate + pulled[W, y, here]
-            if f == W:
-                rate = rate + coupling
-            where = pl.ds(f * depth * rows + y, depth, stride=rows)
-            out[where, :] = value + time_step * rate - prior[where, :]
-        return 0
-
-    lax.fori_loop(0, rows, row, 0, unroll=4)
-
-
-def last_step(visc, below, above, prior, chunks, states):
+                rate = rate + (coupling[y] - lost)
+            result = value + time_step * rate - (prior[f, y] - state[f, y, main])
+            planes[f, pl.ds(y, depth, stride=rows), :] = result
+            return 0
+
+        lax.fori_loop(0, rows, row, 0, unroll=8)
+        copy = pltpu.make_async_copy(planes.at[f], out.at[f], sem.at[fields, 1 + f])
+        copy.start()
+        leaving.append(copy)
+    wait_all(leaving)
+
+
+def last_step(visc, below, above, chunks, states, priors):
     rows, depth, width = visc.shape
     slabs = chunks.shape[0]
     return call(
         last_kernel,
-        [(x, whole()) for x in (visc, below, above, prior)]
-        + [(chunks, anywhere()), (states, anywhere())],
-        [((fields * depth * rows, width), whole())],
+        [(x, whole()) for x in (visc, below, above)]
+        + [(x, anywhere()) for x in (chunks, *states, *priors)],
+        [((fields, depth * rows, width), anywhere())],
         [
             vmem(fields, rows, depth + 2 * pad, width),
             vmem(fields, rows, depth + 2 * pad, width),
+            vmem(fields, rows, depth, width),
+            vmem(fields, depth * rows, width),
+            vmem(rows, depth, width),
             vmem(slabs, 2, depth, width),
-            vmem(fields, depth, width),
-            dmas(2 * fields * slabs + 1),
+            vmem(depth, width),
+            pltpu.SemaphoreType.DMA((fields + 1, fields + 1)),
         ],
         30 * fields * rows * depth * width,
         "last_step",
@@ -596,33 +637,41 @@
     start = states[0]
     _, depth, rows, width = start.shape
     slabs, segs = lax.axis_size("slab"), lax.axis_size("seg")
-    block = rows // slabs
-    share = -(-(block + 4) // segs)
-
-    send, visc, ends = to_chunks(start, viscosity, slabs, share)
+    share = -(-(rows // slabs + 4) // segs)
+
+    visc, visc_send = visc_chunks(viscosity, slabs, share)
+    visc_share = exchange(visc_send)
+    visc_in = lax.all_gather(visc_share, "seg", axis=0)
     target_planes = around(start, "seg", -1)
-    chunks = exchange(send)
+    send_half, _ = to_chunks(start, slabs, 0, 2, visc_send)
+    main_half = exchange(send_half)
+    send_other, ends = to_chunks(start, slabs, 2, 2, visc_share)
+    main_other = exchange(send_other)
     forward = [(i, i + 1) for i in range(slabs - 1)]
     below = lax.ppermute(ends[1], "slab", forward)
     above = lax.ppermute(ends[0], "slab", [(i, j) for j, i in forward])
     mat_high, mat_low, adj_high, adj_low = split(inverse)
 
-    low_rows, high_rows, visc_rows = outer_rows(chunks, share, target_planes)
-    low_in = around(high_rows, "slab", 1)
-    high_in = around(low_rows, "slab", -1)
-    visc_in = lax.all_gather(visc_rows, "seg", axis=0)
-    target = around(chunks, "seg", -1)
-
-    first, frame = first_step(chunks, low_in, high_in, visc_in, mat_high, mat_low)
-    halves = second_step(first, frame, mat_high, mat_low, slabs)
+    main = (main_half, main_other)
+    low_in, high_in, later = [], [], visc_share
+    for part in main:
+        low_rows, high_rows = outer_rows(part, later)
+        low_in.append(around(high_rows, "slab", 1))
+        high_in.append(around(low_rows, "slab", -1))
+        later = low_in[0]
+    target = [around(part, "seg", -1) for part in main]
+
+    first, frame = first_step(
+        main, low_in, high_in, target_planes, visc_in, mat_high, mat_low
+    )
+    halves = second_step(first, frame, mat_high, mat_low, slabs, target[0])
     half = exchange(halves[0])
     low_edge, high_edge = edge_rows(halves, target, half)
     low_edge, high_edge = around(high_edge, "slab", 1), around(low_edge, "slab", -1)
     pulled = adjoint_step(halves, target, low_edge, high_edge, first, frame, adj_high, adj_low)
-    other = exchange(halves[1])
-    residual = residual_planes((half, other), target_planes, pulled)
-    prior = around(residual, "seg", 1)
-    gradient = last_step(visc, below, above, prior, exchange(pulled), send)
+    residual, other = residual_planes((half, exchange(halves[1])), target_planes, pulled)
+    priors = [around(part, "seg", 1) for part in (half, other)]
+    gradient = last_step(visc, below, above, exchange(pulled), (send_half, send_other), priors)
     shape = (1, fields, depth, rows, width)
     return (residual.reshape(shape), gradient.reshape(shape))
 

time: 540 us -> 546 us (1.011)
  Pallas kernels: 169 us -> 96.9 us
  blocking collectives: 0 us -> 51.5 us
  starting transfers between devices: 38.5 us -> 50.2 us
  local copies, waits for them, and re-layouts: 0.84 us -> 8.93 us
  waiting for transfers between devices: 315 us -> 323 us
    all_gather x1, waiting for transfers between devices: 6.97 us -> 90.6 us  [local(): visc_in = lax.all_gather(visc_share, 'seg', axis=0)]
    ppermute x1, waiting for transfers between devices: 75.4 us -> 0.01 us  [local(): below = lax.ppermute(ends[1], 'slab', forward)]
    ppermute x1, waiting for transfers between devices: 2.03 us -> 76.4 us  [local(): above = lax.ppermute(ends[0], 'slab', [(i, j) for j, i in forward])]
    pallas_call x9 -> x12, Pallas kernels: 169 us -> 96.9 us  [call(): pl.pallas_call(kernel, in_specs=[spec for _, spec in ins], out_specs=tupl...]
    ppermute x7 -> x11, waiting for transfers between devices: 180 us -> 109 us  [around(): lax.ppermute(value, axis, [(i, (i + steps) % count) for i in range(count)])]
    all_to_all x0 -> x1, blocking collectives: none -> 51.5 us  [exchange(): lax.all_to_all(chunks, 'slab', split_axis=0, concat_axis=0, tiled=True)]
    unnamed x16 -> x32, local copies, waits for them, and re-layouts: 0.82 us -> 8.91 us
    all_to_all x4 -> x5, starting transfers between devices: 23.5 us -> 31.5 us  [exchange(): lax.all_to_all(chunks, 'slab', split_axis=0, concat_axis=0, tiled=True)]
  transfers between devices with their start and end apart: 14 -> 19, of which waited for: 12 -> 8; matrix products, arithmetic and copies ran while one was open for 0% -> 0% of each run, Pallas kernels for 7% -> 12%
where the time goes in v3:
time: 546 us; the launch traced here: 544 us
  waiting for transfers between devices  323 us (59%)
  Pallas kernels  96.9 us (18%)
  blocking collectives  51.5 us (9%)
  starting transfers between devices  50.2 us (9%)
  between operations  14.2 us (3%)
  local copies, waits for them, and re-layouts  8.93 us (2%)
    ppermute x11, waiting for transfers between devices, around(): lax.ppermute(value, axis, [(i, (i + steps) % count) for i in range(count)])  109 us
    pallas_call x12, Pallas kernels, call(): pl.pallas_call(kernel, in_specs=[spec for _, spec in ins], out_specs=tupl...  96.9 us
    all_gather x1, waiting for transfers between devices, local(): visc_in = lax.all_gather(visc_share, 'seg', axis=0)  90.6 us
    ppermute x1, waiting for transfers between devices, local(): above = lax.ppermute(ends[0], 'slab', [(i, j) for j, i in forward])  76.4 us
    all_to_all x1, blocking collectives, exchange(): lax.all_to_all(chunks, 'slab', split_axis=0, concat_axis=0, tiled=True)  51.5 us
    all_to_all x5, waiting for transfers between devices, exchange(): lax.all_to_all(chunks, 'slab', split_axis=0, concat_axis=0, tiled=True)  46.6 us
    all_to_all x5, starting transfers between devices, exchange(): lax.all_to_all(chunks, 'slab', split_axis=0, concat_axis=0, tiled=True)  31.5 us
    ppermute x11, starting transfers between devices, around(): lax.ppermute(value, axis, [(i, (i + steps) % count) for i in range(count)])  13 us
  transfers between devices with their start and end apart: 19, of which 8 were waited for; matrix products, arithmetic and copies ran while one was open for 0% of the time, Pallas kernels for 12%

profile of v3, /device:TPU:9, one launch (start us, length us, event | category | flops | bytes accessed | tf_op | source)
XLA Modules:
  0.0 544.4 jit_solution(2017400641936024983)
XLA Ops:
  7.2 2.9 visc_chunks.1
  10.1 5.6 %all-to-all-start.1 = ((f32[8,3,32,128]{3,2,1,0:T(8,128)}), f32[8,3,32,128]{3,2,1,0:T(8,128)S(1)}, u32[]{:S(2)}, u32[]{:S(2)}) async-start(f32[8,3,32,128]{3,2,1,0:T(8,128)} %get-tuple-element.23._), calls=%async_computation.1 | async-start | bytes 786432 | tf_op jit(solution)/shard_map/all_to_all | solution.py:628
  15.7 4.2 to_chunks.2
  19.9 5.3 all-to-all-done.1._
  25.9 6.6 %all-to-all-start = ((f32[8,2,8,32,128]{4,3,2,1,0:T(8,128)}), f32[8,2,8,32,128]{4,3,2,1,0:T(8,128)S(1)}, u32[]{:S(2)}, u32[]{:S(2)}) async-start(f32[8,2,8,32,128]{4,3,2,1,0:T(8,128)} %get-tuple-element.24.refs_4_), calls=%async_computation | async-start | bytes 4194304 | tf_op jit(solution)/shard_map/all_to_all | solution.py:628
  32.5 4.2 to_chunks.3
  36.7 41.3 %all-to-all-done.chunks.refs_0_ = f32[8,2,8,32,128]{4,3,2,1,0:T(8,128)S(1)} async-done(((f32[8,2,8,32,128]{4,3,2,1,0:T(8,128)}), f32[8,2,8,32,128]{4,3,2,1,0:T(8,128)S(1)}, u32[]{:S(2)}, u32[]{:S(2)}) %all-to-all-start) | async-done | bytes 2097184 | tf_op jit(solution)/shard_map/all_to_all | solution.py:628
  79.4 7.1 %all-to-all-start.2 = ((f32[8,2,8,32,128]{4,3,2,1,0:T(8,128)}), f32[8,2,8,32,128]{4,3,2,1,0:T(8,128)S(1)}, u32[]{:S(2)}, u32[]{:S(2)}) async-start(f32[8,2,8,32,128]{4,3,2,1,0:T(8,128)} %get-tuple-element.25.refs_5_), calls=%async_computation.2 | async-start | bytes 4194304 | tf_op jit(solution)/shard_map/all_to_all | solution.py:628
  86.5 2.2 collective-permute-start.4
  89.4 2.2 outer_rows.2
  93.4 49.9 %collective-permute-done._.refs_2_ = f32[8,2,2,32,128]{4,3,2,1,0:T(8,128)S(1)} collective-permute-done((f32[8,2,2,32,128]{4,3,2,1,0:T(8,128)}, f32[8,2,2,32,128]{4,3,2,1,0:T(8,128)S(1)}, u32[]{:S(2)}, u32[]{:S(2)}) %collective-permute-start) | collective-permute-done | bytes 524320 | tf_op jit(solution)/shard_map/ppermute | solution.py:633
  145.4 2.2 outer_rows.3
  147.7 2.4 collective-permute-start.1
  150.1 2.9 split.1
  153.0 90.6 %all-gather.3.cloned.1.call-done = f32[32,3,32,128]{3,2,1,0:T(8,128)} async-done(((f32[8,3,32,128]{3,2,1,0:T(8,128)}), f32[32,3,32,128]{3,2,1,0:T(8,128)}) %all-gather.3.cloned.1.call-update) | async-done | bytes 1572880 | tf_op jit(solution)/shard_map/all_gather | solution.py:644
  244.9 14.9 %first_step.1 = (f32[4,10,272,128]{3,2,1,0:T(8,128)}, f32[12,256,128]{2,1,0:T(8,128)}) custom-call(f32[8,2,8,32,128]{4,3,2,1,0:T(8,128)} %copy-done.3, f32[8,2,8,32,128]{4,3,2,1,0:T(8,128)} %copy-done.1, f32[8,2,2,32,128]{4,3,2,1,0:T(8,128)} %copy-done.7, f32[8,2,2,32,128]{4,3,2,1,0:T(8,128)} %copy-done.9, f32[8,2,2,32,128]{4,3,2,1,0:T(8,128)} %copy-done.8, ...), custom_call_target="tpu_custom_call" | custom-call | flops 2013265920 | bytes 14155776 | tf_op jit(solution)/shard_map/first_step/pallas_call | solution.py:41
  259.8 11.4 %second_step.1 = (f32[8,2,8,32,128]{4,3,2,1,0:T(8,128)}, f32[8,2,8,32,128]{4,3,2,1,0:T(8,128)}) custom-call(f32[4,10,272,128]{3,2,1,0:T(8,128)} %get-tuple-element.32.first.refs_6_, f32[12,256,128]{2,1,0:T(8,128)} %get-tuple-element.33.visc.refs_7_, bf16[4,256,256]{2,1,0:T(8,128)(2,1)} %get-tuple-element.30.refs_8_.mat_high, ...), custom_call_target="tpu_custom_call" | custom-call | flops 1610612736 | bytes 11337728 | tf_op jit(solution)/shard_map/second_step/pallas_call | solution.py:41
  271.1 51.5 %all_to_all.30.refs_4_.half = f32[8,2,8,32,128]{4,3,2,1,0:T(8,128)} all-to-all(f32[8,2,8,32,128]{4,3,2,1,0:T(8,128)} %get-tuple-element.34.refs_0_), channel_id=1, replica_groups=mesh['seg'=4,'slab'=8] {'slab'}, dimensions={0} | all-to-all | bytes 4194304 | tf_op jit(solution)/shard_map/all_to_all | solution.py:628
  322.6 7.5 %all-to-all-start.4 = ((f32[8,2,8,32,128]{4,3,2,1,0:T(8,128)}), f32[8,2,8,32,128]{4,3,2,1,0:T(8,128)}, u32[]{:S(2)}, u32[]{:S(2)}) async-start(f32[8,2,8,32,128]{4,3,2,1,0:T(8,128)} %get-tuple-element.35.refs_1_), calls=%async_computation.4 | async-start | bytes 4194304 | tf_op jit(solution)/shard_map/all_to_all | solution.py:628
  331.3 45.7 %collective-permute-done.6.refs_3_ = f32[8,2,8,32,128]{4,3,2,1,0:T(8,128)S(1)} collective-permute-done((f32[8,2,8,32,128]{4,3,2,1,0:T(8,128)S(1)}, f32[8,2,8,32,128]{4,3,2,1,0:T(8,128)S(1)}, u32[]{:S(2)}, u32[]{:S(2)}) %collective-permute-start.6) | collective-permute-done | bytes 2097184 | tf_op jit(solution)/shard_map/ppermute | solution.py:633
  378.3 2.7 edge_rows.1
  381.0 2.3 collective-permute-start.7
  383.4 9.4 %collective-permute-done.7.refs_4_ = f32[8,4,32,128]{3,2,1,0:T(8,128)S(1)} collective-permute-done((f32[8,4,32,128]{3,2,1,0:T(8,128)}, f32[8,4,32,128]{3,2,1,0:T(8,128)S(1)}, u32[]{:S(2)}, u32[]{:S(2)}) %collective-permute-start.7) | collective-permute-done | bytes 524320 | tf_op jit(solution)/shard_map/ppermute | solution.py:633
  392.8 3.9 collective-permute-done.8.refs_5_
  397.5 19.4 %adjoint_step.1._ = f32[8,34,32,128]{3,2,1,0:T(8,128)} custom-call(f32[8,2,8,32,128]{4,3,2,1,0:T(8,128)} %get-tuple-element.34.refs_0_, f32[8,2,8,32,128]{4,3,2,1,0:T(8,128)} %get-tuple-element.35.refs_1_, f32[8,2,8,32,128]{4,3,2,1,0:T(8,128)} %collective-permute-done.5._.refs_2_, f32[8,2,8,32,128]{4,3,2,1,0:T(8,128)} %copy-done.4, ...), custom_call_target="tpu_custom_call" | custom-call | flops 3623878656 | bytes 18677760 | tf_op jit(solution)/shard_map/adjoint_step/pallas_call | solution.py:41
  416.9 4.7 all-to-all-start.5
  421.6 2.2 collective-permute-start.11
  423.8 14.5 %residual_planes.1 = (f32[8192,128]{1,0:T(8,128)}, f32[8,2,8,32,128]{4,3,2,1,0:T(8,128)}) custom-call(f32[8,2,8,32,128]{4,3,2,1,0:T(8,128)} %all_to_all.30.refs_4_.half, f32[8,2,8,32,128]{4,3,2,1,0:T(8,128)} %all-to-all-done.4.other, f32[8192,128]{1,0:T(8,128)} %bitcast.5.target, f32[8,34,32,128]{3,2,1,0:T(8,128)} %adjoint_step.1._), custom_call_target="tpu_custom_call" | custom-call | bytes 12845056 | tf_op jit(solution)/shard_map/residual_planes/pallas_call | solution.py:41
  438.6 2.6 collective-permute-start.10
  441.2 3.0 collective-permute-start.9
  444.2 76.4 %collective-permute-done.10.refs_2_ = f32[4,64,128]{2,1,0:T(8,128)S(1)} collective-permute-done((f32[4,64,128]{2,1,0:T(8,128)S(1)}, f32[4,64,128]{2,1,0:T(8,128)S(1)}, u32[]{:S(2)}, u32[]{:S(2)}) %collective-permute-start.10) | collective-permute-done | bytes 131104 | tf_op jit(solution)/shard_map/ppermute | solution.py:652
  522.1 15.5 %last_step.1 = f32[4,2048,128]{2,1,0:T(8,128)} custom-call(f32[64,32,128]{2,1,0:T(8,128)} %get-tuple-element.41.refs_0_, f32[4,64,128]{2,1,0:T(8,128)} %copy-done.15, f32[4,64,128]{2,1,0:T(8,128)} %copy-done.14, f32[8,34,32,128]{3,2,1,0:T(8,128)} %all-to-all-done.5.refs_3_, f32[8,2,8,32,128]{4,3,2,1,0:T(8,128)} %get-tuple-element.24.refs_4_, ...), custom_call_target="tpu_custom_call" | custom-call | flops 31457280 | bytes 14155776 | tf_op jit(solution)/shard_map/last_step/pallas_call | solution.py:41
  (53 shorter events, 12.9 us)
Async XLA Ops:
  10.1 15.1 %all-to-all-start.1 = ((f32[8,3,32,128]{3,2,1,0:T(8,128)}), f32[8,3,32,128]{3,2,1,0:T(8,128)S(1)}, u32[]{:S(2)}, u32[]{:S(2)}) async-start(f32[8,3,32,128]{3,2,1,0:T(8,128)} %get-tuple-element.23._), calls=%async_computation.1 | async-start | bytes 786432 | tf_op jit(solution)/shard_map/all_to_all | solution.py:628
  25.9 52.1 %all-to-all-start = ((f32[8,2,8,32,128]{4,3,2,1,0:T(8,128)}), f32[8,2,8,32,128]{4,3,2,1,0:T(8,128)S(1)}, u32[]{:S(2)}, u32[]{:S(2)}) async-start(f32[8,2,8,32,128]{4,3,2,1,0:T(8,128)} %get-tuple-element.24.refs_4_), calls=%async_computation | async-start | bytes 4194304 | tf_op jit(solution)/shard_map/all_to_all | solution.py:628
  78.1 1.3 copy-start.3
  79.4 63.9 %all-to-all-start.2 = ((f32[8,2,8,32,128]{4,3,2,1,0:T(8,128)}), f32[8,2,8,32,128]{4,3,2,1,0:T(8,128)S(1)}, u32[]{:S(2)}, u32[]{:S(2)}) async-start(f32[8,2,8,32,128]{4,3,2,1,0:T(8,128)} %get-tuple-element.25.refs_5_), calls=%async_computation.2 | async-start | bytes 4194304 | tf_op jit(solution)/shard_map/all_to_all | solution.py:628
  86.5 157.2 %all-gather.3.cloned.1.call-start = ((), (), s32[]{:S(2)}) async-start(), calls=%async_computation.6 | async-start | bytes 1966080 | tf_op jit(solution)/shard_map/all_gather | solution.py:644
  86.5 157.2 %collective-permute-start.4 = (f32[4,32,64,128]{3,2,1,0:T(8,128)}, f32[4,32,64,128]{3,2,1,0:T(8,128)}, u32[]{:S(2)}, u32[]{:S(2)}) collective-permute-start(f32[4,32,64,128]{3,2,1,0:T(8,128)} %bitcast.14), channel_id=1, source_target_pairs={{0,24},{8,0},{16,8},{24,16},{1,25},{9,1},{17,9},{25,17},{2,26},{10... | collective-permute-start | bytes 12582920 | tf_op jit(solution)/shard_map/ppermute | solution.py:633
  88.7 171.1 %collective-permute-start.5 = (f32[8,2,8,32,128]{4,3,2,1,0:T(8,128)}, f32[8,2,8,32,128]{4,3,2,1,0:T(8,128)}, u32[]{:S(2)}, u32[]{:S(2)}) collective-permute-start(f32[8,2,8,32,128]{4,3,2,1,0:T(8,128)} %copy-done.3), channel_id=1, source_target_pairs={{0,24},{8,0},{16,8},{24,16},{1,25},{9,1},{17,9},{25,17},{2,26},{10... | collective-permute-start | bytes 6291464 | tf_op jit(solution)/shard_map/ppermute | solution.py:633
  91.6 51.7 %collective-permute-start = (f32[8,2,2,32,128]{4,3,2,1,0:T(8,128)}, f32[8,2,2,32,128]{4,3,2,1,0:T(8,128)S(1)}, u32[]{:S(2)}, u32[]{:S(2)}) collective-permute-start(f32[8,2,2,32,128]{4,3,2,1,0:T(8,128)} %get-tuple-element.26), channel_id=1, source_target_pairs={{0,1},{1,2},{2,3},{3,4},{4,5},{5,6},{6,7},{7,0},{8,9},{9,10},{10,1... | collective-permute-start | bytes 1572872 | tf_op jit(solution)/shard_map/ppermute | solution.py:633
  93.4 150.3 %collective-permute-start.2 = (f32[8,2,2,32,128]{4,3,2,1,0:T(8,128)}, f32[8,2,2,32,128]{4,3,2,1,0:T(8,128)S(1)}, u32[]{:S(2)}, u32[]{:S(2)}) collective-permute-start(f32[8,2,2,32,128]{4,3,2,1,0:T(8,128)} %get-tuple-element.28), channel_id=1, source_target_pairs={{0,7},{1,0},{2,1},{3,2},{4,3},{5,4},{6,5},{7,6},{8,15},{9,8},{10,9... | collective-permute-start | bytes 1572872 | tf_op jit(solution)/shard_map/ppermute | solution.py:633
  143.3 0.9 copy-start.7
  144.1 1.3 copy-start.1
  147.7 96.0 %collective-permute-start.1 = (f32[8,2,2,32,128]{4,3,2,1,0:T(8,128)}, f32[8,2,2,32,128]{4,3,2,1,0:T(8,128)S(1)}, u32[]{:S(2)}, u32[]{:S(2)}) collective-permute-start(f32[8,2,2,32,128]{4,3,2,1,0:T(8,128)} %get-tuple-element.27), channel_id=1, source_target_pairs={{0,1},{1,2},{2,3},{3,4},{4,5},{5,6},{6,7},{7,0},{8,9},{9,10},{10,1... | collective-permute-start | bytes 1572872 | tf_op jit(solution)/shard_map/ppermute | solution.py:633
  150.1 93.6 %collective-permute-start.3 = (f32[8,2,2,32,128]{4,3,2,1,0:T(8,128)}, f32[8,2,2,32,128]{4,3,2,1,0:T(8,128)S(1)}, u32[]{:S(2)}, u32[]{:S(2)}) collective-permute-start(f32[8,2,2,32,128]{4,3,2,1,0:T(8,128)} %get-tuple-element.29), channel_id=1, source_target_pairs={{0,7},{1,0},{2,1},{3,2},{4,3},{5,4},{6,5},{7,6},{8,15},{9,8},{10,9... | collective-permute-start | bytes 1572872 | tf_op jit(solution)/shard_map/ppermute | solution.py:633
  243.7 1.0 copy-start.9
  243.7 1.2 copy-start.10
  322.6 7.5 %copy-start.2 = (f32[8,2,8,32,128]{4,3,2,1,0:T(8,128)S(1)}, f32[8,2,8,32,128]{4,3,2,1,0:T(8,128)}, u32[]{:S(2)}) copy-start(f32[8,2,8,32,128]{4,3,2,1,0:T(8,128)} %copy-done.1) | copy-start | bytes 6291460
  322.6 94.3 %all-to-all-start.4 = ((f32[8,2,8,32,128]{4,3,2,1,0:T(8,128)}), f32[8,2,8,32,128]{4,3,2,1,0:T(8,128)}, u32[]{:S(2)}, u32[]{:S(2)}) async-start(f32[8,2,8,32,128]{4,3,2,1,0:T(8,128)} %get-tuple-element.35.refs_1_), calls=%async_computation.4 | async-start | bytes 4194304 | tf_op jit(solution)/shard_map/all_to_all | solution.py:628
  330.2 46.9 %collective-permute-start.6 = (f32[8,2,8,32,128]{4,3,2,1,0:T(8,128)S(1)}, f32[8,2,8,32,128]{4,3,2,1,0:T(8,128)S(1)}, u32[]{:S(2)}, u32[]{:S(2)}) collective-permute-start(f32[8,2,8,32,128]{4,3,2,1,0:T(8,128)S(1)} %copy-done.2), channel_id=1, source_target_pairs={{0,24},{8,0},{16,8},{24,16},{1,25},{9,1},{17,9},{25,17},{2,26},{10... | collective-permute-start | bytes 6291464 | tf_op jit(solution)/shard_map/ppermute | solution.py:633
  377.0 1.3 copy-start.4
  381.0 11.7 %collective-permute-start.7 = (f32[8,4,32,128]{3,2,1,0:T(8,128)}, f32[8,4,32,128]{3,2,1,0:T(8,128)S(1)}, u32[]{:S(2)}, u32[]{:S(2)}) collective-permute-start(f32[8,4,32,128]{3,2,1,0:T(8,128)} %get-tuple-element.36), channel_id=1, source_target_pairs={{0,1},{1,2},{2,3},{3,4},{4,5},{5,6},{6,7},{7,0},{8,9},{9,10},{10,1... | collective-permute-start | bytes 1572872 | tf_op jit(solution)/shard_map/ppermute | solution.py:633
  383.4 13.4 %collective-permute-start.8 = (f32[8,4,32,128]{3,2,1,0:T(8,128)}, f32[8,4,32,128]{3,2,1,0:T(8,128)S(1)}, u32[]{:S(2)}, u32[]{:S(2)}) collective-permute-start(f32[8,4,32,128]{3,2,1,0:T(8,128)} %get-tuple-element.37), channel_id=1, source_target_pairs={{0,7},{1,0},{2,1},{3,2},{4,3},{5,4},{6,5},{7,6},{8,15},{9,8},{10,9... | collective-permute-start | bytes 1572872 | tf_op jit(solution)/shard_map/ppermute | solution.py:633
  392.8 3.9 copy-start.11
  416.9 4.7 copy-start
  416.9 105.1 %all-to-all-start.5 = ((f32[8,34,32,128]{3,2,1,0:T(8,128)}), f32[8,34,32,128]{3,2,1,0:T(8,128)}, u32[]{:S(2)}, u32[]{:S(2)}) async-start(f32[8,34,32,128]{3,2,1,0:T(8,128)} %adjoint_step.1._), calls=%async_computation.5 | async-start | bytes 8912896 | tf_op jit(solution)/shard_map/all_to_all | solution.py:628
  421.6 99.0 %collective-permute-start.11 = (f32[8,2,8,32,128]{4,3,2,1,0:T(8,128)S(1)}, f32[8,2,8,32,128]{4,3,2,1,0:T(8,128)S(1)}, u32[]{:S(2)}, u32[]{:S(2)}) collective-permute-start(f32[8,2,8,32,128]{4,3,2,1,0:T(8,128)S(1)} %copy-done), channel_id=1, source_target_pairs={{0,8},{8,16},{16,24},{24,0},{1,9},{9,17},{17,25},{25,1},{2,10},{10... | collective-permute-start | bytes 6291464 | tf_op jit(solution)/shard_map/ppermute | solution.py:633
  423.8 14.8 %copy-start.13 = (f32[2,4,64,128]{3,2,1,0:T(8,128)S(1)}, f32[2,4,64,128]{3,2,1,0:T(8,128)}, u32[]{:S(2)}) copy-start(f32[2,4,64,128]{3,2,1,0:T(8,128)} %get-tuple-element.42) | copy-start | bytes 786436
  438.3 83.7 %collective-permute-start.12 = (f32[8,2,8,32,128]{4,3,2,1,0:T(8,128)}, f32[8,2,8,32,128]{4,3,2,1,0:T(8,128)}, u32[]{:S(2)}, u32[]{:S(2)}) collective-permute-start(f32[8,2,8,32,128]{4,3,2,1,0:T(8,128)} %get-tuple-element.43), channel_id=1, source_target_pairs={{0,8},{8,16},{16,24},{24,0},{1,9},{9,17},{17,25},{25,1},{2,10},{10... | collective-permute-start | bytes 6291464 | tf_op jit(solution)/shard_map/ppermute | solution.py:633
  438.6 82.0 %collective-permute-start.10 = (f32[4,64,128]{2,1,0:T(8,128)S(1)}, f32[4,64,128]{2,1,0:T(8,128)S(1)}, u32[]{:S(2)}, u32[]{:S(2)}) collective-permute-start(f32[4,64,128]{2,1,0:T(8,128)S(1)} %get-tuple-element.44), channel_id=1, source_target_pairs={{1,0},{2,1},{3,2},{4,3},{5,4},{6,5},{7,6},{9,8},{10,9},{11,10},{12... | collective-permute-start | bytes 393224 | tf_op jit(solution)/shard_map/ppermute | solution.py:652
  441.2 79.4 %collective-permute-start.9 = (f32[4,64,128]{2,1,0:T(8,128)S(1)}, f32[4,64,128]{2,1,0:T(8,128)S(1)}, u32[]{:S(2)}, u32[]{:S(2)}) collective-permute-start(f32[4,64,128]{2,1,0:T(8,128)S(1)} %get-tuple-element.45), channel_id=1, source_target_pairs={{0,1},{1,2},{2,3},{3,4},{4,5},{5,6},{6,7},{8,9},{9,10},{10,11},{11... | collective-permute-start | bytes 393224 | tf_op jit(solution)/shard_map/ppermute | solution.py:651
  520.6 1.4 copy-start.14
  520.6 1.4 copy-start.15
  520.6 1.4 copy-start.6
  (3 other events, 2.4 us)
Sparse Core Ops, SparseCore 0:
  89.1 154.4 all-gather.2

commit v4 on v3

--- a/solution.py
+++ b/solution.py
@@ -173,7 +173,7 @@
     )
 
 
-def planes_kernel(half, other, target, _, o_ref, again, held, sem):
+def planes_kernel(half, other, _, o_ref, again, held, sem):
     slabs, _, block, depth, _ = half.shape
     rows = slabs * block
     pairs = []
@@ -182,32 +182,30 @@
         pairs.append((half.at[p], held.at[pl.ds(0, 2), place]))
         pairs.append((other.at[p], held.at[pl.ds(2, 2), place]))
     wait_all(start_all(pairs, sem))
+    places = [held.at[pl.ds(2, 2), pl.ds(p * block, block)] for p in range(slabs)]
+    copies = start_all([(places[p], again.at[p]) for p in range(slabs)], sem)
 
     def row(y, _):
         for f in range(fields):
-            where = pl.ds(f * depth * rows + y, depth, stride=rows)
-            o_ref[where, :] = held[f, y] - target[where, :]
+            o_ref[pl.ds(f * depth * rows + y, depth, stride=rows), :] = held[f, y]
         return 0
 
-    places = [held.at[pl.ds(2, 2), pl.ds(p * block, block)] for p in range(slabs)]
-    copies = start_all([(places[p], again.at[p]) for p in range(slabs)], sem)
     lax.fori_loop(0, rows, row, 0, unroll=4)
     wait_all(copies)
 
 
-def residual_planes(halves, target, later):
+def to_planes(halves, later):
     slabs, _, block, depth, width = halves[0].shape
     return call(
         planes_kernel,
-        [(halves[0], anywhere()), (halves[1], anywhere())]
-        + [(target.reshape(-1, width), whole()), (later, anywhere())],
+        [(x, anywhere()) for x in (*halves, later)],
         [
             ((fields * depth * slabs * block, width), whole()),
             (halves[1].shape, anywhere()),
         ],
         [vmem(fields, slabs * block, depth, width), dmas(2 * slabs)],
         0,
-        "residual_planes",
+        "to_planes",
     )
 
 
@@ -218,12 +216,12 @@
         ref[f, :, ref.shape[2] - pad :] = edge
 
 
-def first_fluxes(state, visc, shift, carry):
+def first_fluxes(state, visc, shift, carry, some=range(fields)):
     order = visc.shape[1]
     for z in range(0, order, tall):
         here, pads = pl.ds(z, tall), pl.ds(z + pad, tall)
         along_y = 0.5 * (visc[shift, here] + visc[shift + 1, here])
-        for f in range(fields):
+        for f in some:
             carry[f, here] = along_y * (state[f, 1, pads] - state[f, 0, pads])
 
 
@@ -235,9 +233,10 @@
     return spread
 
 
-def advance_rows(state, visc, shift, mat_high, mat_low, carry, high, low, count, finish):
+def advance_rows(state, visc, shift, mats, scratch, count, finish, some=range(fields)):
+    mat_high, mat_low, carry, high, low = *mats, *scratch
     order, width = visc.shape[1:]
-    first_fluxes(state, visc, shift, carry)
+    first_fluxes(state, visc, shift, carry, some)
 
     def pair(k, _):
         for half in range(2):
@@ -250,7 +249,7 @@
                 along_x = 0.5 * (own + east(own))
                 along_y = 0.5 * (own + visc[j + shift + 1, here])
                 speed = state[W, j, pads]
-                for f in range(fields):
+                for f in some:
                     value = state[f, j, pads]
                     rate = spread_of(state, f, j, value, here, pads, along_x, along_y, carry)
                     rate = rate - speed * (state[f, j, above] - state[f, j, below])
@@ -259,7 +258,7 @@
                     if f == T:
                         rate = rate + speed
                     high[f, here, side], low[f, here, side] = parts_of(value + time_step * rate)
-        for f in range(fields):
+        for f in some:
             out = product(mat_high[f], mat_low[f], high[f], low[f])
             finish(f, 2 * k, out[:, :width])
             finish(f, 2 * k + 1, out[:, width:])
@@ -298,17 +297,18 @@
     def finish(f, row, piece):
         first[f, row, pl.ds(pad, order)] = piece
 
-    advance_rows(state, visc, 0, mat_high, mat_low, carry, high, low, block + 2, finish)
-
-
-def first_step(halves, low_in, high_in, later, visc_in, mat_high, mat_low):
+    scratch = (carry, high, low)
+    advance_rows(state, visc, 0, (mat_high, mat_low), scratch, block + 2, finish)
+
+
+def first_step(halves, low_in, high_in, visc_in, mat_high, mat_low):
     slabs, _, block, depth, width = halves[0].shape
     segs, _, share = visc_in.shape[:3]
     order = slabs * depth
     volume = fields * (block + 2) * order * width
     return call(
         first_kernel,
-        [(x, anywhere()) for x in (*halves, *low_in, *high_in, later, visc_in)]
+        [(x, anywhere()) for x in (*halves, *low_in, *high_in, visc_in)]
         + [(mat_high, whole()), (mat_low, whole())],
         [
             ((fields, block + 2, order + 2 * pad, width), whole()),
@@ -322,108 +322,83 @@
     )
 
 
-def second_kernel(first, visc, mat_high, mat_low, _, half, other, carry, high, low, held, sem):
-    slabs, _, block, depth, _ = half.shape
+def second_kernel(some, first, visc, mat_high, mat_low, target, out, low_edge, high_edge, *rest):
+    state, *scratch, held, sem = rest
+    slabs, _, block, depth, _ = out.shape
+    needed = pl.ds(min(some), 3) if W not in some else pl.ds(W, 2)
+    places = [held.at[:, :, pl.ds(p * depth, depth)] for p in range(slabs)]
+    pairs = [(target.at[p], places[p]) for p in range(slabs)]
+    pairs.append((first.at[needed], state.at[needed]))
+    wait_all(start_all(pairs, sem))
 
     def finish(f, row, piece):
-        held[f, row] = piece
-
-    advance_rows(first, visc, 1, mat_high, mat_low, carry, high, low, block, finish)
-    pairs = []
-    for p in range(slabs):
-        planes = pl.ds(p * depth, depth)
-        pairs.append((held.at[pl.ds(0, 2), :, planes], half.at[p]))
-        pairs.append((held.at[pl.ds(2, 2), :, planes], other.at[p]))
-    wait_all(start_all(pairs, sem))
-
-
-def second_step(first, visc, mat_high, mat_low, slabs, later):
-    _, block, _, width = first.shape
-    block, order = block - 2, visc.shape[1]
-    return call(
-        second_kernel,
-        [(x, whole()) for x in (first, visc, mat_high, mat_low)] + [(later, anywhere())],
-        [((slabs, 2, block, order // slabs, width), anywhere())] * 2,
-        step_scratch(order, width) + [vmem(fields, block, order, width), dmas(2 * slabs)],
-        6 * order * fields * block * order * width,
+        held[f - some[0], row] = piece - held[f - some[0], row]
+
+    advance_rows(state, visc, 1, (mat_high, mat_low), scratch, block, finish, some)
+    copies = start_all([(places[p], out.at[p]) for p in range(slabs)], sem)
+    low_edge[...] = held[:, 0]
+    high_edge[...] = held[:, block - 1]
+    wait_all(copies)
+
+
+def second_step(first, visc, mat_high, mat_low, some, target):
+    width, order = visc.shape[2], visc.shape[1]
+    slabs, _, block, _, _ = target.shape
+    return call(
+        functools.partial(second_kernel, some),
+        [(first, anywhere())]
+        + [(x, whole()) for x in (visc, mat_high, mat_low)]
+        + [(target, anywhere())],
+        [(target.shape, anywhere())] + [((2, order, width), whole())] * 2,
+        [vmem(*first.shape)]
+        + step_scratch(order, width)
+        + [vmem(2, block, order, width), dmas(slabs + 1)],
+        6 * order * 2 * block * order * width,
         "second_step",
     )
 
 
-def outer_kernel(chunks, _, low_rows, high_rows, sem):
+def outer_kernel(chunks, _, low_rows, high_rows, again, sem):
     block = chunks.shape[2]
-    low, high = chunks.at[:, :, pl.ds(0, 2)], chunks.at[:, :, pl.ds(block - 2, 2)]
-    wait_all(start_all([(high, high_rows), (low, low_rows)], sem))
+    wait_all(start_all([(chunks, again)], sem))
+    low_rows[...] = again[:, :, 0:2]
+    high_rows[...] = again[:, :, block - 2 :]
 
 
 def outer_rows(chunks, later):
-    slabs, _, _, depth, width = chunks.shape
-    rows = ((slabs, chunks.shape[1], 2, depth, width), whole())
+    slabs, count, _, depth, width = chunks.shape
+    rows = ((slabs, count, 2, depth, width), whole())
     return call(
         outer_kernel,
         [(chunks, anywhere()), (later, anywhere())],
-        [rows, rows],
-        [dmas(2)],
+        [rows, rows, (chunks.shape, whole())],
+        [dmas(1)],
         0,
         "outer_rows",
     )
 
 
-def edge_kernel(*refs):
-    half, other, *targets, _, low_edge, high_edge, ours, theirs, sem = refs
-    block = half.shape[2]
-    pairs = []
-    for side, row in ((0, 0), (1, block - 1)):
-        for source, span in spans((half, other)):
-            pairs.append((source.at[:, :, row], ours.at[side, :, span]))
-        for source, span in spans(targets):
-            pairs.append((source.at[:, :, row], theirs.at[side, :, span]))
-    wait_all(start_all(pairs, sem))
-    low_edge[...] = ours[0] - theirs[0]
-    high_edge[...] = ours[1] - theirs[1]
-
-
-def edge_rows(halves, targets, later):
-    slabs, _, _, depth, width = halves[0].shape
-    edge = ((slabs, fields, depth, width), whole())
-    both = vmem(2, slabs, fields, depth, width)
-    return call(
-        edge_kernel,
-        [(x, anywhere()) for x in (*halves, *targets, later)],
-        [edge, edge],
-        [both, both, dmas(4 * fields)],
-        0,
-        "edge_rows",
-    )
-
-
 def adjoint_kernel(*refs):
-    half, other, *targets, low_edge, high_edge = refs[:-13]
-    first, visc, mat_high, mat_low = refs[-13:-9]
-    out, cot, less, pulled, ends, carry, high, low, sem = refs[-9:]
-    slabs, _, block, depth, width = half.shape
+    halves, low_edges, high_edges = refs[0:2], refs[2:4], refs[4:6]
+    first, visc, mat_high, mat_low = refs[6:10]
+    out, cot, pulled, ends, carry, high, low, sem = refs[10:]
+    slabs, _, block, depth, width = halves[0].shape
     order = slabs * depth
     main = pl.ds(1, block)
     pairs = []
-    for p in range(slabs):
-        planes = pl.ds(p * depth, depth)
-        for source, span in spans((half, other)):
-            pairs.append((source.at[p], cot.at[span, main, planes]))
-        for source, span in spans(targets):
-            pairs.append((source.at[p], less.at[span, main, planes]))
-        pairs.append((low_edge.at[p], cot.at[:, 0, planes]))
-        pairs.append((high_edge.at[p], cot.at[:, block + 1, planes]))
+    for source, span in spans(halves):
+        for p in range(slabs):
+            pairs.append((source.at[p], cot.at[span, main, pl.ds(p * depth, depth)]))
+    for i in range(2):
+        pairs.append((low_edges[i], cot.at[pl.ds(2 * i, 2), 0]))
+        pairs.append((high_edges[i], cot.at[pl.ds(2 * i, 2), block + 1]))
     copies = start_all(pairs, sem)
     clear_pads(pulled)
-    for f in range(fields):
-        less[f, 0] = jnp.zeros((order, width), f32)
-        less[f, block + 1] = jnp.zeros((order, width), f32)
     wait_all(copies)
 
     def pull(k, _):
         for f in range(fields):
-            pair = [cot[f, 2 * k + i] - less[f, 2 * k + i] for i in range(2)]
-            pair = jnp.concatenate(pair, axis=1)
+            pair = jnp.concatenate([cot[f, 2 * k], cot[f, 2 * k + 1]], axis=1)
             out = product(mat_high[f], mat_low[f], *parts_of(pair))
             pulled[f, 2 * k, pl.ds(pad, order)] = out[:, :width]
             pulled[f, 2 * k + 1, pl.ds(pad, order)] = out[:, width:]
@@ -489,23 +464,22 @@
     ends_copy.wait()
 
 
-def adjoint_step(halves, targets, low_edge, high_edge, first, visc, mat_high, mat_low):
+def adjoint_step(halves, low_edges, high_edges, first, visc, mat_high, mat_low):
     slabs, _, block, depth, width = halves[0].shape
     order = slabs * depth
     volume = fields * (block + 1) * order * width
     return call(
         adjoint_kernel,
-        [(x, anywhere()) for x in (*halves, *targets, low_edge, high_edge)]
+        [(x, anywhere()) for x in (*halves, *low_edges, *high_edges)]
         + [(x, whole()) for x in (first, visc, mat_high, mat_low)],
         [((slabs, fields * block + 2, depth, width), anywhere())],
         [
-            vmem(fields, block + 2, order, width),
             vmem(fields, block + 2, order, width),
             vmem(fields, block + 2, order + 2 * pad, width),
             vmem(slabs, 2, depth, width),
         ]
         + step_scratch(order, width)
-        + [dmas(slabs * (fields + 6))],
+        + [dmas(slabs * fields + 1)],
         12 * order * volume,
         "adjoint_step",
     )[0]
@@ -590,7 +564,7 @@
                 rate = rate + pulled[W, y, main]
             else:
                 rate = rate + (coupling[y] - lost)
-            result = value + time_step * rate - (prior[f, y] - state[f, y, main])
+            result = value + time_step * rate - prior[f, y]
             planes[f, pl.ds(y, depth, stride=rows), :] = result
             return 0
 
@@ -642,7 +616,6 @@
     visc, visc_send = visc_chunks(viscosity, slabs, share)
     visc_share = exchange(visc_send)
     visc_in = lax.all_gather(visc_share, "seg", axis=0)
-    target_planes = around(start, "seg", -1)
     send_half, _ = to_chunks(start, slabs, 0, 2, visc_send)
     main_half = exchange(send_half)
     send_other, ends = to_chunks(start, slabs, 2, 2, visc_share)
@@ -653,27 +626,28 @@
     mat_high, mat_low, adj_high, adj_low = split(inverse)
 
     main = (main_half, main_other)
-    low_in, high_in, later = [], [], visc_share
+    low_in, high_in, target, later = [], [], [], visc_in
     for part in main:
-        low_rows, high_rows = outer_rows(part, later)
+        low_rows, high_rows, again = outer_rows(part, later)
         low_in.append(around(high_rows, "slab", 1))
         high_in.append(around(low_rows, "slab", -1))
+        target.append(around(again, "seg", -1))
         later = low_in[0]
-    target = [around(part, "seg", -1) for part in main]
-
-    first, frame = first_step(
-        main, low_in, high_in, target_planes, visc_in, mat_high, mat_low
-    )
-    halves = second_step(first, frame, mat_high, mat_low, slabs, target[0])
-    half = exchange(halves[0])
-    low_edge, high_edge = edge_rows(halves, target, half)
-    low_edge, high_edge = around(high_edge, "slab", 1), around(low_edge, "slab", -1)
-    pulled = adjoint_step(halves, target, low_edge, high_edge, first, frame, adj_high, adj_low)
-    residual, other = residual_planes((half, exchange(halves[1])), target_planes, pulled)
+
+    first, frame = first_step(main, low_in, high_in, visc_in, mat_high, mat_low)
+    residual, low_edges, high_edges = [], [], []
+    for some, part in zip(((U, V), (W, T)), target):
+        out, low_edge, high_edge = second_step(first, frame, mat_high, mat_low, some, part)
+        residual.append(out)
+        low_edges.append(around(high_edge, "slab", 1))
+        high_edges.append(around(low_edge, "slab", -1))
+    half = exchange(residual[0])
+    pulled = adjoint_step(residual, low_edges, high_edges, first, frame, adj_high, adj_low)
+    planes, other = to_planes((half, exchange(residual[1])), pulled)
     priors = [around(part, "seg", 1) for part in (half, other)]
     gradient = last_step(visc, below, above, exchange(pulled), (send_half, send_other), priors)
     shape = (1, fields, depth, rows, width)
-    return (residual.reshape(shape), gradient.reshape(shape))
+    return (planes.reshape(shape), gradient.reshape(shape))
 
 
 def solution(mesh):

time: 546 us -> 465 us (0.85)
  blocking collectives: 51.5 us -> 0 us
  waiting for transfers between devices: 323 us -> 287 us
    all_gather x1, waiting for transfers between devices: 90.6 us -> 0.01 us  [local(): visc_in = lax.all_gather(visc_share, 'seg', axis=0)]
    ppermute x1, waiting for transfers between devices: 0.01 us -> 80.1 us  [local(): below = lax.ppermute(ends[1], 'slab', forward)]
    ppermute x1, waiting for transfers between devices: 76.4 us -> 1.82 us  [local(): above = lax.ppermute(ends[0], 'slab', [(i, j) for j, i in forward])]
    all_to_all x1 -> x0, blocking collectives: 51.5 us -> none  [exchange(): lax.all_to_all(chunks, 'slab', split_axis=0, concat_axis=0, tiled=True)]
    ppermute x11 -> x12, waiting for transfers between devices: 109 us -> 159 us  [around(): lax.ppermute(value, axis, [(i, (i + steps) % count) for i in range(count)])]
    all_to_all x5 -> x6, starting transfers between devices: 31.5 us -> 35.5 us  [exchange(): lax.all_to_all(chunks, 'slab', split_axis=0, concat_axis=0, tiled=True)]
    ppermute x11 -> x12, starting transfers between devices: 13 us -> 14.2 us  [around(): lax.ppermute(value, axis, [(i, (i + steps) % count) for i in range(count)])]
    all_to_all x5 -> x6, waiting for transfers between devices: 46.6 us -> 45.9 us  [exchange(): lax.all_to_all(chunks, 'slab', split_axis=0, concat_axis=0, tiled=True)]
  transfers between devices with their start and end apart: 19 -> 21, of which waited for: 8 -> 12; matrix products, arithmetic and copies ran while one was open for 0% -> 0% of each run, Pallas kernels for 12% -> 15%
where the time goes in v4:
time: 465 us; the launch traced here: 463 us
  waiting for transfers between devices  287 us (62%)
  Pallas kernels  97.9 us (21%)
  starting transfers between devices  54.8 us (12%)
  between operations  14.3 us (3%)
  local copies, waits for them, and re-layouts  8.46 us (2%)
    ppermute x12, waiting for transfers between devices, around(): lax.ppermute(value, axis, [(i, (i + steps) % count) for i in range(count)])  159 us
    pallas_call x12, Pallas kernels, call(): pl.pallas_call(kernel, in_specs=[spec for _, spec in ins], out_specs=tupl...  97.9 us
    ppermute x1, waiting for transfers between devices, local(): below = lax.ppermute(ends[1], 'slab', forward)  80.1 us
    all_to_all x6, waiting for transfers between devices, exchange(): lax.all_to_all(chunks, 'slab', split_axis=0, concat_axis=0, tiled=True)  45.9 us
    all_to_all x6, starting transfers between devices, exchange(): lax.all_to_all(chunks, 'slab', split_axis=0, concat_axis=0, tiled=True)  35.5 us
    ppermute x12, starting transfers between devices, around(): lax.ppermute(value, axis, [(i, (i + steps) % count) for i in range(count)])  14.2 us
  transfers between devices with their start and end apart: 21, of which 12 were waited for; matrix products, arithmetic and copies ran while one was open for 0% of the time, Pallas kernels for 15%

profile of v4, /device:TPU:9, one launch (start us, length us, event | category | flops | bytes accessed | tf_op | source)
XLA Modules:
  0.0 462.8 jit_solution(6848016480634368521)
XLA Ops:
  7.2 2.9 visc_chunks.1
  10.1 5.6 %all-to-all-start.1 = ((f32[8,3,32,128]{3,2,1,0:T(8,128)}), f32[8,3,32,128]{3,2,1,0:T(8,128)S(1)}, u32[]{:S(2)}, u32[]{:S(2)}) async-start(f32[8,3,32,128]{3,2,1,0:T(8,128)} %get-tuple-element.27._), calls=%async_computation.1 | async-start | bytes 786432 | tf_op jit(solution)/shard_map/all_to_all | solution.py:602
  15.7 4.2 to_chunks.2
  19.9 5.3 %all-to-all-done.1._ = f32[8,3,32,128]{3,2,1,0:T(8,128)S(1)} async-done(((f32[8,3,32,128]{3,2,1,0:T(8,128)}), f32[8,3,32,128]{3,2,1,0:T(8,128)S(1)}, u32[]{:S(2)}, u32[]{:S(2)}) %all-to-all-start.1) | async-done | bytes 393248 | tf_op jit(solution)/shard_map/all_to_all | solution.py:602
  25.9 6.6 %all-to-all-start = ((f32[8,2,8,32,128]{4,3,2,1,0:T(8,128)}), f32[8,2,8,32,128]{4,3,2,1,0:T(8,128)S(1)}, u32[]{:S(2)}, u32[]{:S(2)}) async-start(f32[8,2,8,32,128]{4,3,2,1,0:T(8,128)} %get-tuple-element.28.refs_4_), calls=%async_computation | async-start | bytes 4194304 | tf_op jit(solution)/shard_map/all_to_all | solution.py:602
  33.3 4.2 to_chunks.3
  37.5 40.6 %all-to-all-done.chunks.refs_0_ = f32[8,2,8,32,128]{4,3,2,1,0:T(8,128)S(1)} async-done(((f32[8,2,8,32,128]{4,3,2,1,0:T(8,128)}), f32[8,2,8,32,128]{4,3,2,1,0:T(8,128)S(1)}, u32[]{:S(2)}, u32[]{:S(2)}) %all-to-all-start) | async-done | bytes 2097184 | tf_op jit(solution)/shard_map/all_to_all | solution.py:602
  79.4 7.8 %all-to-all-start.2 = ((f32[8,2,8,32,128]{4,3,2,1,0:T(8,128)}), f32[8,2,8,32,128]{4,3,2,1,0:T(8,128)}, u32[]{:S(2)}, u32[]{:S(2)}) async-start(f32[8,2,8,32,128]{4,3,2,1,0:T(8,128)} %get-tuple-element.29.refs_5_), calls=%async_computation.2 | async-start | bytes 4194304 | tf_op jit(solution)/shard_map/all_to_all | solution.py:602
  87.2 3.3 outer_rows.2
  90.5 2.2 collective-permute-start.4
  94.4 49.5 %collective-permute-done._.refs_2_ = f32[8,2,2,32,128]{4,3,2,1,0:T(8,128)S(1)} collective-permute-done((f32[8,2,2,32,128]{4,3,2,1,0:T(8,128)}, f32[8,2,2,32,128]{4,3,2,1,0:T(8,128)S(1)}, u32[]{:S(2)}, u32[]{:S(2)}) %collective-permute-start) | collective-permute-done | bytes 524320 | tf_op jit(solution)/shard_map/ppermute | solution.py:607
  144.8 3.4 outer_rows.3
  148.2 2.4 collective-permute-start.1
  150.6 2.9 split.1
  153.5 8.4 %collective-permute-done.1.refs_3_ = f32[8,2,2,32,128]{4,3,2,1,0:T(8,128)S(1)} collective-permute-done((f32[8,2,2,32,128]{4,3,2,1,0:T(8,128)}, f32[8,2,2,32,128]{4,3,2,1,0:T(8,128)S(1)}, u32[]{:S(2)}, u32[]{:S(2)}) %collective-permute-start.1) | collective-permute-done | bytes 524320 | tf_op jit(solution)/shard_map/ppermute | solution.py:607
  163.3 14.9 %first_step.1 = (f32[4,10,272,128]{3,2,1,0:T(8,128)}, f32[12,256,128]{2,1,0:T(8,128)}) custom-call(f32[8,2,8,32,128]{4,3,2,1,0:T(8,128)} %copy-done, f32[8,2,8,32,128]{4,3,2,1,0:T(8,128)} %all-to-all-done.2.chunks.refs_1_, f32[8,2,2,32,128]{4,3,2,1,0:T(8,128)} %copy-done.6, f32[8,2,2,32,128]{4,3,2,1,0:T(8,128)} %copy-done.8, ...), custom_call_target="tpu_custom_call" | custom-call | flops 2013265920 | bytes 9961472 | tf_op jit(solution)/shard_map/first_step/pallas_call | solution.py:41
  179.5 10.6 %second_step.2 = (f32[8,2,8,32,128]{4,3,2,1,0:T(8,128)}, f32[2,256,128]{2,1,0:T(8,128)}, f32[2,256,128]{2,1,0:T(8,128)}) custom-call(f32[4,10,272,128]{3,2,1,0:T(8,128)} %get-tuple-element.36.first.refs_6_, f32[12,256,128]{2,1,0:T(8,128)} %get-tuple-element.37.visc.refs_7_, bf16[4,256,256]{2,1,0:T(8,128)(2,1)} %get-tuple-element.34.refs_7_.mat_high, ...), custom_call_target="tpu_custom_call" | custom-call | flops 805306368 | bytes 11337728 | tf_op jit(solution)/shard_map/second_step/pallas_call | solution.py:41
  190.1 4.7 %all-to-all-start.3 = ((f32[8,2,8,32,128]{4,3,2,1,0:T(8,128)}), f32[8,2,8,32,128]{4,3,2,1,0:T(8,128)S(1)}, u32[]{:S(2)}, u32[]{:S(2)}) async-start(f32[8,2,8,32,128]{4,3,2,1,0:T(8,128)} %get-tuple-element.39.refs_0_), calls=%async_computation.3 | async-start | bytes 4194304 | tf_op jit(solution)/shard_map/all_to_all | solution.py:602
  194.8 2.2 collective-permute-start.5
  197.0 45.0 %collective-permute-done.5.target = f32[8,2,8,32,128]{4,3,2,1,0:T(8,128)S(1)} collective-permute-done((f32[8,2,8,32,128]{4,3,2,1,0:T(8,128)}, f32[8,2,8,32,128]{4,3,2,1,0:T(8,128)S(1)}, u32[]{:S(2)}, u32[]{:S(2)}) %collective-permute-start.5) | collective-permute-done | bytes 2097184 | tf_op jit(solution)/shard_map/ppermute | solution.py:607
  243.3 10.2 %second_step.3 = (f32[8,2,8,32,128]{4,3,2,1,0:T(8,128)}, f32[2,256,128]{2,1,0:T(8,128)}, f32[2,256,128]{2,1,0:T(8,128)}) custom-call(f32[4,10,272,128]{3,2,1,0:T(8,128)} %get-tuple-element.36.first.refs_6_, f32[12,256,128]{2,1,0:T(8,128)} %get-tuple-element.37.visc.refs_7_, bf16[4,256,256]{2,1,0:T(8,128)(2,1)} %get-tuple-element.34.refs_7_.mat_high, ...), custom_call_target="tpu_custom_call" | custom-call | flops 805306368 | bytes 11337728 | tf_op jit(solution)/shard_map/second_step/pallas_call | solution.py:41
  253.6 6.2 %all-to-all-start.4 = ((f32[8,2,8,32,128]{4,3,2,1,0:T(8,128)}), f32[8,2,8,32,128]{4,3,2,1,0:T(8,128)}, u32[]{:S(2)}, u32[]{:S(2)}) async-start(f32[8,2,8,32,128]{4,3,2,1,0:T(8,128)} %get-tuple-element.41.refs_1_), calls=%async_computation.4 | async-start | bytes 4194304 | tf_op jit(solution)/shard_map/all_to_all | solution.py:602
  263.0 50.7 %collective-permute-done.6.refs_2_ = f32[2,256,128]{2,1,0:T(8,128)S(1)} collective-permute-done((f32[2,256,128]{2,1,0:T(8,128)S(1)}, f32[2,256,128]{2,1,0:T(8,128)S(1)}, u32[]{:S(2)}, u32[]{:S(2)}) %collective-permute-start.6) | collective-permute-done | bytes 262176 | tf_op jit(solution)/shard_map/ppermute | solution.py:607
  313.7 1.8 collective-permute-done.8.refs_4_
  319.0 17.5 %adjoint_step.1._ = f32[8,34,32,128]{3,2,1,0:T(8,128)} custom-call(f32[8,2,8,32,128]{4,3,2,1,0:T(8,128)} %get-tuple-element.39.refs_0_, f32[8,2,8,32,128]{4,3,2,1,0:T(8,128)} %get-tuple-element.41.refs_1_, f32[2,256,128]{2,1,0:T(8,128)} %copy-done.10, f32[2,256,128]{2,1,0:T(8,128)} %copy-done.12, f32[2,256,128]{2,1,0:T(8,128)} %copy-done.11, ...), custom_call_target="tpu_custom_call" | custom-call | flops 3623878656 | bytes 14483456 | tf_op jit(solution)/shard_map/adjoint_step/pallas_call | solution.py:41
  336.5 4.5 all-to-all-start.5
  341.1 2.1 collective-permute-start.12
  343.2 8.6 %to_planes.1 = (f32[8192,128]{1,0:T(8,128)}, f32[8,2,8,32,128]{4,3,2,1,0:T(8,128)}) custom-call(f32[8,2,8,32,128]{4,3,2,1,0:T(8,128)} %copy-done.1, f32[8,2,8,32,128]{4,3,2,1,0:T(8,128)} %all-to-all-done.4.other, f32[8,34,32,128]{3,2,1,0:T(8,128)} %adjoint_step.1._), custom_call_target="tpu_custom_call" | custom-call | bytes 8650752 | tf_op jit(solution)/shard_map/to_planes/pallas_call | solution.py:41
  352.2 3.2 collective-permute-start.10
  355.4 1.9 collective-permute-start.11
  357.4 80.1 %collective-permute-done.10.refs_1_ = f32[4,64,128]{2,1,0:T(8,128)S(1)} collective-permute-done((f32[4,64,128]{2,1,0:T(8,128)S(1)}, f32[4,64,128]{2,1,0:T(8,128)S(1)}, u32[]{:S(2)}, u32[]{:S(2)}) %collective-permute-start.10) | collective-permute-done | bytes 131104 | tf_op jit(solution)/shard_map/ppermute | solution.py:624
  440.7 15.2 %last_step.1 = f32[4,2048,128]{2,1,0:T(8,128)} custom-call(f32[64,32,128]{2,1,0:T(8,128)} %get-tuple-element.49.refs_0_, f32[4,64,128]{2,1,0:T(8,128)} %copy-done.15, f32[4,64,128]{2,1,0:T(8,128)} %copy-done.16, f32[8,34,32,128]{3,2,1,0:T(8,128)} %all-to-all-done.5.refs_3_, f32[8,2,8,32,128]{4,3,2,1,0:T(8,128)} %get-tuple-element.28.refs_4_, ...), custom_call_target="tpu_custom_call" | custom-call | flops 31457280 | bytes 14155776 | tf_op jit(solution)/shard_map/last_step/pallas_call | solution.py:41
  (66 shorter events, 19.7 us)
Async XLA Ops:
  10.1 15.1 %all-to-all-start.1 = ((f32[8,3,32,128]{3,2,1,0:T(8,128)}), f32[8,3,32,128]{3,2,1,0:T(8,128)S(1)}, u32[]{:S(2)}, u32[]{:S(2)}) async-start(f32[8,3,32,128]{3,2,1,0:T(8,128)} %get-tuple-element.27._), calls=%async_computation.1 | async-start | bytes 786432 | tf_op jit(solution)/shard_map/all_to_all | solution.py:602
  25.9 52.1 %all-to-all-start = ((f32[8,2,8,32,128]{4,3,2,1,0:T(8,128)}), f32[8,2,8,32,128]{4,3,2,1,0:T(8,128)S(1)}, u32[]{:S(2)}, u32[]{:S(2)}) async-start(f32[8,2,8,32,128]{4,3,2,1,0:T(8,128)} %get-tuple-element.28.refs_4_), calls=%async_computation | async-start | bytes 4194304 | tf_op jit(solution)/shard_map/all_to_all | solution.py:602
  32.5 54.6 %all-gather.3.cloned.1.call-start = ((), (), s32[]{:S(2)}) async-start(), calls=%async_computation.6 | async-start | bytes 1966080 | tf_op jit(solution)/shard_map/all_gather | solution.py:618
  79.4 64.6 %all-to-all-start.2 = ((f32[8,2,8,32,128]{4,3,2,1,0:T(8,128)}), f32[8,2,8,32,128]{4,3,2,1,0:T(8,128)}, u32[]{:S(2)}, u32[]{:S(2)}) async-start(f32[8,2,8,32,128]{4,3,2,1,0:T(8,128)} %get-tuple-element.29.refs_5_), calls=%async_computation.2 | async-start | bytes 4194304 | tf_op jit(solution)/shard_map/all_to_all | solution.py:602
  90.5 87.7 %collective-permute-start.4 = (f32[8,2,8,32,128]{4,3,2,1,0:T(8,128)}, f32[8,2,8,32,128]{4,3,2,1,0:T(8,128)S(1)}, u32[]{:S(2)}, u32[]{:S(2)}) collective-permute-start(f32[8,2,8,32,128]{4,3,2,1,0:T(8,128)} %get-tuple-element.38), channel_id=1, source_target_pairs={{0,24},{8,0},{16,8},{24,16},{1,25},{9,1},{17,9},{25,17},{2,26},{10... | collective-permute-start | bytes 6291464 | tf_op jit(solution)/shard_map/ppermute | solution.py:607
  92.7 51.2 %collective-permute-start = (f32[8,2,2,32,128]{4,3,2,1,0:T(8,128)}, f32[8,2,2,32,128]{4,3,2,1,0:T(8,128)S(1)}, u32[]{:S(2)}, u32[]{:S(2)}) collective-permute-start(f32[8,2,2,32,128]{4,3,2,1,0:T(8,128)} %get-tuple-element.30), channel_id=1, source_target_pairs={{0,1},{1,2},{2,3},{3,4},{4,5},{5,6},{6,7},{7,0},{8,9},{9,10},{10,1... | collective-permute-start | bytes 1572872 | tf_op jit(solution)/shard_map/ppermute | solution.py:607
  94.4 59.0 %collective-permute-start.2 = (f32[8,2,2,32,128]{4,3,2,1,0:T(8,128)}, f32[8,2,2,32,128]{4,3,2,1,0:T(8,128)S(1)}, u32[]{:S(2)}, u32[]{:S(2)}) collective-permute-start(f32[8,2,2,32,128]{4,3,2,1,0:T(8,128)} %get-tuple-element.32), channel_id=1, source_target_pairs={{0,7},{1,0},{2,1},{3,2},{4,3},{5,4},{6,5},{7,6},{8,15},{9,8},{10,9... | collective-permute-start | bytes 1572872 | tf_op jit(solution)/shard_map/ppermute | solution.py:607
  148.2 13.7 %collective-permute-start.1 = (f32[8,2,2,32,128]{4,3,2,1,0:T(8,128)}, f32[8,2,2,32,128]{4,3,2,1,0:T(8,128)S(1)}, u32[]{:S(2)}, u32[]{:S(2)}) collective-permute-start(f32[8,2,2,32,128]{4,3,2,1,0:T(8,128)} %get-tuple-element.31), channel_id=1, source_target_pairs={{0,1},{1,2},{2,3},{3,4},{4,5},{5,6},{6,7},{7,0},{8,9},{9,10},{10,1... | collective-permute-start | bytes 1572872 | tf_op jit(solution)/shard_map/ppermute | solution.py:607
  150.6 11.9 %collective-permute-start.3 = (f32[8,2,2,32,128]{4,3,2,1,0:T(8,128)}, f32[8,2,2,32,128]{4,3,2,1,0:T(8,128)S(1)}, u32[]{:S(2)}, u32[]{:S(2)}) collective-permute-start(f32[8,2,2,32,128]{4,3,2,1,0:T(8,128)} %get-tuple-element.33), channel_id=1, source_target_pairs={{0,7},{1,0},{2,1},{3,2},{4,3},{5,4},{6,5},{7,6},{8,15},{9,8},{10,9... | collective-permute-start | bytes 1572872 | tf_op jit(solution)/shard_map/ppermute | solution.py:607
  153.5 9.0 %copy-start.7 = (f32[8,2,2,32,128]{4,3,2,1,0:T(8,128)}, f32[8,2,2,32,128]{4,3,2,1,0:T(8,128)S(1)}, u32[]{:S(2)}) copy-start(f32[8,2,2,32,128]{4,3,2,1,0:T(8,128)S(1)} %collective-permute-done.2.refs_4_) | copy-start | bytes 1572868
  190.1 63.5 %all-to-all-start.3 = ((f32[8,2,8,32,128]{4,3,2,1,0:T(8,128)}), f32[8,2,8,32,128]{4,3,2,1,0:T(8,128)S(1)}, u32[]{:S(2)}, u32[]{:S(2)}) async-start(f32[8,2,8,32,128]{4,3,2,1,0:T(8,128)} %get-tuple-element.39.refs_0_), calls=%async_computation.3 | async-start | bytes 4194304 | tf_op jit(solution)/shard_map/all_to_all | solution.py:602
  194.8 47.1 %collective-permute-start.5 = (f32[8,2,8,32,128]{4,3,2,1,0:T(8,128)}, f32[8,2,8,32,128]{4,3,2,1,0:T(8,128)S(1)}, u32[]{:S(2)}, u32[]{:S(2)}) collective-permute-start(f32[8,2,8,32,128]{4,3,2,1,0:T(8,128)} %get-tuple-element.40), channel_id=1, source_target_pairs={{0,24},{8,0},{16,8},{24,16},{1,25},{9,1},{17,9},{25,17},{2,26},{10... | collective-permute-start | bytes 6291464 | tf_op jit(solution)/shard_map/ppermute | solution.py:607
  253.6 87.5 %copy-start.1 = (f32[8,2,8,32,128]{4,3,2,1,0:T(8,128)}, f32[8,2,8,32,128]{4,3,2,1,0:T(8,128)S(1)}, u32[]{:S(2)}) copy-start(f32[8,2,8,32,128]{4,3,2,1,0:T(8,128)S(1)} %all-to-all-done.3.half) | copy-start | bytes 6291460
  253.6 6.2 %copy-start.18 = (f32[2,256,128]{2,1,0:T(8,128)S(1)}, f32[2,256,128]{2,1,0:T(8,128)}, u32[]{:S(2)}) copy-start(f32[2,256,128]{2,1,0:T(8,128)} %get-tuple-element.42) | copy-start | bytes 786436
  253.6 7.7 %copy-start.17 = (f32[2,256,128]{2,1,0:T(8,128)S(1)}, f32[2,256,128]{2,1,0:T(8,128)}, u32[]{:S(2)}) copy-start(f32[2,256,128]{2,1,0:T(8,128)} %get-tuple-element.44) | copy-start | bytes 786436
  253.6 7.7 %copy-start.20 = (f32[2,256,128]{2,1,0:T(8,128)S(1)}, f32[2,256,128]{2,1,0:T(8,128)}, u32[]{:S(2)}) copy-start(f32[2,256,128]{2,1,0:T(8,128)} %get-tuple-element.43) | copy-start | bytes 786436
  253.6 9.4 %copy-start.19 = (f32[2,256,128]{2,1,0:T(8,128)S(1)}, f32[2,256,128]{2,1,0:T(8,128)}, u32[]{:S(2)}) copy-start(f32[2,256,128]{2,1,0:T(8,128)} %get-tuple-element.45) | copy-start | bytes 786436
  253.6 82.9 %all-to-all-start.4 = ((f32[8,2,8,32,128]{4,3,2,1,0:T(8,128)}), f32[8,2,8,32,128]{4,3,2,1,0:T(8,128)}, u32[]{:S(2)}, u32[]{:S(2)}) async-start(f32[8,2,8,32,128]{4,3,2,1,0:T(8,128)} %get-tuple-element.41.refs_1_), calls=%async_computation.4 | async-start | bytes 4194304 | tf_op jit(solution)/shard_map/all_to_all | solution.py:602
  259.8 53.9 %collective-permute-start.6 = (f32[2,256,128]{2,1,0:T(8,128)S(1)}, f32[2,256,128]{2,1,0:T(8,128)S(1)}, u32[]{:S(2)}, u32[]{:S(2)}) collective-permute-start(f32[2,256,128]{2,1,0:T(8,128)S(1)} %copy-done.18), channel_id=1, source_target_pairs={{0,1},{1,2},{2,3},{3,4},{4,5},{5,6},{6,7},{7,0},{8,9},{9,10},{10,1... | collective-permute-start | bytes 786440 | tf_op jit(solution)/shard_map/ppermute | solution.py:607
  261.2 54.3 %collective-permute-start.8 = (f32[2,256,128]{2,1,0:T(8,128)S(1)}, f32[2,256,128]{2,1,0:T(8,128)S(1)}, u32[]{:S(2)}, u32[]{:S(2)}) collective-permute-start(f32[2,256,128]{2,1,0:T(8,128)S(1)} %copy-done.17), channel_id=1, source_target_pairs={{0,7},{1,0},{2,1},{3,2},{4,3},{5,4},{6,5},{7,6},{8,15},{9,8},{10,9... | collective-permute-start | bytes 786440 | tf_op jit(solution)/shard_map/ppermute | solution.py:607
  261.3 55.2 %collective-permute-start.7 = (f32[2,256,128]{2,1,0:T(8,128)S(1)}, f32[2,256,128]{2,1,0:T(8,128)S(1)}, u32[]{:S(2)}, u32[]{:S(2)}) collective-permute-start(f32[2,256,128]{2,1,0:T(8,128)S(1)} %copy-done.20), channel_id=1, source_target_pairs={{0,1},{1,2},{2,3},{3,4},{4,5},{5,6},{6,7},{7,0},{8,9},{9,10},{10,1... | collective-permute-start | bytes 786440 | tf_op jit(solution)/shard_map/ppermute | solution.py:607
  263.0 55.3 %collective-permute-start.9 = (f32[2,256,128]{2,1,0:T(8,128)S(1)}, f32[2,256,128]{2,1,0:T(8,128)S(1)}, u32[]{:S(2)}, u32[]{:S(2)}) collective-permute-start(f32[2,256,128]{2,1,0:T(8,128)S(1)} %copy-done.19), channel_id=1, source_target_pairs={{0,7},{1,0},{2,1},{3,2},{4,3},{5,4},{6,5},{7,6},{8,15},{9,8},{10,9... | collective-permute-start | bytes 786440 | tf_op jit(solution)/shard_map/ppermute | solution.py:607
  313.7 4.6 %copy-start.10 = (f32[2,256,128]{2,1,0:T(8,128)}, f32[2,256,128]{2,1,0:T(8,128)S(1)}, u32[]{:S(2)}) copy-start(f32[2,256,128]{2,1,0:T(8,128)S(1)} %collective-permute-done.6.refs_2_) | copy-start | bytes 786436
  315.5 2.8 copy-start.11
  316.5 1.8 copy-start.12
  336.5 104.2 %all-to-all-start.5 = ((f32[8,34,32,128]{3,2,1,0:T(8,128)}), f32[8,34,32,128]{3,2,1,0:T(8,128)}, u32[]{:S(2)}, u32[]{:S(2)}) async-start(f32[8,34,32,128]{3,2,1,0:T(8,128)} %adjoint_step.1._), calls=%async_computation.5 | async-start | bytes 8912896 | tf_op jit(solution)/shard_map/all_to_all | solution.py:602
  341.1 11.1 %copy-start.14 = (f32[2,4,64,128]{3,2,1,0:T(8,128)S(1)}, f32[2,4,64,128]{3,2,1,0:T(8,128)}, u32[]{:S(2)}) copy-start(f32[2,4,64,128]{3,2,1,0:T(8,128)} %get-tuple-element.50) | copy-start | bytes 786436
  341.1 98.2 %collective-permute-start.12 = (f32[8,2,8,32,128]{4,3,2,1,0:T(8,128)S(1)}, f32[8,2,8,32,128]{4,3,2,1,0:T(8,128)S(1)}, u32[]{:S(2)}, u32[]{:S(2)}) collective-permute-start(f32[8,2,8,32,128]{4,3,2,1,0:T(8,128)S(1)} %all-to-all-done.3.half), channel_id=1, source_target_pairs={{0,8},{8,16},{16,24},{24,0},{1,9},{9,17},{17,25},{25,1},{2,10},{10... | collective-permute-start | bytes 6291464 | tf_op jit(solution)/shard_map/ppermute | solution.py:607
  351.9 88.9 %collective-permute-start.13 = (f32[8,2,8,32,128]{4,3,2,1,0:T(8,128)}, f32[8,2,8,32,128]{4,3,2,1,0:T(8,128)}, u32[]{:S(2)}, u32[]{:S(2)}) collective-permute-start(f32[8,2,8,32,128]{4,3,2,1,0:T(8,128)} %get-tuple-element.51), channel_id=1, source_target_pairs={{0,8},{8,16},{16,24},{24,0},{1,9},{9,17},{17,25},{25,1},{2,10},{10... | collective-permute-start | bytes 6291464 | tf_op jit(solution)/shard_map/ppermute | solution.py:607
  352.2 85.3 %collective-permute-start.10 = (f32[4,64,128]{2,1,0:T(8,128)S(1)}, f32[4,64,128]{2,1,0:T(8,128)S(1)}, u32[]{:S(2)}, u32[]{:S(2)}) collective-permute-start(f32[4,64,128]{2,1,0:T(8,128)S(1)} %get-tuple-element.53), channel_id=1, source_target_pairs={{0,1},{1,2},{2,3},{3,4},{4,5},{5,6},{6,7},{8,9},{9,10},{10,11},{11... | collective-permute-start | bytes 393224 | tf_op jit(solution)/shard_map/ppermute | solution.py:624
  355.4 83.9 %collective-permute-start.11 = (f32[4,64,128]{2,1,0:T(8,128)S(1)}, f32[4,64,128]{2,1,0:T(8,128)S(1)}, u32[]{:S(2)}, u32[]{:S(2)}) collective-permute-start(f32[4,64,128]{2,1,0:T(8,128)S(1)} %get-tuple-element.52), channel_id=1, source_target_pairs={{1,0},{2,1},{3,2},{4,3},{5,4},{6,5},{7,6},{9,8},{10,9},{11,10},{12... | collective-permute-start | bytes 393224 | tf_op jit(solution)/shard_map/ppermute | solution.py:625
  437.5 3.2 copy-start.15
  (10 other events, 10.6 us)
Sparse Core Ops, SparseCore 0:
  35.8 31.6 all-gather.2

commit v5 on v4

--- a/solution.py
+++ b/solution.py
@@ -10,8 +10,9 @@
 time_step = 0.1
 vmem_bytes = 56 * 1024 * 1024
 f32, bf16 = jnp.float32, jnp.bfloat16
-U, V, W, T = range(4)
 fields = 4
+W, T, U, V = range(4)
+outside = (2, 3, 0, 1)
 pad = 8
 tall = 32
 
@@ -92,8 +93,8 @@
 
 def split_kernel(x_ref, high, low, adj_high, adj_low):
     for f in range(fields):
-        high[f], low[f] = parts_of(x_ref[f])
-        adj_high[f], adj_low[f] = parts_of(x_ref[f].T)
+        high[f], low[f] = parts_of(x_ref[outside[f]])
+        adj_high[f], adj_low[f] = parts_of(x_ref[outside[f]].T)
 
 
 def split(inverse):
@@ -187,7 +188,8 @@
 
     def row(y, _):
         for f in range(fields):
-            o_ref[pl.ds(f * depth * rows + y, depth, stride=rows), :] = held[f, y]
+            where = pl.ds(outside[f] * depth * rows + y, depth, stride=rows)
+            o_ref[where, :] = held[f, y]
         return 0
 
     lax.fori_loop(0, rows, row, 0, unroll=4)
@@ -211,17 +213,17 @@
 
 def clear_pads(ref):
     edge = jnp.zeros(ref.shape[1:2] + (pad, ref.shape[3]), f32)
-    for f in range(fields):
+    for f in range(ref.shape[0]):
         ref[f, :, 0:pad] = edge
         ref[f, :, ref.shape[2] - pad :] = edge
 
 
-def first_fluxes(state, visc, shift, carry, some=range(fields)):
+def first_fluxes(state, visc, shift, carry):
     order = visc.shape[1]
     for z in range(0, order, tall):
         here, pads = pl.ds(z, tall), pl.ds(z + pad, tall)
         along_y = 0.5 * (visc[shift, here] + visc[shift + 1, here])
-        for f in some:
+        for f in range(state.shape[0]):
             carry[f, here] = along_y * (state[f, 1, pads] - state[f, 0, pads])
 
 
@@ -233,10 +235,10 @@
     return spread
 
 
-def advance_rows(state, visc, shift, mats, scratch, count, finish, some=range(fields)):
+def advance_rows(state, speeds, visc, shift, mats, base, scratch, count, finish):
     mat_high, mat_low, carry, high, low = *mats, *scratch
     order, width = visc.shape[1:]
-    first_fluxes(state, visc, shift, carry, some)
+    first_fluxes(state, visc, shift, carry)
 
     def pair(k, _):
         for half in range(2):
@@ -248,18 +250,16 @@
                 own = visc[j + shift, here]
                 along_x = 0.5 * (own + east(own))
                 along_y = 0.5 * (own + visc[j + shift + 1, here])
-                speed = state[W, j, pads]
-                for f in some:
+                speed = speeds[j, pads]
+                for f in range(2):
                     value = state[f, j, pads]
                     rate = spread_of(state, f, j, value, here, pads, along_x, along_y, carry)
                     rate = rate - speed * (state[f, j, above] - state[f, j, below])
-                    if f == W:
-                        rate = rate + state[T, j, pads]
-                    if f == T:
-                        rate = rate + speed
+                    if base == W:
+                        rate = rate + state[1 - f, j, pads]
                     high[f, here, side], low[f, here, side] = parts_of(value + time_step * rate)
-        for f in some:
-            out = product(mat_high[f], mat_low[f], high[f], low[f])
+        for f in range(2):
+            out = product(mat_high[base + f], mat_low[base + f], high[f], low[f])
             finish(f, 2 * k, out[:, :width])
             finish(f, 2 * k + 1, out[:, width:])
         return 0
@@ -267,112 +267,178 @@
     lax.fori_loop(0, count // 2, pair, 0)
 
 
-def step_scratch(order, width):
+def step_scratch(order, width, count):
     return [
-        vmem(fields, order, width),
-        pltpu.VMEM((fields, order, 2 * width), bf16),
-        pltpu.VMEM((fields, order, 2 * width), bf16),
+        vmem(count, order, width),
+        pltpu.VMEM((count, order, 2 * width), bf16),
+        pltpu.VMEM((count, order, 2 * width), bf16),
     ]
 
 
-def first_kernel(*refs):
-    visc_in, mat_high, mat_low, first, visc, state, carry, high, low, sem = refs[-10:]
-    halves, low_in, high_in = refs[0:2], refs[2:4], refs[4:6]
-    slabs, _, block, depth, _ = halves[0].shape
+def rows_of(low_in, main, high_in, p, target):
+    _, _, block, depth, _ = main.shape
+    padded = pl.ds(p * depth + pad, depth)
+    for row, count, part in ((0, 2, low_in), (2, block, main), (block + 2, 2, high_in)):
+        yield part, target.at[:, pl.ds(row, count), padded]
+
+
+def first_finish(first, order):
+    def finish(f, row, piece):
+        first[f, row, pl.ds(pad, order)] = piece
+
+    return finish
+
+
+def first_kernel(low_in, main, high_in, visc_in, mat_high, mat_low, first, visc, *scratch):
+    state, *scratch, sem = scratch
+    slabs, _, block, depth, _ = main.shape
     segs, _, share = visc_in.shape[:3]
-    order = visc.shape[1]
     pairs = []
     for p in range(slabs):
-        planes, padded = pl.ds(p * depth, depth), pl.ds(p * depth + pad, depth)
-        for row, count, parts in ((0, 2, low_in), (2, block, halves), (block + 2, 2, high_in)):
-            for part, span in spans(parts):
-                pairs.append((part.at[p], state.at[span, pl.ds(row, count), padded]))
-        for s in range(segs):
-            pairs.append((visc_in.at[s, p], visc.at[pl.ds(share * s, share), planes]))
+        pairs += [(a.at[p], b) for a, b in rows_of(low_in, main, high_in, p, state)]
+        planes = pl.ds(p * depth, depth)
+        for i in range(segs):
+            pairs.append((visc_in.at[i, p], visc.at[pl.ds(share * i, share), planes]))
     copies = start_all(pairs, sem)
     clear_pads(state)
     clear_pads(first)
     wait_all(copies)
-
-    def finish(f, row, piece):
-        first[f, row, pl.ds(pad, order)] = piece
-
-    scratch = (carry, high, low)
-    advance_rows(state, visc, 0, (mat_high, mat_low), scratch, block + 2, finish)
-
-
-def first_step(halves, low_in, high_in, visc_in, mat_high, mat_low):
-    slabs, _, block, depth, width = halves[0].shape
+    mats, finish = (mat_high, mat_low), first_finish(first, slabs * depth)
+    advance_rows(state, state.at[W], visc, 0, mats, W, scratch, block + 2, finish)
+
+
+def first_step(low_in, main, high_in, visc_in, mat_high, mat_low):
+    slabs, _, block, depth, width = main.shape
     segs, _, share = visc_in.shape[:3]
     order = slabs * depth
-    volume = fields * (block + 2) * order * width
+    volume = 2 * (block + 2) * order * width
     return call(
         first_kernel,
-        [(x, anywhere()) for x in (*halves, *low_in, *high_in, visc_in)]
+        [(x, anywhere()) for x in (low_in, main, high_in, visc_in)]
         + [(mat_high, whole()), (mat_low, whole())],
         [
-            ((fields, block + 2, order + 2 * pad, width), whole()),
+            ((2, block + 2, order + 2 * pad, width), whole()),
             ((segs * share, order, width), whole()),
         ],
-        [vmem(fields, block + 4, order + 2 * pad, width)]
-        + step_scratch(order, width)
-        + [dmas(slabs * (6 + segs))],
+        [vmem(2, block + 4, order + 2 * pad, width)]
+        + step_scratch(order, width, 2)
+        + [dmas(slabs * (3 + segs))],
         6 * order * volume,
         "first_step",
     )
 
 
-def second_kernel(some, first, visc, mat_high, mat_low, target, out, low_edge, high_edge, *rest):
-    state, *scratch, held, sem = rest
+def carried_kernel(*refs):
+    low_in, main, high_in, low_w, main_w, high_w, _, _, visc, mat_high, mat_low = refs[:11]
+    first, state, speeds, *scratch, sem = refs[11:]
+    slabs, _, block, depth, _ = main.shape
+    pairs = []
+    for p in range(slabs):
+        pairs += [(a.at[p], b) for a, b in rows_of(low_in, main, high_in, p, state)]
+        w_rows = rows_of(low_w, main_w, high_w, p, speeds)
+        pairs += [(a.at[p, pl.ds(W, 1)], b) for a, b in w_rows]
+    copies = start_all(pairs, sem)
+    clear_pads(state)
+    clear_pads(first)
+    wait_all(copies)
+    mats, finish = (mat_high, mat_low), first_finish(first, slabs * depth)
+    advance_rows(state, speeds.at[0], visc, 0, mats, U, scratch, block + 2, finish)
+
+
+def carried_step(own, with_w, later, visc, mat_high, mat_low):
+    slabs, _, block, depth, width = own[1].shape
+    order = slabs * depth
+    volume = 2 * (block + 2) * order * width
+    return call(
+        carried_kernel,
+        [(x, anywhere()) for x in (*own, *with_w, *later)]
+        + [(x, whole()) for x in (visc, mat_high, mat_low)],
+        [((2, block + 2, order + 2 * pad, width), whole())],
+        [
+            vmem(2, block + 4, order + 2 * pad, width),
+            vmem(1, block + 4, order + 2 * pad, width),
+        ]
+        + step_scratch(order, width, 2)
+        + [dmas(6 * slabs)],
+        6 * order * volume,
+        "carried_step",
+    )[0]
+
+
+def second_kernel(base, first, with_w, visc, mat_high, mat_low, *refs):
+    targets, (out, low_edge, high_edge, state, speeds) = refs[:-10], refs[-10:-5]
+    *scratch, held, sem = refs[-5:]
     slabs, _, block, depth, _ = out.shape
-    needed = pl.ds(min(some), 3) if W not in some else pl.ds(W, 2)
     places = [held.at[:, :, pl.ds(p * depth, depth)] for p in range(slabs)]
-    pairs = [(target.at[p], places[p]) for p in range(slabs)]
-    pairs.append((first.at[needed], state.at[needed]))
+    pairs = [(first, state)] + ([(with_w.at[W], speeds)] if base != W else [])
+    for target, span in spans(targets):
+        for p in range(slabs):
+            pairs.append((target.at[p], held.at[span, :, pl.ds(p * depth, depth)]))
     wait_all(start_all(pairs, sem))
 
     def finish(f, row, piece):
-        held[f - some[0], row] = piece - held[f - some[0], row]
-
-    advance_rows(state, visc, 1, (mat_high, mat_low), scratch, block, finish, some)
+        held[f, row] = piece - held[f, row]
+
+    mats, speeds = (mat_high, mat_low), state.at[W] if base == W else speeds
+    advance_rows(state, speeds, visc, 1, mats, base, scratch, block, finish)
     copies = start_all([(places[p], out.at[p]) for p in range(slabs)], sem)
     low_edge[...] = held[:, 0]
     high_edge[...] = held[:, block - 1]
     wait_all(copies)
 
 
-def second_step(first, visc, mat_high, mat_low, some, target):
+def second_step(first, with_w, visc, mat_high, mat_low, base, targets):
     width, order = visc.shape[2], visc.shape[1]
-    slabs, _, block, _, _ = target.shape
-    return call(
-        functools.partial(second_kernel, some),
-        [(first, anywhere())]
+    slabs, _, block, depth, _ = targets[0].shape
+    return call(
+        functools.partial(second_kernel, base),
+        [(first, anywhere()), (with_w, anywhere())]
         + [(x, whole()) for x in (visc, mat_high, mat_low)]
-        + [(target, anywhere())],
-        [(target.shape, anywhere())] + [((2, order, width), whole())] * 2,
-        [vmem(*first.shape)]
-        + step_scratch(order, width)
-        + [vmem(2, block, order, width), dmas(slabs + 1)],
+        + [(x, anywhere()) for x in targets],
+        [((slabs, 2, block, depth, width), anywhere())] + [((2, order, width), whole())] * 2,
+        [vmem(*first.shape), vmem(*first.shape[1:])]
+        + step_scratch(order, width, 2)
+        + [vmem(2, block, order, width), dmas(2 * slabs + 2)],
         6 * order * 2 * block * order * width,
         "second_step",
     )
 
 
-def outer_kernel(chunks, _, low_rows, high_rows, again, sem):
+def after_kernel(x_ref, *refs):
+    o_ref, sem = refs[-2:]
+    wait_all(start_all([(x_ref, o_ref)], sem))
+
+
+def after(value, later):
+    return call(
+        after_kernel,
+        [(x, anywhere()) for x in (value, *later)],
+        [(value.shape, whole())],
+        [dmas(1)],
+        0,
+        "after",
+    )[0]
+
+
+def outer_kernel(chunks, _, low_rows, high_rows, *refs):
+    *again, sem = refs
     block = chunks.shape[2]
-    wait_all(start_all([(chunks, again)], sem))
-    low_rows[...] = again[:, :, 0:2]
-    high_rows[...] = again[:, :, block - 2 :]
-
-
-def outer_rows(chunks, later):
-    slabs, count, _, depth, width = chunks.shape
+    pairs = [(chunks.at[:, span], part) for part, span in spans(again)]
+    wait_all(start_all(pairs, sem))
+    for part, span in spans(again):
+        low_rows[:, span] = part[:, :, 0:2]
+        high_rows[:, span] = part[:, :, block - 2 :]
+
+
+def outer_rows(chunks, later, pieces):
+    slabs, count, block, depth, width = chunks.shape
     rows = ((slabs, count, 2, depth, width), whole())
+    again = ((slabs, count // pieces, block, depth, width), whole())
     return call(
         outer_kernel,
         [(chunks, anywhere()), (later, anywhere())],
-        [rows, rows, (chunks.shape, whole())],
-        [dmas(1)],
+        [rows, rows] + [again] * pieces,
+        [dmas(pieces)],
         0,
         "outer_rows",
     )
@@ -380,8 +446,8 @@
 
 def adjoint_kernel(*refs):
     halves, low_edges, high_edges = refs[0:2], refs[2:4], refs[4:6]
-    first, visc, mat_high, mat_low = refs[6:10]
-    out, cot, pulled, ends, carry, high, low, sem = refs[10:]
+    firsts, (visc, mat_high, mat_low) = refs[6:8], refs[8:11]
+    out, cot, pulled, ends, carry, high, low, sem = refs[11:]
     slabs, _, block, depth, width = halves[0].shape
     order = slabs * depth
     main = pl.ds(1, block)
@@ -417,7 +483,7 @@
                 own = visc[j + 1, here]
                 along_x = 0.5 * (own + east(own))
                 along_y = 0.5 * (own + visc[j + 2, here])
-                speed_above, speed_below = first[W, j, above], first[W, j, below]
+                speed_above, speed_below = firsts[0][W, j, above], firsts[0][W, j, below]
                 coupling = pulled[T, j, pads]
                 for f in (U, V, T, W):
                     value = pulled[f, j, pads]
@@ -427,7 +493,8 @@
                     if f == W:
                         slope = speed_above - speed_below
                     else:
-                        slope = first[f, j, above] - first[f, j, below]
+                        ref, i = firsts[f // 2], f % 2
+                        slope = ref[i, j, above] - ref[i, j, below]
                     coupling = coupling - value * slope
                     if f == T:
                         rate = rate + pulled[W, j, pads]
@@ -464,21 +531,21 @@
     ends_copy.wait()
 
 
-def adjoint_step(halves, low_edges, high_edges, first, visc, mat_high, mat_low):
+def adjoint_step(halves, low_edges, high_edges, firsts, visc, mat_high, mat_low):
     slabs, _, block, depth, width = halves[0].shape
     order = slabs * depth
     volume = fields * (block + 1) * order * width
     return call(
         adjoint_kernel,
         [(x, anywhere()) for x in (*halves, *low_edges, *high_edges)]
-        + [(x, whole()) for x in (first, visc, mat_high, mat_low)],
+        + [(x, whole()) for x in (*firsts, visc, mat_high, mat_low)],
         [((slabs, fields * block + 2, depth, width), anywhere())],
         [
             vmem(fields, block + 2, order, width),
             vmem(fields, block + 2, order + 2 * pad, width),
             vmem(slabs, 2, depth, width),
         ]
-        + step_scratch(order, width)
+        + step_scratch(order, width, fields)
         + [dmas(slabs * fields + 1)],
         12 * order * volume,
         "adjoint_step",
@@ -522,8 +589,8 @@
             ends_copy.start()
     for f in range(fields):
         for y in range(rows):
-            state[f, y, first] = edges_below[f, y : y + 1]
-            state[f, y, last] = edges_above[f, y : y + 1]
+            state[f, y, first] = edges_below[outside[f], y : y + 1]
+            state[f, y, last] = edges_above[outside[f], y : y + 1]
     ends_copy.wait()
     for f in range(fields):
         for y in range(rows):
@@ -569,7 +636,7 @@
             return 0
 
         lax.fori_loop(0, rows, row, 0, unroll=8)
-        copy = pltpu.make_async_copy(planes.at[f], out.at[f], sem.at[fields, 1 + f])
+        copy = pltpu.make_async_copy(planes.at[f], out.at[outside[f]], sem.at[fields, 1 + f])
         copy.start()
         leaving.append(copy)
     wait_all(leaving)
@@ -616,33 +683,34 @@
     visc, visc_send = visc_chunks(viscosity, slabs, share)
     visc_share = exchange(visc_send)
     visc_in = lax.all_gather(visc_share, "seg", axis=0)
-    send_half, _ = to_chunks(start, slabs, 0, 2, visc_send)
+    send_half, _ = to_chunks(start, slabs, outside[W], 2, visc_send)
     main_half = exchange(send_half)
-    send_other, ends = to_chunks(start, slabs, 2, 2, visc_share)
+    send_other, ends = to_chunks(start, slabs, outside[U], 2, visc_share)
     main_other = exchange(send_other)
     forward = [(i, i + 1) for i in range(slabs - 1)]
     below = lax.ppermute(ends[1], "slab", forward)
     above = lax.ppermute(ends[0], "slab", [(i, j) for j, i in forward])
     mat_high, mat_low, adj_high, adj_low = split(inverse)
 
-    main = (main_half, main_other)
-    low_in, high_in, target, later = [], [], [], visc_in
-    for part in main:
-        low_rows, high_rows, again = outer_rows(part, later)
-        low_in.append(around(high_rows, "slab", 1))
-        high_in.append(around(low_rows, "slab", -1))
-        target.append(around(again, "seg", -1))
-        later = low_in[0]
-
-    first, frame = first_step(main, low_in, high_in, visc_in, mat_high, mat_low)
-    residual, low_edges, high_edges = [], [], []
-    for some, part in zip(((U, V), (W, T)), target):
-        out, low_edge, high_edge = second_step(first, frame, mat_high, mat_low, some, part)
-        residual.append(out)
-        low_edges.append(around(high_edge, "slab", 1))
-        high_edges.append(around(low_edge, "slab", -1))
-    half = exchange(residual[0])
-    pulled = adjoint_step(residual, low_edges, high_edges, first, frame, adj_high, adj_low)
+    own, targets, later = [], [], visc_in
+    for part, pieces in ((main_half, 1), (main_other, 2)):
+        low_rows, high_rows, *again = outer_rows(part, later, pieces)
+        low_in = around(high_rows, "slab", 1)
+        own.append((low_in, part, around(low_rows, "slab", -1)))
+        targets.append([around(piece, "seg", -1) for piece in again])
+        later = low_in
+
+    mats = mat_high, mat_low
+    first_half, frame = first_step(*own[0], visc_in, *mats)
+    out, low_edge, high_edge = second_step(first_half, first_half, frame, *mats, W, targets[0])
+    first_other = carried_step(own[1], own[0], (targets[1][0], out), frame, *mats)
+    other, *more = second_step(first_other, first_half, frame, *mats, U, targets[1])
+    low_edges = [around(edge, "slab", 1) for edge in (high_edge, more[1])]
+    high_edges = [around(edge, "slab", -1) for edge in (low_edge, more[0])]
+    half = exchange(out)
+    residual = (out, after(other, (*low_edges, *high_edges, half)))
+    firsts = (first_half, first_other)
+    pulled = adjoint_step(residual, low_edges, high_edges, firsts, frame, adj_high, adj_low)
     planes, other = to_planes((half, exchange(residual[1])), pulled)
     priors = [around(part, "seg", 1) for part in (half, other)]
     gradient = last_step(visc, below, above, exchange(pulled), (send_half, send_other), priors)

time: 465 us -> 450 us (0.968)
  waiting for transfers between devices: 287 us -> 262 us
  Pallas kernels: 97.9 us -> 107 us
    ppermute x12 -> x13, waiting for transfers between devices: 159 us -> 106 us  [around(): lax.ppermute(value, axis, [(i, (i + steps) % count) for i in range(count)])]
    all_to_all x6, waiting for transfers between devices: 45.9 us -> 73.9 us  [exchange(): lax.all_to_all(chunks, 'slab', split_axis=0, concat_axis=0, tiled=True)]
    pallas_call x12 -> x14, Pallas kernels: 97.9 us -> 107 us  [call(): pl.pallas_call(kernel, in_specs=[spec for _, spec in ins], out_specs=tupl...]
    ppermute x12 -> x13, starting transfers between devices: 14.2 us -> 13.2 us  [around(): lax.ppermute(value, axis, [(i, (i + steps) % count) for i in range(count)])]
  transfers between devices with their start and end apart: 21 -> 22, of which waited for: 12 -> 12; matrix products, arithmetic and copies ran while one was open for 0% -> 0% of each run, Pallas kernels for 15% -> 19%
where the time goes in v5:
time: 450 us; the launch traced here: 449 us
  waiting for transfers between devices  262 us (58%)
  Pallas kernels  107 us (24%)
  starting transfers between devices  55.5 us (12%)
  between operations  14.3 us (3%)
  local copies, waits for them, and re-layouts  9.73 us (2%)
    pallas_call x14, Pallas kernels, call(): pl.pallas_call(kernel, in_specs=[spec for _, spec in ins], out_specs=tupl...  107 us
    ppermute x13, waiting for transfers between devices, around(): lax.ppermute(value, axis, [(i, (i + steps) % count) for i in range(count)])  106 us
    ppermute x1, waiting for transfers between devices, local(): below = lax.ppermute(ends[1], 'slab', forward)  80.4 us
    all_to_all x6, waiting for transfers between devices, exchange(): lax.all_to_all(chunks, 'slab', split_axis=0, concat_axis=0, tiled=True)  73.9 us
    all_to_all x6, starting transfers between devices, exchange(): lax.all_to_all(chunks, 'slab', split_axis=0, concat_axis=0, tiled=True)  36.4 us
    ppermute x13, starting transfers between devices, around(): lax.ppermute(value, axis, [(i, (i + steps) % count) for i in range(count)])  13.2 us
    unnamed x42, local copies, waits for them, and re-layouts  9.71 us
  transfers between devices with their start and end apart: 22, of which 12 were waited for; matrix products, arithmetic and copies ran while one was open for 0% of the time, Pallas kernels for 19%

profile of v5, /device:TPU:9, one launch (start us, length us, event | category | flops | bytes accessed | tf_op | source)
XLA Modules:
  0.0 449.0 jit_solution(17077333911497610137)
XLA Ops:
  7.2 2.9 visc_chunks.1
  10.1 5.6 %all-to-all-start.1 = ((f32[8,3,32,128]{3,2,1,0:T(8,128)}), f32[8,3,32,128]{3,2,1,0:T(8,128)S(1)}, u32[]{:S(2)}, u32[]{:S(2)}) async-start(f32[8,3,32,128]{3,2,1,0:T(8,128)} %get-tuple-element.28._), calls=%async_computation.1 | async-start | bytes 786432 | tf_op jit(solution)/shard_map/all_to_all | solution.py:669
  15.7 4.2 to_chunks.2
  19.9 5.3 %all-to-all-done.1._ = f32[8,3,32,128]{3,2,1,0:T(8,128)S(1)} async-done(((f32[8,3,32,128]{3,2,1,0:T(8,128)}), f32[8,3,32,128]{3,2,1,0:T(8,128)S(1)}, u32[]{:S(2)}, u32[]{:S(2)}) %all-to-all-start.1) | async-done | bytes 393248 | tf_op jit(solution)/shard_map/all_to_all | solution.py:669
  25.9 6.6 %all-to-all-start = ((f32[8,2,8,32,128]{4,3,2,1,0:T(8,128)}), f32[8,2,8,32,128]{4,3,2,1,0:T(8,128)S(1)}, u32[]{:S(2)}, u32[]{:S(2)}) async-start(f32[8,2,8,32,128]{4,3,2,1,0:T(8,128)} %get-tuple-element.29.refs_4_), calls=%async_computation | async-start | bytes 4194304 | tf_op jit(solution)/shard_map/all_to_all | solution.py:669
  33.3 4.2 to_chunks.3
  37.5 40.6 %all-to-all-done.chunks.main.refs_4_ = f32[8,2,8,32,128]{4,3,2,1,0:T(8,128)S(1)} async-done(((f32[8,2,8,32,128]{4,3,2,1,0:T(8,128)}), f32[8,2,8,32,128]{4,3,2,1,0:T(8,128)S(1)}, u32[]{:S(2)}, u32[]{:S(2)}) %all-to-all-start) | async-done | bytes 2097184 | tf_op jit(solution)/shard_map/all_to_all | solution.py:669
  79.4 7.8 %all-to-all-start.3 = ((f32[8,2,8,32,128]{4,3,2,1,0:T(8,128)}), f32[8,2,8,32,128]{4,3,2,1,0:T(8,128)}, u32[]{:S(2)}, u32[]{:S(2)}) async-start(f32[8,2,8,32,128]{4,3,2,1,0:T(8,128)} %get-tuple-element.38.refs_5_), calls=%async_computation.3 | async-start | bytes 4194304 | tf_op jit(solution)/shard_map/all_to_all | solution.py:669
  87.2 3.3 outer_rows.2
  90.5 2.2 collective-permute-start.2
  94.4 2.9 split.1
  97.4 46.6 %collective-permute-done.low_in._.refs_3_ = f32[8,2,2,32,128]{4,3,2,1,0:T(8,128)S(1)} collective-permute-done((f32[8,2,2,32,128]{4,3,2,1,0:T(8,128)}, f32[8,2,2,32,128]{4,3,2,1,0:T(8,128)S(1)}, u32[]{:S(2)}, u32[]{:S(2)}) %collective-permute-start) | collective-permute-done | bytes 524320 | tf_op jit(solution)/shard_map/ppermute | solution.py:674
  146.5 10.4 %first_step.1 = (f32[2,10,272,128]{3,2,1,0:T(8,128)}, f32[12,256,128]{2,1,0:T(8,128)}) custom-call(f32[8,2,2,32,128]{4,3,2,1,0:T(8,128)} %copy-done.3, f32[8,2,8,32,128]{4,3,2,1,0:T(8,128)} %copy-done, f32[8,2,2,32,128]{4,3,2,1,0:T(8,128)} %copy-done.8, f32[4,8,3,32,128]{4,3,2,1,0:T(8,128)} %bitcast.13, ...), custom_call_target="tpu_custom_call" | custom-call | flops 1006632960 | bytes 6815744 | tf_op jit(solution)/shard_map/first_step/pallas_call | solution.py:42
  158.3 10.2 %second_step.2 = (f32[8,2,8,32,128]{4,3,2,1,0:T(8,128)}, f32[2,256,128]{2,1,0:T(8,128)}, f32[2,256,128]{2,1,0:T(8,128)}) custom-call(f32[2,10,272,128]{3,2,1,0:T(8,128)} %get-tuple-element.34.first.with_w.refs_6_, f32[2,10,272,128]{3,2,1,0:T(8,128)} %get-tuple-element.34.first.with_w.refs_6_, f32[12,256,128]{2,1,0:T(8,128)} %get-tuple-element.35.visc.refs_8_, ...), custom_call_target="tpu_custom_call" | custom-call | flops 805306368 | bytes 11337728 | tf_op jit(solution)/shard_map/second_step/pallas_call | solution.py:42
  168.5 3.6 all-to-all-start.2
  172.1 3.2 outer_rows.3
  175.4 2.2 collective-permute-start.5
  177.9 2.0 collective-permute-start.3
  179.8 49.1 %collective-permute-done.3.refs_0_ = f32[8,2,2,32,128]{4,3,2,1,0:T(8,128)S(1)} collective-permute-done((f32[8,2,2,32,128]{4,3,2,1,0:T(8,128)}, f32[8,2,2,32,128]{4,3,2,1,0:T(8,128)S(1)}, u32[]{:S(2)}, u32[]{:S(2)}) %collective-permute-start.3) | collective-permute-done | bytes 524320 | tf_op jit(solution)/shard_map/ppermute | solution.py:674
  232.4 10.8 %carried_step.1.first.refs_7_ = f32[2,10,272,128]{3,2,1,0:T(8,128)} custom-call(f32[8,2,2,32,128]{4,3,2,1,0:T(8,128)} %copy-done.14, f32[8,2,8,32,128]{4,3,2,1,0:T(8,128)} %all-to-all-done.3.chunks.refs_1_, f32[8,2,2,32,128]{4,3,2,1,0:T(8,128)} %copy-done.15, f32[8,2,2,32,128]{4,3,2,1,0:T(8,128)} %copy-done.3, f32[8,2,8,32,128]{4,3,2,1,0:T(8,128)} %copy-done, ...), custom_call_target="tpu_custom_call" | custom-call | flops 1006632960 | bytes 13107200 | tf_op jit(solution)/shard_map/carried_step/pallas_call | solution.py:42
  244.3 10.6 %second_step.3 = (f32[8,2,8,32,128]{4,3,2,1,0:T(8,128)}, f32[2,256,128]{2,1,0:T(8,128)}, f32[2,256,128]{2,1,0:T(8,128)}) custom-call(f32[2,10,272,128]{3,2,1,0:T(8,128)} %carried_step.1.first.refs_7_, f32[2,10,272,128]{3,2,1,0:T(8,128)} %get-tuple-element.34.first.with_w.refs_6_, f32[12,256,128]{2,1,0:T(8,128)} %get-tuple-element.35.visc.refs_8_, ...), custom_call_target="tpu_custom_call" | custom-call | flops 805306368 | bytes 11337728 | tf_op jit(solution)/shard_map/second_step/pallas_call | solution.py:42
  257.2 3.7 collective-permute-done.10.refs_3_.refs_5_
  260.9 2.1 collective-permute-done.7.refs_0_.refs_2_
  265.1 2.9 after.1.refs_1_
  268.0 4.6 %all-to-all-start.4 = ((f32[8,2,8,32,128]{4,3,2,1,0:T(8,128)}), f32[8,2,8,32,128]{4,3,2,1,0:T(8,128)}, u32[]{:S(2)}, u32[]{:S(2)}) async-start(f32[8,2,8,32,128]{4,3,2,1,0:T(8,128)} %after.1.refs_1_), calls=%async_computation.4 | async-start | bytes 4194304 | tf_op jit(solution)/shard_map/all_to_all | solution.py:669
  272.6 17.5 %adjoint_step.1._ = f32[8,34,32,128]{3,2,1,0:T(8,128)} custom-call(f32[8,2,8,32,128]{4,3,2,1,0:T(8,128)} %get-tuple-element.37.refs_7_.refs_0_, f32[8,2,8,32,128]{4,3,2,1,0:T(8,128)} %after.1.refs_1_, f32[2,256,128]{2,1,0:T(8,128)} %copy-done.11, f32[2,256,128]{2,1,0:T(8,128)} %copy-done.10, f32[2,256,128]{2,1,0:T(8,128)} %copy-done.12, ...), custom_call_target="tpu_custom_call" | custom-call | flops 3623878656 | bytes 14483456 | tf_op jit(solution)/shard_map/adjoint_step/pallas_call | solution.py:42
  290.1 28.0 %all-to-all-done.4.other = f32[8,2,8,32,128]{4,3,2,1,0:T(8,128)} async-done(((f32[8,2,8,32,128]{4,3,2,1,0:T(8,128)}), f32[8,2,8,32,128]{4,3,2,1,0:T(8,128)}, u32[]{:S(2)}, u32[]{:S(2)}) %all-to-all-start.4) | async-done | bytes 2097184 | tf_op jit(solution)/shard_map/all_to_all | solution.py:669
  318.2 8.1 %all-to-all-start.5 = ((f32[8,34,32,128]{3,2,1,0:T(8,128)}), f32[8,34,32,128]{3,2,1,0:T(8,128)}, u32[]{:S(2)}, u32[]{:S(2)}) async-start(f32[8,34,32,128]{3,2,1,0:T(8,128)} %adjoint_step.1._), calls=%async_computation.5 | async-start | bytes 8912896 | tf_op jit(solution)/shard_map/all_to_all | solution.py:669
  327.5 8.6 %to_planes.1 = (f32[8192,128]{1,0:T(8,128)}, f32[8,2,8,32,128]{4,3,2,1,0:T(8,128)}) custom-call(f32[8,2,8,32,128]{4,3,2,1,0:T(8,128)} %copy-done.1, f32[8,2,8,32,128]{4,3,2,1,0:T(8,128)} %all-to-all-done.4.other, f32[8,34,32,128]{3,2,1,0:T(8,128)} %adjoint_step.1._), custom_call_target="tpu_custom_call" | custom-call | bytes 8650752 | tf_op jit(solution)/shard_map/to_planes/pallas_call | solution.py:42
  337.5 3.9 collective-permute-start.11
  343.3 80.4 %collective-permute-done.11.refs_1_ = f32[4,64,128]{2,1,0:T(8,128)S(1)} collective-permute-done((f32[4,64,128]{2,1,0:T(8,128)S(1)}, f32[4,64,128]{2,1,0:T(8,128)S(1)}, u32[]{:S(2)}, u32[]{:S(2)}) %collective-permute-start.11) | collective-permute-done | bytes 131104 | tf_op jit(solution)/shard_map/ppermute | solution.py:691
  427.0 15.2 %last_step.1 = f32[4,2048,128]{2,1,0:T(8,128)} custom-call(f32[64,32,128]{2,1,0:T(8,128)} %get-tuple-element.51.refs_0_, f32[4,64,128]{2,1,0:T(8,128)} %copy-done.17, f32[4,64,128]{2,1,0:T(8,128)} %copy-done.18, f32[8,34,32,128]{3,2,1,0:T(8,128)} %all-to-all-done.5.refs_3_, f32[8,2,8,32,128]{4,3,2,1,0:T(8,128)} %get-tuple-element.29.refs_4_, ...), custom_call_target="tpu_custom_call" | custom-call | flops 31457280 | bytes 14155776 | tf_op jit(solution)/shard_map/last_step/pallas_call | solution.py:42
  (70 shorter events, 25.2 us)
Async XLA Ops:
  10.1 15.1 %all-to-all-start.1 = ((f32[8,3,32,128]{3,2,1,0:T(8,128)}), f32[8,3,32,128]{3,2,1,0:T(8,128)S(1)}, u32[]{:S(2)}, u32[]{:S(2)}) async-start(f32[8,3,32,128]{3,2,1,0:T(8,128)} %get-tuple-element.28._), calls=%async_computation.1 | async-start | bytes 786432 | tf_op jit(solution)/shard_map/all_to_all | solution.py:669
  25.9 52.1 %all-to-all-start = ((f32[8,2,8,32,128]{4,3,2,1,0:T(8,128)}), f32[8,2,8,32,128]{4,3,2,1,0:T(8,128)S(1)}, u32[]{:S(2)}, u32[]{:S(2)}) async-start(f32[8,2,8,32,128]{4,3,2,1,0:T(8,128)} %get-tuple-element.29.refs_4_), calls=%async_computation | async-start | bytes 4194304 | tf_op jit(solution)/shard_map/all_to_all | solution.py:669
  32.5 54.6 %all-gather.3.cloned.1.call-start = ((), (), s32[]{:S(2)}) async-start(), calls=%async_computation.6 | async-start | bytes 1966080 | tf_op jit(solution)/shard_map/all_gather | solution.py:685
  79.4 89.2 %all-to-all-start.3 = ((f32[8,2,8,32,128]{4,3,2,1,0:T(8,128)}), f32[8,2,8,32,128]{4,3,2,1,0:T(8,128)}, u32[]{:S(2)}, u32[]{:S(2)}) async-start(f32[8,2,8,32,128]{4,3,2,1,0:T(8,128)} %get-tuple-element.38.refs_5_), calls=%async_computation.3 | async-start | bytes 4194304 | tf_op jit(solution)/shard_map/all_to_all | solution.py:669
  90.5 66.5 %collective-permute-start.2 = (f32[8,2,8,32,128]{4,3,2,1,0:T(8,128)}, f32[8,2,8,32,128]{4,3,2,1,0:T(8,128)S(1)}, u32[]{:S(2)}, u32[]{:S(2)}) collective-permute-start(f32[8,2,8,32,128]{4,3,2,1,0:T(8,128)} %get-tuple-element.36), channel_id=1, source_target_pairs={{0,24},{8,0},{16,8},{24,16},{1,25},{9,1},{17,9},{25,17},{2,26},{10... | collective-permute-start | bytes 6291464 | tf_op jit(solution)/shard_map/ppermute | solution.py:674
  92.7 51.3 %collective-permute-start = (f32[8,2,2,32,128]{4,3,2,1,0:T(8,128)}, f32[8,2,2,32,128]{4,3,2,1,0:T(8,128)S(1)}, u32[]{:S(2)}, u32[]{:S(2)}) collective-permute-start(f32[8,2,2,32,128]{4,3,2,1,0:T(8,128)} %get-tuple-element.30), channel_id=1, source_target_pairs={{0,1},{1,2},{2,3},{3,4},{4,5},{5,6},{6,7},{7,0},{8,9},{9,10},{10,1... | collective-permute-start | bytes 1572872 | tf_op jit(solution)/shard_map/ppermute | solution.py:674
  94.4 51.3 %collective-permute-start.1 = (f32[8,2,2,32,128]{4,3,2,1,0:T(8,128)}, f32[8,2,2,32,128]{4,3,2,1,0:T(8,128)S(1)}, u32[]{:S(2)}, u32[]{:S(2)}) collective-permute-start(f32[8,2,2,32,128]{4,3,2,1,0:T(8,128)} %get-tuple-element.31), channel_id=1, source_target_pairs={{0,7},{1,0},{2,1},{3,2},{4,3},{5,4},{6,5},{7,6},{8,15},{9,8},{10,9... | collective-permute-start | bytes 1572872 | tf_op jit(solution)/shard_map/ppermute | solution.py:674
  144.0 1.7 copy-start.3
  168.5 95.2 %all-to-all-start.2 = ((f32[8,2,8,32,128]{4,3,2,1,0:T(8,128)}), f32[8,2,8,32,128]{4,3,2,1,0:T(8,128)S(1)}, u32[]{:S(2)}, u32[]{:S(2)}) async-start(f32[8,2,8,32,128]{4,3,2,1,0:T(8,128)} %get-tuple-element.37.refs_7_.refs_0_), calls=%async_computation.2 | async-start | bytes 4194304 | tf_op jit(solution)/shard_map/all_to_all | solution.py:669
  175.4 55.3 %collective-permute-start.5 = (f32[8,1,8,32,128]{4,3,2,1,0:T(8,128)}, f32[8,1,8,32,128]{4,3,2,1,0:T(8,128)S(1)}, u32[]{:S(2)}, u32[]{:S(2)}) collective-permute-start(f32[8,1,8,32,128]{4,3,2,1,0:T(8,128)} %get-tuple-element.41), channel_id=1, source_target_pairs={{0,24},{8,0},{16,8},{24,16},{1,25},{9,1},{17,9},{25,17},{2,26},{10... | collective-permute-start | bytes 3145736 | tf_op jit(solution)/shard_map/ppermute | solution.py:674
  177.6 65.7 %collective-permute-start.6 = (f32[8,1,8,32,128]{4,3,2,1,0:T(8,128)}, f32[8,1,8,32,128]{4,3,2,1,0:T(8,128)S(1)}, u32[]{:S(2)}, u32[]{:S(2)}) collective-permute-start(f32[8,1,8,32,128]{4,3,2,1,0:T(8,128)} %get-tuple-element.42), channel_id=1, source_target_pairs={{0,24},{8,0},{16,8},{24,16},{1,25},{9,1},{17,9},{25,17},{2,26},{10... | collective-permute-start | bytes 3145736 | tf_op jit(solution)/shard_map/ppermute | solution.py:674
  177.9 51.0 %collective-permute-start.3 = (f32[8,2,2,32,128]{4,3,2,1,0:T(8,128)}, f32[8,2,2,32,128]{4,3,2,1,0:T(8,128)S(1)}, u32[]{:S(2)}, u32[]{:S(2)}) collective-permute-start(f32[8,2,2,32,128]{4,3,2,1,0:T(8,128)} %get-tuple-element.39), channel_id=1, source_target_pairs={{0,1},{1,2},{2,3},{3,4},{4,5},{5,6},{6,7},{7,0},{8,9},{9,10},{10,1... | collective-permute-start | bytes 1572872 | tf_op jit(solution)/shard_map/ppermute | solution.py:674
  179.8 50.8 %collective-permute-start.4 = (f32[8,2,2,32,128]{4,3,2,1,0:T(8,128)}, f32[8,2,2,32,128]{4,3,2,1,0:T(8,128)S(1)}, u32[]{:S(2)}, u32[]{:S(2)}) collective-permute-start(f32[8,2,2,32,128]{4,3,2,1,0:T(8,128)} %get-tuple-element.40), channel_id=1, source_target_pairs={{0,7},{1,0},{2,1},{3,2},{4,3},{5,4},{6,5},{7,6},{8,15},{9,8},{10,9... | collective-permute-start | bytes 1572872 | tf_op jit(solution)/shard_map/ppermute | solution.py:674
  228.9 1.7 copy-start.14
  243.2 13.4 %copy-start.20 = (f32[2,256,128]{2,1,0:T(8,128)S(1)}, f32[2,256,128]{2,1,0:T(8,128)}, u32[]{:S(2)}) copy-start(f32[2,256,128]{2,1,0:T(8,128)} %get-tuple-element.44) | copy-start | bytes 786436
  243.2 13.4 %copy-start.19 = (f32[2,256,128]{2,1,0:T(8,128)S(1)}, f32[2,256,128]{2,1,0:T(8,128)}, u32[]{:S(2)}) copy-start(f32[2,256,128]{2,1,0:T(8,128)} %get-tuple-element.46) | copy-start | bytes 786436
  254.8 6.1 %collective-permute-start.10 = (f32[2,256,128]{2,1,0:T(8,128)}, f32[2,256,128]{2,1,0:T(8,128)S(1)}, u32[]{:S(2)}, u32[]{:S(2)}) collective-permute-start(f32[2,256,128]{2,1,0:T(8,128)} %get-tuple-element.47), channel_id=1, source_target_pairs={{0,7},{1,0},{2,1},{3,2},{4,3},{5,4},{6,5},{7,6},{8,15},{9,8},{10,9... | collective-permute-start | bytes 786440 | tf_op jit(solution)/shard_map/ppermute | solution.py:674
  254.9 6.0 %collective-permute-start.8 = (f32[2,256,128]{2,1,0:T(8,128)}, f32[2,256,128]{2,1,0:T(8,128)S(1)}, u32[]{:S(2)}, u32[]{:S(2)}) collective-permute-start(f32[2,256,128]{2,1,0:T(8,128)} %get-tuple-element.45), channel_id=1, source_target_pairs={{0,1},{1,2},{2,3},{3,4},{4,5},{5,6},{6,7},{7,0},{8,9},{9,10},{10,1... | collective-permute-start | bytes 786440 | tf_op jit(solution)/shard_map/ppermute | solution.py:674
  256.6 6.3 %collective-permute-start.7 = (f32[2,256,128]{2,1,0:T(8,128)S(1)}, f32[2,256,128]{2,1,0:T(8,128)S(1)}, u32[]{:S(2)}, u32[]{:S(2)}) collective-permute-start(f32[2,256,128]{2,1,0:T(8,128)S(1)} %copy-done.20), channel_id=1, source_target_pairs={{0,1},{1,2},{2,3},{3,4},{4,5},{5,6},{6,7},{7,0},{8,9},{9,10},{10,1... | collective-permute-start | bytes 786440 | tf_op jit(solution)/shard_map/ppermute | solution.py:674
  256.7 7.0 %collective-permute-start.9 = (f32[2,256,128]{2,1,0:T(8,128)S(1)}, f32[2,256,128]{2,1,0:T(8,128)S(1)}, u32[]{:S(2)}, u32[]{:S(2)}) collective-permute-start(f32[2,256,128]{2,1,0:T(8,128)S(1)} %copy-done.19), channel_id=1, source_target_pairs={{0,7},{1,0},{2,1},{3,2},{4,3},{5,4},{6,5},{7,6},{8,15},{9,8},{10,9... | collective-permute-start | bytes 786440 | tf_op jit(solution)/shard_map/ppermute | solution.py:674
  260.9 2.8 copy-start.9
  260.9 2.8 copy-start.10
  268.0 50.1 %all-to-all-start.4 = ((f32[8,2,8,32,128]{4,3,2,1,0:T(8,128)}), f32[8,2,8,32,128]{4,3,2,1,0:T(8,128)}, u32[]{:S(2)}, u32[]{:S(2)}) async-start(f32[8,2,8,32,128]{4,3,2,1,0:T(8,128)} %after.1.refs_1_), calls=%async_computation.4 | async-start | bytes 4194304 | tf_op jit(solution)/shard_map/all_to_all | solution.py:669
  290.1 36.2 %copy-start.2 = (f32[8,2,8,32,128]{4,3,2,1,0:T(8,128)S(1)}, f32[8,2,8,32,128]{4,3,2,1,0:T(8,128)}, u32[]{:S(2)}) copy-start(f32[8,2,8,32,128]{4,3,2,1,0:T(8,128)} %copy-done.1) | copy-start | bytes 6291460
  318.2 108.8 %all-to-all-start.5 = ((f32[8,34,32,128]{3,2,1,0:T(8,128)}), f32[8,34,32,128]{3,2,1,0:T(8,128)}, u32[]{:S(2)}, u32[]{:S(2)}) async-start(f32[8,34,32,128]{3,2,1,0:T(8,128)} %adjoint_step.1._), calls=%async_computation.5 | async-start | bytes 8912896 | tf_op jit(solution)/shard_map/all_to_all | solution.py:669
  326.3 11.2 %copy-start.16 = (f32[2,4,64,128]{3,2,1,0:T(8,128)S(1)}, f32[2,4,64,128]{3,2,1,0:T(8,128)}, u32[]{:S(2)}) copy-start(f32[2,4,64,128]{3,2,1,0:T(8,128)} %get-tuple-element.52) | copy-start | bytes 786436
  326.3 99.3 %collective-permute-start.13 = (f32[8,2,8,32,128]{4,3,2,1,0:T(8,128)S(1)}, f32[8,2,8,32,128]{4,3,2,1,0:T(8,128)S(1)}, u32[]{:S(2)}, u32[]{:S(2)}) collective-permute-start(f32[8,2,8,32,128]{4,3,2,1,0:T(8,128)S(1)} %copy-done.2), channel_id=1, source_target_pairs={{0,8},{8,16},{16,24},{24,0},{1,9},{9,17},{17,25},{25,1},{2,10},{10... | collective-permute-start | bytes 6291464 | tf_op jit(solution)/shard_map/ppermute | solution.py:674
  336.2 90.7 %collective-permute-start.14 = (f32[8,2,8,32,128]{4,3,2,1,0:T(8,128)}, f32[8,2,8,32,128]{4,3,2,1,0:T(8,128)}, u32[]{:S(2)}, u32[]{:S(2)}) collective-permute-start(f32[8,2,8,32,128]{4,3,2,1,0:T(8,128)} %get-tuple-element.53), channel_id=1, source_target_pairs={{0,8},{8,16},{16,24},{24,0},{1,9},{9,17},{17,25},{25,1},{2,10},{10... | collective-permute-start | bytes 6291464 | tf_op jit(solution)/shard_map/ppermute | solution.py:674
  337.5 86.2 %collective-permute-start.11 = (f32[4,64,128]{2,1,0:T(8,128)S(1)}, f32[4,64,128]{2,1,0:T(8,128)S(1)}, u32[]{:S(2)}, u32[]{:S(2)}) collective-permute-start(f32[4,64,128]{2,1,0:T(8,128)S(1)} %get-tuple-element.55), channel_id=1, source_target_pairs={{0,1},{1,2},{2,3},{3,4},{4,5},{5,6},{6,7},{8,9},{9,10},{10,11},{11... | collective-permute-start | bytes 393224 | tf_op jit(solution)/shard_map/ppermute | solution.py:691
  341.4 84.1 %collective-permute-start.12 = (f32[4,64,128]{2,1,0:T(8,128)S(1)}, f32[4,64,128]{2,1,0:T(8,128)S(1)}, u32[]{:S(2)}, u32[]{:S(2)}) collective-permute-start(f32[4,64,128]{2,1,0:T(8,128)S(1)} %get-tuple-element.54), channel_id=1, source_target_pairs={{1,0},{2,1},{3,2},{4,3},{5,4},{6,5},{7,6},{9,8},{10,9},{11,10},{12... | collective-permute-start | bytes 393224 | tf_op jit(solution)/shard_map/ppermute | solution.py:692
  423.7 3.2 copy-start.17
  425.5 1.4 copy-start.18
  (11 other events, 11.2 us)
Sparse Core Ops, SparseCore 0:
  35.8 31.6 all-gather.2

commit v6 on v5

--- a/solution.py
+++ b/solution.py
@@ -120,9 +120,8 @@
             send[p, i] = visc[lax.rem(p * block - 2 + share * own[0] + i + rows, rows)]
 
 
-def visc_chunks(viscosity, slabs, share):
+def visc_chunks(own, viscosity, slabs, share):
     depth, rows, width = viscosity.shape
-    own = jnp.full((1,), lax.axis_index("seg"), jnp.int32)
     return call(
         visc_kernel,
         [(own, scalars()), (viscosity.reshape(-1, width), whole())],
@@ -133,7 +132,8 @@
     )
 
 
-def chunks_kernel(start, x_ref, _, send, edges, planes, held, sem):
+def chunks_kernel(start, x_ref, *refs):
+    send, edges, planes, held, sem = refs[-5:]
     count, slabs, block, depth, _ = held.shape
     rows = slabs * block
     copies = start_all([(x_ref.at[start + f], planes.at[f]) for f in range(count)], sem)
@@ -159,7 +159,8 @@
     block = rows // slabs
     return call(
         functools.partial(chunks_kernel, start),
-        [(states.reshape(fields, -1, width), anywhere()), (later, anywhere())],
+        [(states.reshape(fields, -1, width), anywhere())]
+        + [(x, anywhere()) for x in later],
         [
             ((slabs, count, block, depth, width), anywhere()),
             ((2, fields, rows, width), whole()),
@@ -289,16 +290,17 @@
     return finish
 
 
-def first_kernel(low_in, main, high_in, visc_in, mat_high, mat_low, first, visc, *scratch):
-    state, *scratch, sem = scratch
+def first_kernel(segs, own, low_in, main, high_in, _, mat_high, mat_low, *refs):
+    visc_in, (first, visc, state, *scratch, sem) = refs[:segs], refs[segs:]
     slabs, _, block, depth, _ = main.shape
-    segs, _, share = visc_in.shape[:3]
+    share = visc_in[0].shape[1]
     pairs = []
     for p in range(slabs):
         pairs += [(a.at[p], b) for a, b in rows_of(low_in, main, high_in, p, state)]
         planes = pl.ds(p * depth, depth)
         for i in range(segs):
-            pairs.append((visc_in.at[i, p], visc.at[pl.ds(share * i, share), planes]))
+            start = lax.rem(own[0] + i, segs) * share
+            pairs.append((visc_in[i].at[p], visc.at[pl.ds(start, share), planes]))
     copies = start_all(pairs, sem)
     clear_pads(state)
     clear_pads(first)
@@ -307,15 +309,17 @@
     advance_rows(state, state.at[W], visc, 0, mats, W, scratch, block + 2, finish)
 
 
-def first_step(low_in, main, high_in, visc_in, mat_high, mat_low):
+def first_step(own, low_in, main, high_in, later, visc_in, mat_high, mat_low):
     slabs, _, block, depth, width = main.shape
-    segs, _, share = visc_in.shape[:3]
+    segs, share = len(visc_in), visc_in[0].shape[1]
     order = slabs * depth
     volume = 2 * (block + 2) * order * width
     return call(
-        first_kernel,
-        [(x, anywhere()) for x in (low_in, main, high_in, visc_in)]
-        + [(mat_high, whole()), (mat_low, whole())],
+        functools.partial(first_kernel, segs),
+        [(own, scalars())]
+        + [(x, anywhere()) for x in (low_in, main, high_in, later)]
+        + [(mat_high, whole()), (mat_low, whole())]
+        + [(x, anywhere()) for x in visc_in],
         [
             ((2, block + 2, order + 2 * pad, width), whole()),
             ((segs * share, order, width), whole()),
@@ -366,7 +370,7 @@
 
 
 def second_kernel(base, first, with_w, visc, mat_high, mat_low, *refs):
-    targets, (out, low_edge, high_edge, state, speeds) = refs[:-10], refs[-10:-5]
+    targets, (_, _, out, low_edge, high_edge, state, speeds) = refs[:-12], refs[-12:-5]
     *scratch, held, sem = refs[-5:]
     slabs, _, block, depth, _ = out.shape
     places = [held.at[:, :, pl.ds(p * depth, depth)] for p in range(slabs)]
@@ -387,14 +391,14 @@
     wait_all(copies)
 
 
-def second_step(first, with_w, visc, mat_high, mat_low, base, targets):
+def second_step(first, with_w, visc, mat_high, mat_low, base, targets, later):
     width, order = visc.shape[2], visc.shape[1]
     slabs, _, block, depth, _ = targets[0].shape
     return call(
         functools.partial(second_kernel, base),
         [(first, anywhere()), (with_w, anywhere())]
         + [(x, whole()) for x in (visc, mat_high, mat_low)]
-        + [(x, anywhere()) for x in targets],
+        + [(x, anywhere()) for x in (*targets, *later)],
         [((slabs, 2, block, depth, width), anywhere())] + [((2, order, width), whole())] * 2,
         [vmem(*first.shape), vmem(*first.shape[1:])]
         + step_scratch(order, width, 2)
@@ -680,31 +684,38 @@
     slabs, segs = lax.axis_size("slab"), lax.axis_size("seg")
     share = -(-(rows // slabs + 4) // segs)
 
-    visc, visc_send = visc_chunks(viscosity, slabs, share)
+    own_seg = jnp.full((1,), lax.axis_index("seg"), jnp.int32)
+    visc, visc_send = visc_chunks(own_seg, viscosity, slabs, share)
     visc_share = exchange(visc_send)
-    visc_in = lax.all_gather(visc_share, "seg", axis=0)
-    send_half, _ = to_chunks(start, slabs, outside[W], 2, visc_send)
+    visc_in = [visc_share] + [around(visc_share, "seg", -i) for i in range(1, segs)]
+    send_half, _ = to_chunks(start, slabs, outside[W], 2, [visc_send])
     main_half = exchange(send_half)
-    send_other, ends = to_chunks(start, slabs, outside[U], 2, visc_share)
+    send_other, ends = to_chunks(start, slabs, outside[U], 2, visc_in)
     main_other = exchange(send_other)
     forward = [(i, i + 1) for i in range(slabs - 1)]
     below = lax.ppermute(ends[1], "slab", forward)
     above = lax.ppermute(ends[0], "slab", [(i, j) for j, i in forward])
     mat_high, mat_low, adj_high, adj_low = split(inverse)
 
-    own, targets, later = [], [], visc_in
+    own, outer, targets, later = [], [], [], visc_share
     for part, pieces in ((main_half, 1), (main_other, 2)):
         low_rows, high_rows, *again = outer_rows(part, later, pieces)
         low_in = around(high_rows, "slab", 1)
         own.append((low_in, part, around(low_rows, "slab", -1)))
+        outer.append(low_rows)
         targets.append([around(piece, "seg", -1) for piece in again])
         later = low_in
 
     mats = mat_high, mat_low
-    first_half, frame = first_step(*own[0], visc_in, *mats)
-    out, low_edge, high_edge = second_step(first_half, first_half, frame, *mats, W, targets[0])
+    first_half, frame = first_step(own_seg, *own[0], outer[1], visc_in, *mats)
+    later = (own[1][0], own[1][2])
+    out, low_edge, high_edge = second_step(
+        first_half, first_half, frame, *mats, W, targets[0], later
+    )
     first_other = carried_step(own[1], own[0], (targets[1][0], out), frame, *mats)
-    other, *more = second_step(first_other, first_half, frame, *mats, U, targets[1])
+    other, *more = second_step(
+        first_other, first_half, frame, *mats, U, targets[1], (out, out)
+    )
     low_edges = [around(edge, "slab", 1) for edge in (high_edge, more[1])]
     high_edges = [around(edge, "slab", -1) for edge in (low_edge, more[0])]
     half = exchange(out)

time: 450 us -> 423 us (0.940)
  waiting for transfers between devices: 262 us -> 240 us
  between operations: 14.3 us -> 1.07 us
  starting transfers between devices: 55.5 us -> 62 us
    ppermute x1, waiting for transfers between devices: 1.84 us -> 82.3 us  [local(): above = lax.ppermute(ends[0], 'slab', [(i, j) for j, i in forward])]
    ppermute x1, waiting for transfers between devices: 80.4 us -> 0.01 us  [local(): below = lax.ppermute(ends[1], 'slab', forward)]
    all_to_all x6, waiting for transfers between devices: 73.9 us -> 52.8 us  [exchange(): lax.all_to_all(chunks, 'slab', split_axis=0, concat_axis=0, tiled=True)]
    ppermute x13 -> x16, starting transfers between devices: 13.2 us -> 19.2 us  [around(): lax.ppermute(value, axis, [(i, (i + steps) % count) for i in range(count)])]
    unnamed x42 -> x46, local copies, waits for them, and re-layouts: 9.71 us -> 10.8 us
    ppermute x13 -> x16, waiting for transfers between devices: 106 us -> 105 us  [around(): lax.ppermute(value, axis, [(i, (i + steps) % count) for i in range(count)])]
  transfers between devices with their start and end apart: 22 -> 24, of which waited for: 12 -> 11; matrix products, arithmetic and copies ran while one was open for 0% -> 0% of each run, Pallas kernels for 19% -> 18%
where the time goes in v6:
time: 423 us; the launch traced here: 421 us
  waiting for transfers between devices  240 us (57%)
  Pallas kernels  107 us (25%)
  starting transfers between devices  62 us (15%)
  local copies, waits for them, and re-layouts  10.8 us (3%)
    pallas_call x14, Pallas kernels, call(): pl.pallas_call(kernel, in_specs=[spec for _, spec in ins], out_specs=tupl...  107 us
    ppermute x16, waiting for transfers between devices, around(): lax.ppermute(value, axis, [(i, (i + steps) % count) for i in range(count)])  105 us
    ppermute x1, waiting for transfers between devices, local(): above = lax.ppermute(ends[0], 'slab', [(i, j) for j, i in forward])  82.3 us
    all_to_all x6, waiting for transfers between devices, exchange(): lax.all_to_all(chunks, 'slab', split_axis=0, concat_axis=0, tiled=True)  52.8 us
    all_to_all x6, starting transfers between devices, exchange(): lax.all_to_all(chunks, 'slab', split_axis=0, concat_axis=0, tiled=True)  37 us
    ppermute x16, starting transfers between devices, around(): lax.ppermute(value, axis, [(i, (i + steps) % count) for i in range(count)])  19.2 us
    unnamed x46, local copies, waits for them, and re-layouts  10.8 us
  transfers between devices with their start and end apart: 24, of which 11 were waited for; matrix products, arithmetic and copies ran while one was open for 0% of the time, Pallas kernels for 18%

profile of v6, /device:TPU:9, one launch (start us, length us, event | category | flops | bytes accessed | tf_op | source)
XLA Modules:
  0.0 420.9 jit_solution(2105600065866370796)
XLA Ops:
  0.6 2.9 visc_chunks.1
  3.6 5.6 %all-to-all-start.1 = ((f32[8,3,32,128]{3,2,1,0:T(8,128)}), f32[8,3,32,128]{3,2,1,0:T(8,128)S(1)}, u32[]{:S(2)}, u32[]{:S(2)}) async-start(f32[8,3,32,128]{3,2,1,0:T(8,128)} %get-tuple-element.28.refs_0_), calls=%async_computation.1 | async-start | bytes 786432 | tf_op jit(solution)/shard_map/all_to_all | solution.py:673
  9.2 4.2 to_chunks.2
  13.4 5.3 %all-to-all-done.1._.refs_0_ = f32[8,3,32,128]{3,2,1,0:T(8,128)S(1)} async-done(((f32[8,3,32,128]{3,2,1,0:T(8,128)}), f32[8,3,32,128]{3,2,1,0:T(8,128)S(1)}, u32[]{:S(2)}, u32[]{:S(2)}) %all-to-all-start.1) | async-done | bytes 393248 | tf_op jit(solution)/shard_map/all_to_all | solution.py:673
  18.7 6.6 %all-to-all-start = ((f32[8,2,8,32,128]{4,3,2,1,0:T(8,128)}), f32[8,2,8,32,128]{4,3,2,1,0:T(8,128)S(1)}, u32[]{:S(2)}, u32[]{:S(2)}) async-start(f32[8,2,8,32,128]{4,3,2,1,0:T(8,128)} %get-tuple-element.29.refs_4_), calls=%async_computation | async-start | bytes 4194304 | tf_op jit(solution)/shard_map/all_to_all | solution.py:673
  28.9 7.7 %collective-permute-done.4.refs_3_ = f32[8,3,32,128]{3,2,1,0:T(8,128)S(1)} collective-permute-done((f32[8,3,32,128]{3,2,1,0:T(8,128)S(1)}, f32[8,3,32,128]{3,2,1,0:T(8,128)S(1)}, u32[]{:S(2)}, u32[]{:S(2)}) %collective-permute-start.4) | collective-permute-done | bytes 393248 | tf_op jit(solution)/shard_map/ppermute | solution.py:678
  36.6 9.1 %collective-permute-done.3.refs_2_ = f32[8,3,32,128]{3,2,1,0:T(8,128)S(1)} collective-permute-done((f32[8,3,32,128]{3,2,1,0:T(8,128)S(1)}, f32[8,3,32,128]{3,2,1,0:T(8,128)S(1)}, u32[]{:S(2)}, u32[]{:S(2)}) %collective-permute-start.3) | collective-permute-done | bytes 393248 | tf_op jit(solution)/shard_map/ppermute | solution.py:678
  47.1 4.2 to_chunks.3
  51.3 19.4 %all-to-all-done.chunks.main.refs_4_ = f32[8,2,8,32,128]{4,3,2,1,0:T(8,128)S(1)} async-done(((f32[8,2,8,32,128]{4,3,2,1,0:T(8,128)}), f32[8,2,8,32,128]{4,3,2,1,0:T(8,128)S(1)}, u32[]{:S(2)}, u32[]{:S(2)}) %all-to-all-start) | async-done | bytes 2097184 | tf_op jit(solution)/shard_map/all_to_all | solution.py:673
  72.1 7.8 %all-to-all-start.2 = ((f32[8,2,8,32,128]{4,3,2,1,0:T(8,128)}), f32[8,2,8,32,128]{4,3,2,1,0:T(8,128)}, u32[]{:S(2)}, u32[]{:S(2)}) async-start(f32[8,2,8,32,128]{4,3,2,1,0:T(8,128)} %get-tuple-element.32.refs_5_), calls=%async_computation.2 | async-start | bytes 4194304 | tf_op jit(solution)/shard_map/all_to_all | solution.py:673
  79.9 3.3 outer_rows.2
  87.2 49.5 %collective-permute-done._.low_in.refs_3_ = f32[8,2,2,32,128]{4,3,2,1,0:T(8,128)S(1)} collective-permute-done((f32[8,2,2,32,128]{4,3,2,1,0:T(8,128)}, f32[8,2,2,32,128]{4,3,2,1,0:T(8,128)S(1)}, u32[]{:S(2)}, u32[]{:S(2)}) %collective-permute-start) | collective-permute-done | bytes 524320 | tf_op jit(solution)/shard_map/ppermute | solution.py:678
  137.5 3.2 outer_rows.3
  143.1 3.0 split.1
  146.9 10.4 %first_step.1 = (f32[2,10,272,128]{3,2,1,0:T(8,128)}, f32[12,256,128]{2,1,0:T(8,128)}) custom-call(s32[1]{0:T(128)} %bitcast.own, f32[8,2,2,32,128]{4,3,2,1,0:T(8,128)} %copy-done.4, f32[8,2,8,32,128]{4,3,2,1,0:T(8,128)} %copy-done, f32[8,2,2,32,128]{4,3,2,1,0:T(8,128)} %copy-done.7, f32[8,2,2,32,128]{4,3,2,1,0:T(8,128)} %get-tuple-element.33._, ...), custom_call_target="tpu_custom_call" | custom-call | flops 1006632960 | bytes 7340036 | tf_op jit(solution)/shard_map/first_step/pallas_call | solution.py:42
  159.0 10.2 %second_step.2 = (f32[8,2,8,32,128]{4,3,2,1,0:T(8,128)}, f32[2,256,128]{2,1,0:T(8,128)}, f32[2,256,128]{2,1,0:T(8,128)}) custom-call(f32[2,10,272,128]{3,2,1,0:T(8,128)} %get-tuple-element.36.first.with_w.refs_6_, f32[2,10,272,128]{3,2,1,0:T(8,128)} %get-tuple-element.36.first.with_w.refs_6_, f32[12,256,128]{2,1,0:T(8,128)} %get-tuple-element.37.visc.refs_8_, ...), custom_call_target="tpu_custom_call" | custom-call | flops 805306368 | bytes 12386304 | tf_op jit(solution)/shard_map/second_step/pallas_call | solution.py:42
  169.3 4.7 %all-to-all-start.3 = ((f32[8,2,8,32,128]{4,3,2,1,0:T(8,128)}), f32[8,2,8,32,128]{4,3,2,1,0:T(8,128)S(1)}, u32[]{:S(2)}, u32[]{:S(2)}) async-start(f32[8,2,8,32,128]{4,3,2,1,0:T(8,128)} %get-tuple-element.40.refs_7_.refs_2_.refs_3_.refs_0_), calls=%async_computation.3 | async-start | bytes 4194304 | tf_op jit(solution)/shard_map/all_to_all | solution.py:673
  178.4 20.2 %collective-permute-done.8.refs_6_.refs_0_ = f32[8,1,8,32,128]{4,3,2,1,0:T(8,128)S(1)} collective-permute-done((f32[8,1,8,32,128]{4,3,2,1,0:T(8,128)}, f32[8,1,8,32,128]{4,3,2,1,0:T(8,128)S(1)}, u32[]{:S(2)}, u32[]{:S(2)}) %collective-permute-start.8) | collective-permute-done | bytes 1048608 | tf_op jit(solution)/shard_map/ppermute | solution.py:678
  199.6 10.8 %carried_step.1.first.refs_7_ = f32[2,10,272,128]{3,2,1,0:T(8,128)} custom-call(f32[8,2,2,32,128]{4,3,2,1,0:T(8,128)} %copy-done.8, f32[8,2,8,32,128]{4,3,2,1,0:T(8,128)} %all-to-all-done.2.chunks.refs_1_, f32[8,2,2,32,128]{4,3,2,1,0:T(8,128)} %copy-done.9, f32[8,2,2,32,128]{4,3,2,1,0:T(8,128)} %copy-done.4, f32[8,2,8,32,128]{4,3,2,1,0:T(8,128)} %copy-done, ...), custom_call_target="tpu_custom_call" | custom-call | flops 1006632960 | bytes 13107200 | tf_op jit(solution)/shard_map/carried_step/pallas_call | solution.py:42
  210.4 10.7 %collective-permute-done.9.refs_1_ = f32[8,1,8,32,128]{4,3,2,1,0:T(8,128)S(1)} collective-permute-done((f32[8,1,8,32,128]{4,3,2,1,0:T(8,128)}, f32[8,1,8,32,128]{4,3,2,1,0:T(8,128)S(1)}, u32[]{:S(2)}, u32[]{:S(2)}) %collective-permute-start.9) | collective-permute-done | bytes 1048608 | tf_op jit(solution)/shard_map/ppermute | solution.py:678
  222.0 10.6 %second_step.3 = (f32[8,2,8,32,128]{4,3,2,1,0:T(8,128)}, f32[2,256,128]{2,1,0:T(8,128)}, f32[2,256,128]{2,1,0:T(8,128)}) custom-call(f32[2,10,272,128]{3,2,1,0:T(8,128)} %carried_step.1.first.refs_7_, f32[2,10,272,128]{3,2,1,0:T(8,128)} %get-tuple-element.36.first.with_w.refs_6_, f32[12,256,128]{2,1,0:T(8,128)} %get-tuple-element.37.visc.refs_8_, ...), custom_call_target="tpu_custom_call" | custom-call | flops 805306368 | bytes 15532032 | tf_op jit(solution)/shard_map/second_step/pallas_call | solution.py:42
  235.0 3.7 collective-permute-done.11.refs_1_.refs_3_
  238.7 4.0 collective-permute-done.13.refs_3_.refs_5_
  244.1 2.9 after.1.refs_1_
  247.0 4.5 %all-to-all-start.4 = ((f32[8,2,8,32,128]{4,3,2,1,0:T(8,128)}), f32[8,2,8,32,128]{4,3,2,1,0:T(8,128)}, u32[]{:S(2)}, u32[]{:S(2)}) async-start(f32[8,2,8,32,128]{4,3,2,1,0:T(8,128)} %after.1.refs_1_), calls=%async_computation.4 | async-start | bytes 4194304 | tf_op jit(solution)/shard_map/all_to_all | solution.py:673
  251.5 17.5 %adjoint_step.1._ = f32[8,34,32,128]{3,2,1,0:T(8,128)} custom-call(f32[8,2,8,32,128]{4,3,2,1,0:T(8,128)} %get-tuple-element.40.refs_7_.refs_2_.refs_3_.refs_0_, f32[8,2,8,32,128]{4,3,2,1,0:T(8,128)} %after.1.refs_1_, f32[2,256,128]{2,1,0:T(8,128)} %copy-done.14, f32[2,256,128]{2,1,0:T(8,128)} %copy-done.16, f32[2,256,128]{2,1,0:T(8,128)} %copy-done.15, ...), custom_call_target="tpu_custom_call" | custom-call | flops 3623878656 | bytes 14483456 | tf_op jit(solution)/shard_map/adjoint_step/pallas_call | solution.py:42
  269.0 28.1 %all-to-all-done.4.other = f32[8,2,8,32,128]{4,3,2,1,0:T(8,128)} async-done(((f32[8,2,8,32,128]{4,3,2,1,0:T(8,128)}), f32[8,2,8,32,128]{4,3,2,1,0:T(8,128)}, u32[]{:S(2)}, u32[]{:S(2)}) %all-to-all-start.4) | async-done | bytes 2097184 | tf_op jit(solution)/shard_map/all_to_all | solution.py:673
  297.1 7.8 %all-to-all-start.5 = ((f32[8,34,32,128]{3,2,1,0:T(8,128)}), f32[8,34,32,128]{3,2,1,0:T(8,128)}, u32[]{:S(2)}, u32[]{:S(2)}) async-start(f32[8,34,32,128]{3,2,1,0:T(8,128)} %adjoint_step.1._), calls=%async_computation.5 | async-start | bytes 8912896 | tf_op jit(solution)/shard_map/all_to_all | solution.py:673
  306.9 8.6 %to_planes.1 = (f32[8192,128]{1,0:T(8,128)}, f32[8,2,8,32,128]{4,3,2,1,0:T(8,128)}) custom-call(f32[8,2,8,32,128]{4,3,2,1,0:T(8,128)} %copy-done.1, f32[8,2,8,32,128]{4,3,2,1,0:T(8,128)} %all-to-all-done.4.other, f32[8,34,32,128]{3,2,1,0:T(8,128)} %adjoint_step.1._), custom_call_target="tpu_custom_call" | custom-call | bytes 8650752 | tf_op jit(solution)/shard_map/to_planes/pallas_call | solution.py:42
  318.8 3.0 collective-permute-start.14
  321.8 82.3 %collective-permute-done.15.refs_2_ = f32[4,64,128]{2,1,0:T(8,128)S(1)} collective-permute-done((f32[4,64,128]{2,1,0:T(8,128)S(1)}, f32[4,64,128]{2,1,0:T(8,128)S(1)}, u32[]{:S(2)}, u32[]{:S(2)}) %collective-permute-start.15) | collective-permute-done | bytes 131104 | tf_op jit(solution)/shard_map/ppermute | solution.py:697
  405.5 15.2 %last_step.1 = f32[4,2048,128]{2,1,0:T(8,128)} custom-call(f32[64,32,128]{2,1,0:T(8,128)} %get-tuple-element.51.refs_0_, f32[4,64,128]{2,1,0:T(8,128)} %copy-done.21, f32[4,64,128]{2,1,0:T(8,128)} %copy-done.20, f32[8,34,32,128]{3,2,1,0:T(8,128)} %all-to-all-done.5.refs_3_, f32[8,2,8,32,128]{4,3,2,1,0:T(8,128)} %get-tuple-element.29.refs_4_, ...), custom_call_target="tpu_custom_call" | custom-call | flops 31457280 | bytes 14155776 | tf_op jit(solution)/shard_map/last_step/pallas_call | solution.py:42
  (77 shorter events, 32.8 us)
Async XLA Ops:
  3.6 15.1 %all-to-all-start.1 = ((f32[8,3,32,128]{3,2,1,0:T(8,128)}), f32[8,3,32,128]{3,2,1,0:T(8,128)S(1)}, u32[]{:S(2)}, u32[]{:S(2)}) async-start(f32[8,3,32,128]{3,2,1,0:T(8,128)} %get-tuple-element.28.refs_0_), calls=%async_computation.1 | async-start | bytes 786432 | tf_op jit(solution)/shard_map/all_to_all | solution.py:673
  18.7 9.1 %copy-start.3 = (f32[8,3,32,128]{3,2,1,0:T(8,128)}, f32[8,3,32,128]{3,2,1,0:T(8,128)S(1)}, u32[]{:S(2)}) copy-start(f32[8,3,32,128]{3,2,1,0:T(8,128)S(1)} %all-to-all-done.1._.refs_0_) | copy-start | bytes 1179652
  18.7 52.1 %all-to-all-start = ((f32[8,2,8,32,128]{4,3,2,1,0:T(8,128)}), f32[8,2,8,32,128]{4,3,2,1,0:T(8,128)S(1)}, u32[]{:S(2)}, u32[]{:S(2)}) async-start(f32[8,2,8,32,128]{4,3,2,1,0:T(8,128)} %get-tuple-element.29.refs_4_), calls=%async_computation | async-start | bytes 4194304 | tf_op jit(solution)/shard_map/all_to_all | solution.py:673
  25.3 11.3 %collective-permute-start.4 = (f32[8,3,32,128]{3,2,1,0:T(8,128)S(1)}, f32[8,3,32,128]{3,2,1,0:T(8,128)S(1)}, u32[]{:S(2)}, u32[]{:S(2)}) collective-permute-start(f32[8,3,32,128]{3,2,1,0:T(8,128)S(1)} %all-to-all-done.1._.refs_0_), channel_id=1, source_target_pairs={{0,8},{8,16},{16,24},{24,0},{1,9},{9,17},{17,25},{25,1},{2,10},{10... | collective-permute-start | bytes 1179656 | tf_op jit(solution)/shard_map/ppermute | solution.py:678
  26.5 19.2 %collective-permute-start.3 = (f32[8,3,32,128]{3,2,1,0:T(8,128)S(1)}, f32[8,3,32,128]{3,2,1,0:T(8,128)S(1)}, u32[]{:S(2)}, u32[]{:S(2)}) collective-permute-start(f32[8,3,32,128]{3,2,1,0:T(8,128)S(1)} %all-to-all-done.1._.refs_0_), channel_id=1, source_target_pairs={{0,16},{8,24},{16,0},{24,8},{1,17},{9,25},{17,1},{25,9},{2,18},{10... | collective-permute-start | bytes 1179656 | tf_op jit(solution)/shard_map/ppermute | solution.py:678
  27.7 17.9 %collective-permute-start.2 = (f32[8,3,32,128]{3,2,1,0:T(8,128)S(1)}, f32[8,3,32,128]{3,2,1,0:T(8,128)S(1)}, u32[]{:S(2)}, u32[]{:S(2)}) collective-permute-start(f32[8,3,32,128]{3,2,1,0:T(8,128)S(1)} %all-to-all-done.1._.refs_0_), channel_id=1, source_target_pairs={{0,24},{8,0},{16,8},{24,16},{1,25},{9,1},{17,9},{25,17},{2,26},{10... | collective-permute-start | bytes 1179656 | tf_op jit(solution)/shard_map/ppermute | solution.py:678
  36.6 9.1 %copy-start.11 = (f32[8,3,32,128]{3,2,1,0:T(8,128)}, f32[8,3,32,128]{3,2,1,0:T(8,128)S(1)}, u32[]{:S(2)}) copy-start(f32[8,3,32,128]{3,2,1,0:T(8,128)S(1)} %collective-permute-done.4.refs_3_) | copy-start | bytes 1179652
  72.1 64.6 %all-to-all-start.2 = ((f32[8,2,8,32,128]{4,3,2,1,0:T(8,128)}), f32[8,2,8,32,128]{4,3,2,1,0:T(8,128)}, u32[]{:S(2)}, u32[]{:S(2)}) async-start(f32[8,2,8,32,128]{4,3,2,1,0:T(8,128)} %get-tuple-element.32.refs_5_), calls=%async_computation.2 | async-start | bytes 4194304 | tf_op jit(solution)/shard_map/all_to_all | solution.py:673
  83.2 74.2 %collective-permute-start.5 = (f32[8,2,8,32,128]{4,3,2,1,0:T(8,128)}, f32[8,2,8,32,128]{4,3,2,1,0:T(8,128)S(1)}, u32[]{:S(2)}, u32[]{:S(2)}) collective-permute-start(f32[8,2,8,32,128]{4,3,2,1,0:T(8,128)} %get-tuple-element.38), channel_id=1, source_target_pairs={{0,24},{8,0},{16,8},{24,16},{1,25},{9,1},{17,9},{25,17},{2,26},{10... | collective-permute-start | bytes 6291464 | tf_op jit(solution)/shard_map/ppermute | solution.py:678
  85.4 51.3 %collective-permute-start = (f32[8,2,2,32,128]{4,3,2,1,0:T(8,128)}, f32[8,2,2,32,128]{4,3,2,1,0:T(8,128)S(1)}, u32[]{:S(2)}, u32[]{:S(2)}) collective-permute-start(f32[8,2,2,32,128]{4,3,2,1,0:T(8,128)} %get-tuple-element.30), channel_id=1, source_target_pairs={{0,1},{1,2},{2,3},{3,4},{4,5},{5,6},{6,7},{7,0},{8,9},{9,10},{10,1... | collective-permute-start | bytes 1572872 | tf_op jit(solution)/shard_map/ppermute | solution.py:678
  87.2 59.0 %collective-permute-start.1 = (f32[8,2,2,32,128]{4,3,2,1,0:T(8,128)}, f32[8,2,2,32,128]{4,3,2,1,0:T(8,128)S(1)}, u32[]{:S(2)}, u32[]{:S(2)}) collective-permute-start(f32[8,2,2,32,128]{4,3,2,1,0:T(8,128)} %get-tuple-element.31), channel_id=1, source_target_pairs={{0,7},{1,0},{2,1},{3,2},{4,3},{5,4},{6,5},{7,6},{8,15},{9,8},{10,9... | collective-permute-start | bytes 1572872 | tf_op jit(solution)/shard_map/ppermute | solution.py:678
  140.7 16.7 %collective-permute-start.6 = (f32[8,2,2,32,128]{4,3,2,1,0:T(8,128)}, f32[8,2,2,32,128]{4,3,2,1,0:T(8,128)S(1)}, u32[]{:S(2)}, u32[]{:S(2)}) collective-permute-start(f32[8,2,2,32,128]{4,3,2,1,0:T(8,128)} %get-tuple-element.39), channel_id=1, source_target_pairs={{0,1},{1,2},{2,3},{3,4},{4,5},{5,6},{6,7},{7,0},{8,9},{9,10},{10,1... | collective-permute-start | bytes 1572872 | tf_op jit(solution)/shard_map/ppermute | solution.py:678
  143.1 14.3 %collective-permute-start.7 = (f32[8,2,2,32,128]{4,3,2,1,0:T(8,128)}, f32[8,2,2,32,128]{4,3,2,1,0:T(8,128)S(1)}, u32[]{:S(2)}, u32[]{:S(2)}) collective-permute-start(f32[8,2,2,32,128]{4,3,2,1,0:T(8,128)} %get-tuple-element.33._), channel_id=1, source_target_pairs={{0,7},{1,0},{2,1},{3,2},{4,3},{5,4},{6,5},{7,6},{8,15},{9,8},{10,9... | collective-permute-start | bytes 1572872 | tf_op jit(solution)/shard_map/ppermute | solution.py:678
  169.3 9.1 %copy-start.22 = (f32[2,256,128]{2,1,0:T(8,128)S(1)}, f32[2,256,128]{2,1,0:T(8,128)}, u32[]{:S(2)}) copy-start(f32[2,256,128]{2,1,0:T(8,128)} %get-tuple-element.46) | copy-start | bytes 786436
  169.3 73.4 %all-to-all-start.3 = ((f32[8,2,8,32,128]{4,3,2,1,0:T(8,128)}), f32[8,2,8,32,128]{4,3,2,1,0:T(8,128)S(1)}, u32[]{:S(2)}, u32[]{:S(2)}) async-start(f32[8,2,8,32,128]{4,3,2,1,0:T(8,128)} %get-tuple-element.40.refs_7_.refs_2_.refs_3_.refs_0_), calls=%async_computation.3 | async-start | bytes 4194304 | tf_op jit(solution)/shard_map/all_to_all | solution.py:673
  173.9 24.7 %collective-permute-start.8 = (f32[8,1,8,32,128]{4,3,2,1,0:T(8,128)}, f32[8,1,8,32,128]{4,3,2,1,0:T(8,128)S(1)}, u32[]{:S(2)}, u32[]{:S(2)}) collective-permute-start(f32[8,1,8,32,128]{4,3,2,1,0:T(8,128)} %get-tuple-element.41), channel_id=1, source_target_pairs={{0,24},{8,0},{16,8},{24,16},{1,25},{9,1},{17,9},{25,17},{2,26},{10... | collective-permute-start | bytes 3145736 | tf_op jit(solution)/shard_map/ppermute | solution.py:678
  176.1 45.0 %collective-permute-start.9 = (f32[8,1,8,32,128]{4,3,2,1,0:T(8,128)}, f32[8,1,8,32,128]{4,3,2,1,0:T(8,128)S(1)}, u32[]{:S(2)}, u32[]{:S(2)}) collective-permute-start(f32[8,1,8,32,128]{4,3,2,1,0:T(8,128)} %get-tuple-element.42), channel_id=1, source_target_pairs={{0,24},{8,0},{16,8},{24,16},{1,25},{9,1},{17,9},{25,17},{2,26},{10... | collective-permute-start | bytes 3145736 | tf_op jit(solution)/shard_map/ppermute | solution.py:678
  176.4 58.6 %collective-permute-start.10 = (f32[2,256,128]{2,1,0:T(8,128)}, f32[2,256,128]{2,1,0:T(8,128)S(1)}, u32[]{:S(2)}, u32[]{:S(2)}) collective-permute-start(f32[2,256,128]{2,1,0:T(8,128)} %get-tuple-element.44), channel_id=1, source_target_pairs={{0,1},{1,2},{2,3},{3,4},{4,5},{5,6},{6,7},{7,0},{8,9},{9,10},{10,1... | collective-permute-start | bytes 786440 | tf_op jit(solution)/shard_map/ppermute | solution.py:678
  178.4 56.6 %collective-permute-start.12 = (f32[2,256,128]{2,1,0:T(8,128)S(1)}, f32[2,256,128]{2,1,0:T(8,128)S(1)}, u32[]{:S(2)}, u32[]{:S(2)}) collective-permute-start(f32[2,256,128]{2,1,0:T(8,128)S(1)} %copy-done.22), channel_id=1, source_target_pairs={{0,7},{1,0},{2,1},{3,2},{4,3},{5,4},{6,5},{7,6},{8,15},{9,8},{10,9... | collective-permute-start | bytes 786440 | tf_op jit(solution)/shard_map/ppermute | solution.py:678
  232.7 6.1 %collective-permute-start.11 = (f32[2,256,128]{2,1,0:T(8,128)}, f32[2,256,128]{2,1,0:T(8,128)S(1)}, u32[]{:S(2)}, u32[]{:S(2)}) collective-permute-start(f32[2,256,128]{2,1,0:T(8,128)} %get-tuple-element.45), channel_id=1, source_target_pairs={{0,1},{1,2},{2,3},{3,4},{4,5},{5,6},{6,7},{7,0},{8,9},{9,10},{10,1... | collective-permute-start | bytes 786440 | tf_op jit(solution)/shard_map/ppermute | solution.py:678
  235.0 7.8 %collective-permute-start.13 = (f32[2,256,128]{2,1,0:T(8,128)}, f32[2,256,128]{2,1,0:T(8,128)S(1)}, u32[]{:S(2)}, u32[]{:S(2)}) collective-permute-start(f32[2,256,128]{2,1,0:T(8,128)} %get-tuple-element.47), channel_id=1, source_target_pairs={{0,7},{1,0},{2,1},{3,2},{4,3},{5,4},{6,5},{7,6},{8,15},{9,8},{10,9... | collective-permute-start | bytes 786440 | tf_op jit(solution)/shard_map/ppermute | solution.py:678
  235.0 7.8 %copy-start.14 = (f32[2,256,128]{2,1,0:T(8,128)}, f32[2,256,128]{2,1,0:T(8,128)S(1)}, u32[]{:S(2)}) copy-start(f32[2,256,128]{2,1,0:T(8,128)S(1)} %collective-permute-done.10.refs_0_.refs_2_) | copy-start | bytes 786436
  235.0 7.7 %copy-start.15 = (f32[2,256,128]{2,1,0:T(8,128)}, f32[2,256,128]{2,1,0:T(8,128)S(1)}, u32[]{:S(2)}) copy-start(f32[2,256,128]{2,1,0:T(8,128)S(1)} %collective-permute-done.12.refs_2_.refs_4_) | copy-start | bytes 786436
  238.7 4.0 copy-start.16
  247.0 50.1 %all-to-all-start.4 = ((f32[8,2,8,32,128]{4,3,2,1,0:T(8,128)}), f32[8,2,8,32,128]{4,3,2,1,0:T(8,128)}, u32[]{:S(2)}, u32[]{:S(2)}) async-start(f32[8,2,8,32,128]{4,3,2,1,0:T(8,128)} %after.1.refs_1_), calls=%async_computation.4 | async-start | bytes 4194304 | tf_op jit(solution)/shard_map/all_to_all | solution.py:673
  269.0 35.8 %copy-start.2 = (f32[8,2,8,32,128]{4,3,2,1,0:T(8,128)S(1)}, f32[8,2,8,32,128]{4,3,2,1,0:T(8,128)}, u32[]{:S(2)}) copy-start(f32[8,2,8,32,128]{4,3,2,1,0:T(8,128)} %copy-done.1) | copy-start | bytes 6291460
  297.1 108.4 %all-to-all-start.5 = ((f32[8,34,32,128]{3,2,1,0:T(8,128)}), f32[8,34,32,128]{3,2,1,0:T(8,128)}, u32[]{:S(2)}, u32[]{:S(2)}) async-start(f32[8,34,32,128]{3,2,1,0:T(8,128)} %adjoint_step.1._), calls=%async_computation.5 | async-start | bytes 8912896 | tf_op jit(solution)/shard_map/all_to_all | solution.py:673
  304.9 11.1 %copy-start.19 = (f32[2,4,64,128]{3,2,1,0:T(8,128)S(1)}, f32[2,4,64,128]{3,2,1,0:T(8,128)}, u32[]{:S(2)}) copy-start(f32[2,4,64,128]{3,2,1,0:T(8,128)} %get-tuple-element.52) | copy-start | bytes 786436
  304.9 99.3 %collective-permute-start.16 = (f32[8,2,8,32,128]{4,3,2,1,0:T(8,128)S(1)}, f32[8,2,8,32,128]{4,3,2,1,0:T(8,128)S(1)}, u32[]{:S(2)}, u32[]{:S(2)}) collective-permute-start(f32[8,2,8,32,128]{4,3,2,1,0:T(8,128)S(1)} %copy-done.2), channel_id=1, source_target_pairs={{0,8},{8,16},{16,24},{24,0},{1,9},{9,17},{17,25},{25,1},{2,10},{10... | collective-permute-start | bytes 6291464 | tf_op jit(solution)/shard_map/ppermute | solution.py:678
  315.6 89.9 %collective-permute-start.17 = (f32[8,2,8,32,128]{4,3,2,1,0:T(8,128)}, f32[8,2,8,32,128]{4,3,2,1,0:T(8,128)}, u32[]{:S(2)}, u32[]{:S(2)}) collective-permute-start(f32[8,2,8,32,128]{4,3,2,1,0:T(8,128)} %get-tuple-element.53), channel_id=1, source_target_pairs={{0,8},{8,16},{16,24},{24,0},{1,9},{9,17},{17,25},{25,1},{2,10},{10... | collective-permute-start | bytes 6291464 | tf_op jit(solution)/shard_map/ppermute | solution.py:678
  316.0 88.1 %collective-permute-start.15 = (f32[4,64,128]{2,1,0:T(8,128)S(1)}, f32[4,64,128]{2,1,0:T(8,128)S(1)}, u32[]{:S(2)}, u32[]{:S(2)}) collective-permute-start(f32[4,64,128]{2,1,0:T(8,128)S(1)} %get-tuple-element.54), channel_id=1, source_target_pairs={{1,0},{2,1},{3,2},{4,3},{5,4},{6,5},{7,6},{9,8},{10,9},{11,10},{12... | collective-permute-start | bytes 393224 | tf_op jit(solution)/shard_map/ppermute | solution.py:697
  318.8 85.3 %collective-permute-start.14 = (f32[4,64,128]{2,1,0:T(8,128)S(1)}, f32[4,64,128]{2,1,0:T(8,128)S(1)}, u32[]{:S(2)}, u32[]{:S(2)}) collective-permute-start(f32[4,64,128]{2,1,0:T(8,128)S(1)} %get-tuple-element.55), channel_id=1, source_target_pairs={{0,1},{1,2},{2,3},{3,4},{4,5},{5,6},{6,7},{8,9},{9,10},{10,11},{11... | collective-permute-start | bytes 393224 | tf_op jit(solution)/shard_map/ppermute | solution.py:696
  (15 other events, 16.1 us)

commit v7 on v6

--- a/solution.py
+++ b/solution.py
@@ -66,11 +66,11 @@
         copy.wait()
 
 
-def spans(parts):
+def spans(parts, axis=1):
     start = 0
     for part in parts:
-        yield part, pl.ds(start, part.shape[1])
-        start += part.shape[1]
+        yield part, pl.ds(start, part.shape[axis])
+        start += part.shape[axis]
 
 
 def east(value):
@@ -370,14 +370,14 @@
 
 
 def second_kernel(base, first, with_w, visc, mat_high, mat_low, *refs):
-    targets, (_, _, out, low_edge, high_edge, state, speeds) = refs[:-12], refs[-12:-5]
+    targets, (out, low_edge, high_edge, state, speeds) = refs[:-13], refs[-10:-5]
     *scratch, held, sem = refs[-5:]
     slabs, _, block, depth, _ = out.shape
     places = [held.at[:, :, pl.ds(p * depth, depth)] for p in range(slabs)]
     pairs = [(first, state)] + ([(with_w.at[W], speeds)] if base != W else [])
-    for target, span in spans(targets):
+    for target, span in spans(targets, 2):
         for p in range(slabs):
-            pairs.append((target.at[p], held.at[span, :, pl.ds(p * depth, depth)]))
+            pairs.append((target.at[p], held.at[:, span, pl.ds(p * depth, depth)]))
     wait_all(start_all(pairs, sem))
 
     def finish(f, row, piece):
@@ -393,7 +393,8 @@
 
 def second_step(first, with_w, visc, mat_high, mat_low, base, targets, later):
     width, order = visc.shape[2], visc.shape[1]
-    slabs, _, block, depth, _ = targets[0].shape
+    slabs, _, _, depth, _ = targets[0].shape
+    block = sum(target.shape[2] for target in targets)
     return call(
         functools.partial(second_kernel, base),
         [(first, anywhere()), (with_w, anywhere())]
@@ -427,22 +428,20 @@
 def outer_kernel(chunks, _, low_rows, high_rows, *refs):
     *again, sem = refs
     block = chunks.shape[2]
-    pairs = [(chunks.at[:, span], part) for part, span in spans(again)]
+    low, high = chunks.at[:, :, pl.ds(0, 2)], chunks.at[:, :, pl.ds(block - 2, 2)]
+    pairs = [(low, low_rows), (high, high_rows)]
+    pairs += [(chunks.at[:, :, span], part) for part, span in spans(again, 2)]
     wait_all(start_all(pairs, sem))
-    for part, span in spans(again):
-        low_rows[:, span] = part[:, :, 0:2]
-        high_rows[:, span] = part[:, :, block - 2 :]
 
 
 def outer_rows(chunks, later, pieces):
-    slabs, count, block, depth, width = chunks.shape
-    rows = ((slabs, count, 2, depth, width), whole())
-    again = ((slabs, count // pieces, block, depth, width), whole())
+    slabs, count, _, depth, width = chunks.shape
+    rows = [((slabs, count, size, depth, width), whole()) for size in (2, 2, *pieces)]
     return call(
         outer_kernel,
         [(chunks, anywhere()), (later, anywhere())],
-        [rows, rows] + [again] * pieces,
-        [dmas(pieces)],
+        rows,
+        [dmas(len(rows))],
         0,
         "outer_rows",
     )
@@ -682,7 +681,8 @@
     start = states[0]
     _, depth, rows, width = start.shape
     slabs, segs = lax.axis_size("slab"), lax.axis_size("seg")
-    share = -(-(rows // slabs + 4) // segs)
+    block = rows // slabs
+    share = -(-(block + 4) // segs)
 
     own_seg = jnp.full((1,), lax.axis_index("seg"), jnp.int32)
     visc, visc_send = visc_chunks(own_seg, viscosity, slabs, share)
@@ -690,15 +690,16 @@
     visc_in = [visc_share] + [around(visc_share, "seg", -i) for i in range(1, segs)]
     send_half, _ = to_chunks(start, slabs, outside[W], 2, [visc_send])
     main_half = exchange(send_half)
-    send_other, ends = to_chunks(start, slabs, outside[U], 2, visc_in)
+    mat_high, mat_low, adj_high, adj_low = split(inverse)
+    send_other, ends = to_chunks(start, slabs, outside[U], 2, [*visc_in, mat_high])
     main_other = exchange(send_other)
     forward = [(i, i + 1) for i in range(slabs - 1)]
     below = lax.ppermute(ends[1], "slab", forward)
     above = lax.ppermute(ends[0], "slab", [(i, j) for j, i in forward])
-    mat_high, mat_low, adj_high, adj_low = split(inverse)
 
     own, outer, targets, later = [], [], [], visc_share
-    for part, pieces in ((main_half, 1), (main_other, 2)):
+    few = max(1, 3 * block // 8)
+    for part, pieces in ((main_half, (block,)), (main_other, (few, block - few))):
         low_rows, high_rows, *again = outer_rows(part, later, pieces)
         low_in = around(high_rows, "slab", 1)
         own.append((low_in, part, around(low_rows, "slab", -1)))
@@ -708,13 +709,13 @@
 
     mats = mat_high, mat_low
     first_half, frame = first_step(own_seg, *own[0], outer[1], visc_in, *mats)
-    later = (own[1][0], own[1][2])
+    later = (own[1][0], own[1][2], targets[1][0])
     out, low_edge, high_edge = second_step(
         first_half, first_half, frame, *mats, W, targets[0], later
     )
-    first_other = carried_step(own[1], own[0], (targets[1][0], out), frame, *mats)
+    first_other = carried_step(own[1], own[0], (out, out), frame, *mats)
     other, *more = second_step(
-        first_other, first_half, frame, *mats, U, targets[1], (out, out)
+        first_other, first_half, frame, *mats, U, targets[1], (out, out, out)
     )
     low_edges = [around(edge, "slab", 1) for edge in (high_edge, more[1])]
     high_edges = [around(edge, "slab", -1) for edge in (low_edge, more[0])]

time: 423 us -> 418 us (0.988)
  waiting for transfers between devices: 240 us -> 235 us
    ppermute x16, waiting for transfers between devices: 105 us -> 99.5 us  [around(): lax.ppermute(value, axis, [(i, (i + steps) % count) for i in range(count)])]
    unnamed x46 -> x48, local copies, waits for them, and re-layouts: 10.8 us -> 9.56 us
  transfers between devices with their start and end apart: 24 -> 24, of which waited for: 11 -> 13; matrix products, arithmetic and copies ran while one was open for 0% -> 0% of each run, Pallas kernels for 18% -> 18%
where the time goes in v7:
time: 418 us; the launch traced here: 417 us
  waiting for transfers between devices  235 us (56%)
  Pallas kernels  108 us (26%)
  starting transfers between devices  63.7 us (15%)
  local copies, waits for them, and re-layouts  9.57 us (2%)
    pallas_call x14, Pallas kernels, call(): pl.pallas_call(kernel, in_specs=[spec for _, spec in ins], out_specs=tupl...  108 us
    ppermute x16, waiting for transfers between devices, around(): lax.ppermute(value, axis, [(i, (i + steps) % count) for i in range(count)])  99.5 us
    ppermute x1, waiting for transfers between devices, local(): above = lax.ppermute(ends[0], 'slab', [(i, j) for j, i in forward])  83.2 us
    all_to_all x6, waiting for transfers between devices, exchange(): lax.all_to_all(chunks, 'slab', split_axis=0, concat_axis=0, tiled=True)  52.5 us
    all_to_all x6, starting transfers between devices, exchange(): lax.all_to_all(chunks, 'slab', split_axis=0, concat_axis=0, tiled=True)  39.7 us
    ppermute x16, starting transfers between devices, around(): lax.ppermute(value, axis, [(i, (i + steps) % count) for i in range(count)])  18.2 us
    unnamed x48, local copies, waits for them, and re-layouts  9.56 us
  transfers between devices with their start and end apart: 24, of which 13 were waited for; matrix products, arithmetic and copies ran while one was open for 0% of the time, Pallas kernels for 18%

profile of v7, /device:TPU:9, one launch (start us, length us, event | category | flops | bytes accessed | tf_op | source)
XLA Modules:
  0.0 417.2 jit_solution(13942514235399853871)
XLA Ops:
  0.6 2.9 visc_chunks.1
  3.6 5.6 %all-to-all-start.1 = ((f32[8,3,32,128]{3,2,1,0:T(8,128)}), f32[8,3,32,128]{3,2,1,0:T(8,128)S(1)}, u32[]{:S(2)}, u32[]{:S(2)}) async-start(f32[8,3,32,128]{3,2,1,0:T(8,128)} %get-tuple-element.28.refs_0_), calls=%async_computation.1 | async-start | bytes 786432 | tf_op jit(solution)/shard_map/all_to_all | solution.py:672
  9.2 4.2 to_chunks.2
  13.4 5.3 %all-to-all-done.1._.refs_0_ = f32[8,3,32,128]{3,2,1,0:T(8,128)S(1)} async-done(((f32[8,3,32,128]{3,2,1,0:T(8,128)}), f32[8,3,32,128]{3,2,1,0:T(8,128)S(1)}, u32[]{:S(2)}, u32[]{:S(2)}) %all-to-all-start.1) | async-done | bytes 393248 | tf_op jit(solution)/shard_map/all_to_all | solution.py:672
  18.7 6.6 %all-to-all-start = ((f32[8,2,8,32,128]{4,3,2,1,0:T(8,128)}), f32[8,2,8,32,128]{4,3,2,1,0:T(8,128)S(1)}, u32[]{:S(2)}, u32[]{:S(2)}) async-start(f32[8,2,8,32,128]{4,3,2,1,0:T(8,128)} %get-tuple-element.29.refs_4_), calls=%async_computation | async-start | bytes 4194304 | tf_op jit(solution)/shard_map/all_to_all | solution.py:672
  28.9 3.0 split.1
  31.8 4.7 %collective-permute-done.4.refs_3_ = f32[8,3,32,128]{3,2,1,0:T(8,128)S(1)} collective-permute-done((f32[8,3,32,128]{3,2,1,0:T(8,128)S(1)}, f32[8,3,32,128]{3,2,1,0:T(8,128)S(1)}, u32[]{:S(2)}, u32[]{:S(2)}) %collective-permute-start.4) | collective-permute-done | bytes 393248 | tf_op jit(solution)/shard_map/ppermute | solution.py:677
  36.6 9.1 %collective-permute-done.3.refs_2_ = f32[8,3,32,128]{3,2,1,0:T(8,128)S(1)} collective-permute-done((f32[8,3,32,128]{3,2,1,0:T(8,128)S(1)}, f32[8,3,32,128]{3,2,1,0:T(8,128)S(1)}, u32[]{:S(2)}, u32[]{:S(2)}) %collective-permute-start.3) | collective-permute-done | bytes 393248 | tf_op jit(solution)/shard_map/ppermute | solution.py:677
  46.5 4.2 %to_chunks.3 = (f32[8,2,8,32,128]{4,3,2,1,0:T(8,128)}, f32[2,4,64,128]{3,2,1,0:T(8,128)}) custom-call(f32[4,2048,128]{2,1,0:T(8,128)} %bitcast.10, f32[8,3,32,128]{3,2,1,0:T(8,128)} %copy-done.3, f32[8,3,32,128]{3,2,1,0:T(8,128)} %copy-done.13, f32[8,3,32,128]{3,2,1,0:T(8,128)} %copy-done.12, f32[8,3,32,128]{3,2,1,0:T(8,128)} %copy-done.11, ...), custom_call_target="tpu_custom_call" | custom-call | bytes 6815744 | tf_op jit(solution)/shard_map/to_chunks/pallas_call | solution.py:42
  50.7 20.0 %all-to-all-done.chunks.main.refs_4_ = f32[8,2,8,32,128]{4,3,2,1,0:T(8,128)S(1)} async-done(((f32[8,2,8,32,128]{4,3,2,1,0:T(8,128)}), f32[8,2,8,32,128]{4,3,2,1,0:T(8,128)S(1)}, u32[]{:S(2)}, u32[]{:S(2)}) %all-to-all-start) | async-done | bytes 2097184 | tf_op jit(solution)/shard_map/all_to_all | solution.py:672
  72.1 7.8 %all-to-all-start.2 = ((f32[8,2,8,32,128]{4,3,2,1,0:T(8,128)}), f32[8,2,8,32,128]{4,3,2,1,0:T(8,128)}, u32[]{:S(2)}, u32[]{:S(2)}) async-start(f32[8,2,8,32,128]{4,3,2,1,0:T(8,128)} %get-tuple-element.33.refs_5_), calls=%async_computation.2 | async-start | bytes 4194304 | tf_op jit(solution)/shard_map/all_to_all | solution.py:672
  79.9 3.6 outer_rows.2
  87.5 43.6 %collective-permute-done._.low_in.refs_3_ = f32[8,2,2,32,128]{4,3,2,1,0:T(8,128)S(1)} collective-permute-done((f32[8,2,2,32,128]{4,3,2,1,0:T(8,128)}, f32[8,2,2,32,128]{4,3,2,1,0:T(8,128)S(1)}, u32[]{:S(2)}, u32[]{:S(2)}) %collective-permute-start) | collective-permute-done | bytes 524320 | tf_op jit(solution)/shard_map/ppermute | solution.py:677
  131.9 3.6 outer_rows.3
  140.4 10.3 %collective-permute-done.1.high_in.refs_5_ = f32[8,2,2,32,128]{4,3,2,1,0:T(8,128)S(1)} collective-permute-done((f32[8,2,2,32,128]{4,3,2,1,0:T(8,128)S(1)}, f32[8,2,2,32,128]{4,3,2,1,0:T(8,128)S(1)}, u32[]{:S(2)}, u32[]{:S(2)}) %collective-permute-start.1) | collective-permute-done | bytes 524320 | tf_op jit(solution)/shard_map/ppermute | solution.py:677
  151.5 10.4 %first_step.1 = (f32[2,10,272,128]{3,2,1,0:T(8,128)}, f32[12,256,128]{2,1,0:T(8,128)}) custom-call(s32[1]{0:T(128)} %bitcast.own, f32[8,2,2,32,128]{4,3,2,1,0:T(8,128)} %copy-done.4, f32[8,2,8,32,128]{4,3,2,1,0:T(8,128)} %copy-done, f32[8,2,2,32,128]{4,3,2,1,0:T(8,128)} %copy-done.7, f32[8,2,2,32,128]{4,3,2,1,0:T(8,128)} %get-tuple-element.34._, ...), custom_call_target="tpu_custom_call" | custom-call | flops 1006632960 | bytes 7340036 | tf_op jit(solution)/shard_map/first_step/pallas_call | solution.py:42
  163.9 10.2 %second_step.2 = (f32[8,2,8,32,128]{4,3,2,1,0:T(8,128)}, f32[2,256,128]{2,1,0:T(8,128)}, f32[2,256,128]{2,1,0:T(8,128)}) custom-call(f32[2,10,272,128]{3,2,1,0:T(8,128)} %get-tuple-element.36.first.with_w.refs_6_, f32[2,10,272,128]{3,2,1,0:T(8,128)} %get-tuple-element.36.first.with_w.refs_6_, f32[12,256,128]{2,1,0:T(8,128)} %get-tuple-element.37.visc.refs_8_, ...), custom_call_target="tpu_custom_call" | custom-call | flops 805306368 | bytes 13172736 | tf_op jit(solution)/shard_map/second_step/pallas_call | solution.py:42
  174.1 7.0 %all-to-all-start.3 = ((f32[8,2,8,32,128]{4,3,2,1,0:T(8,128)}), f32[8,2,8,32,128]{4,3,2,1,0:T(8,128)S(1)}, u32[]{:S(2)}, u32[]{:S(2)}) async-start(f32[8,2,8,32,128]{4,3,2,1,0:T(8,128)} %get-tuple-element.41.refs_6_.refs_7_.refs_2_.refs_3_.refs_4_.refs_0_), calls=%async_computation.3 | async-start | bytes 4194304 | tf_op jit(solution)/shard_map/all_to_all | solution.py:672
  183.1 10.8 %carried_step.1.first.refs_7_ = f32[2,10,272,128]{3,2,1,0:T(8,128)} custom-call(f32[8,2,2,32,128]{4,3,2,1,0:T(8,128)} %copy-done.8, f32[8,2,8,32,128]{4,3,2,1,0:T(8,128)} %all-to-all-done.2.chunks.refs_1_, f32[8,2,2,32,128]{4,3,2,1,0:T(8,128)} %copy-done.9, f32[8,2,2,32,128]{4,3,2,1,0:T(8,128)} %copy-done.4, f32[8,2,8,32,128]{4,3,2,1,0:T(8,128)} %copy-done, ...), custom_call_target="tpu_custom_call" | custom-call | flops 1006632960 | bytes 14155776 | tf_op jit(solution)/shard_map/carried_step/pallas_call | solution.py:42
  193.9 17.4 %collective-permute-done.9.refs_1_ = f32[8,2,5,32,128]{4,3,2,1,0:T(8,128)S(1)} collective-permute-done((f32[8,2,5,32,128]{4,3,2,1,0:T(8,128)}, f32[8,2,5,32,128]{4,3,2,1,0:T(8,128)S(1)}, u32[]{:S(2)}, u32[]{:S(2)}) %collective-permute-start.9) | collective-permute-done | bytes 1310752 | tf_op jit(solution)/shard_map/ppermute | solution.py:677
  212.4 10.6 %second_step.3 = (f32[8,2,8,32,128]{4,3,2,1,0:T(8,128)}, f32[2,256,128]{2,1,0:T(8,128)}, f32[2,256,128]{2,1,0:T(8,128)}) custom-call(f32[2,10,272,128]{3,2,1,0:T(8,128)} %carried_step.1.first.refs_7_, f32[2,10,272,128]{3,2,1,0:T(8,128)} %get-tuple-element.36.first.with_w.refs_6_, f32[12,256,128]{2,1,0:T(8,128)} %get-tuple-element.37.visc.refs_8_, ...), custom_call_target="tpu_custom_call" | custom-call | flops 805306368 | bytes 17629184 | tf_op jit(solution)/shard_map/second_step/pallas_call | solution.py:42
  225.4 9.8 %collective-permute-done.10.refs_0_.refs_2_ = f32[2,256,128]{2,1,0:T(8,128)S(1)} collective-permute-done((f32[2,256,128]{2,1,0:T(8,128)}, f32[2,256,128]{2,1,0:T(8,128)S(1)}, u32[]{:S(2)}, u32[]{:S(2)}) %collective-permute-start.10) | collective-permute-done | bytes 262176 | tf_op jit(solution)/shard_map/ppermute | solution.py:677
  241.1 2.9 after.1.refs_1_
  244.1 4.5 %all-to-all-start.4 = ((f32[8,2,8,32,128]{4,3,2,1,0:T(8,128)}), f32[8,2,8,32,128]{4,3,2,1,0:T(8,128)}, u32[]{:S(2)}, u32[]{:S(2)}) async-start(f32[8,2,8,32,128]{4,3,2,1,0:T(8,128)} %after.1.refs_1_), calls=%async_computation.4 | async-start | bytes 4194304 | tf_op jit(solution)/shard_map/all_to_all | solution.py:672
  248.6 17.4 %adjoint_step.1._ = f32[8,34,32,128]{3,2,1,0:T(8,128)} custom-call(f32[8,2,8,32,128]{4,3,2,1,0:T(8,128)} %get-tuple-element.41.refs_6_.refs_7_.refs_2_.refs_3_.refs_4_.refs_0_, f32[8,2,8,32,128]{4,3,2,1,0:T(8,128)} %after.1.refs_1_, f32[2,256,128]{2,1,0:T(8,128)} %copy-done.15, f32[2,256,128]{2,1,0:T(8,128)} %copy-done.17, f32[2,256,128]{2,1,0:T(8,128)} %copy-done.16, ...), custom_call_target="tpu_custom_call" | custom-call | flops 3623878656 | bytes 14483456 | tf_op jit(solution)/shard_map/adjoint_step/pallas_call | solution.py:42
  266.0 27.2 %all-to-all-done.4.other = f32[8,2,8,32,128]{4,3,2,1,0:T(8,128)} async-done(((f32[8,2,8,32,128]{4,3,2,1,0:T(8,128)}), f32[8,2,8,32,128]{4,3,2,1,0:T(8,128)}, u32[]{:S(2)}, u32[]{:S(2)}) %all-to-all-start.4) | async-done | bytes 2097184 | tf_op jit(solution)/shard_map/all_to_all | solution.py:672
  293.2 8.0 %all-to-all-start.5 = ((f32[8,34,32,128]{3,2,1,0:T(8,128)}), f32[8,34,32,128]{3,2,1,0:T(8,128)}, u32[]{:S(2)}, u32[]{:S(2)}) async-start(f32[8,34,32,128]{3,2,1,0:T(8,128)} %adjoint_step.1._), calls=%async_computation.5 | async-start | bytes 8912896 | tf_op jit(solution)/shard_map/all_to_all | solution.py:672
  301.3 8.7 %to_planes.1 = (f32[8192,128]{1,0:T(8,128)}, f32[8,2,8,32,128]{4,3,2,1,0:T(8,128)}) custom-call(f32[8,2,8,32,128]{4,3,2,1,0:T(8,128)} %copy-done.1, f32[8,2,8,32,128]{4,3,2,1,0:T(8,128)} %all-to-all-done.4.other, f32[8,34,32,128]{3,2,1,0:T(8,128)} %adjoint_step.1._), custom_call_target="tpu_custom_call" | custom-call | bytes 8650752 | tf_op jit(solution)/shard_map/to_planes/pallas_call | solution.py:42
  311.4 2.8 collective-permute-start.15
  314.2 3.0 collective-permute-start.14
  317.2 83.2 %collective-permute-done.15.refs_2_ = f32[4,64,128]{2,1,0:T(8,128)S(1)} collective-permute-done((f32[4,64,128]{2,1,0:T(8,128)S(1)}, f32[4,64,128]{2,1,0:T(8,128)S(1)}, u32[]{:S(2)}, u32[]{:S(2)}) %collective-permute-start.15) | collective-permute-done | bytes 131104 | tf_op jit(solution)/shard_map/ppermute | solution.py:698
  401.8 15.2 %last_step.1 = f32[4,2048,128]{2,1,0:T(8,128)} custom-call(f32[64,32,128]{2,1,0:T(8,128)} %get-tuple-element.51.refs_0_, f32[4,64,128]{2,1,0:T(8,128)} %copy-done.21, f32[4,64,128]{2,1,0:T(8,128)} %copy-done.20, f32[8,34,32,128]{3,2,1,0:T(8,128)} %all-to-all-done.5.refs_3_, f32[8,2,8,32,128]{4,3,2,1,0:T(8,128)} %get-tuple-element.29.refs_4_, ...), custom_call_target="tpu_custom_call" | custom-call | flops 31457280 | bytes 14155776 | tf_op jit(solution)/shard_map/last_step/pallas_call | solution.py:42
  (79 shorter events, 32.3 us)
Async XLA Ops:
  3.6 15.1 %all-to-all-start.1 = ((f32[8,3,32,128]{3,2,1,0:T(8,128)}), f32[8,3,32,128]{3,2,1,0:T(8,128)S(1)}, u32[]{:S(2)}, u32[]{:S(2)}) async-start(f32[8,3,32,128]{3,2,1,0:T(8,128)} %get-tuple-element.28.refs_0_), calls=%async_computation.1 | async-start | bytes 786432 | tf_op jit(solution)/shard_map/all_to_all | solution.py:672
  18.7 9.1 %copy-start.3 = (f32[8,3,32,128]{3,2,1,0:T(8,128)}, f32[8,3,32,128]{3,2,1,0:T(8,128)S(1)}, u32[]{:S(2)}) copy-start(f32[8,3,32,128]{3,2,1,0:T(8,128)S(1)} %all-to-all-done.1._.refs_0_) | copy-start | bytes 1179652
  18.7 52.1 %all-to-all-start = ((f32[8,2,8,32,128]{4,3,2,1,0:T(8,128)}), f32[8,2,8,32,128]{4,3,2,1,0:T(8,128)S(1)}, u32[]{:S(2)}, u32[]{:S(2)}) async-start(f32[8,2,8,32,128]{4,3,2,1,0:T(8,128)} %get-tuple-element.29.refs_4_), calls=%async_computation | async-start | bytes 4194304 | tf_op jit(solution)/shard_map/all_to_all | solution.py:672
  25.3 11.3 %collective-permute-start.4 = (f32[8,3,32,128]{3,2,1,0:T(8,128)S(1)}, f32[8,3,32,128]{3,2,1,0:T(8,128)S(1)}, u32[]{:S(2)}, u32[]{:S(2)}) collective-permute-start(f32[8,3,32,128]{3,2,1,0:T(8,128)S(1)} %all-to-all-done.1._.refs_0_), channel_id=1, source_target_pairs={{0,8},{8,16},{16,24},{24,0},{1,9},{9,17},{17,25},{25,1},{2,10},{10... | collective-permute-start | bytes 1179656 | tf_op jit(solution)/shard_map/ppermute | solution.py:677
  26.5 19.2 %collective-permute-start.3 = (f32[8,3,32,128]{3,2,1,0:T(8,128)S(1)}, f32[8,3,32,128]{3,2,1,0:T(8,128)S(1)}, u32[]{:S(2)}, u32[]{:S(2)}) collective-permute-start(f32[8,3,32,128]{3,2,1,0:T(8,128)S(1)} %all-to-all-done.1._.refs_0_), channel_id=1, source_target_pairs={{0,16},{8,24},{16,0},{24,8},{1,17},{9,25},{17,1},{25,9},{2,18},{10... | collective-permute-start | bytes 1179656 | tf_op jit(solution)/shard_map/ppermute | solution.py:677
  27.7 17.9 %collective-permute-start.2 = (f32[8,3,32,128]{3,2,1,0:T(8,128)S(1)}, f32[8,3,32,128]{3,2,1,0:T(8,128)S(1)}, u32[]{:S(2)}, u32[]{:S(2)}) collective-permute-start(f32[8,3,32,128]{3,2,1,0:T(8,128)S(1)} %all-to-all-done.1._.refs_0_), channel_id=1, source_target_pairs={{0,24},{8,0},{16,8},{24,16},{1,25},{9,1},{17,9},{25,17},{2,26},{10... | collective-permute-start | bytes 1179656 | tf_op jit(solution)/shard_map/ppermute | solution.py:677
  36.6 9.1 %copy-start.11 = (f32[8,3,32,128]{3,2,1,0:T(8,128)}, f32[8,3,32,128]{3,2,1,0:T(8,128)S(1)}, u32[]{:S(2)}) copy-start(f32[8,3,32,128]{3,2,1,0:T(8,128)S(1)} %collective-permute-done.4.refs_3_) | copy-start | bytes 1179652
  72.1 59.0 %all-to-all-start.2 = ((f32[8,2,8,32,128]{4,3,2,1,0:T(8,128)}), f32[8,2,8,32,128]{4,3,2,1,0:T(8,128)}, u32[]{:S(2)}, u32[]{:S(2)}) async-start(f32[8,2,8,32,128]{4,3,2,1,0:T(8,128)} %get-tuple-element.33.refs_5_), calls=%async_computation.2 | async-start | bytes 4194304 | tf_op jit(solution)/shard_map/all_to_all | solution.py:672
  83.5 78.5 %collective-permute-start.5 = (f32[8,2,8,32,128]{4,3,2,1,0:T(8,128)}, f32[8,2,8,32,128]{4,3,2,1,0:T(8,128)S(1)}, u32[]{:S(2)}, u32[]{:S(2)}) collective-permute-start(f32[8,2,8,32,128]{4,3,2,1,0:T(8,128)} %get-tuple-element.38), channel_id=1, source_target_pairs={{0,24},{8,0},{16,8},{24,16},{1,25},{9,1},{17,9},{25,17},{2,26},{10... | collective-permute-start | bytes 6291464 | tf_op jit(solution)/shard_map/ppermute | solution.py:677
  85.8 45.3 %collective-permute-start = (f32[8,2,2,32,128]{4,3,2,1,0:T(8,128)}, f32[8,2,2,32,128]{4,3,2,1,0:T(8,128)S(1)}, u32[]{:S(2)}, u32[]{:S(2)}) collective-permute-start(f32[8,2,2,32,128]{4,3,2,1,0:T(8,128)} %get-tuple-element.30), channel_id=1, source_target_pairs={{0,1},{1,2},{2,3},{3,4},{4,5},{5,6},{6,7},{7,0},{8,9},{9,10},{10,1... | collective-permute-start | bytes 1572872 | tf_op jit(solution)/shard_map/ppermute | solution.py:677
  131.9 5.8 %copy-start.22 = (f32[8,2,2,32,128]{4,3,2,1,0:T(8,128)S(1)}, f32[8,2,2,32,128]{4,3,2,1,0:T(8,128)}, u32[]{:S(2)}) copy-start(f32[8,2,2,32,128]{4,3,2,1,0:T(8,128)} %get-tuple-element.31) | copy-start | bytes 1572868
  135.5 26.5 %collective-permute-start.8 = (f32[8,2,3,32,128]{4,3,2,1,0:T(8,128)}, f32[8,2,3,32,128]{4,3,2,1,0:T(8,128)S(1)}, u32[]{:S(2)}, u32[]{:S(2)}) collective-permute-start(f32[8,2,3,32,128]{4,3,2,1,0:T(8,128)} %get-tuple-element.40), channel_id=1, source_target_pairs={{0,24},{8,0},{16,8},{24,16},{1,25},{9,1},{17,9},{25,17},{2,26},{10... | collective-permute-start | bytes 2359304 | tf_op jit(solution)/shard_map/ppermute | solution.py:677
  137.7 13.0 %collective-permute-start.1 = (f32[8,2,2,32,128]{4,3,2,1,0:T(8,128)S(1)}, f32[8,2,2,32,128]{4,3,2,1,0:T(8,128)S(1)}, u32[]{:S(2)}, u32[]{:S(2)}) collective-permute-start(f32[8,2,2,32,128]{4,3,2,1,0:T(8,128)S(1)} %copy-done.22), channel_id=1, source_target_pairs={{0,7},{1,0},{2,1},{3,2},{4,3},{5,4},{6,5},{7,6},{8,15},{9,8},{10,9... | collective-permute-start | bytes 1572872 | tf_op jit(solution)/shard_map/ppermute | solution.py:677
  137.7 24.2 %collective-permute-start.6 = (f32[8,2,2,32,128]{4,3,2,1,0:T(8,128)}, f32[8,2,2,32,128]{4,3,2,1,0:T(8,128)S(1)}, u32[]{:S(2)}, u32[]{:S(2)}) collective-permute-start(f32[8,2,2,32,128]{4,3,2,1,0:T(8,128)} %get-tuple-element.39), channel_id=1, source_target_pairs={{0,1},{1,2},{2,3},{3,4},{4,5},{5,6},{6,7},{7,0},{8,9},{9,10},{10,1... | collective-permute-start | bytes 1572872 | tf_op jit(solution)/shard_map/ppermute | solution.py:677
  140.4 21.6 %collective-permute-start.7 = (f32[8,2,2,32,128]{4,3,2,1,0:T(8,128)}, f32[8,2,2,32,128]{4,3,2,1,0:T(8,128)S(1)}, u32[]{:S(2)}, u32[]{:S(2)}) collective-permute-start(f32[8,2,2,32,128]{4,3,2,1,0:T(8,128)} %get-tuple-element.34._), channel_id=1, source_target_pairs={{0,7},{1,0},{2,1},{3,2},{4,3},{5,4},{6,5},{7,6},{8,15},{9,8},{10,9... | collective-permute-start | bytes 1572872 | tf_op jit(solution)/shard_map/ppermute | solution.py:677
  174.1 9.0 %copy-start.23 = (f32[2,256,128]{2,1,0:T(8,128)S(1)}, f32[2,256,128]{2,1,0:T(8,128)}, u32[]{:S(2)}) copy-start(f32[2,256,128]{2,1,0:T(8,128)} %get-tuple-element.46) | copy-start | bytes 786436
  174.1 65.6 %all-to-all-start.3 = ((f32[8,2,8,32,128]{4,3,2,1,0:T(8,128)}), f32[8,2,8,32,128]{4,3,2,1,0:T(8,128)S(1)}, u32[]{:S(2)}, u32[]{:S(2)}) async-start(f32[8,2,8,32,128]{4,3,2,1,0:T(8,128)} %get-tuple-element.41.refs_6_.refs_7_.refs_2_.refs_3_.refs_4_.refs_0_), calls=%async_computation.3 | async-start | bytes 4194304 | tf_op jit(solution)/shard_map/all_to_all | solution.py:672
  181.1 30.2 %collective-permute-start.9 = (f32[8,2,5,32,128]{4,3,2,1,0:T(8,128)}, f32[8,2,5,32,128]{4,3,2,1,0:T(8,128)S(1)}, u32[]{:S(2)}, u32[]{:S(2)}) collective-permute-start(f32[8,2,5,32,128]{4,3,2,1,0:T(8,128)} %get-tuple-element.42), channel_id=1, source_target_pairs={{0,24},{8,0},{16,8},{24,16},{1,25},{9,1},{17,9},{25,17},{2,26},{10... | collective-permute-start | bytes 3932168 | tf_op jit(solution)/shard_map/ppermute | solution.py:677
  181.4 53.8 %collective-permute-start.10 = (f32[2,256,128]{2,1,0:T(8,128)}, f32[2,256,128]{2,1,0:T(8,128)S(1)}, u32[]{:S(2)}, u32[]{:S(2)}) collective-permute-start(f32[2,256,128]{2,1,0:T(8,128)} %get-tuple-element.44), channel_id=1, source_target_pairs={{0,1},{1,2},{2,3},{3,4},{4,5},{5,6},{6,7},{7,0},{8,9},{9,10},{10,1... | collective-permute-start | bytes 786440 | tf_op jit(solution)/shard_map/ppermute | solution.py:677
  183.1 53.8 %collective-permute-start.12 = (f32[2,256,128]{2,1,0:T(8,128)S(1)}, f32[2,256,128]{2,1,0:T(8,128)S(1)}, u32[]{:S(2)}, u32[]{:S(2)}) collective-permute-start(f32[2,256,128]{2,1,0:T(8,128)S(1)} %copy-done.23), channel_id=1, source_target_pairs={{0,7},{1,0},{2,1},{3,2},{4,3},{5,4},{6,5},{7,6},{8,15},{9,8},{10,9... | collective-permute-start | bytes 786440 | tf_op jit(solution)/shard_map/ppermute | solution.py:677
  223.1 14.9 %collective-permute-start.11 = (f32[2,256,128]{2,1,0:T(8,128)}, f32[2,256,128]{2,1,0:T(8,128)S(1)}, u32[]{:S(2)}, u32[]{:S(2)}) collective-permute-start(f32[2,256,128]{2,1,0:T(8,128)} %get-tuple-element.45), channel_id=1, source_target_pairs={{0,1},{1,2},{2,3},{3,4},{4,5},{5,6},{6,7},{7,0},{8,9},{9,10},{10,1... | collective-permute-start | bytes 786440 | tf_op jit(solution)/shard_map/ppermute | solution.py:677
  225.4 14.3 %collective-permute-start.13 = (f32[2,256,128]{2,1,0:T(8,128)}, f32[2,256,128]{2,1,0:T(8,128)S(1)}, u32[]{:S(2)}, u32[]{:S(2)}) collective-permute-start(f32[2,256,128]{2,1,0:T(8,128)} %get-tuple-element.47), channel_id=1, source_target_pairs={{0,7},{1,0},{2,1},{3,2},{4,3},{5,4},{6,5},{7,6},{8,15},{9,8},{10,9... | collective-permute-start | bytes 786440 | tf_op jit(solution)/shard_map/ppermute | solution.py:677
  235.2 4.5 %copy-start.15 = (f32[2,256,128]{2,1,0:T(8,128)}, f32[2,256,128]{2,1,0:T(8,128)S(1)}, u32[]{:S(2)}) copy-start(f32[2,256,128]{2,1,0:T(8,128)S(1)} %collective-permute-done.10.refs_0_.refs_2_) | copy-start | bytes 786436
  236.9 2.8 copy-start.16
  244.1 49.1 %all-to-all-start.4 = ((f32[8,2,8,32,128]{4,3,2,1,0:T(8,128)}), f32[8,2,8,32,128]{4,3,2,1,0:T(8,128)}, u32[]{:S(2)}, u32[]{:S(2)}) async-start(f32[8,2,8,32,128]{4,3,2,1,0:T(8,128)} %after.1.refs_1_), calls=%async_computation.4 | async-start | bytes 4194304 | tf_op jit(solution)/shard_map/all_to_all | solution.py:672
  266.0 35.2 %copy-start.2 = (f32[8,2,8,32,128]{4,3,2,1,0:T(8,128)S(1)}, f32[8,2,8,32,128]{4,3,2,1,0:T(8,128)}, u32[]{:S(2)}) copy-start(f32[8,2,8,32,128]{4,3,2,1,0:T(8,128)} %copy-done.1) | copy-start | bytes 6291460
  293.2 108.6 %all-to-all-start.5 = ((f32[8,34,32,128]{3,2,1,0:T(8,128)}), f32[8,34,32,128]{3,2,1,0:T(8,128)}, u32[]{:S(2)}, u32[]{:S(2)}) async-start(f32[8,34,32,128]{3,2,1,0:T(8,128)} %adjoint_step.1._), calls=%async_computation.5 | async-start | bytes 8912896 | tf_op jit(solution)/shard_map/all_to_all | solution.py:672
  301.2 10.2 %copy-start.19 = (f32[2,4,64,128]{3,2,1,0:T(8,128)S(1)}, f32[2,4,64,128]{3,2,1,0:T(8,128)}, u32[]{:S(2)}) copy-start(f32[2,4,64,128]{3,2,1,0:T(8,128)} %get-tuple-element.52) | copy-start | bytes 786436
  301.2 99.3 %collective-permute-start.16 = (f32[8,2,8,32,128]{4,3,2,1,0:T(8,128)S(1)}, f32[8,2,8,32,128]{4,3,2,1,0:T(8,128)S(1)}, u32[]{:S(2)}, u32[]{:S(2)}) collective-permute-start(f32[8,2,8,32,128]{4,3,2,1,0:T(8,128)S(1)} %copy-done.2), channel_id=1, source_target_pairs={{0,8},{8,16},{16,24},{24,0},{1,9},{9,17},{17,25},{25,1},{2,10},{10... | collective-permute-start | bytes 6291464 | tf_op jit(solution)/shard_map/ppermute | solution.py:677
  310.0 91.9 %collective-permute-start.17 = (f32[8,2,8,32,128]{4,3,2,1,0:T(8,128)}, f32[8,2,8,32,128]{4,3,2,1,0:T(8,128)}, u32[]{:S(2)}, u32[]{:S(2)}) collective-permute-start(f32[8,2,8,32,128]{4,3,2,1,0:T(8,128)} %get-tuple-element.53), channel_id=1, source_target_pairs={{0,8},{8,16},{16,24},{24,0},{1,9},{9,17},{17,25},{25,1},{2,10},{10... | collective-permute-start | bytes 6291464 | tf_op jit(solution)/shard_map/ppermute | solution.py:677
  311.4 89.1 %collective-permute-start.15 = (f32[4,64,128]{2,1,0:T(8,128)S(1)}, f32[4,64,128]{2,1,0:T(8,128)S(1)}, u32[]{:S(2)}, u32[]{:S(2)}) collective-permute-start(f32[4,64,128]{2,1,0:T(8,128)S(1)} %get-tuple-element.54), channel_id=1, source_target_pairs={{1,0},{2,1},{3,2},{4,3},{5,4},{6,5},{7,6},{9,8},{10,9},{11,10},{12... | collective-permute-start | bytes 393224 | tf_op jit(solution)/shard_map/ppermute | solution.py:698
  314.2 86.2 %collective-permute-start.14 = (f32[4,64,128]{2,1,0:T(8,128)S(1)}, f32[4,64,128]{2,1,0:T(8,128)S(1)}, u32[]{:S(2)}, u32[]{:S(2)}) collective-permute-start(f32[4,64,128]{2,1,0:T(8,128)S(1)} %get-tuple-element.55), channel_id=1, source_target_pairs={{0,1},{1,2},{2,3},{3,4},{4,5},{5,6},{6,7},{8,9},{9,10},{10,11},{11... | collective-permute-start | bytes 393224 | tf_op jit(solution)/shard_map/ppermute | solution.py:697
  (16 other events, 18.5 us)

commit v8 on v7

--- a/solution.py
+++ b/solution.py
@@ -37,7 +37,7 @@
     return pltpu.SemaphoreType.DMA((count,))
 
 
-def call(kernel, ins, outs, scratch, flops, name, kind=f32):
+def call(kernel, ins, outs, scratch, flops, name, kind=f32, aliases=None):
     moved = sum(4 * x.size for x, _ in ins)
     return pl.pallas_call(
         kernel,
@@ -45,6 +45,7 @@
         out_specs=tuple(spec for _, spec in outs),
         out_shape=tuple(jax.ShapeDtypeStruct(shape, kind) for shape, _ in outs),
         scratch_shapes=scratch,
+        input_output_aliases=aliases or {},
         compiler_params=pltpu.CompilerParams(vmem_limit_bytes=vmem_bytes),
         cost_estimate=pl.CostEstimate(flops=flops, bytes_accessed=moved, transcendentals=0),
         name=name,
@@ -130,6 +131,29 @@
         0,
         "visc_chunks",
     )
+
+
+def frame_kernel(own, *refs):
+    *shares, frame, sem = refs
+    slabs, share, depth, _ = shares[0].shape
+    pairs = []
+    for i, part in enumerate(shares):
+        start = lax.rem(own[0] + i, len(shares)) * share
+        for p in range(slabs):
+            pairs.append((part.at[p], frame.at[pl.ds(start, share), pl.ds(p * depth, depth)]))
+    wait_all(start_all(pairs, sem))
+
+
+def to_frame(own, shares):
+    slabs, share, depth, width = shares[0].shape
+    return call(
+        frame_kernel,
+        [(own, scalars())] + [(x, anywhere()) for x in shares],
+        [((len(shares) * share, slabs * depth, width), whole())],
+        [dmas(len(shares) * slabs)],
+        0,
+        "to_frame",
+    )[0]
 
 
 def chunks_kernel(start, x_ref, *refs):
@@ -236,8 +260,8 @@
     return spread
 
 
-def advance_rows(state, speeds, visc, shift, mats, base, scratch, count, finish):
-    mat_high, mat_low, carry, high, low = *mats, *scratch
+def advance_rows(state, speeds, shift, coupled, scratch, count, finish):
+    visc, mat_high, mat_low, carry, high, low = scratch
     order, width = visc.shape[1:]
     first_fluxes(state, visc, shift, carry)
 
@@ -256,11 +280,11 @@
                     value = state[f, j, pads]
                     rate = spread_of(state, f, j, value, here, pads, along_x, along_y, carry)
                     rate = rate - speed * (state[f, j, above] - state[f, j, below])
-                    if base == W:
+                    if coupled:
                         rate = rate + state[1 - f, j, pads]
                     high[f, here, side], low[f, here, side] = parts_of(value + time_step * rate)
         for f in range(2):
-            out = product(mat_high[base + f], mat_low[base + f], high[f], low[f])
+            out = product(mat_high[f], mat_low[f], high[f], low[f])
             finish(f, 2 * k, out[:, :width])
             finish(f, 2 * k + 1, out[:, width:])
         return 0
@@ -276,6 +300,18 @@
     ]
 
 
+def two_scratch(frame):
+    _, order, width = frame.shape
+    matrix = pltpu.VMEM((2, order, order), bf16)
+    return [vmem(*frame.shape), matrix, matrix] + step_scratch(order, width, 2)
+
+
+def constants(base, sources, scratch):
+    frame, mat_high, mat_low = sources
+    two = pl.ds(base, 2)
+    return [(frame, scratch[0]), (mat_high.at[two], scratch[1]), (mat_low.at[two], scratch[2])]
+
+
 def rows_of(low_in, main, high_in, p, target):
     _, _, block, depth, _ = main.shape
     padded = pl.ds(p * depth + pad, depth)
@@ -290,53 +326,41 @@
     return finish
 
 
-def first_kernel(segs, own, low_in, main, high_in, _, mat_high, mat_low, *refs):
-    visc_in, (first, visc, state, *scratch, sem) = refs[:segs], refs[segs:]
+def first_kernel(low_in, main, high_in, _, *refs):
+    sources, (first, state, *scratch, sem) = refs[:3], refs[3:]
     slabs, _, block, depth, _ = main.shape
-    share = visc_in[0].shape[1]
-    pairs = []
+    pairs = constants(W, sources, scratch)
     for p in range(slabs):
         pairs += [(a.at[p], b) for a, b in rows_of(low_in, main, high_in, p, state)]
-        planes = pl.ds(p * depth, depth)
-        for i in range(segs):
-            start = lax.rem(own[0] + i, segs) * share
-            pairs.append((visc_in[i].at[p], visc.at[pl.ds(start, share), planes]))
     copies = start_all(pairs, sem)
     clear_pads(state)
     clear_pads(first)
     wait_all(copies)
-    mats, finish = (mat_high, mat_low), first_finish(first, slabs * depth)
-    advance_rows(state, state.at[W], visc, 0, mats, W, scratch, block + 2, finish)
-
-
-def first_step(own, low_in, main, high_in, later, visc_in, mat_high, mat_low):
+    finish = first_finish(first, slabs * depth)
+    advance_rows(state, state.at[W], 0, True, scratch, block + 2, finish)
+
+
+def first_step(low_in, main, high_in, later, frame, mat_high, mat_low):
     slabs, _, block, depth, width = main.shape
-    segs, share = len(visc_in), visc_in[0].shape[1]
     order = slabs * depth
     volume = 2 * (block + 2) * order * width
     return call(
-        functools.partial(first_kernel, segs),
-        [(own, scalars())]
-        + [(x, anywhere()) for x in (low_in, main, high_in, later)]
-        + [(mat_high, whole()), (mat_low, whole())]
-        + [(x, anywhere()) for x in visc_in],
-        [
-            ((2, block + 2, order + 2 * pad, width), whole()),
-            ((segs * share, order, width), whole()),
-        ],
+        first_kernel,
+        [(x, anywhere()) for x in (low_in, main, high_in, later, frame, mat_high, mat_low)],
+        [((2, block + 2, order + 2 * pad, width), whole())],
         [vmem(2, block + 4, order + 2 * pad, width)]
-        + step_scratch(order, width, 2)
-        + [dmas(slabs * (3 + segs))],
+        + two_scratch(frame)
+        + [dmas(3 * slabs + 3)],
         6 * order * volume,
         "first_step",
-    )
+    )[0]
 
 
 def carried_kernel(*refs):
-    low_in, main, high_in, low_w, main_w, high_w, _, _, visc, mat_high, mat_low = refs[:11]
-    first, state, speeds, *scratch, sem = refs[11:]
+    low_in, main, high_in, low_w, main_w, high_w, _ = refs[:7]
+    sources, (first, state, speeds, *scratch, sem) = refs[7:10], refs[10:]
     slabs, _, block, depth, _ = main.shape
-    pairs = []
+    pairs = constants(U, sources, scratch)
     for p in range(slabs):
         pairs += [(a.at[p], b) for a, b in rows_of(low_in, main, high_in, p, state)]
         w_rows = rows_of(low_w, main_w, high_w, p, speeds)
@@ -345,36 +369,37 @@
     clear_pads(state)
     clear_pads(first)
     wait_all(copies)
-    mats, finish = (mat_high, mat_low), first_finish(first, slabs * depth)
-    advance_rows(state, speeds.at[0], visc, 0, mats, U, scratch, block + 2, finish)
-
-
-def carried_step(own, with_w, later, visc, mat_high, mat_low):
+    finish = first_finish(first, slabs * depth)
+    advance_rows(state, speeds.at[0], 0, False, scratch, block + 2, finish)
+
+
+def carried_step(own, with_w, later, frame, mat_high, mat_low):
     slabs, _, block, depth, width = own[1].shape
     order = slabs * depth
     volume = 2 * (block + 2) * order * width
     return call(
         carried_kernel,
-        [(x, anywhere()) for x in (*own, *with_w, *later)]
-        + [(x, whole()) for x in (visc, mat_high, mat_low)],
+        [(x, anywhere()) for x in (*own, *with_w, later, frame, mat_high, mat_low)],
         [((2, block + 2, order + 2 * pad, width), whole())],
         [
             vmem(2, block + 4, order + 2 * pad, width),
             vmem(1, block + 4, order + 2 * pad, width),
         ]
-        + step_scratch(order, width, 2)
-        + [dmas(6 * slabs)],
+        + two_scratch(frame)
+        + [dmas(6 * slabs + 3)],
         6 * order * volume,
         "carried_step",
     )[0]
 
 
-def second_kernel(base, first, with_w, visc, mat_high, mat_low, *refs):
-    targets, (out, low_edge, high_edge, state, speeds) = refs[:-13], refs[-10:-5]
-    *scratch, held, sem = refs[-5:]
+def second_kernel(base, count, first, with_w, *refs):
+    sources, targets = refs[:3], refs[3 : 3 + count]
+    out, low_edge, high_edge, state, speeds, *scratch, held, sem = refs[-13:]
     slabs, _, block, depth, _ = out.shape
     places = [held.at[:, :, pl.ds(p * depth, depth)] for p in range(slabs)]
-    pairs = [(first, state)] + ([(with_w.at[W], speeds)] if base != W else [])
+    pairs = constants(base, sources, scratch) + [(first, state)]
+    if base != W:
+        pairs.append((with_w.at[W], speeds))
     for target, span in spans(targets, 2):
         for p in range(slabs):
             pairs.append((target.at[p], held.at[:, span, pl.ds(p * depth, depth)]))
@@ -383,49 +408,48 @@
     def finish(f, row, piece):
         held[f, row] = piece - held[f, row]
 
-    mats, speeds = (mat_high, mat_low), state.at[W] if base == W else speeds
-    advance_rows(state, speeds, visc, 1, mats, base, scratch, block, finish)
+    speeds = state.at[W] if base == W else speeds
+    advance_rows(state, speeds, 1, base == W, scratch, block, finish)
     copies = start_all([(places[p], out.at[p]) for p in range(slabs)], sem)
     low_edge[...] = held[:, 0]
     high_edge[...] = held[:, block - 1]
     wait_all(copies)
 
 
-def second_step(first, with_w, visc, mat_high, mat_low, base, targets, later):
-    width, order = visc.shape[2], visc.shape[1]
+def second_step(first, with_w, frame, mat_high, mat_low, base, targets, later):
+    _, order, width = frame.shape
     slabs, _, _, depth, _ = targets[0].shape
     block = sum(target.shape[2] for target in targets)
-    return call(
-        functools.partial(second_kernel, base),
-        [(first, anywhere()), (with_w, anywhere())]
-        + [(x, whole()) for x in (visc, mat_high, mat_low)]
-        + [(x, anywhere()) for x in (*targets, *later)],
+    operands = (first, with_w, frame, mat_high, mat_low, *targets, *later)
+    return call(
+        functools.partial(second_kernel, base, len(targets)),
+        [(x, anywhere()) for x in operands],
         [((slabs, 2, block, depth, width), anywhere())] + [((2, order, width), whole())] * 2,
         [vmem(*first.shape), vmem(*first.shape[1:])]
-        + step_scratch(order, width, 2)
-        + [vmem(2, block, order, width), dmas(2 * slabs + 2)],
+        + two_scratch(frame)
+        + [vmem(2, block, order, width), dmas(2 * slabs + 5)],
         6 * order * 2 * block * order * width,
         "second_step",
     )
 
 
-def after_kernel(x_ref, *refs):
-    o_ref, sem = refs[-2:]
-    wait_all(start_all([(x_ref, o_ref)], sem))
+def after_kernel(*refs):
+    del refs
 
 
 def after(value, later):
     return call(
         after_kernel,
         [(x, anywhere()) for x in (value, *later)],
-        [(value.shape, whole())],
-        [dmas(1)],
+        [(value.shape, anywhere())],
+        [],
         0,
         "after",
+        aliases={0: 0},
     )[0]
 
 
-def outer_kernel(chunks, _, low_rows, high_rows, *refs):
+def outer_kernel(chunks, _before, _after, low_rows, high_rows, *refs):
     *again, sem = refs
     block = chunks.shape[2]
     low, high = chunks.at[:, :, pl.ds(0, 2)], chunks.at[:, :, pl.ds(block - 2, 2)]
@@ -439,7 +463,7 @@
     rows = [((slabs, count, size, depth, width), whole()) for size in (2, 2, *pieces)]
     return call(
         outer_kernel,
-        [(chunks, anywhere()), (later, anywhere())],
+        [(chunks, anywhere())] + [(x, anywhere()) for x in later],
         rows,
         [dmas(len(rows))],
         0,
@@ -556,9 +580,11 @@
 
 
 def last_kernel(*refs):
-    visc, edges_below, edges_above, chunks, *states, half, other, out = refs[:9]
-    pulled, state, prior, planes, coupling, ends, carry, sem = refs[9:]
+    visc_in, edges_below, edges_above, chunks, *states, half, other, out = refs[:9]
+    pulled, state, prior, planes, coupling, ends, visc, sem = refs[9:]
     slabs = chunks.shape[0]
+    visc_copy = pltpu.make_async_copy(visc_in, visc, sem.at[fields, fields + 1])
+    visc_copy.start()
     rows, depth, width = visc.shape
     block = rows // slabs
     main = pl.ds(pad, depth)
@@ -600,6 +626,7 @@
             row = f * block + y % block
             pulled[f, y, first] = ends[y // block, 0, row : row + 1]
             pulled[f, y, last] = ends[y // block, 1, row : row + 1]
+    visc_copy.wait()
     wait_all(copies[W, "state"])
     leaving = []
     for f in (U, V, T, W):
@@ -610,9 +637,9 @@
             wait_all(copies[W, "pulled"])
             copies[W, "pulled"] = []
         along_y = 0.5 * (visc[rows - 1] + visc[0])
-        carry[...] = along_y * (pulled[f, 0, main] - pulled[f, rows - 1, main])
-
-        def row(y, _):
+        south = along_y * (pulled[f, 0, main] - pulled[f, rows - 1, main])
+
+        def row(y, south):
             north = lax.rem(y + 1, rows)
             own = visc[y]
             along_x = 0.5 * (own + east(own))
@@ -620,8 +647,7 @@
             value = pulled[f, y, main]
             flux_x = along_x * (east(value) - value)
             flux_y = along_y * (pulled[f, north, main] - value)
-            rate = flux_x - west(flux_x) + (flux_y - carry[...])
-            carry[...] = flux_y
+            rate = flux_x - west(flux_x) + (flux_y - south)
             flow = state[W, y, above] * pulled[f, y, above]
             rate = rate + (flow - state[W, y, below] * pulled[f, y, below])
             lost = value * (state[f, y, above] - state[f, y, below])
@@ -636,9 +662,9 @@
                 rate = rate + (coupling[y] - lost)
             result = value + time_step * rate - prior[f, y]
             planes[f, pl.ds(y, depth, stride=rows), :] = result
-            return 0
-
-        lax.fori_loop(0, rows, row, 0, unroll=8)
+            return flux_y
+
+        lax.fori_loop(0, rows, row, south, unroll=8)
         copy = pltpu.make_async_copy(planes.at[f], out.at[outside[f]], sem.at[fields, 1 + f])
         copy.start()
         leaving.append(copy)
@@ -650,7 +676,7 @@
     slabs = chunks.shape[0]
     return call(
         last_kernel,
-        [(x, whole()) for x in (visc, below, above)]
+        [(visc, anywhere()), (below, whole()), (above, whole())]
         + [(x, anywhere()) for x in (chunks, *states, *priors)],
         [((fields, depth * rows, width), anywhere())],
         [
@@ -660,8 +686,8 @@
             vmem(fields, depth * rows, width),
             vmem(rows, depth, width),
             vmem(slabs, 2, depth, width),
-            vmem(depth, width),
-            pltpu.SemaphoreType.DMA((fields + 1, fields + 1)),
+            vmem(rows, depth, width),
+            pltpu.SemaphoreType.DMA((fields + 1, fields + 2)),
         ],
         30 * fields * rows * depth * width,
         "last_step",
@@ -691,31 +717,33 @@
     send_half, _ = to_chunks(start, slabs, outside[W], 2, [visc_send])
     main_half = exchange(send_half)
     mat_high, mat_low, adj_high, adj_low = split(inverse)
-    send_other, ends = to_chunks(start, slabs, outside[U], 2, [*visc_in, mat_high])
+    frame = to_frame(own_seg, visc_in)
+    send_other, ends = to_chunks(start, slabs, outside[U], 2, [frame, mat_high])
     main_other = exchange(send_other)
     forward = [(i, i + 1) for i in range(slabs - 1)]
     below = lax.ppermute(ends[1], "slab", forward)
     above = lax.ppermute(ends[0], "slab", [(i, j) for j, i in forward])
 
-    own, outer, targets, later = [], [], [], visc_share
+    own, outer, targets, later = [], [], [], (visc_share, visc_share)
     few = max(1, 3 * block // 8)
     for part, pieces in ((main_half, (block,)), (main_other, (few, block - few))):
         low_rows, high_rows, *again = outer_rows(part, later, pieces)
         low_in = around(high_rows, "slab", 1)
-        own.append((low_in, part, around(low_rows, "slab", -1)))
+        high_in = around(low_rows, "slab", -1)
+        own.append((low_in, part, high_in))
         outer.append(low_rows)
         targets.append([around(piece, "seg", -1) for piece in again])
-        later = low_in
+        later = (low_in, high_in)
 
     mats = mat_high, mat_low
-    first_half, frame = first_step(own_seg, *own[0], outer[1], visc_in, *mats)
+    first_half = first_step(*own[0], outer[1], frame, *mats)
     later = (own[1][0], own[1][2], targets[1][0])
     out, low_edge, high_edge = second_step(
         first_half, first_half, frame, *mats, W, targets[0], later
     )
-    first_other = carried_step(own[1], own[0], (out, out), frame, *mats)
+    first_other = carried_step(own[1], own[0], out, frame, *mats)
     other, *more = second_step(
-        first_other, first_half, frame, *mats, U, targets[1], (out, out, out)
+        first_other, first_half, frame, *mats, U, targets[1], (out,)
     )
     low_edges = [around(edge, "slab", 1) for edge in (high_edge, more[1])]
     high_edges = [around(edge, "slab", -1) for edge in (low_edge, more[0])]

time: 418 us -> 408 us (0.976)
  Pallas kernels: 108 us -> 103 us
    pallas_call x14 -> x15, Pallas kernels: 108 us -> 103 us  [call(): pl.pallas_call(kernel, in_specs=[spec for _, spec in ins], out_specs=tupl...]
    unnamed x48 -> x46, local copies, waits for them, and re-layouts: 9.56 us -> 9.86 us
  transfers between devices with their start and end apart: 24 -> 24, of which waited for: 13 -> 15; matrix products, arithmetic and copies ran while one was open for 0% -> 0% of each run, Pallas kernels for 18% -> 19%
where the time goes in v8:
time: 408 us; the launch traced here: 407 us
  waiting for transfers between devices  233 us (57%)
  Pallas kernels  103 us (25%)
  starting transfers between devices  60.9 us (15%)
  local copies, waits for them, and re-layouts  9.87 us (2%)
    pallas_call x15, Pallas kernels, call(): pl.pallas_call(kernel, in_specs=[spec for _, spec in ins], out_specs=tupl...  103 us
    ppermute x16, waiting for transfers between devices, around(): lax.ppermute(value, axis, [(i, (i + steps) % count) for i in range(count)])  100 us
    ppermute x1, waiting for transfers between devices, local(): above = lax.ppermute(ends[0], 'slab', [(i, j) for j, i in forward])  83.2 us
    all_to_all x6, waiting for transfers between devices, exchange(): lax.all_to_all(chunks, 'slab', split_axis=0, concat_axis=0, tiled=True)  49.1 us
    all_to_all x6, starting transfers between devices, exchange(): lax.all_to_all(chunks, 'slab', split_axis=0, concat_axis=0, tiled=True)  37.3 us
    ppermute x16, starting transfers between devices, around(): lax.ppermute(value, axis, [(i, (i + steps) % count) for i in range(count)])  17.7 us
    unnamed x46, local copies, waits for them, and re-layouts  9.86 us
  transfers between devices with their start and end apart: 24, of which 15 were waited for; matrix products, arithmetic and copies ran while one was open for 0% of the time, Pallas kernels for 19%

profile of v8, /device:TPU:9, one launch (start us, length us, event | category | flops | bytes accessed | tf_op | source)
XLA Modules:
  0.0 407.4 jit_solution(15592135038077082787)
XLA Ops:
  0.6 2.9 visc_chunks.1
  3.6 5.6 %all-to-all-start.1 = ((f32[8,3,32,128]{3,2,1,0:T(8,128)}), f32[8,3,32,128]{3,2,1,0:T(8,128)S(1)}, u32[]{:S(2)}, u32[]{:S(2)}) async-start(f32[8,3,32,128]{3,2,1,0:T(8,128)} %get-tuple-element.26.refs_0_), calls=%async_computation.1 | async-start | bytes 786432 | tf_op jit(solution)/shard_map/all_to_all | solution.py:698
  9.2 4.2 %to_chunks.2 = (f32[8,2,8,32,128]{4,3,2,1,0:T(8,128)}, f32[2,4,64,128]{3,2,1,0:T(8,128)}) custom-call(f32[4,2048,128]{2,1,0:T(8,128)} %bitcast.9, f32[8,3,32,128]{3,2,1,0:T(8,128)} %get-tuple-element.26.refs_0_), custom_call_target="tpu_custom_call" | custom-call | bytes 4587520 | tf_op jit(solution)/shard_map/to_chunks/pallas_call | solution.py:42
  13.4 5.3 %all-to-all-done.1._before._after.refs_0_ = f32[8,3,32,128]{3,2,1,0:T(8,128)S(1)} async-done(((f32[8,3,32,128]{3,2,1,0:T(8,128)}), f32[8,3,32,128]{3,2,1,0:T(8,128)S(1)}, u32[]{:S(2)}, u32[]{:S(2)}) %all-to-all-start.1) | async-done | bytes 393248 | tf_op jit(solution)/shard_map/all_to_all | solution.py:698
  18.7 6.6 %all-to-all-start = ((f32[8,2,8,32,128]{4,3,2,1,0:T(8,128)}), f32[8,2,8,32,128]{4,3,2,1,0:T(8,128)S(1)}, u32[]{:S(2)}, u32[]{:S(2)}) async-start(f32[8,2,8,32,128]{4,3,2,1,0:T(8,128)} %get-tuple-element.27.refs_4_), calls=%async_computation | async-start | bytes 4194304 | tf_op jit(solution)/shard_map/all_to_all | solution.py:698
  28.9 3.0 split.1
  31.8 4.7 %collective-permute-done.4.refs_3_ = f32[8,3,32,128]{3,2,1,0:T(8,128)S(1)} collective-permute-done((f32[8,3,32,128]{3,2,1,0:T(8,128)S(1)}, f32[8,3,32,128]{3,2,1,0:T(8,128)S(1)}, u32[]{:S(2)}, u32[]{:S(2)}) %collective-permute-start.4) | collective-permute-done | bytes 393248 | tf_op jit(solution)/shard_map/ppermute | solution.py:703
  36.6 9.1 %collective-permute-done.3.refs_2_ = f32[8,3,32,128]{3,2,1,0:T(8,128)S(1)} collective-permute-done((f32[8,3,32,128]{3,2,1,0:T(8,128)S(1)}, f32[8,3,32,128]{3,2,1,0:T(8,128)S(1)}, u32[]{:S(2)}, u32[]{:S(2)}) %collective-permute-start.3) | collective-permute-done | bytes 393248 | tf_op jit(solution)/shard_map/ppermute | solution.py:703
  47.1 2.8 to_frame.1.refs_0_.refs_7_.refs_8_
  49.9 4.2 %to_chunks.3 = (f32[8,2,8,32,128]{4,3,2,1,0:T(8,128)}, f32[2,4,64,128]{3,2,1,0:T(8,128)}) custom-call(f32[4,2048,128]{2,1,0:T(8,128)} %bitcast.10, f32[12,256,128]{2,1,0:T(8,128)} %to_frame.1.refs_0_.refs_7_.refs_8_, bf16[4,256,256]{2,1,0:T(8,128)(2,1)} %get-tuple-element.30.refs_1_.refs_8_), custom_call_target="tpu_custom_call" | custom-call | bytes 6815744 | tf_op jit(solution)/shard_map/to_chunks/pallas_call | solution.py:42
  54.2 16.6 %all-to-all-done.chunks.main.refs_4_ = f32[8,2,8,32,128]{4,3,2,1,0:T(8,128)S(1)} async-done(((f32[8,2,8,32,128]{4,3,2,1,0:T(8,128)}), f32[8,2,8,32,128]{4,3,2,1,0:T(8,128)S(1)}, u32[]{:S(2)}, u32[]{:S(2)}) %all-to-all-start) | async-done | bytes 2097184 | tf_op jit(solution)/shard_map/all_to_all | solution.py:698
  72.1 7.8 %all-to-all-start.2 = ((f32[8,2,8,32,128]{4,3,2,1,0:T(8,128)}), f32[8,2,8,32,128]{4,3,2,1,0:T(8,128)}, u32[]{:S(2)}, u32[]{:S(2)}) async-start(f32[8,2,8,32,128]{4,3,2,1,0:T(8,128)} %get-tuple-element.31.refs_5_), calls=%async_computation.2 | async-start | bytes 4194304 | tf_op jit(solution)/shard_map/all_to_all | solution.py:698
  79.9 3.6 outer_rows.2
  87.5 49.2 %collective-permute-done._before.low_in.refs_3_ = f32[8,2,2,32,128]{4,3,2,1,0:T(8,128)S(1)} collective-permute-done((f32[8,2,2,32,128]{4,3,2,1,0:T(8,128)}, f32[8,2,2,32,128]{4,3,2,1,0:T(8,128)S(1)}, u32[]{:S(2)}, u32[]{:S(2)}) %collective-permute-start) | collective-permute-done | bytes 524320 | tf_op jit(solution)/shard_map/ppermute | solution.py:703
  139.6 3.6 outer_rows.3
  146.2 9.1 %first_step.1.first.with_w.refs_6_ = f32[2,10,272,128]{3,2,1,0:T(8,128)} custom-call(f32[8,2,2,32,128]{4,3,2,1,0:T(8,128)} %copy-done.4, f32[8,2,8,32,128]{4,3,2,1,0:T(8,128)} %copy-done, f32[8,2,2,32,128]{4,3,2,1,0:T(8,128)} %copy-done.5, f32[8,2,2,32,128]{4,3,2,1,0:T(8,128)} %get-tuple-element.32._, f32[12,256,128]{2,1,0:T(8,128)} %to_frame.1.refs_0_.refs_7_.refs_8_, ...), custom_call_target="tpu_custom_call" | custom-call | flops 1006632960 | bytes 7340032 | tf_op jit(solution)/shard_map/first_step/pallas_call | solution.py:42
  160.4 9.2 %second_step.2 = (f32[8,2,8,32,128]{4,3,2,1,0:T(8,128)}, f32[2,256,128]{2,1,0:T(8,128)}, f32[2,256,128]{2,1,0:T(8,128)}) custom-call(f32[2,10,272,128]{3,2,1,0:T(8,128)} %first_step.1.first.with_w.refs_6_, f32[2,10,272,128]{3,2,1,0:T(8,128)} %first_step.1.first.with_w.refs_6_, f32[12,256,128]{2,1,0:T(8,128)} %to_frame.1.refs_0_.refs_7_.refs_8_, ...), custom_call_target="tpu_custom_call" | custom-call | flops 805306368 | bytes 13172736 | tf_op jit(solution)/shard_map/second_step/pallas_call | solution.py:42
  169.6 4.7 %all-to-all-start.3 = ((f32[8,2,8,32,128]{4,3,2,1,0:T(8,128)}), f32[8,2,8,32,128]{4,3,2,1,0:T(8,128)S(1)}, u32[]{:S(2)}, u32[]{:S(2)}) async-start(f32[8,2,8,32,128]{4,3,2,1,0:T(8,128)} %get-tuple-element.37.refs_6_.refs_5_.refs_0_), calls=%async_computation.3 | async-start | bytes 4194304 | tf_op jit(solution)/shard_map/all_to_all | solution.py:698
  177.7 9.7 %carried_step.1.first.refs_7_ = f32[2,10,272,128]{3,2,1,0:T(8,128)} custom-call(f32[8,2,2,32,128]{4,3,2,1,0:T(8,128)} %copy-done.9, f32[8,2,8,32,128]{4,3,2,1,0:T(8,128)} %all-to-all-done.2.chunks.refs_1_, f32[8,2,2,32,128]{4,3,2,1,0:T(8,128)} %copy-done.10, f32[8,2,2,32,128]{4,3,2,1,0:T(8,128)} %copy-done.4, f32[8,2,8,32,128]{4,3,2,1,0:T(8,128)} %copy-done, ...), custom_call_target="tpu_custom_call" | custom-call | flops 1006632960 | bytes 12058624 | tf_op jit(solution)/shard_map/carried_step/pallas_call | solution.py:42
  187.4 17.1 %collective-permute-done.9.refs_4_ = f32[8,2,5,32,128]{4,3,2,1,0:T(8,128)S(1)} collective-permute-done((f32[8,2,5,32,128]{4,3,2,1,0:T(8,128)}, f32[8,2,5,32,128]{4,3,2,1,0:T(8,128)S(1)}, u32[]{:S(2)}, u32[]{:S(2)}) %collective-permute-start.9) | collective-permute-done | bytes 1310752 | tf_op jit(solution)/shard_map/ppermute | solution.py:703
  205.5 9.6 %second_step.3 = (f32[8,2,8,32,128]{4,3,2,1,0:T(8,128)}, f32[2,256,128]{2,1,0:T(8,128)}, f32[2,256,128]{2,1,0:T(8,128)}) custom-call(f32[2,10,272,128]{3,2,1,0:T(8,128)} %carried_step.1.first.refs_7_, f32[2,10,272,128]{3,2,1,0:T(8,128)} %first_step.1.first.with_w.refs_6_, f32[12,256,128]{2,1,0:T(8,128)} %to_frame.1.refs_0_.refs_7_.refs_8_, ...), custom_call_target="tpu_custom_call" | custom-call | flops 805306368 | bytes 13434880 | tf_op jit(solution)/shard_map/second_step/pallas_call | solution.py:42
  215.1 2.3 collective-permute-start.11
  217.5 10.9 %collective-permute-done.10.refs_1_.refs_2_ = f32[2,256,128]{2,1,0:T(8,128)S(1)} collective-permute-done((f32[2,256,128]{2,1,0:T(8,128)}, f32[2,256,128]{2,1,0:T(8,128)S(1)}, u32[]{:S(2)}, u32[]{:S(2)}) %collective-permute-start.10) | collective-permute-done | bytes 262176 | tf_op jit(solution)/shard_map/ppermute | solution.py:703
  234.3 4.5 %all-to-all-start.4 = ((f32[8,2,8,32,128]{4,3,2,1,0:T(8,128)}), f32[8,2,8,32,128]{4,3,2,1,0:T(8,128)}, u32[]{:S(2)}, u32[]{:S(2)}) async-start(f32[8,2,8,32,128]{4,3,2,1,0:T(8,128)} %after.1.refs_1_), calls=%async_computation.4 | async-start | bytes 4194304 | tf_op jit(solution)/shard_map/all_to_all | solution.py:698
  238.8 17.4 %adjoint_step.1._ = f32[8,34,32,128]{3,2,1,0:T(8,128)} custom-call(f32[8,2,8,32,128]{4,3,2,1,0:T(8,128)} %get-tuple-element.37.refs_6_.refs_5_.refs_0_, f32[8,2,8,32,128]{4,3,2,1,0:T(8,128)} %after.1.refs_1_, f32[2,256,128]{2,1,0:T(8,128)} %copy-done.12, f32[2,256,128]{2,1,0:T(8,128)} %copy-done.14, f32[2,256,128]{2,1,0:T(8,128)} %copy-done.13, ...), custom_call_target="tpu_custom_call" | custom-call | flops 3623878656 | bytes 14483456 | tf_op jit(solution)/shard_map/adjoint_step/pallas_call | solution.py:42
  256.2 27.2 %all-to-all-done.4.other = f32[8,2,8,32,128]{4,3,2,1,0:T(8,128)} async-done(((f32[8,2,8,32,128]{4,3,2,1,0:T(8,128)}), f32[8,2,8,32,128]{4,3,2,1,0:T(8,128)}, u32[]{:S(2)}, u32[]{:S(2)}) %all-to-all-start.4) | async-done | bytes 2097184 | tf_op jit(solution)/shard_map/all_to_all | solution.py:698
  283.4 8.1 %all-to-all-start.5 = ((f32[8,34,32,128]{3,2,1,0:T(8,128)}), f32[8,34,32,128]{3,2,1,0:T(8,128)}, u32[]{:S(2)}, u32[]{:S(2)}) async-start(f32[8,34,32,128]{3,2,1,0:T(8,128)} %adjoint_step.1._), calls=%async_computation.5 | async-start | bytes 8912896 | tf_op jit(solution)/shard_map/all_to_all | solution.py:698
  292.2 8.6 %to_planes.1 = (f32[8192,128]{1,0:T(8,128)}, f32[8,2,8,32,128]{4,3,2,1,0:T(8,128)}) custom-call(f32[8,2,8,32,128]{4,3,2,1,0:T(8,128)} %copy-done.1, f32[8,2,8,32,128]{4,3,2,1,0:T(8,128)} %all-to-all-done.4.other, f32[8,34,32,128]{3,2,1,0:T(8,128)} %adjoint_step.1._), custom_call_target="tpu_custom_call" | custom-call | bytes 8650752 | tf_op jit(solution)/shard_map/to_planes/pallas_call | solution.py:42
  301.6 2.8 collective-permute-start.15
  304.4 3.0 collective-permute-start.14
  307.5 83.2 %collective-permute-done.15.refs_2_ = f32[4,64,128]{2,1,0:T(8,128)S(1)} collective-permute-done((f32[4,64,128]{2,1,0:T(8,128)S(1)}, f32[4,64,128]{2,1,0:T(8,128)S(1)}, u32[]{:S(2)}, u32[]{:S(2)}) %collective-permute-start.15) | collective-permute-done | bytes 131104 | tf_op jit(solution)/shard_map/ppermute | solution.py:725
  392.1 15.2 %last_step.1 = f32[4,2048,128]{2,1,0:T(8,128)} custom-call(f32[64,32,128]{2,1,0:T(8,128)} %get-tuple-element.47.refs_0_, f32[4,64,128]{2,1,0:T(8,128)} %copy-done.21, f32[4,64,128]{2,1,0:T(8,128)} %copy-done.20, f32[8,34,32,128]{3,2,1,0:T(8,128)} %all-to-all-done.5.refs_3_, f32[8,2,8,32,128]{4,3,2,1,0:T(8,128)} %get-tuple-element.27.refs_4_, ...), custom_call_target="tpu_custom_call" | custom-call | flops 31457280 | bytes 14155776 | tf_op jit(solution)/shard_map/last_step/pallas_call | solution.py:42
  (78 shorter events, 34.5 us)
Async XLA Ops:
  3.6 15.1 %all-to-all-start.1 = ((f32[8,3,32,128]{3,2,1,0:T(8,128)}), f32[8,3,32,128]{3,2,1,0:T(8,128)S(1)}, u32[]{:S(2)}, u32[]{:S(2)}) async-start(f32[8,3,32,128]{3,2,1,0:T(8,128)} %get-tuple-element.26.refs_0_), calls=%async_computation.1 | async-start | bytes 786432 | tf_op jit(solution)/shard_map/all_to_all | solution.py:698
  18.7 9.1 %copy-start.3 = (f32[8,3,32,128]{3,2,1,0:T(8,128)}, f32[8,3,32,128]{3,2,1,0:T(8,128)S(1)}, u32[]{:S(2)}) copy-start(f32[8,3,32,128]{3,2,1,0:T(8,128)S(1)} %all-to-all-done.1._before._after.refs_0_) | copy-start | bytes 1179652
  18.7 52.1 %all-to-all-start = ((f32[8,2,8,32,128]{4,3,2,1,0:T(8,128)}), f32[8,2,8,32,128]{4,3,2,1,0:T(8,128)S(1)}, u32[]{:S(2)}, u32[]{:S(2)}) async-start(f32[8,2,8,32,128]{4,3,2,1,0:T(8,128)} %get-tuple-element.27.refs_4_), calls=%async_computation | async-start | bytes 4194304 | tf_op jit(solution)/shard_map/all_to_all | solution.py:698
  25.3 11.3 %collective-permute-start.4 = (f32[8,3,32,128]{3,2,1,0:T(8,128)S(1)}, f32[8,3,32,128]{3,2,1,0:T(8,128)S(1)}, u32[]{:S(2)}, u32[]{:S(2)}) collective-permute-start(f32[8,3,32,128]{3,2,1,0:T(8,128)S(1)} %all-to-all-done.1._before._after.refs_0_), channel_id=1, source_target_pairs={{0,8},{8,16},{16,24},{24,0},{1,9},{9,17},{17,25},{25,1},{2,10},{10... | collective-permute-start | bytes 1179656 | tf_op jit(solution)/shard_map/ppermute | solution.py:703
  26.5 19.2 %collective-permute-start.3 = (f32[8,3,32,128]{3,2,1,0:T(8,128)S(1)}, f32[8,3,32,128]{3,2,1,0:T(8,128)S(1)}, u32[]{:S(2)}, u32[]{:S(2)}) collective-permute-start(f32[8,3,32,128]{3,2,1,0:T(8,128)S(1)} %all-to-all-done.1._before._after.refs_0_), channel_id=1, source_target_pairs={{0,16},{8,24},{16,0},{24,8},{1,17},{9,25},{17,1},{25,9},{2,18},{10... | collective-permute-start | bytes 1179656 | tf_op jit(solution)/shard_map/ppermute | solution.py:703
  27.7 17.9 %collective-permute-start.2 = (f32[8,3,32,128]{3,2,1,0:T(8,128)S(1)}, f32[8,3,32,128]{3,2,1,0:T(8,128)S(1)}, u32[]{:S(2)}, u32[]{:S(2)}) collective-permute-start(f32[8,3,32,128]{3,2,1,0:T(8,128)S(1)} %all-to-all-done.1._before._after.refs_0_), channel_id=1, source_target_pairs={{0,24},{8,0},{16,8},{24,16},{1,25},{9,1},{17,9},{25,17},{2,26},{10... | collective-permute-start | bytes 1179656 | tf_op jit(solution)/shard_map/ppermute | solution.py:703
  36.6 9.1 %copy-start.16 = (f32[8,3,32,128]{3,2,1,0:T(8,128)}, f32[8,3,32,128]{3,2,1,0:T(8,128)S(1)}, u32[]{:S(2)}) copy-start(f32[8,3,32,128]{3,2,1,0:T(8,128)S(1)} %collective-permute-done.4.refs_3_) | copy-start | bytes 1179652
  72.1 66.6 %all-to-all-start.2 = ((f32[8,2,8,32,128]{4,3,2,1,0:T(8,128)}), f32[8,2,8,32,128]{4,3,2,1,0:T(8,128)}, u32[]{:S(2)}, u32[]{:S(2)}) async-start(f32[8,2,8,32,128]{4,3,2,1,0:T(8,128)} %get-tuple-element.31.refs_5_), calls=%async_computation.2 | async-start | bytes 4194304 | tf_op jit(solution)/shard_map/all_to_all | solution.py:698
  83.6 74.4 %collective-permute-start.5 = (f32[8,2,8,32,128]{4,3,2,1,0:T(8,128)}, f32[8,2,8,32,128]{4,3,2,1,0:T(8,128)S(1)}, u32[]{:S(2)}, u32[]{:S(2)}) collective-permute-start(f32[8,2,8,32,128]{4,3,2,1,0:T(8,128)} %get-tuple-element.34), channel_id=1, source_target_pairs={{0,24},{8,0},{16,8},{24,16},{1,25},{9,1},{17,9},{25,17},{2,26},{10... | collective-permute-start | bytes 6291464 | tf_op jit(solution)/shard_map/ppermute | solution.py:703
  85.8 50.9 %collective-permute-start = (f32[8,2,2,32,128]{4,3,2,1,0:T(8,128)}, f32[8,2,2,32,128]{4,3,2,1,0:T(8,128)S(1)}, u32[]{:S(2)}, u32[]{:S(2)}) collective-permute-start(f32[8,2,2,32,128]{4,3,2,1,0:T(8,128)} %get-tuple-element.28), channel_id=1, source_target_pairs={{0,1},{1,2},{2,3},{3,4},{4,5},{5,6},{6,7},{7,0},{8,9},{9,10},{10,1... | collective-permute-start | bytes 1572872 | tf_op jit(solution)/shard_map/ppermute | solution.py:703
  87.5 51.3 %collective-permute-start.1 = (f32[8,2,2,32,128]{4,3,2,1,0:T(8,128)}, f32[8,2,2,32,128]{4,3,2,1,0:T(8,128)S(1)}, u32[]{:S(2)}, u32[]{:S(2)}) collective-permute-start(f32[8,2,2,32,128]{4,3,2,1,0:T(8,128)} %get-tuple-element.29), channel_id=1, source_target_pairs={{0,7},{1,0},{2,1},{3,2},{4,3},{5,4},{6,5},{7,6},{8,15},{9,8},{10,9... | collective-permute-start | bytes 1572872 | tf_op jit(solution)/shard_map/ppermute | solution.py:703
  136.7 2.0 copy-start.4
  143.2 14.8 %collective-permute-start.8 = (f32[8,2,3,32,128]{4,3,2,1,0:T(8,128)}, f32[8,2,3,32,128]{4,3,2,1,0:T(8,128)S(1)}, u32[]{:S(2)}, u32[]{:S(2)}) collective-permute-start(f32[8,2,3,32,128]{4,3,2,1,0:T(8,128)} %get-tuple-element.36), channel_id=1, source_target_pairs={{0,24},{8,0},{16,8},{24,16},{1,25},{9,1},{17,9},{25,17},{2,26},{10... | collective-permute-start | bytes 2359304 | tf_op jit(solution)/shard_map/ppermute | solution.py:703
  145.1 12.1 %collective-permute-start.6 = (f32[8,2,2,32,128]{4,3,2,1,0:T(8,128)}, f32[8,2,2,32,128]{4,3,2,1,0:T(8,128)S(1)}, u32[]{:S(2)}, u32[]{:S(2)}) collective-permute-start(f32[8,2,2,32,128]{4,3,2,1,0:T(8,128)} %get-tuple-element.35), channel_id=1, source_target_pairs={{0,1},{1,2},{2,3},{3,4},{4,5},{5,6},{6,7},{7,0},{8,9},{9,10},{10,1... | collective-permute-start | bytes 1572872 | tf_op jit(solution)/shard_map/ppermute | solution.py:703
  146.2 11.8 %collective-permute-start.7 = (f32[8,2,2,32,128]{4,3,2,1,0:T(8,128)}, f32[8,2,2,32,128]{4,3,2,1,0:T(8,128)S(1)}, u32[]{:S(2)}, u32[]{:S(2)}) collective-permute-start(f32[8,2,2,32,128]{4,3,2,1,0:T(8,128)} %get-tuple-element.32._), channel_id=1, source_target_pairs={{0,7},{1,0},{2,1},{3,2},{4,3},{5,4},{6,5},{7,6},{8,15},{9,8},{10,9... | collective-permute-start | bytes 1572872 | tf_op jit(solution)/shard_map/ppermute | solution.py:703
  169.6 8.0 %copy-start.22 = (f32[2,256,128]{2,1,0:T(8,128)S(1)}, f32[2,256,128]{2,1,0:T(8,128)}, u32[]{:S(2)}) copy-start(f32[2,256,128]{2,1,0:T(8,128)} %get-tuple-element.42) | copy-start | bytes 786436
  169.6 63.2 %all-to-all-start.3 = ((f32[8,2,8,32,128]{4,3,2,1,0:T(8,128)}), f32[8,2,8,32,128]{4,3,2,1,0:T(8,128)S(1)}, u32[]{:S(2)}, u32[]{:S(2)}) async-start(f32[8,2,8,32,128]{4,3,2,1,0:T(8,128)} %get-tuple-element.37.refs_6_.refs_5_.refs_0_), calls=%async_computation.3 | async-start | bytes 4194304 | tf_op jit(solution)/shard_map/all_to_all | solution.py:698
  174.3 30.2 %collective-permute-start.9 = (f32[8,2,5,32,128]{4,3,2,1,0:T(8,128)}, f32[8,2,5,32,128]{4,3,2,1,0:T(8,128)S(1)}, u32[]{:S(2)}, u32[]{:S(2)}) collective-permute-start(f32[8,2,5,32,128]{4,3,2,1,0:T(8,128)} %get-tuple-element.38), channel_id=1, source_target_pairs={{0,24},{8,0},{16,8},{24,16},{1,25},{9,1},{17,9},{25,17},{2,26},{10... | collective-permute-start | bytes 3932168 | tf_op jit(solution)/shard_map/ppermute | solution.py:703
  175.9 52.4 %collective-permute-start.10 = (f32[2,256,128]{2,1,0:T(8,128)}, f32[2,256,128]{2,1,0:T(8,128)S(1)}, u32[]{:S(2)}, u32[]{:S(2)}) collective-permute-start(f32[2,256,128]{2,1,0:T(8,128)} %get-tuple-element.40), channel_id=1, source_target_pairs={{0,1},{1,2},{2,3},{3,4},{4,5},{5,6},{6,7},{7,0},{8,9},{9,10},{10,1... | collective-permute-start | bytes 786440 | tf_op jit(solution)/shard_map/ppermute | solution.py:703
  177.6 52.4 %collective-permute-start.12 = (f32[2,256,128]{2,1,0:T(8,128)S(1)}, f32[2,256,128]{2,1,0:T(8,128)S(1)}, u32[]{:S(2)}, u32[]{:S(2)}) collective-permute-start(f32[2,256,128]{2,1,0:T(8,128)S(1)} %copy-done.22), channel_id=1, source_target_pairs={{0,7},{1,0},{2,1},{3,2},{4,3},{5,4},{6,5},{7,6},{8,15},{9,8},{10,9... | collective-permute-start | bytes 786440 | tf_op jit(solution)/shard_map/ppermute | solution.py:703
  215.1 16.0 %collective-permute-start.11 = (f32[2,256,128]{2,1,0:T(8,128)}, f32[2,256,128]{2,1,0:T(8,128)S(1)}, u32[]{:S(2)}, u32[]{:S(2)}) collective-permute-start(f32[2,256,128]{2,1,0:T(8,128)} %get-tuple-element.41), channel_id=1, source_target_pairs={{0,1},{1,2},{2,3},{3,4},{4,5},{5,6},{6,7},{7,0},{8,9},{9,10},{10,1... | collective-permute-start | bytes 786440 | tf_op jit(solution)/shard_map/ppermute | solution.py:703
  217.5 15.4 %collective-permute-start.13 = (f32[2,256,128]{2,1,0:T(8,128)}, f32[2,256,128]{2,1,0:T(8,128)S(1)}, u32[]{:S(2)}, u32[]{:S(2)}) collective-permute-start(f32[2,256,128]{2,1,0:T(8,128)} %get-tuple-element.43), channel_id=1, source_target_pairs={{0,7},{1,0},{2,1},{3,2},{4,3},{5,4},{6,5},{7,6},{8,15},{9,8},{10,9... | collective-permute-start | bytes 786440 | tf_op jit(solution)/shard_map/ppermute | solution.py:703
  228.3 4.5 %copy-start.12 = (f32[2,256,128]{2,1,0:T(8,128)}, f32[2,256,128]{2,1,0:T(8,128)S(1)}, u32[]{:S(2)}) copy-start(f32[2,256,128]{2,1,0:T(8,128)S(1)} %collective-permute-done.10.refs_1_.refs_2_) | copy-start | bytes 786436
  230.0 2.8 copy-start.13
  234.3 49.1 %all-to-all-start.4 = ((f32[8,2,8,32,128]{4,3,2,1,0:T(8,128)}), f32[8,2,8,32,128]{4,3,2,1,0:T(8,128)}, u32[]{:S(2)}, u32[]{:S(2)}) async-start(f32[8,2,8,32,128]{4,3,2,1,0:T(8,128)} %after.1.refs_1_), calls=%async_computation.4 | async-start | bytes 4194304 | tf_op jit(solution)/shard_map/all_to_all | solution.py:698
  256.2 35.3 %copy-start.2 = (f32[8,2,8,32,128]{4,3,2,1,0:T(8,128)S(1)}, f32[8,2,8,32,128]{4,3,2,1,0:T(8,128)}, u32[]{:S(2)}) copy-start(f32[8,2,8,32,128]{4,3,2,1,0:T(8,128)} %copy-done.1) | copy-start | bytes 6291460
  283.4 108.7 %all-to-all-start.5 = ((f32[8,34,32,128]{3,2,1,0:T(8,128)}), f32[8,34,32,128]{3,2,1,0:T(8,128)}, u32[]{:S(2)}, u32[]{:S(2)}) async-start(f32[8,34,32,128]{3,2,1,0:T(8,128)} %adjoint_step.1._), calls=%async_computation.5 | async-start | bytes 8912896 | tf_op jit(solution)/shard_map/all_to_all | solution.py:698
  291.4 10.2 %copy-start.19 = (f32[2,4,64,128]{3,2,1,0:T(8,128)S(1)}, f32[2,4,64,128]{3,2,1,0:T(8,128)}, u32[]{:S(2)}) copy-start(f32[2,4,64,128]{3,2,1,0:T(8,128)} %get-tuple-element.48) | copy-start | bytes 786436
  291.4 99.3 %collective-permute-start.16 = (f32[8,2,8,32,128]{4,3,2,1,0:T(8,128)S(1)}, f32[8,2,8,32,128]{4,3,2,1,0:T(8,128)S(1)}, u32[]{:S(2)}, u32[]{:S(2)}) collective-permute-start(f32[8,2,8,32,128]{4,3,2,1,0:T(8,128)S(1)} %copy-done.2), channel_id=1, source_target_pairs={{0,8},{8,16},{16,24},{24,0},{1,9},{9,17},{17,25},{25,1},{2,10},{10... | collective-permute-start | bytes 6291464 | tf_op jit(solution)/shard_map/ppermute | solution.py:703
  300.8 91.2 %collective-permute-start.17 = (f32[8,2,8,32,128]{4,3,2,1,0:T(8,128)}, f32[8,2,8,32,128]{4,3,2,1,0:T(8,128)}, u32[]{:S(2)}, u32[]{:S(2)}) collective-permute-start(f32[8,2,8,32,128]{4,3,2,1,0:T(8,128)} %get-tuple-element.49), channel_id=1, source_target_pairs={{0,8},{8,16},{16,24},{24,0},{1,9},{9,17},{17,25},{25,1},{2,10},{10... | collective-permute-start | bytes 6291464 | tf_op jit(solution)/shard_map/ppermute | solution.py:703
  301.6 89.1 %collective-permute-start.15 = (f32[4,64,128]{2,1,0:T(8,128)S(1)}, f32[4,64,128]{2,1,0:T(8,128)S(1)}, u32[]{:S(2)}, u32[]{:S(2)}) collective-permute-start(f32[4,64,128]{2,1,0:T(8,128)S(1)} %get-tuple-element.50), channel_id=1, source_target_pairs={{1,0},{2,1},{3,2},{4,3},{5,4},{6,5},{7,6},{9,8},{10,9},{11,10},{12... | collective-permute-start | bytes 393224 | tf_op jit(solution)/shard_map/ppermute | solution.py:725
  304.4 86.2 %collective-permute-start.14 = (f32[4,64,128]{2,1,0:T(8,128)S(1)}, f32[4,64,128]{2,1,0:T(8,128)S(1)}, u32[]{:S(2)}, u32[]{:S(2)}) collective-permute-start(f32[4,64,128]{2,1,0:T(8,128)S(1)} %get-tuple-element.51), channel_id=1, source_target_pairs={{0,1},{1,2},{2,3},{3,4},{4,5},{5,6},{6,7},{8,9},{9,10},{10,11},{11... | collective-permute-start | bytes 393224 | tf_op jit(solution)/shard_map/ppermute | solution.py:724
  (15 other events, 16.7 us)

commit v9 on v8

--- a/solution.py
+++ b/solution.py
@@ -582,112 +582,110 @@
 def last_kernel(*refs):
     visc_in, edges_below, edges_above, chunks, *states, half, other, out = refs[:9]
     pulled, state, prior, planes, coupling, ends, visc, sem = refs[9:]
-    slabs = chunks.shape[0]
-    visc_copy = pltpu.make_async_copy(visc_in, visc, sem.at[fields, fields + 1])
-    visc_copy.start()
-    rows, depth, width = visc.shape
-    block = rows // slabs
+    slabs, block, depth, width = visc.shape
+    rows, step = slabs * block, pulled.shape[3]
     main = pl.ds(pad, depth)
     above, below = pl.ds(pad + 1, depth), pl.ds(pad - 1, depth)
-    first, last = slice(pad - 1, pad), slice(pad + depth, pad + depth + 1)
-
-    def arrive(f, which):
-        pairs = []
+
+    def copy(source, target, which):
+        return pltpu.make_async_copy(source, target, sem.at[which])
+
+    arrive = {"visc": copy(visc_in, visc, 0)}
+    arrive["ends"] = copy(chunks.at[:, pl.ds(fields * block, 2)], ends, 1)
+    for f in range(fields):
+        source = chunks.at[:, pl.ds(f * block, block)]
+        arrive["pulled", f] = copy(source, pulled.at[f, :, :, main], 2 + f)
+        source = states[f // 2].at[:, f % 2]
+        arrive["state", f] = copy(source, state.at[f, :, :, main], 2 + fields + f)
+        source = (half, other)[f // 2].at[:, f % 2]
+        arrive["prior", f] = copy(source, prior.at[f], 2 + 2 * fields + f)
+    order = ["visc", "ends", ("state", W)]
+    order += [(which, f) for f in (U, V, T, W) for which in ("pulled", "state", "prior")]
+    for which in dict.fromkeys(order):
+        arrive[which].start()
+
+    def ready(*which):
+        for name in which:
+            if name in arrive:
+                arrive.pop(name).wait()
+
+    flat = (fields * rows * step, width)
+    state_rows, pulled_rows = state.reshape(flat), pulled.reshape(flat)
+    first, last = pad - 1, pad + depth
+    for f in range(fields):
+        base = f * rows * step
+        state_rows[pl.ds(base + first, rows, stride=step), :] = edges_below[outside[f]]
+        state_rows[pl.ds(base + last, rows, stride=step), :] = edges_above[outside[f]]
+    ready("visc", "ends")
+    for f in range(fields):
         for p in range(slabs):
-            place, rest = pl.ds(p * block, block), pl.ds(f * block, block)
-            if which == "pulled":
-                pairs.append((chunks.at[p, rest], pulled.at[f, place, main]))
-            if which == "state":
-                pairs.append((states[f // 2].at[p, f % 2], state.at[f, place, main]))
-            if which == "prior":
-                pairs.append(((half, other)[f // 2].at[p, f % 2], prior.at[f, place]))
-        return [pltpu.make_async_copy(a, b, sem.at[f, which_of[which]]) for a, b in pairs]
-
-    which_of = {"pulled": 0, "state": 1, "prior": 2}
-    ends_copy = pltpu.make_async_copy(
-        chunks.at[:, pl.ds(fields * block, 2)], ends, sem.at[fields, 0]
-    )
-    copies = {}
-    for f, which in [(W, "state"), (U, "pulled"), (U, "state"), (U, "prior")] + [
-        (f, which) for f in (V, T, W) for which in which_of if (f, which) != (W, "state")
-    ]:
-        copies[f, which] = arrive(f, which)
-        for copy in copies[f, which]:
-            copy.start()
-        if (f, which) == (U, "pulled"):
-            ends_copy.start()
-    for f in range(fields):
-        for y in range(rows):
-            state[f, y, first] = edges_below[outside[f], y : y + 1]
-            state[f, y, last] = edges_above[outside[f], y : y + 1]
-    ends_copy.wait()
-    for f in range(fields):
-        for y in range(rows):
-            row = f * block + y % block
-            pulled[f, y, first] = ends[y // block, 0, row : row + 1]
-            pulled[f, y, last] = ends[y // block, 1, row : row + 1]
-    visc_copy.wait()
-    wait_all(copies[W, "state"])
+            base, part = (f * rows + p * block) * step, pl.ds(f * block, block)
+            pulled_rows[pl.ds(base + first, block, stride=step), :] = ends[p, 0, part]
+            pulled_rows[pl.ds(base + last, block, stride=step), :] = ends[p, 1, part]
+    ready(("state", W))
     leaving = []
     for f in (U, V, T, W):
-        for which in which_of:
-            if (f, which) != (W, "state"):
-                wait_all(copies[f, which])
+        ready(("pulled", f), ("state", f), ("prior", f))
         if f == T:
-            wait_all(copies[W, "pulled"])
-            copies[W, "pulled"] = []
-        along_y = 0.5 * (visc[rows - 1] + visc[0])
-        south = along_y * (pulled[f, 0, main] - pulled[f, rows - 1, main])
-
-        def row(y, south):
-            north = lax.rem(y + 1, rows)
-            own = visc[y]
-            along_x = 0.5 * (own + east(own))
-            along_y = 0.5 * (own + visc[north])
-            value = pulled[f, y, main]
-            flux_x = along_x * (east(value) - value)
-            flux_y = along_y * (pulled[f, north, main] - value)
-            rate = flux_x - west(flux_x) + (flux_y - south)
-            flow = state[W, y, above] * pulled[f, y, above]
-            rate = rate + (flow - state[W, y, below] * pulled[f, y, below])
-            lost = value * (state[f, y, above] - state[f, y, below])
-            if f == U:
-                coupling[y] = lost
-            elif f == V:
-                coupling[y] = coupling[y] + lost
-            elif f == T:
-                coupling[y] = value - (coupling[y] + lost)
-                rate = rate + pulled[W, y, main]
-            else:
-                rate = rate + (coupling[y] - lost)
-            result = value + time_step * rate - prior[f, y]
-            planes[f, pl.ds(y, depth, stride=rows), :] = result
-            return flux_y
-
-        lax.fori_loop(0, rows, row, south, unroll=8)
-        copy = pltpu.make_async_copy(planes.at[f], out.at[outside[f]], sem.at[fields, 1 + f])
-        copy.start()
-        leaving.append(copy)
+            ready(("pulled", W))
+        along_y = 0.5 * (visc[slabs - 1, block - 1] + visc[0, 0])
+        south = along_y * (pulled[f, 0, 0, main] - pulled[f, slabs - 1, block - 1, main])
+
+        def group(p, south):
+            after = lax.rem(p + 1, slabs)
+            for i in range(block):
+                n, m = (p, i + 1) if i + 1 < block else (after, 0)
+                own = visc[p, i]
+                along_x = 0.5 * (own + east(own))
+                along_y = 0.5 * (own + visc[n, m])
+                value = pulled[f, p, i, main]
+                flux_x = along_x * (east(value) - value)
+                flux_y = along_y * (pulled[f, n, m, main] - value)
+                rate = flux_x - west(flux_x) + (flux_y - south)
+                south = flux_y
+                flow = state[W, p, i, above] * pulled[f, p, i, above]
+                rate = rate + (flow - state[W, p, i, below] * pulled[f, p, i, below])
+                lost = value * (state[f, p, i, above] - state[f, p, i, below])
+                if f == U:
+                    coupling[p, i] = lost
+                elif f == V:
+                    coupling[p, i] = coupling[p, i] + lost
+                elif f == T:
+                    coupling[p, i] = value - (coupling[p, i] + lost)
+                    rate = rate + pulled[W, p, i, main]
+                else:
+                    rate = rate + (coupling[p, i] - lost)
+                result = value + time_step * rate - prior[f, p, i]
+                planes[f, pl.ds(p * block + i, depth, stride=rows), :] = result
+            return south
+
+        lax.fori_loop(0, slabs, group, south)
+        leave = copy(planes.at[f], out.at[outside[f]], 2 + f)
+        leave.start()
+        leaving.append(leave)
     wait_all(leaving)
 
 
 def last_step(visc, below, above, chunks, states, priors):
     rows, depth, width = visc.shape
     slabs = chunks.shape[0]
+    block = rows // slabs
+    padded = vmem(fields, slabs, block, depth + 2 * pad, width)
+    one = (slabs, block, depth, width)
     return call(
         last_kernel,
-        [(visc, anywhere()), (below, whole()), (above, whole())]
+        [(visc.reshape(one), anywhere()), (below, whole()), (above, whole())]
         + [(x, anywhere()) for x in (chunks, *states, *priors)],
         [((fields, depth * rows, width), anywhere())],
         [
-            vmem(fields, rows, depth + 2 * pad, width),
-            vmem(fields, rows, depth + 2 * pad, width),
-            vmem(fields, rows, depth, width),
+            padded,
+            padded,
+            vmem(fields, *one),
             vmem(fields, depth * rows, width),
-            vmem(rows, depth, width),
+            vmem(*one),
             vmem(slabs, 2, depth, width),
-            vmem(rows, depth, width),
-            pltpu.SemaphoreType.DMA((fields + 1, fields + 2)),
+            vmem(*one),
+            dmas(2 + 3 * fields),
         ],
         30 * fields * rows * depth * width,
         "last_step",
@@ -737,10 +735,10 @@
 
     mats = mat_high, mat_low
     first_half = first_step(*own[0], outer[1], frame, *mats)
-    later = (own[1][0], own[1][2], targets[1][0])
     out, low_edge, high_edge = second_step(
-        first_half, first_half, frame, *mats, W, targets[0], later
-    )
+        first_half, first_half, frame, *mats, W, targets[0], ()
+    )
+    out = after(out, (own[1][0], own[1][2], targets[1][0]))
     first_other = carried_step(own[1], own[0], out, frame, *mats)
     other, *more = second_step(
         first_other, first_half, frame, *mats, U, targets[1], (out,)

time: 408 us -> 405 us (level)
    pallas_call x15 -> x16, Pallas kernels: 103 us -> 103 us  [call(): pl.pallas_call(kernel, in_specs=[spec for _, spec in ins], out_specs=tupl...]
  transfers between devices with their start and end apart: 24 -> 24, of which waited for: 15 -> 13; matrix products, arithmetic and copies ran while one was open for 0% -> 0% of each run, Pallas kernels for 19% -> 21%
where the time goes in v9:
time: 405 us
  waiting for transfers between devices  231 us (57%)
  Pallas kernels  103 us (25%)
  starting transfers between devices  59.4 us (15%)
  local copies, waits for them, and re-layouts  10 us (2%)
    pallas_call x16, Pallas kernels, call(): pl.pallas_call(kernel, in_specs=[spec for _, spec in ins], out_specs=tupl...  103 us
    ppermute x16, waiting for transfers between devices, around(): lax.ppermute(value, axis, [(i, (i + steps) % count) for i in range(count)])  99 us
    ppermute x1, waiting for transfers between devices, local(): above = lax.ppermute(ends[0], 'slab', [(i, j) for j, i in forward])  83.2 us
    all_to_all x6, waiting for transfers between devices, exchange(): lax.all_to_all(chunks, 'slab', split_axis=0, concat_axis=0, tiled=True)  49.1 us
    all_to_all x6, starting transfers between devices, exchange(): lax.all_to_all(chunks, 'slab', split_axis=0, concat_axis=0, tiled=True)  37.3 us
    ppermute x16, starting transfers between devices, around(): lax.ppermute(value, axis, [(i, (i + steps) % count) for i in range(count)])  16.3 us
    unnamed x46, local copies, waits for them, and re-layouts  10 us
  transfers between devices with their start and end apart: 24, of which 13 were waited for; matrix products, arithmetic and copies ran while one was open for 0% of the time, Pallas kernels for 21%

profile of v9, /device:TPU:9, one launch (start us, length us, event | category | flops | bytes accessed | tf_op | source)
XLA Modules:
  0.0 404.6 jit_solution(11124613221928324036)
XLA Ops:
  0.6 2.9 visc_chunks.1
  3.6 5.6 %all-to-all-start.1 = ((f32[8,3,32,128]{3,2,1,0:T(8,128)}), f32[8,3,32,128]{3,2,1,0:T(8,128)S(1)}, u32[]{:S(2)}, u32[]{:S(2)}) async-start(f32[8,3,32,128]{3,2,1,0:T(8,128)} %get-tuple-element.26.refs_0_), calls=%async_computation.1 | async-start | bytes 786432 | tf_op jit(solution)/shard_map/all_to_all | solution.py:696
  9.2 4.2 %to_chunks.2 = (f32[8,2,8,32,128]{4,3,2,1,0:T(8,128)}, f32[2,4,64,128]{3,2,1,0:T(8,128)}) custom-call(f32[4,2048,128]{2,1,0:T(8,128)} %bitcast.10, f32[8,3,32,128]{3,2,1,0:T(8,128)} %get-tuple-element.26.refs_0_), custom_call_target="tpu_custom_call" | custom-call | bytes 4587520 | tf_op jit(solution)/shard_map/to_chunks/pallas_call | solution.py:42
  13.4 5.3 %all-to-all-done.1._before._after.refs_0_ = f32[8,3,32,128]{3,2,1,0:T(8,128)S(1)} async-done(((f32[8,3,32,128]{3,2,1,0:T(8,128)}), f32[8,3,32,128]{3,2,1,0:T(8,128)S(1)}, u32[]{:S(2)}, u32[]{:S(2)}) %all-to-all-start.1) | async-done | bytes 393248 | tf_op jit(solution)/shard_map/all_to_all | solution.py:696
  18.7 6.6 %all-to-all-start = ((f32[8,2,8,32,128]{4,3,2,1,0:T(8,128)}), f32[8,2,8,32,128]{4,3,2,1,0:T(8,128)S(1)}, u32[]{:S(2)}, u32[]{:S(2)}) async-start(f32[8,2,8,32,128]{4,3,2,1,0:T(8,128)} %get-tuple-element.27.refs_4_), calls=%async_computation | async-start | bytes 4194304 | tf_op jit(solution)/shard_map/all_to_all | solution.py:696
  28.9 2.9 split.1
  31.8 4.8 %collective-permute-done.4.refs_3_ = f32[8,3,32,128]{3,2,1,0:T(8,128)S(1)} collective-permute-done((f32[8,3,32,128]{3,2,1,0:T(8,128)S(1)}, f32[8,3,32,128]{3,2,1,0:T(8,128)S(1)}, u32[]{:S(2)}, u32[]{:S(2)}) %collective-permute-start.4) | collective-permute-done | bytes 393248 | tf_op jit(solution)/shard_map/ppermute | solution.py:701
  36.6 9.1 %collective-permute-done.3.refs_2_ = f32[8,3,32,128]{3,2,1,0:T(8,128)S(1)} collective-permute-done((f32[8,3,32,128]{3,2,1,0:T(8,128)S(1)}, f32[8,3,32,128]{3,2,1,0:T(8,128)S(1)}, u32[]{:S(2)}, u32[]{:S(2)}) %collective-permute-start.3) | collective-permute-done | bytes 393248 | tf_op jit(solution)/shard_map/ppermute | solution.py:701
  47.1 2.8 to_frame.1.refs_0_.refs_7_.refs_8_
  49.9 4.2 %to_chunks.3 = (f32[8,2,8,32,128]{4,3,2,1,0:T(8,128)}, f32[2,4,64,128]{3,2,1,0:T(8,128)}) custom-call(f32[4,2048,128]{2,1,0:T(8,128)} %bitcast.11, f32[12,256,128]{2,1,0:T(8,128)} %to_frame.1.refs_0_.refs_7_.refs_8_, bf16[4,256,256]{2,1,0:T(8,128)(2,1)} %get-tuple-element.30.refs_1_.refs_8_), custom_call_target="tpu_custom_call" | custom-call | bytes 6815744 | tf_op jit(solution)/shard_map/to_chunks/pallas_call | solution.py:42
  54.2 16.6 %all-to-all-done.chunks.main.refs_4_ = f32[8,2,8,32,128]{4,3,2,1,0:T(8,128)S(1)} async-done(((f32[8,2,8,32,128]{4,3,2,1,0:T(8,128)}), f32[8,2,8,32,128]{4,3,2,1,0:T(8,128)S(1)}, u32[]{:S(2)}, u32[]{:S(2)}) %all-to-all-start) | async-done | bytes 2097184 | tf_op jit(solution)/shard_map/all_to_all | solution.py:696
  72.1 7.8 %all-to-all-start.2 = ((f32[8,2,8,32,128]{4,3,2,1,0:T(8,128)}), f32[8,2,8,32,128]{4,3,2,1,0:T(8,128)}, u32[]{:S(2)}, u32[]{:S(2)}) async-start(f32[8,2,8,32,128]{4,3,2,1,0:T(8,128)} %get-tuple-element.31.refs_5_), calls=%async_computation.2 | async-start | bytes 4194304 | tf_op jit(solution)/shard_map/all_to_all | solution.py:696
  80.0 3.6 outer_rows.2
  87.5 49.2 %collective-permute-done._before.low_in.refs_3_ = f32[8,2,2,32,128]{4,3,2,1,0:T(8,128)S(1)} collective-permute-done((f32[8,2,2,32,128]{4,3,2,1,0:T(8,128)}, f32[8,2,2,32,128]{4,3,2,1,0:T(8,128)S(1)}, u32[]{:S(2)}, u32[]{:S(2)}) %collective-permute-start) | collective-permute-done | bytes 524320 | tf_op jit(solution)/shard_map/ppermute | solution.py:701
  139.6 3.6 outer_rows.3
  146.2 9.1 %first_step.1.first.with_w.refs_6_ = f32[2,10,272,128]{3,2,1,0:T(8,128)} custom-call(f32[8,2,2,32,128]{4,3,2,1,0:T(8,128)} %copy-done.4, f32[8,2,8,32,128]{4,3,2,1,0:T(8,128)} %copy-done, f32[8,2,2,32,128]{4,3,2,1,0:T(8,128)} %copy-done.5, f32[8,2,2,32,128]{4,3,2,1,0:T(8,128)} %get-tuple-element.32._, f32[12,256,128]{2,1,0:T(8,128)} %to_frame.1.refs_0_.refs_7_.refs_8_, ...), custom_call_target="tpu_custom_call" | custom-call | flops 1006632960 | bytes 7340032 | tf_op jit(solution)/shard_map/first_step/pallas_call | solution.py:42
  156.7 9.3 %second_step.2 = (f32[8,2,8,32,128]{4,3,2,1,0:T(8,128)}, f32[2,256,128]{2,1,0:T(8,128)}, f32[2,256,128]{2,1,0:T(8,128)}) custom-call(f32[2,10,272,128]{3,2,1,0:T(8,128)} %first_step.1.first.with_w.refs_6_, f32[2,10,272,128]{3,2,1,0:T(8,128)} %first_step.1.first.with_w.refs_6_, f32[12,256,128]{2,1,0:T(8,128)} %to_frame.1.refs_0_.refs_7_.refs_8_, ...), custom_call_target="tpu_custom_call" | custom-call | flops 805306368 | bytes 11337728 | tf_op jit(solution)/shard_map/second_step/pallas_call | solution.py:42
  167.2 4.6 %all-to-all-start.3 = ((f32[8,2,8,32,128]{4,3,2,1,0:T(8,128)}), f32[8,2,8,32,128]{4,3,2,1,0:T(8,128)S(1)}, u32[]{:S(2)}, u32[]{:S(2)}) async-start(f32[8,2,8,32,128]{4,3,2,1,0:T(8,128)} %after.2.refs_6_.refs_5_.refs_0_), calls=%async_computation.3 | async-start | bytes 4194304 | tf_op jit(solution)/shard_map/all_to_all | solution.py:696
  173.8 9.7 %carried_step.1.first.refs_7_ = f32[2,10,272,128]{3,2,1,0:T(8,128)} custom-call(f32[8,2,2,32,128]{4,3,2,1,0:T(8,128)} %copy-done.9, f32[8,2,8,32,128]{4,3,2,1,0:T(8,128)} %all-to-all-done.2.chunks.refs_1_, f32[8,2,2,32,128]{4,3,2,1,0:T(8,128)} %copy-done.10, f32[8,2,2,32,128]{4,3,2,1,0:T(8,128)} %copy-done.4, f32[8,2,8,32,128]{4,3,2,1,0:T(8,128)} %copy-done, ...), custom_call_target="tpu_custom_call" | custom-call | flops 1006632960 | bytes 12058624 | tf_op jit(solution)/shard_map/carried_step/pallas_call | solution.py:42
  183.5 18.5 %collective-permute-done.9.refs_4_ = f32[8,2,5,32,128]{4,3,2,1,0:T(8,128)S(1)} collective-permute-done((f32[8,2,5,32,128]{4,3,2,1,0:T(8,128)}, f32[8,2,5,32,128]{4,3,2,1,0:T(8,128)S(1)}, u32[]{:S(2)}, u32[]{:S(2)}) %collective-permute-start.9) | collective-permute-done | bytes 1310752 | tf_op jit(solution)/shard_map/ppermute | solution.py:701
  203.1 9.6 %second_step.3 = (f32[8,2,8,32,128]{4,3,2,1,0:T(8,128)}, f32[2,256,128]{2,1,0:T(8,128)}, f32[2,256,128]{2,1,0:T(8,128)}) custom-call(f32[2,10,272,128]{3,2,1,0:T(8,128)} %carried_step.1.first.refs_7_, f32[2,10,272,128]{3,2,1,0:T(8,128)} %first_step.1.first.with_w.refs_6_, f32[12,256,128]{2,1,0:T(8,128)} %to_frame.1.refs_0_.refs_7_.refs_8_, ...), custom_call_target="tpu_custom_call" | custom-call | flops 805306368 | bytes 13434880 | tf_op jit(solution)/shard_map/second_step/pallas_call | solution.py:42
  212.7 2.3 collective-permute-start.11
  215.0 10.9 %collective-permute-done.10.refs_1_.refs_2_ = f32[2,256,128]{2,1,0:T(8,128)S(1)} collective-permute-done((f32[2,256,128]{2,1,0:T(8,128)}, f32[2,256,128]{2,1,0:T(8,128)S(1)}, u32[]{:S(2)}, u32[]{:S(2)}) %collective-permute-start.10) | collective-permute-done | bytes 262176 | tf_op jit(solution)/shard_map/ppermute | solution.py:701
  231.8 4.5 %all-to-all-start.4 = ((f32[8,2,8,32,128]{4,3,2,1,0:T(8,128)}), f32[8,2,8,32,128]{4,3,2,1,0:T(8,128)}, u32[]{:S(2)}, u32[]{:S(2)}) async-start(f32[8,2,8,32,128]{4,3,2,1,0:T(8,128)} %after.3.refs_1_), calls=%async_computation.4 | async-start | bytes 4194304 | tf_op jit(solution)/shard_map/all_to_all | solution.py:696
  236.3 17.4 %adjoint_step.1._ = f32[8,34,32,128]{3,2,1,0:T(8,128)} custom-call(f32[8,2,8,32,128]{4,3,2,1,0:T(8,128)} %after.2.refs_6_.refs_5_.refs_0_, f32[8,2,8,32,128]{4,3,2,1,0:T(8,128)} %after.3.refs_1_, f32[2,256,128]{2,1,0:T(8,128)} %copy-done.12, f32[2,256,128]{2,1,0:T(8,128)} %copy-done.14, f32[2,256,128]{2,1,0:T(8,128)} %copy-done.13, ...), custom_call_target="tpu_custom_call" | custom-call | flops 3623878656 | bytes 14483456 | tf_op jit(solution)/shard_map/adjoint_step/pallas_call | solution.py:42
  253.7 27.2 %all-to-all-done.4.other = f32[8,2,8,32,128]{4,3,2,1,0:T(8,128)} async-done(((f32[8,2,8,32,128]{4,3,2,1,0:T(8,128)}), f32[8,2,8,32,128]{4,3,2,1,0:T(8,128)}, u32[]{:S(2)}, u32[]{:S(2)}) %all-to-all-start.4) | async-done | bytes 2097184 | tf_op jit(solution)/shard_map/all_to_all | solution.py:696
  280.9 8.1 %all-to-all-start.5 = ((f32[8,34,32,128]{3,2,1,0:T(8,128)}), f32[8,34,32,128]{3,2,1,0:T(8,128)}, u32[]{:S(2)}, u32[]{:S(2)}) async-start(f32[8,34,32,128]{3,2,1,0:T(8,128)} %adjoint_step.1._), calls=%async_computation.5 | async-start | bytes 8912896 | tf_op jit(solution)/shard_map/all_to_all | solution.py:696
  289.0 8.7 %to_planes.1 = (f32[8192,128]{1,0:T(8,128)}, f32[8,2,8,32,128]{4,3,2,1,0:T(8,128)}) custom-call(f32[8,2,8,32,128]{4,3,2,1,0:T(8,128)} %copy-done.1, f32[8,2,8,32,128]{4,3,2,1,0:T(8,128)} %all-to-all-done.4.other, f32[8,34,32,128]{3,2,1,0:T(8,128)} %adjoint_step.1._), custom_call_target="tpu_custom_call" | custom-call | bytes 8650752 | tf_op jit(solution)/shard_map/to_planes/pallas_call | solution.py:42
  299.2 2.8 collective-permute-start.15
  302.0 3.0 collective-permute-start.14
  305.0 83.2 %collective-permute-done.15.refs_2_ = f32[4,64,128]{2,1,0:T(8,128)S(1)} collective-permute-done((f32[4,64,128]{2,1,0:T(8,128)S(1)}, f32[4,64,128]{2,1,0:T(8,128)S(1)}, u32[]{:S(2)}, u32[]{:S(2)}) %collective-permute-start.15) | collective-permute-done | bytes 131104 | tf_op jit(solution)/shard_map/ppermute | solution.py:723
  389.6 14.8 %last_step.1 = f32[4,2048,128]{2,1,0:T(8,128)} custom-call(f32[8,8,32,128]{3,2,1,0:T(8,128)} %bitcast.13, f32[4,64,128]{2,1,0:T(8,128)} %copy-done.21, f32[4,64,128]{2,1,0:T(8,128)} %copy-done.20, f32[8,34,32,128]{3,2,1,0:T(8,128)} %all-to-all-done.5.refs_3_, f32[8,2,8,32,128]{4,3,2,1,0:T(8,128)} %get-tuple-element.27.refs_4_, ...), custom_call_target="tpu_custom_call" | custom-call | flops 31457280 | bytes 14155776 | tf_op jit(solution)/shard_map/last_step/pallas_call | solution.py:42
  (79 shorter events, 30.6 us)
Async XLA Ops:
  3.6 15.1 %all-to-all-start.1 = ((f32[8,3,32,128]{3,2,1,0:T(8,128)}), f32[8,3,32,128]{3,2,1,0:T(8,128)S(1)}, u32[]{:S(2)}, u32[]{:S(2)}) async-start(f32[8,3,32,128]{3,2,1,0:T(8,128)} %get-tuple-element.26.refs_0_), calls=%async_computation.1 | async-start | bytes 786432 | tf_op jit(solution)/shard_map/all_to_all | solution.py:696
  18.7 9.1 %copy-start.3 = (f32[8,3,32,128]{3,2,1,0:T(8,128)}, f32[8,3,32,128]{3,2,1,0:T(8,128)S(1)}, u32[]{:S(2)}) copy-start(f32[8,3,32,128]{3,2,1,0:T(8,128)S(1)} %all-to-all-done.1._before._after.refs_0_) | copy-start | bytes 1179652
  18.7 52.1 %all-to-all-start = ((f32[8,2,8,32,128]{4,3,2,1,0:T(8,128)}), f32[8,2,8,32,128]{4,3,2,1,0:T(8,128)S(1)}, u32[]{:S(2)}, u32[]{:S(2)}) async-start(f32[8,2,8,32,128]{4,3,2,1,0:T(8,128)} %get-tuple-element.27.refs_4_), calls=%async_computation | async-start | bytes 4194304 | tf_op jit(solution)/shard_map/all_to_all | solution.py:696
  25.3 11.3 %collective-permute-start.4 = (f32[8,3,32,128]{3,2,1,0:T(8,128)S(1)}, f32[8,3,32,128]{3,2,1,0:T(8,128)S(1)}, u32[]{:S(2)}, u32[]{:S(2)}) collective-permute-start(f32[8,3,32,128]{3,2,1,0:T(8,128)S(1)} %all-to-all-done.1._before._after.refs_0_), channel_id=1, source_target_pairs={{0,8},{8,16},{16,24},{24,0},{1,9},{9,17},{17,25},{25,1},{2,10},{10... | collective-permute-start | bytes 1179656 | tf_op jit(solution)/shard_map/ppermute | solution.py:701
  26.5 19.2 %collective-permute-start.3 = (f32[8,3,32,128]{3,2,1,0:T(8,128)S(1)}, f32[8,3,32,128]{3,2,1,0:T(8,128)S(1)}, u32[]{:S(2)}, u32[]{:S(2)}) collective-permute-start(f32[8,3,32,128]{3,2,1,0:T(8,128)S(1)} %all-to-all-done.1._before._after.refs_0_), channel_id=1, source_target_pairs={{0,16},{8,24},{16,0},{24,8},{1,17},{9,25},{17,1},{25,9},{2,18},{10... | collective-permute-start | bytes 1179656 | tf_op jit(solution)/shard_map/ppermute | solution.py:701
  27.7 17.9 %collective-permute-start.2 = (f32[8,3,32,128]{3,2,1,0:T(8,128)S(1)}, f32[8,3,32,128]{3,2,1,0:T(8,128)S(1)}, u32[]{:S(2)}, u32[]{:S(2)}) collective-permute-start(f32[8,3,32,128]{3,2,1,0:T(8,128)S(1)} %all-to-all-done.1._before._after.refs_0_), channel_id=1, source_target_pairs={{0,24},{8,0},{16,8},{24,16},{1,25},{9,1},{17,9},{25,17},{2,26},{10... | collective-permute-start | bytes 1179656 | tf_op jit(solution)/shard_map/ppermute | solution.py:701
  36.6 9.1 %copy-start.16 = (f32[8,3,32,128]{3,2,1,0:T(8,128)}, f32[8,3,32,128]{3,2,1,0:T(8,128)S(1)}, u32[]{:S(2)}) copy-start(f32[8,3,32,128]{3,2,1,0:T(8,128)S(1)} %collective-permute-done.4.refs_3_) | copy-start | bytes 1179652
  72.1 66.7 %all-to-all-start.2 = ((f32[8,2,8,32,128]{4,3,2,1,0:T(8,128)}), f32[8,2,8,32,128]{4,3,2,1,0:T(8,128)}, u32[]{:S(2)}, u32[]{:S(2)}) async-start(f32[8,2,8,32,128]{4,3,2,1,0:T(8,128)} %get-tuple-element.31.refs_5_), calls=%async_computation.2 | async-start | bytes 4194304 | tf_op jit(solution)/shard_map/all_to_all | solution.py:696
  83.6 71.7 %collective-permute-start.5 = (f32[8,2,8,32,128]{4,3,2,1,0:T(8,128)}, f32[8,2,8,32,128]{4,3,2,1,0:T(8,128)S(1)}, u32[]{:S(2)}, u32[]{:S(2)}) collective-permute-start(f32[8,2,8,32,128]{4,3,2,1,0:T(8,128)} %get-tuple-element.34), channel_id=1, source_target_pairs={{0,24},{8,0},{16,8},{24,16},{1,25},{9,1},{17,9},{25,17},{2,26},{10... | collective-permute-start | bytes 6291464 | tf_op jit(solution)/shard_map/ppermute | solution.py:701
  85.8 50.9 %collective-permute-start = (f32[8,2,2,32,128]{4,3,2,1,0:T(8,128)}, f32[8,2,2,32,128]{4,3,2,1,0:T(8,128)S(1)}, u32[]{:S(2)}, u32[]{:S(2)}) collective-permute-start(f32[8,2,2,32,128]{4,3,2,1,0:T(8,128)} %get-tuple-element.28), channel_id=1, source_target_pairs={{0,1},{1,2},{2,3},{3,4},{4,5},{5,6},{6,7},{7,0},{8,9},{9,10},{10,1... | collective-permute-start | bytes 1572872 | tf_op jit(solution)/shard_map/ppermute | solution.py:701
  87.5 51.3 %collective-permute-start.1 = (f32[8,2,2,32,128]{4,3,2,1,0:T(8,128)}, f32[8,2,2,32,128]{4,3,2,1,0:T(8,128)S(1)}, u32[]{:S(2)}, u32[]{:S(2)}) collective-permute-start(f32[8,2,2,32,128]{4,3,2,1,0:T(8,128)} %get-tuple-element.29), channel_id=1, source_target_pairs={{0,7},{1,0},{2,1},{3,2},{4,3},{5,4},{6,5},{7,6},{8,15},{9,8},{10,9... | collective-permute-start | bytes 1572872 | tf_op jit(solution)/shard_map/ppermute | solution.py:701
  136.8 2.0 copy-start.4
  143.2 22.8 %collective-permute-start.8 = (f32[8,2,3,32,128]{4,3,2,1,0:T(8,128)}, f32[8,2,3,32,128]{4,3,2,1,0:T(8,128)S(1)}, u32[]{:S(2)}, u32[]{:S(2)}) collective-permute-start(f32[8,2,3,32,128]{4,3,2,1,0:T(8,128)} %get-tuple-element.37), channel_id=1, source_target_pairs={{0,24},{8,0},{16,8},{24,16},{1,25},{9,1},{17,9},{25,17},{2,26},{10... | collective-permute-start | bytes 2359304 | tf_op jit(solution)/shard_map/ppermute | solution.py:701
  145.1 20.8 %collective-permute-start.6 = (f32[8,2,2,32,128]{4,3,2,1,0:T(8,128)}, f32[8,2,2,32,128]{4,3,2,1,0:T(8,128)S(1)}, u32[]{:S(2)}, u32[]{:S(2)}) collective-permute-start(f32[8,2,2,32,128]{4,3,2,1,0:T(8,128)} %get-tuple-element.36), channel_id=1, source_target_pairs={{0,1},{1,2},{2,3},{3,4},{4,5},{5,6},{6,7},{7,0},{8,9},{9,10},{10,1... | collective-permute-start | bytes 1572872 | tf_op jit(solution)/shard_map/ppermute | solution.py:701
  146.2 19.7 %collective-permute-start.7 = (f32[8,2,2,32,128]{4,3,2,1,0:T(8,128)}, f32[8,2,2,32,128]{4,3,2,1,0:T(8,128)S(1)}, u32[]{:S(2)}, u32[]{:S(2)}) collective-permute-start(f32[8,2,2,32,128]{4,3,2,1,0:T(8,128)} %get-tuple-element.32._), channel_id=1, source_target_pairs={{0,7},{1,0},{2,1},{3,2},{4,3},{5,4},{6,5},{7,6},{8,15},{9,8},{10,9... | collective-permute-start | bytes 1572872 | tf_op jit(solution)/shard_map/ppermute | solution.py:701
  167.2 6.6 %copy-start.22 = (f32[2,256,128]{2,1,0:T(8,128)S(1)}, f32[2,256,128]{2,1,0:T(8,128)}, u32[]{:S(2)}) copy-start(f32[2,256,128]{2,1,0:T(8,128)} %get-tuple-element.42) | copy-start | bytes 786436
  167.2 63.2 %all-to-all-start.3 = ((f32[8,2,8,32,128]{4,3,2,1,0:T(8,128)}), f32[8,2,8,32,128]{4,3,2,1,0:T(8,128)S(1)}, u32[]{:S(2)}, u32[]{:S(2)}) async-start(f32[8,2,8,32,128]{4,3,2,1,0:T(8,128)} %after.2.refs_6_.refs_5_.refs_0_), calls=%async_computation.3 | async-start | bytes 4194304 | tf_op jit(solution)/shard_map/all_to_all | solution.py:696
  171.8 30.2 %collective-permute-start.9 = (f32[8,2,5,32,128]{4,3,2,1,0:T(8,128)}, f32[8,2,5,32,128]{4,3,2,1,0:T(8,128)S(1)}, u32[]{:S(2)}, u32[]{:S(2)}) collective-permute-start(f32[8,2,5,32,128]{4,3,2,1,0:T(8,128)} %get-tuple-element.38), channel_id=1, source_target_pairs={{0,24},{8,0},{16,8},{24,16},{1,25},{9,1},{17,9},{25,17},{2,26},{10... | collective-permute-start | bytes 3932168 | tf_op jit(solution)/shard_map/ppermute | solution.py:701
  172.1 53.8 %collective-permute-start.10 = (f32[2,256,128]{2,1,0:T(8,128)}, f32[2,256,128]{2,1,0:T(8,128)S(1)}, u32[]{:S(2)}, u32[]{:S(2)}) collective-permute-start(f32[2,256,128]{2,1,0:T(8,128)} %get-tuple-element.40), channel_id=1, source_target_pairs={{0,1},{1,2},{2,3},{3,4},{4,5},{5,6},{6,7},{7,0},{8,9},{9,10},{10,1... | collective-permute-start | bytes 786440 | tf_op jit(solution)/shard_map/ppermute | solution.py:701
  173.8 53.8 %collective-permute-start.12 = (f32[2,256,128]{2,1,0:T(8,128)S(1)}, f32[2,256,128]{2,1,0:T(8,128)S(1)}, u32[]{:S(2)}, u32[]{:S(2)}) collective-permute-start(f32[2,256,128]{2,1,0:T(8,128)S(1)} %copy-done.22), channel_id=1, source_target_pairs={{0,7},{1,0},{2,1},{3,2},{4,3},{5,4},{6,5},{7,6},{8,15},{9,8},{10,9... | collective-permute-start | bytes 786440 | tf_op jit(solution)/shard_map/ppermute | solution.py:701
  212.7 16.0 %collective-permute-start.11 = (f32[2,256,128]{2,1,0:T(8,128)}, f32[2,256,128]{2,1,0:T(8,128)S(1)}, u32[]{:S(2)}, u32[]{:S(2)}) collective-permute-start(f32[2,256,128]{2,1,0:T(8,128)} %get-tuple-element.41), channel_id=1, source_target_pairs={{0,1},{1,2},{2,3},{3,4},{4,5},{5,6},{6,7},{7,0},{8,9},{9,10},{10,1... | collective-permute-start | bytes 786440 | tf_op jit(solution)/shard_map/ppermute | solution.py:701
  215.0 15.4 %collective-permute-start.13 = (f32[2,256,128]{2,1,0:T(8,128)}, f32[2,256,128]{2,1,0:T(8,128)S(1)}, u32[]{:S(2)}, u32[]{:S(2)}) collective-permute-start(f32[2,256,128]{2,1,0:T(8,128)} %get-tuple-element.43), channel_id=1, source_target_pairs={{0,7},{1,0},{2,1},{3,2},{4,3},{5,4},{6,5},{7,6},{8,15},{9,8},{10,9... | collective-permute-start | bytes 786440 | tf_op jit(solution)/shard_map/ppermute | solution.py:701
  225.9 4.5 %copy-start.12 = (f32[2,256,128]{2,1,0:T(8,128)}, f32[2,256,128]{2,1,0:T(8,128)S(1)}, u32[]{:S(2)}) copy-start(f32[2,256,128]{2,1,0:T(8,128)S(1)} %collective-permute-done.10.refs_1_.refs_2_) | copy-start | bytes 786436
  227.6 2.8 copy-start.13
  231.8 49.1 %all-to-all-start.4 = ((f32[8,2,8,32,128]{4,3,2,1,0:T(8,128)}), f32[8,2,8,32,128]{4,3,2,1,0:T(8,128)}, u32[]{:S(2)}, u32[]{:S(2)}) async-start(f32[8,2,8,32,128]{4,3,2,1,0:T(8,128)} %after.3.refs_1_), calls=%async_computation.4 | async-start | bytes 4194304 | tf_op jit(solution)/shard_map/all_to_all | solution.py:696
  253.7 35.3 %copy-start.2 = (f32[8,2,8,32,128]{4,3,2,1,0:T(8,128)S(1)}, f32[8,2,8,32,128]{4,3,2,1,0:T(8,128)}, u32[]{:S(2)}) copy-start(f32[8,2,8,32,128]{4,3,2,1,0:T(8,128)} %copy-done.1) | copy-start | bytes 6291460
  280.9 108.7 %all-to-all-start.5 = ((f32[8,34,32,128]{3,2,1,0:T(8,128)}), f32[8,34,32,128]{3,2,1,0:T(8,128)}, u32[]{:S(2)}, u32[]{:S(2)}) async-start(f32[8,34,32,128]{3,2,1,0:T(8,128)} %adjoint_step.1._), calls=%async_computation.5 | async-start | bytes 8912896 | tf_op jit(solution)/shard_map/all_to_all | solution.py:696
  289.0 10.2 %copy-start.19 = (f32[2,4,64,128]{3,2,1,0:T(8,128)S(1)}, f32[2,4,64,128]{3,2,1,0:T(8,128)}, u32[]{:S(2)}) copy-start(f32[2,4,64,128]{3,2,1,0:T(8,128)} %get-tuple-element.48) | copy-start | bytes 786436
  289.0 99.3 %collective-permute-start.16 = (f32[8,2,8,32,128]{4,3,2,1,0:T(8,128)S(1)}, f32[8,2,8,32,128]{4,3,2,1,0:T(8,128)S(1)}, u32[]{:S(2)}, u32[]{:S(2)}) collective-permute-start(f32[8,2,8,32,128]{4,3,2,1,0:T(8,128)S(1)} %copy-done.2), channel_id=1, source_target_pairs={{0,8},{8,16},{16,24},{24,0},{1,9},{9,17},{17,25},{25,1},{2,10},{10... | collective-permute-start | bytes 6291464 | tf_op jit(solution)/shard_map/ppermute | solution.py:701
  297.7 91.9 %collective-permute-start.17 = (f32[8,2,8,32,128]{4,3,2,1,0:T(8,128)}, f32[8,2,8,32,128]{4,3,2,1,0:T(8,128)}, u32[]{:S(2)}, u32[]{:S(2)}) collective-permute-start(f32[8,2,8,32,128]{4,3,2,1,0:T(8,128)} %get-tuple-element.49), channel_id=1, source_target_pairs={{0,8},{8,16},{16,24},{24,0},{1,9},{9,17},{17,25},{25,1},{2,10},{10... | collective-permute-start | bytes 6291464 | tf_op jit(solution)/shard_map/ppermute | solution.py:701
  299.2 89.1 %collective-permute-start.15 = (f32[4,64,128]{2,1,0:T(8,128)S(1)}, f32[4,64,128]{2,1,0:T(8,128)S(1)}, u32[]{:S(2)}, u32[]{:S(2)}) collective-permute-start(f32[4,64,128]{2,1,0:T(8,128)S(1)} %get-tuple-element.50), channel_id=1, source_target_pairs={{1,0},{2,1},{3,2},{4,3},{5,4},{6,5},{7,6},{9,8},{10,9},{11,10},{12... | collective-permute-start | bytes 393224 | tf_op jit(solution)/shard_map/ppermute | solution.py:723
  302.0 86.2 %collective-permute-start.14 = (f32[4,64,128]{2,1,0:T(8,128)S(1)}, f32[4,64,128]{2,1,0:T(8,128)S(1)}, u32[]{:S(2)}, u32[]{:S(2)}) collective-permute-start(f32[4,64,128]{2,1,0:T(8,128)S(1)} %get-tuple-element.51), channel_id=1, source_target_pairs={{0,1},{1,2},{2,3},{3,4},{4,5},{5,6},{6,7},{8,9},{9,10},{10,11},{11... | collective-permute-start | bytes 393224 | tf_op jit(solution)/shard_map/ppermute | solution.py:722
  (15 other events, 17.0 us)

commit v10 on v9

--- a/solution.py
+++ b/solution.py
@@ -110,26 +110,80 @@
     )
 
 
-def visc_kernel(own, x_ref, visc, send):
-    slabs, share = send.shape[:2]
-    rows, depth, _ = visc.shape
-    block = rows // slabs
+def first_chunks_kernel(own, x_ref, visc_in, send, visc, planes, held, extra, flat, sem):
+    count, slabs, block, depth, _ = held.shape
+    rows, share = slabs * block, extra.shape[1]
+    visc_copy = pltpu.make_async_copy(visc_in, flat, sem.at[count])
+    visc_copy.start()
+    copies = start_all([(x_ref.at[outside[W] + f], planes.at[f]) for f in range(count)], sem)
+    visc_copy.wait()
     for y in range(rows):
-        visc[y] = x_ref[pl.ds(y, depth, stride=rows), :]
+        visc[y] = flat[pl.ds(y, depth, stride=rows), :]
     for p in range(slabs):
         for i in range(share):
-            send[p, i] = visc[lax.rem(p * block - 2 + share * own[0] + i + rows, rows)]
-
-
-def visc_chunks(own, viscosity, slabs, share):
-    depth, rows, width = viscosity.shape
-    return call(
-        visc_kernel,
-        [(own, scalars()), (viscosity.reshape(-1, width), whole())],
-        [((rows, depth, width), whole()), ((slabs, share, depth, width), whole())],
-        [],
+            row = lax.rem(p * block - 2 + share * own[0] + i + rows, rows)
+            extra[p, i] = visc[row]
+    places = [send.at[:, pl.ds(f * block, block)] for f in range(count)]
+    leaving = [
+        pltpu.make_async_copy(extra, send.at[:, pl.ds(count * block, share)], sem.at[count])
+    ]
+    leaving[0].start()
+    for f in range(count):
+        copies[f].wait()
+        for y in range(rows):
+            held[f, y // block, y % block] = planes[f, pl.ds(y, depth, stride=rows), :]
+        leaving.append(pltpu.make_async_copy(held.at[f], places[f], sem.at[f]))
+        leaving[-1].start()
+    wait_all(leaving)
+
+
+def to_first_chunks(own, states, viscosity, slabs, share):
+    _, depth, rows, width = states.shape
+    block = rows // slabs
+    return call(
+        first_chunks_kernel,
+        [
+            (own, scalars()),
+            (states.reshape(fields, -1, width), anywhere()),
+            (viscosity.reshape(-1, width), anywhere()),
+        ],
+        [
+            ((slabs, 2 * block + share, depth, width), anywhere()),
+            ((rows, depth, width), whole()),
+        ],
+        [
+            vmem(2, depth * rows, width),
+            vmem(2, slabs, block, depth, width),
+            vmem(slabs, share, depth, width),
+            vmem(depth * rows, width),
+            dmas(3),
+        ],
         0,
-        "visc_chunks",
+        "to_first_chunks",
+    )
+
+
+def unpack_kernel(chunks, _, low_rows, high_rows, main, visc, sem):
+    block, share = main.shape[2], visc.shape[1]
+    pairs = [(chunks.at[:, pl.ds(2 * block, share)], visc)]
+    for f in range(2):
+        start = f * block
+        pairs.append((chunks.at[:, pl.ds(start, 2)], low_rows.at[:, f]))
+        pairs.append((chunks.at[:, pl.ds(start + block - 2, 2)], high_rows.at[:, f]))
+        pairs.append((chunks.at[:, pl.ds(start, block)], main.at[:, f]))
+    wait_all(start_all(pairs, sem))
+
+
+def unpack(chunks, block, later):
+    slabs, total, depth, width = chunks.shape
+    sizes = [(2, 2), (2, 2), (2, block), (total - 2 * block,)]
+    return call(
+        unpack_kernel,
+        [(chunks, anywhere()), (later, anywhere())],
+        [((slabs, *size, depth, width), whole()) for size in sizes],
+        [dmas(7)],
+        0,
+        "unpack",
     )
 
 
@@ -449,25 +503,27 @@
     )[0]
 
 
-def outer_kernel(chunks, _before, _after, low_rows, high_rows, *refs):
-    *again, sem = refs
+def outer_kernel(chunks, *refs):
+    *outs, sem = refs[-3:]
     block = chunks.shape[2]
     low, high = chunks.at[:, :, pl.ds(0, 2)], chunks.at[:, :, pl.ds(block - 2, 2)]
-    pairs = [(low, low_rows), (high, high_rows)]
-    pairs += [(chunks.at[:, :, span], part) for part, span in spans(again, 2)]
-    wait_all(start_all(pairs, sem))
-
-
-def outer_rows(chunks, later, pieces):
+    wait_all(start_all([(low, outs[0]), (high, outs[1])], sem))
+
+
+def pieces_kernel(chunks, _, *refs):
+    *outs, sem = refs
+    wait_all(start_all([(chunks.at[:, :, span], part) for part, span in spans(outs, 2)], sem))
+
+
+def row_parts(kernel, chunks, later, sizes, name):
     slabs, count, _, depth, width = chunks.shape
-    rows = [((slabs, count, size, depth, width), whole()) for size in (2, 2, *pieces)]
-    return call(
-        outer_kernel,
+    return call(
+        kernel,
         [(chunks, anywhere())] + [(x, anywhere()) for x in later],
-        rows,
-        [dmas(len(rows))],
+        [((slabs, count, size, depth, width), whole()) for size in sizes],
+        [dmas(len(sizes))],
         0,
-        "outer_rows",
+        name,
     )
 
 
@@ -595,7 +651,7 @@
     for f in range(fields):
         source = chunks.at[:, pl.ds(f * block, block)]
         arrive["pulled", f] = copy(source, pulled.at[f, :, :, main], 2 + f)
-        source = states[f // 2].at[:, f % 2]
+        source = states[0].at[:, pl.ds(f * block, block)] if f < 2 else states[1].at[:, f - 2]
         arrive["state", f] = copy(source, state.at[f, :, :, main], 2 + fields + f)
         source = (half, other)[f // 2].at[:, f % 2]
         arrive["prior", f] = copy(source, prior.at[f], 2 + 2 * fields + f)
@@ -709,40 +765,40 @@
     share = -(-(block + 4) // segs)
 
     own_seg = jnp.full((1,), lax.axis_index("seg"), jnp.int32)
-    visc, visc_send = visc_chunks(own_seg, viscosity, slabs, share)
-    visc_share = exchange(visc_send)
-    visc_in = [visc_share] + [around(visc_share, "seg", -i) for i in range(1, segs)]
-    send_half, _ = to_chunks(start, slabs, outside[W], 2, [visc_send])
-    main_half = exchange(send_half)
+    send_half, visc = to_first_chunks(own_seg, start, viscosity, slabs, share)
+    packed = exchange(send_half)
     mat_high, mat_low, adj_high, adj_low = split(inverse)
-    frame = to_frame(own_seg, visc_in)
-    send_other, ends = to_chunks(start, slabs, outside[U], 2, [frame, mat_high])
+    send_other, ends = to_chunks(start, slabs, outside[U], 2, [mat_high])
     main_other = exchange(send_other)
     forward = [(i, i + 1) for i in range(slabs - 1)]
     below = lax.ppermute(ends[1], "slab", forward)
     above = lax.ppermute(ends[0], "slab", [(i, j) for j, i in forward])
 
-    own, outer, targets, later = [], [], [], (visc_share, visc_share)
-    few = max(1, 3 * block // 8)
-    for part, pieces in ((main_half, (block,)), (main_other, (few, block - few))):
-        low_rows, high_rows, *again = outer_rows(part, later, pieces)
-        low_in = around(high_rows, "slab", 1)
-        high_in = around(low_rows, "slab", -1)
-        own.append((low_in, part, high_in))
-        outer.append(low_rows)
-        targets.append([around(piece, "seg", -1) for piece in again])
-        later = (low_in, high_in)
+    low_rows, high_rows, main_half, visc_share = unpack(packed, block, send_other)
+    visc_in = [visc_share] + [around(visc_share, "seg", -i) for i in range(1, segs)]
+    low_in, high_in = around(high_rows, "slab", 1), around(low_rows, "slab", -1)
+    frame = to_frame(own_seg, visc_in)
+    main_half = after(main_half, (frame,))
+    half_rows = (low_in, main_half, high_in)
+    target = around(main_half, "seg", -1)
+
+    sizes, few = (2, 2), max(1, block // 8)
+    low_rows, high_rows = row_parts(
+        outer_kernel, main_other, (low_in, high_in, frame), sizes, "outer_rows"
+    )
+    other_rows = (around(high_rows, "slab", 1), main_other, around(low_rows, "slab", -1))
+    sizes = (few, block - few)
+    parts = row_parts(pieces_kernel, main_other, (low_rows,), sizes, "pieces")
+    targets = [around(part, "seg", -1) for part in parts]
 
     mats = mat_high, mat_low
-    first_half = first_step(*own[0], outer[1], frame, *mats)
+    first_half = first_step(*half_rows, parts[0], frame, *mats)
     out, low_edge, high_edge = second_step(
-        first_half, first_half, frame, *mats, W, targets[0], ()
-    )
-    out = after(out, (own[1][0], own[1][2], targets[1][0]))
-    first_other = carried_step(own[1], own[0], out, frame, *mats)
-    other, *more = second_step(
-        first_other, first_half, frame, *mats, U, targets[1], (out,)
-    )
+        first_half, first_half, frame, *mats, W, (target,), ()
+    )
+    out = after(out, (other_rows[0], other_rows[2], targets[0]))
+    first_other = carried_step(other_rows, half_rows, out, frame, *mats)
+    other, *more = second_step(first_other, first_half, frame, *mats, U, targets, (out,))
     low_edges = [around(edge, "slab", 1) for edge in (high_edge, more[1])]
     high_edges = [around(edge, "slab", -1) for edge in (low_edge, more[0])]
     half = exchange(out)

time: 405 us -> 413 us (1.020)
  waiting for transfers between devices: 231 us -> 243 us
  starting transfers between devices: 59.4 us -> 55.1 us
    all_to_all x6 -> x5, waiting for transfers between devices: 49.1 us -> 93.9 us  [exchange(): lax.all_to_all(chunks, 'slab', split_axis=0, concat_axis=0, tiled=True)]
    ppermute x16, waiting for transfers between devices: 99 us -> 67 us  [around(): lax.ppermute(value, axis, [(i, (i + steps) % count) for i in range(count)])]
    all_to_all x6 -> x5, starting transfers between devices: 37.3 us -> 30.5 us  [exchange(): lax.all_to_all(chunks, 'slab', split_axis=0, concat_axis=0, tiled=True)]
    pallas_call x16 -> x17, Pallas kernels: 103 us -> 102 us  [call(): pl.pallas_call(kernel, in_specs=[spec for _, spec in ins], out_specs=tupl...]
  transfers between devices with their start and end apart: 24 -> 23, of which waited for: 13 -> 12; matrix products, arithmetic and copies ran while one was open for 0% -> 0% of each run, Pallas kernels for 21% -> 20%
where the time goes in v10:
time: 413 us; the launch traced here: 411 us
  waiting for transfers between devices  243 us (59%)
  Pallas kernels  102 us (25%)
  starting transfers between devices  55.1 us (13%)
  local copies, waits for them, and re-layouts  8.86 us (2%)
    pallas_call x17, Pallas kernels, call(): pl.pallas_call(kernel, in_specs=[spec for _, spec in ins], out_specs=tupl...  102 us
    all_to_all x5, waiting for transfers between devices, exchange(): lax.all_to_all(chunks, 'slab', split_axis=0, concat_axis=0, tiled=True)  93.9 us
    ppermute x1, waiting for transfers between devices, local(): above = lax.ppermute(ends[0], 'slab', [(i, j) for j, i in forward])  82.5 us
    ppermute x16, waiting for transfers between devices, around(): lax.ppermute(value, axis, [(i, (i + steps) % count) for i in range(count)])  67 us
    all_to_all x5, starting transfers between devices, exchange(): lax.all_to_all(chunks, 'slab', split_axis=0, concat_axis=0, tiled=True)  30.5 us
    ppermute x16, starting transfers between devices, around(): lax.ppermute(value, axis, [(i, (i + steps) % count) for i in range(count)])  19 us
    unnamed x46, local copies, waits for them, and re-layouts  8.84 us
  transfers between devices with their start and end apart: 23, of which 12 were waited for; matrix products, arithmetic and copies ran while one was open for 0% of the time, Pallas kernels for 20%

profile of v10, /device:TPU:9, one launch (start us, length us, event | category | flops | bytes accessed | tf_op | source)
XLA Modules:
  0.0 410.9 jit_solution(7746970674669043240)
XLA Ops:
  0.6 5.1 %to_first_chunks.1 = (f32[8,19,32,128]{3,2,1,0:T(8,128)}, f32[64,32,128]{2,1,0:T(8,128)}) custom-call(s32[1]{0:T(128)} %bitcast.own, f32[4,2048,128]{2,1,0:T(8,128)} %bitcast.10, f32[2048,128]{1,0:T(8,128)} %bitcast.14), custom_call_target="tpu_custom_call" | custom-call | bytes 5242884 | tf_op jit(solution)/shard_map/to_first_chunks/pallas_call | solution.py:42
  5.7 5.6 %all-to-all-start = ((f32[8,19,32,128]{3,2,1,0:T(8,128)}), f32[8,19,32,128]{3,2,1,0:T(8,128)S(1)}, u32[]{:S(2)}, u32[]{:S(2)}) async-start(f32[8,19,32,128]{3,2,1,0:T(8,128)} %get-tuple-element.26.refs_4_), calls=%async_computation | async-start | bytes 4980736 | tf_op jit(solution)/shard_map/all_to_all | solution.py:752
  11.4 2.9 split.1
  14.3 4.2 %to_chunks.1 = (f32[8,2,8,32,128]{4,3,2,1,0:T(8,128)}, f32[2,4,64,128]{3,2,1,0:T(8,128)}) custom-call(f32[4,2048,128]{2,1,0:T(8,128)} %bitcast.11, bf16[4,256,256]{2,1,0:T(8,128)(2,1)} %get-tuple-element.27.refs_0_.refs_1_.refs_8_), custom_call_target="tpu_custom_call" | custom-call | bytes 5242880 | tf_op jit(solution)/shard_map/to_chunks/pallas_call | solution.py:42
  18.5 46.8 %all-to-all-done.chunks = f32[8,19,32,128]{3,2,1,0:T(8,128)S(1)} async-done(((f32[8,19,32,128]{3,2,1,0:T(8,128)}), f32[8,19,32,128]{3,2,1,0:T(8,128)S(1)}, u32[]{:S(2)}, u32[]{:S(2)}) %all-to-all-start) | async-done | bytes 2490400 | tf_op jit(solution)/shard_map/all_to_all | solution.py:752
  66.7 7.1 %all-to-all-start.1 = ((f32[8,2,8,32,128]{4,3,2,1,0:T(8,128)}), f32[8,2,8,32,128]{4,3,2,1,0:T(8,128)S(1)}, u32[]{:S(2)}, u32[]{:S(2)}) async-start(f32[8,2,8,32,128]{4,3,2,1,0:T(8,128)} %get-tuple-element.28._.refs_5_), calls=%async_computation.1 | async-start | bytes 4194304 | tf_op jit(solution)/shard_map/all_to_all | solution.py:752
  73.8 3.9 unpack.1
  81.3 7.9 %collective-permute-done.3.refs_3_ = f32[8,3,32,128]{3,2,1,0:T(8,128)S(1)} collective-permute-done((f32[8,3,32,128]{3,2,1,0:T(8,128)}, f32[8,3,32,128]{3,2,1,0:T(8,128)S(1)}, u32[]{:S(2)}, u32[]{:S(2)}) %collective-permute-start.3) | collective-permute-done | bytes 393248 | tf_op jit(solution)/shard_map/ppermute | solution.py:757
  89.2 9.1 %collective-permute-done.2.refs_2_ = f32[8,3,32,128]{3,2,1,0:T(8,128)S(1)} collective-permute-done((f32[8,3,32,128]{3,2,1,0:T(8,128)}, f32[8,3,32,128]{3,2,1,0:T(8,128)S(1)}, u32[]{:S(2)}, u32[]{:S(2)}) %collective-permute-start.2) | collective-permute-done | bytes 393248 | tf_op jit(solution)/shard_map/ppermute | solution.py:757
  99.8 2.8 to_frame.1.refs_1_.refs_2_.refs_0_.refs_7_.refs_8_
  102.7 3.3 collective-permute-start
  106.0 19.0 %all-to-all-done.1.chunks.refs_1_ = f32[8,2,8,32,128]{4,3,2,1,0:T(8,128)S(1)} async-done(((f32[8,2,8,32,128]{4,3,2,1,0:T(8,128)}), f32[8,2,8,32,128]{4,3,2,1,0:T(8,128)S(1)}, u32[]{:S(2)}, u32[]{:S(2)}) %all-to-all-start.1) | async-done | bytes 2097184 | tf_op jit(solution)/shard_map/all_to_all | solution.py:752
  124.9 5.7 %collective-permute-done.refs_0_.low_in.refs_3_ = f32[8,2,2,32,128]{4,3,2,1,0:T(8,128)S(1)} collective-permute-done((f32[8,2,2,32,128]{4,3,2,1,0:T(8,128)}, f32[8,2,2,32,128]{4,3,2,1,0:T(8,128)S(1)}, u32[]{:S(2)}, u32[]{:S(2)}) %collective-permute-start) | collective-permute-done | bytes 524320 | tf_op jit(solution)/shard_map/ppermute | solution.py:757
  136.9 3.0 pieces.1
  142.0 9.1 %first_step.1.first.with_w.refs_6_ = f32[2,10,272,128]{3,2,1,0:T(8,128)} custom-call(f32[8,2,2,32,128]{4,3,2,1,0:T(8,128)} %copy-done.4, f32[8,2,8,32,128]{4,3,2,1,0:T(8,128)} %after.3.main.refs_4_, f32[8,2,2,32,128]{4,3,2,1,0:T(8,128)} %copy-done.5, f32[8,2,1,32,128]{4,3,2,1,0:T(8,128)} %get-tuple-element.34._, ...), custom_call_target="tpu_custom_call" | custom-call | flops 1006632960 | bytes 7077888 | tf_op jit(solution)/shard_map/first_step/pallas_call | solution.py:42
  151.2 9.2 %second_step.2 = (f32[8,2,8,32,128]{4,3,2,1,0:T(8,128)}, f32[2,256,128]{2,1,0:T(8,128)}, f32[2,256,128]{2,1,0:T(8,128)}) custom-call(f32[2,10,272,128]{3,2,1,0:T(8,128)} %first_step.1.first.with_w.refs_6_, f32[2,10,272,128]{3,2,1,0:T(8,128)} %first_step.1.first.with_w.refs_6_, f32[12,256,128]{2,1,0:T(8,128)} %to_frame.1.refs_1_.refs_2_.refs_0_.refs_7_.refs_8_, ...), custom_call_target="tpu_custom_call" | custom-call | flops 805306368 | bytes 11337728 | tf_op jit(solution)/shard_map/second_step/pallas_call | solution.py:42
  161.5 5.6 %all-to-all-start.2 = ((f32[8,2,8,32,128]{4,3,2,1,0:T(8,128)}), f32[8,2,8,32,128]{4,3,2,1,0:T(8,128)S(1)}, u32[]{:S(2)}, u32[]{:S(2)}) async-start(f32[8,2,8,32,128]{4,3,2,1,0:T(8,128)} %after.4.refs_6_.refs_5_.refs_0_), calls=%async_computation.2 | async-start | bytes 4194304 | tf_op jit(solution)/shard_map/all_to_all | solution.py:752
  167.0 2.4 collective-permute-start.9
  169.5 9.7 %carried_step.1.first.refs_7_ = f32[2,10,272,128]{3,2,1,0:T(8,128)} custom-call(f32[8,2,2,32,128]{4,3,2,1,0:T(8,128)} %copy-done.7, f32[8,2,8,32,128]{4,3,2,1,0:T(8,128)} %copy-done, f32[8,2,2,32,128]{4,3,2,1,0:T(8,128)} %copy-done.8, f32[8,2,2,32,128]{4,3,2,1,0:T(8,128)} %copy-done.4, f32[8,2,8,32,128]{4,3,2,1,0:T(8,128)} %after.3.main.refs_4_, ...), custom_call_target="tpu_custom_call" | custom-call | flops 1006632960 | bytes 12058624 | tf_op jit(solution)/shard_map/carried_step/pallas_call | solution.py:42
  179.2 30.6 %collective-permute-done.9.refs_4_ = f32[8,2,7,32,128]{4,3,2,1,0:T(8,128)S(1)} collective-permute-done((f32[8,2,7,32,128]{4,3,2,1,0:T(8,128)}, f32[8,2,7,32,128]{4,3,2,1,0:T(8,128)S(1)}, u32[]{:S(2)}, u32[]{:S(2)}) %collective-permute-start.9) | collective-permute-done | bytes 1835040 | tf_op jit(solution)/shard_map/ppermute | solution.py:757
  211.1 9.6 %second_step.3 = (f32[8,2,8,32,128]{4,3,2,1,0:T(8,128)}, f32[2,256,128]{2,1,0:T(8,128)}, f32[2,256,128]{2,1,0:T(8,128)}) custom-call(f32[2,10,272,128]{3,2,1,0:T(8,128)} %carried_step.1.first.refs_7_, f32[2,10,272,128]{3,2,1,0:T(8,128)} %first_step.1.first.with_w.refs_6_, f32[12,256,128]{2,1,0:T(8,128)} %to_frame.1.refs_1_.refs_2_.refs_0_.refs_7_.refs_8_, ...), custom_call_target="tpu_custom_call" | custom-call | flops 805306368 | bytes 13434880 | tf_op jit(solution)/shard_map/second_step/pallas_call | solution.py:42
  226.5 6.3 %collective-permute-done.13.refs_4_.refs_5_ = f32[2,256,128]{2,1,0:T(8,128)S(1)} collective-permute-done((f32[2,256,128]{2,1,0:T(8,128)}, f32[2,256,128]{2,1,0:T(8,128)S(1)}, u32[]{:S(2)}, u32[]{:S(2)}) %collective-permute-start.13) | collective-permute-done | bytes 262176 | tf_op jit(solution)/shard_map/ppermute | solution.py:757
  232.8 3.3 collective-permute-done.12.refs_3_.refs_4_
  237.5 4.5 %all-to-all-start.3 = ((f32[8,2,8,32,128]{4,3,2,1,0:T(8,128)}), f32[8,2,8,32,128]{4,3,2,1,0:T(8,128)}, u32[]{:S(2)}, u32[]{:S(2)}) async-start(f32[8,2,8,32,128]{4,3,2,1,0:T(8,128)} %after.5.refs_1_), calls=%async_computation.3 | async-start | bytes 4194304 | tf_op jit(solution)/shard_map/all_to_all | solution.py:752
  241.9 17.4 %adjoint_step.1._ = f32[8,34,32,128]{3,2,1,0:T(8,128)} custom-call(f32[8,2,8,32,128]{4,3,2,1,0:T(8,128)} %after.4.refs_6_.refs_5_.refs_0_, f32[8,2,8,32,128]{4,3,2,1,0:T(8,128)} %after.5.refs_1_, f32[2,256,128]{2,1,0:T(8,128)} %copy-done.12, f32[2,256,128]{2,1,0:T(8,128)} %copy-done.10, f32[2,256,128]{2,1,0:T(8,128)} %copy-done.13, ...), custom_call_target="tpu_custom_call" | custom-call | flops 3623878656 | bytes 14483456 | tf_op jit(solution)/shard_map/adjoint_step/pallas_call | solution.py:42
  259.4 28.1 %all-to-all-done.3.other = f32[8,2,8,32,128]{4,3,2,1,0:T(8,128)} async-done(((f32[8,2,8,32,128]{4,3,2,1,0:T(8,128)}), f32[8,2,8,32,128]{4,3,2,1,0:T(8,128)}, u32[]{:S(2)}, u32[]{:S(2)}) %all-to-all-start.3) | async-done | bytes 2097184 | tf_op jit(solution)/shard_map/all_to_all | solution.py:752
  287.5 7.8 %all-to-all-start.4 = ((f32[8,34,32,128]{3,2,1,0:T(8,128)}), f32[8,34,32,128]{3,2,1,0:T(8,128)}, u32[]{:S(2)}, u32[]{:S(2)}) async-start(f32[8,34,32,128]{3,2,1,0:T(8,128)} %adjoint_step.1._), calls=%async_computation.4 | async-start | bytes 8912896 | tf_op jit(solution)/shard_map/all_to_all | solution.py:752
  297.7 8.6 %to_planes.1 = (f32[8192,128]{1,0:T(8,128)}, f32[8,2,8,32,128]{4,3,2,1,0:T(8,128)}) custom-call(f32[8,2,8,32,128]{4,3,2,1,0:T(8,128)} %copy-done.1, f32[8,2,8,32,128]{4,3,2,1,0:T(8,128)} %all-to-all-done.3.other, f32[8,34,32,128]{3,2,1,0:T(8,128)} %adjoint_step.1._), custom_call_target="tpu_custom_call" | custom-call | bytes 8650752 | tf_op jit(solution)/shard_map/to_planes/pallas_call | solution.py:42
  306.5 2.5 collective-permute-start.15
  309.0 3.0 collective-permute-start.14
  312.0 82.5 %collective-permute-done.15.refs_2_ = f32[4,64,128]{2,1,0:T(8,128)S(1)} collective-permute-done((f32[4,64,128]{2,1,0:T(8,128)S(1)}, f32[4,64,128]{2,1,0:T(8,128)S(1)}, u32[]{:S(2)}, u32[]{:S(2)}) %collective-permute-start.15) | collective-permute-done | bytes 131104 | tf_op jit(solution)/shard_map/ppermute | solution.py:775
  396.0 14.8 %last_step.1 = f32[4,2048,128]{2,1,0:T(8,128)} custom-call(f32[8,8,32,128]{3,2,1,0:T(8,128)} %bitcast.13, f32[4,64,128]{2,1,0:T(8,128)} %copy-done.20, f32[4,64,128]{2,1,0:T(8,128)} %copy-done.19, f32[8,34,32,128]{3,2,1,0:T(8,128)} %all-to-all-done.4.refs_3_, f32[8,19,32,128]{3,2,1,0:T(8,128)} %get-tuple-element.26.refs_4_, ...), custom_call_target="tpu_custom_call" | custom-call | flops 31457280 | bytes 14548992 | tf_op jit(solution)/shard_map/last_step/pallas_call | solution.py:42
  (78 shorter events, 28.5 us)
Async XLA Ops:
  5.7 59.6 %all-to-all-start = ((f32[8,19,32,128]{3,2,1,0:T(8,128)}), f32[8,19,32,128]{3,2,1,0:T(8,128)S(1)}, u32[]{:S(2)}, u32[]{:S(2)}) async-start(f32[8,19,32,128]{3,2,1,0:T(8,128)} %get-tuple-element.26.refs_4_), calls=%async_computation | async-start | bytes 4980736 | tf_op jit(solution)/shard_map/all_to_all | solution.py:752
  66.7 58.2 %all-to-all-start.1 = ((f32[8,2,8,32,128]{4,3,2,1,0:T(8,128)}), f32[8,2,8,32,128]{4,3,2,1,0:T(8,128)S(1)}, u32[]{:S(2)}, u32[]{:S(2)}) async-start(f32[8,2,8,32,128]{4,3,2,1,0:T(8,128)} %get-tuple-element.28._.refs_5_), calls=%async_computation.1 | async-start | bytes 4194304 | tf_op jit(solution)/shard_map/all_to_all | solution.py:752
  77.7 11.5 %collective-permute-start.3 = (f32[8,3,32,128]{3,2,1,0:T(8,128)}, f32[8,3,32,128]{3,2,1,0:T(8,128)S(1)}, u32[]{:S(2)}, u32[]{:S(2)}) collective-permute-start(f32[8,3,32,128]{3,2,1,0:T(8,128)} %get-tuple-element.31.refs_0_), channel_id=1, source_target_pairs={{0,8},{8,16},{16,24},{24,0},{1,9},{9,17},{17,25},{25,1},{2,10},{10... | collective-permute-start | bytes 1179656 | tf_op jit(solution)/shard_map/ppermute | solution.py:757
  78.9 19.4 %collective-permute-start.2 = (f32[8,3,32,128]{3,2,1,0:T(8,128)}, f32[8,3,32,128]{3,2,1,0:T(8,128)S(1)}, u32[]{:S(2)}, u32[]{:S(2)}) collective-permute-start(f32[8,3,32,128]{3,2,1,0:T(8,128)} %get-tuple-element.31.refs_0_), channel_id=1, source_target_pairs={{0,16},{8,24},{16,0},{24,8},{1,17},{9,25},{17,1},{25,9},{2,18},{10... | collective-permute-start | bytes 1179656 | tf_op jit(solution)/shard_map/ppermute | solution.py:757
  80.2 18.1 %collective-permute-start.1 = (f32[8,3,32,128]{3,2,1,0:T(8,128)}, f32[8,3,32,128]{3,2,1,0:T(8,128)S(1)}, u32[]{:S(2)}, u32[]{:S(2)}) collective-permute-start(f32[8,3,32,128]{3,2,1,0:T(8,128)} %get-tuple-element.31.refs_0_), channel_id=1, source_target_pairs={{0,24},{8,0},{16,8},{24,16},{1,25},{9,1},{17,9},{25,17},{2,26},{10... | collective-permute-start | bytes 1179656 | tf_op jit(solution)/shard_map/ppermute | solution.py:757
  89.2 9.1 %copy-start.15 = (f32[8,3,32,128]{3,2,1,0:T(8,128)}, f32[8,3,32,128]{3,2,1,0:T(8,128)S(1)}, u32[]{:S(2)}) copy-start(f32[8,3,32,128]{3,2,1,0:T(8,128)S(1)} %collective-permute-done.3.refs_3_) | copy-start | bytes 1179652
  102.6 48.5 %collective-permute-start.5 = (f32[8,2,8,32,128]{4,3,2,1,0:T(8,128)}, f32[8,2,8,32,128]{4,3,2,1,0:T(8,128)}, u32[]{:S(2)}, u32[]{:S(2)}) collective-permute-start(f32[8,2,8,32,128]{4,3,2,1,0:T(8,128)} %after.3.main.refs_4_), channel_id=1, source_target_pairs={{0,24},{8,0},{16,8},{24,16},{1,25},{9,1},{17,9},{25,17},{2,26},{10... | collective-permute-start | bytes 6291464 | tf_op jit(solution)/shard_map/ppermute | solution.py:757
  102.7 27.9 %collective-permute-start = (f32[8,2,2,32,128]{4,3,2,1,0:T(8,128)}, f32[8,2,2,32,128]{4,3,2,1,0:T(8,128)S(1)}, u32[]{:S(2)}, u32[]{:S(2)}) collective-permute-start(f32[8,2,2,32,128]{4,3,2,1,0:T(8,128)} %get-tuple-element.29), channel_id=1, source_target_pairs={{0,1},{1,2},{2,3},{3,4},{4,5},{5,6},{6,7},{7,0},{8,9},{9,10},{10,1... | collective-permute-start | bytes 1572872 | tf_op jit(solution)/shard_map/ppermute | solution.py:757
  106.0 26.8 %collective-permute-start.4 = (f32[8,2,2,32,128]{4,3,2,1,0:T(8,128)}, f32[8,2,2,32,128]{4,3,2,1,0:T(8,128)S(1)}, u32[]{:S(2)}, u32[]{:S(2)}) collective-permute-start(f32[8,2,2,32,128]{4,3,2,1,0:T(8,128)} %get-tuple-element.32), channel_id=1, source_target_pairs={{0,7},{1,0},{2,1},{3,2},{4,3},{5,4},{6,5},{7,6},{8,15},{9,8},{10,9... | collective-permute-start | bytes 1572872 | tf_op jit(solution)/shard_map/ppermute | solution.py:757
  124.9 7.8 %copy-start = (f32[8,2,8,32,128]{4,3,2,1,0:T(8,128)}, f32[8,2,8,32,128]{4,3,2,1,0:T(8,128)S(1)}, u32[]{:S(2)}) copy-start(f32[8,2,8,32,128]{4,3,2,1,0:T(8,128)S(1)} %all-to-all-done.1.chunks.refs_1_) | copy-start | bytes 6291460
  135.8 24.6 %collective-permute-start.6 = (f32[8,2,2,32,128]{4,3,2,1,0:T(8,128)}, f32[8,2,2,32,128]{4,3,2,1,0:T(8,128)S(1)}, u32[]{:S(2)}, u32[]{:S(2)}) collective-permute-start(f32[8,2,2,32,128]{4,3,2,1,0:T(8,128)} %get-tuple-element.37), channel_id=1, source_target_pairs={{0,1},{1,2},{2,3},{3,4},{4,5},{5,6},{6,7},{7,0},{8,9},{9,10},{10,1... | collective-permute-start | bytes 1572872 | tf_op jit(solution)/shard_map/ppermute | solution.py:757
  136.9 23.6 %collective-permute-start.7 = (f32[8,2,2,32,128]{4,3,2,1,0:T(8,128)}, f32[8,2,2,32,128]{4,3,2,1,0:T(8,128)S(1)}, u32[]{:S(2)}, u32[]{:S(2)}) collective-permute-start(f32[8,2,2,32,128]{4,3,2,1,0:T(8,128)} %get-tuple-element.33._), channel_id=1, source_target_pairs={{0,7},{1,0},{2,1},{3,2},{4,3},{5,4},{6,5},{7,6},{8,15},{9,8},{10,9... | collective-permute-start | bytes 1572872 | tf_op jit(solution)/shard_map/ppermute | solution.py:757
  139.8 20.6 %collective-permute-start.8 = (f32[8,2,1,32,128]{4,3,2,1,0:T(8,128)}, f32[8,2,1,32,128]{4,3,2,1,0:T(8,128)S(1)}, u32[]{:S(2)}, u32[]{:S(2)}) collective-permute-start(f32[8,2,1,32,128]{4,3,2,1,0:T(8,128)} %get-tuple-element.34._), channel_id=1, source_target_pairs={{0,24},{8,0},{16,8},{24,16},{1,25},{9,1},{17,9},{25,17},{2,26},{10... | collective-permute-start | bytes 786440 | tf_op jit(solution)/shard_map/ppermute | solution.py:757
  161.5 74.6 %all-to-all-start.2 = ((f32[8,2,8,32,128]{4,3,2,1,0:T(8,128)}), f32[8,2,8,32,128]{4,3,2,1,0:T(8,128)S(1)}, u32[]{:S(2)}, u32[]{:S(2)}) async-start(f32[8,2,8,32,128]{4,3,2,1,0:T(8,128)} %after.4.refs_6_.refs_5_.refs_0_), calls=%async_computation.2 | async-start | bytes 4194304 | tf_op jit(solution)/shard_map/all_to_all | solution.py:752
  167.0 42.8 %collective-permute-start.9 = (f32[8,2,7,32,128]{4,3,2,1,0:T(8,128)}, f32[8,2,7,32,128]{4,3,2,1,0:T(8,128)S(1)}, u32[]{:S(2)}, u32[]{:S(2)}) collective-permute-start(f32[8,2,7,32,128]{4,3,2,1,0:T(8,128)} %get-tuple-element.38), channel_id=1, source_target_pairs={{0,24},{8,0},{16,8},{24,16},{1,25},{9,1},{17,9},{25,17},{2,26},{10... | collective-permute-start | bytes 5505032 | tf_op jit(solution)/shard_map/ppermute | solution.py:757
  179.2 43.5 %copy-start.22 = (f32[2,256,128]{2,1,0:T(8,128)S(1)}, f32[2,256,128]{2,1,0:T(8,128)}, u32[]{:S(2)}) copy-start(f32[2,256,128]{2,1,0:T(8,128)} %get-tuple-element.40) | copy-start | bytes 786436
  179.2 45.2 %copy-start.21 = (f32[2,256,128]{2,1,0:T(8,128)S(1)}, f32[2,256,128]{2,1,0:T(8,128)}, u32[]{:S(2)}) copy-start(f32[2,256,128]{2,1,0:T(8,128)} %get-tuple-element.42) | copy-start | bytes 786436
  220.7 5.8 %collective-permute-start.11 = (f32[2,256,128]{2,1,0:T(8,128)}, f32[2,256,128]{2,1,0:T(8,128)S(1)}, u32[]{:S(2)}, u32[]{:S(2)}) collective-permute-start(f32[2,256,128]{2,1,0:T(8,128)} %get-tuple-element.41), channel_id=1, source_target_pairs={{0,1},{1,2},{2,3},{3,4},{4,5},{5,6},{6,7},{7,0},{8,9},{9,10},{10,1... | collective-permute-start | bytes 786440 | tf_op jit(solution)/shard_map/ppermute | solution.py:757
  222.7 10.1 %collective-permute-start.13 = (f32[2,256,128]{2,1,0:T(8,128)}, f32[2,256,128]{2,1,0:T(8,128)S(1)}, u32[]{:S(2)}, u32[]{:S(2)}) collective-permute-start(f32[2,256,128]{2,1,0:T(8,128)} %get-tuple-element.43), channel_id=1, source_target_pairs={{0,7},{1,0},{2,1},{3,2},{4,3},{5,4},{6,5},{7,6},{8,15},{9,8},{10,9... | collective-permute-start | bytes 786440 | tf_op jit(solution)/shard_map/ppermute | solution.py:757
  222.7 10.1 %collective-permute-start.10 = (f32[2,256,128]{2,1,0:T(8,128)S(1)}, f32[2,256,128]{2,1,0:T(8,128)S(1)}, u32[]{:S(2)}, u32[]{:S(2)}) collective-permute-start(f32[2,256,128]{2,1,0:T(8,128)S(1)} %copy-done.22), channel_id=1, source_target_pairs={{0,1},{1,2},{2,3},{3,4},{4,5},{5,6},{6,7},{7,0},{8,9},{9,10},{10,1... | collective-permute-start | bytes 786440 | tf_op jit(solution)/shard_map/ppermute | solution.py:757
  224.4 11.6 %collective-permute-start.12 = (f32[2,256,128]{2,1,0:T(8,128)S(1)}, f32[2,256,128]{2,1,0:T(8,128)S(1)}, u32[]{:S(2)}, u32[]{:S(2)}) collective-permute-start(f32[2,256,128]{2,1,0:T(8,128)S(1)} %copy-done.21), channel_id=1, source_target_pairs={{0,7},{1,0},{2,1},{3,2},{4,3},{5,4},{6,5},{7,6},{8,15},{9,8},{10,9... | collective-permute-start | bytes 786440 | tf_op jit(solution)/shard_map/ppermute | solution.py:757
  226.5 9.6 %copy-start.10 = (f32[2,256,128]{2,1,0:T(8,128)}, f32[2,256,128]{2,1,0:T(8,128)S(1)}, u32[]{:S(2)}) copy-start(f32[2,256,128]{2,1,0:T(8,128)S(1)} %collective-permute-done.11.refs_2_.refs_3_) | copy-start | bytes 786436
  232.8 3.3 copy-start.11
  232.8 3.3 copy-start.12
  237.5 50.0 %all-to-all-start.3 = ((f32[8,2,8,32,128]{4,3,2,1,0:T(8,128)}), f32[8,2,8,32,128]{4,3,2,1,0:T(8,128)}, u32[]{:S(2)}, u32[]{:S(2)}) async-start(f32[8,2,8,32,128]{4,3,2,1,0:T(8,128)} %after.5.refs_1_), calls=%async_computation.3 | async-start | bytes 4194304 | tf_op jit(solution)/shard_map/all_to_all | solution.py:752
  259.4 35.9 %copy-start.2 = (f32[8,2,8,32,128]{4,3,2,1,0:T(8,128)S(1)}, f32[8,2,8,32,128]{4,3,2,1,0:T(8,128)}, u32[]{:S(2)}) copy-start(f32[8,2,8,32,128]{4,3,2,1,0:T(8,128)} %copy-done.1) | copy-start | bytes 6291460
  287.5 108.4 %all-to-all-start.4 = ((f32[8,34,32,128]{3,2,1,0:T(8,128)}), f32[8,34,32,128]{3,2,1,0:T(8,128)}, u32[]{:S(2)}, u32[]{:S(2)}) async-start(f32[8,34,32,128]{3,2,1,0:T(8,128)} %adjoint_step.1._), calls=%async_computation.4 | async-start | bytes 8912896 | tf_op jit(solution)/shard_map/all_to_all | solution.py:752
  295.3 11.2 %copy-start.18 = (f32[2,4,64,128]{3,2,1,0:T(8,128)S(1)}, f32[2,4,64,128]{3,2,1,0:T(8,128)}, u32[]{:S(2)}) copy-start(f32[2,4,64,128]{3,2,1,0:T(8,128)} %get-tuple-element.48) | copy-start | bytes 786436
  295.3 99.3 %collective-permute-start.16 = (f32[8,2,8,32,128]{4,3,2,1,0:T(8,128)S(1)}, f32[8,2,8,32,128]{4,3,2,1,0:T(8,128)S(1)}, u32[]{:S(2)}, u32[]{:S(2)}) collective-permute-start(f32[8,2,8,32,128]{4,3,2,1,0:T(8,128)S(1)} %copy-done.2), channel_id=1, source_target_pairs={{0,8},{8,16},{16,24},{24,0},{1,9},{9,17},{17,25},{25,1},{2,10},{10... | collective-permute-start | bytes 6291464 | tf_op jit(solution)/shard_map/ppermute | solution.py:757
  306.3 89.6 %collective-permute-start.17 = (f32[8,2,8,32,128]{4,3,2,1,0:T(8,128)}, f32[8,2,8,32,128]{4,3,2,1,0:T(8,128)}, u32[]{:S(2)}, u32[]{:S(2)}) collective-permute-start(f32[8,2,8,32,128]{4,3,2,1,0:T(8,128)} %get-tuple-element.49), channel_id=1, source_target_pairs={{0,8},{8,16},{16,24},{24,0},{1,9},{9,17},{17,25},{25,1},{2,10},{10... | collective-permute-start | bytes 6291464 | tf_op jit(solution)/shard_map/ppermute | solution.py:757
  306.5 88.1 %collective-permute-start.15 = (f32[4,64,128]{2,1,0:T(8,128)S(1)}, f32[4,64,128]{2,1,0:T(8,128)S(1)}, u32[]{:S(2)}, u32[]{:S(2)}) collective-permute-start(f32[4,64,128]{2,1,0:T(8,128)S(1)} %get-tuple-element.50), channel_id=1, source_target_pairs={{1,0},{2,1},{3,2},{4,3},{5,4},{6,5},{7,6},{9,8},{10,9},{11,10},{12... | collective-permute-start | bytes 393224 | tf_op jit(solution)/shard_map/ppermute | solution.py:775
  309.0 85.5 %collective-permute-start.14 = (f32[4,64,128]{2,1,0:T(8,128)S(1)}, f32[4,64,128]{2,1,0:T(8,128)S(1)}, u32[]{:S(2)}, u32[]{:S(2)}) collective-permute-start(f32[4,64,128]{2,1,0:T(8,128)S(1)} %get-tuple-element.51), channel_id=1, source_target_pairs={{0,1},{1,2},{2,3},{3,4},{4,5},{5,6},{6,7},{8,9},{9,10},{10,11},{11... | collective-permute-start | bytes 393224 | tf_op jit(solution)/shard_map/ppermute | solution.py:774
  (14 other events, 16.1 us)

commit v11 on v10

--- a/solution.py
+++ b/solution.py
@@ -1,4 +1,5 @@
 import functools
+import math
 
 import jax
 import jax.numpy as jnp
@@ -8,7 +9,7 @@
 from jax.sharding import PartitionSpec as P
 
 time_step = 0.1
-vmem_bytes = 56 * 1024 * 1024
+mebibyte = 1024 * 1024
 f32, bf16 = jnp.float32, jnp.bfloat16
 fields = 4
 W, T, U, V = range(4)
@@ -39,6 +40,11 @@
 
 def call(kernel, ins, outs, scratch, flops, name, kind=f32, aliases=None):
     moved = sum(4 * x.size for x, _ in ins)
+    held = [(x.shape, x.dtype) for x, spec in ins if spec.memory_space == pltpu.VMEM]
+    held += [(shape, kind) for shape, spec in outs if spec.memory_space == pltpu.VMEM]
+    held += [(x.shape, x.dtype) for x in scratch if x.memory_space == pltpu.VMEM]
+    needed = sum(math.prod(shape) * jnp.dtype(dtype).itemsize for shape, dtype in held)
+    limit = min(56 * mebibyte, 6 * mebibyte + needed * 9 // 8)
     return pl.pallas_call(
         kernel,
         in_specs=[spec for _, spec in ins],
@@ -46,7 +52,7 @@
         out_shape=tuple(jax.ShapeDtypeStruct(shape, kind) for shape, _ in outs),
         scratch_shapes=scratch,
         input_output_aliases=aliases or {},
-        compiler_params=pltpu.CompilerParams(vmem_limit_bytes=vmem_bytes),
+        compiler_params=pltpu.CompilerParams(vmem_limit_bytes=limit),
         cost_estimate=pl.CostEstimate(flops=flops, bytes_accessed=moved, transcendentals=0),
         name=name,
     )(*[x for x, _ in ins])
@@ -782,16 +788,15 @@
     half_rows = (low_in, main_half, high_in)
     target = around(main_half, "seg", -1)
 
-    sizes, few = (2, 2), max(1, block // 8)
+    sizes, few = (2, 2), max(1, block // 4)
     low_rows, high_rows = row_parts(
         outer_kernel, main_other, (low_in, high_in, frame), sizes, "outer_rows"
     )
     other_rows = (around(high_rows, "slab", 1), main_other, around(low_rows, "slab", -1))
+    mats = mat_high, mat_low
     sizes = (few, block - few)
     parts = row_parts(pieces_kernel, main_other, (low_rows,), sizes, "pieces")
     targets = [around(part, "seg", -1) for part in parts]
-
-    mats = mat_high, mat_low
     first_half = first_step(*half_rows, parts[0], frame, *mats)
     out, low_edge, high_edge = second_step(
         first_half, first_half, frame, *mats, W, (target,), ()

time: 413 us -> 414 us (level)
  local copies, waits for them, and re-layouts: 8.86 us -> 47.5 us
  Pallas kernels: 102 us -> 70.9 us
  waiting for transfers between devices: 243 us -> 237 us
    unnamed x46 -> x90, local copies, waits for them, and re-layouts: 8.84 us -> 47.5 us
    pallas_call x17, Pallas kernels: 102 us -> 70.9 us  [call(): pl.pallas_call(kernel, in_specs=[spec for _, spec in ins], out_specs=tupl...]
  transfers between devices with their start and end apart: 23 -> 23, of which waited for: 12 -> 14; matrix products, arithmetic and copies ran while one was open for 0% -> 0% of each run, Pallas kernels for 20% -> 14%
where the time goes in v11:
time: 414 us; the launch traced here: 412 us
  waiting for transfers between devices  237 us (57%)
  Pallas kernels  70.9 us (17%)
  starting transfers between devices  55.3 us (13%)
  local copies, waits for them, and re-layouts  47.5 us (11%)
    all_to_all x5, waiting for transfers between devices, exchange(): lax.all_to_all(chunks, 'slab', split_axis=0, concat_axis=0, tiled=True)  92.4 us
    ppermute x1, waiting for transfers between devices, local(): above = lax.ppermute(ends[0], 'slab', [(i, j) for j, i in forward])  79.8 us
    pallas_call x17, Pallas kernels, call(): pl.pallas_call(kernel, in_specs=[spec for _, spec in ins], out_specs=tupl...  70.9 us
    ppermute x16, waiting for transfers between devices, around(): lax.ppermute(value, axis, [(i, (i + steps) % count) for i in range(count)])  64.6 us
    unnamed x90, local copies, waits for them, and re-layouts  47.5 us
    all_to_all x5, starting transfers between devices, exchange(): lax.all_to_all(chunks, 'slab', split_axis=0, concat_axis=0, tiled=True)  32.1 us
    ppermute x16, starting transfers between devices, around(): lax.ppermute(value, axis, [(i, (i + steps) % count) for i in range(count)])  17.4 us
  transfers between devices with their start and end apart: 23, of which 14 were waited for; matrix products, arithmetic and copies ran while one was open for 0% of the time, Pallas kernels for 14%

profile of v11, /device:TPU:9, one launch (start us, length us, event | category | flops | bytes accessed | tf_op | source)
XLA Modules:
  0.0 411.7 jit_solution(5710204914044736533)
XLA Ops:
  0.6 2.2 copy-done.18
  4.0 2.3 to_first_chunks.1
  8.8 5.8 %all-to-all-start = ((f32[8,19,32,128]{3,2,1,0:T(8,128)}), f32[8,19,32,128]{3,2,1,0:T(8,128)}, u32[]{:S(2)}, u32[]{:S(2)}) async-start(f32[8,19,32,128]{3,2,1,0:T(8,128)} %copy-done.20), calls=%async_computation | async-start | bytes 4980736 | tf_op jit(solution)/shard_map/all_to_all | solution.py:758
  15.9 2.4 copy-done.19
  21.3 47.2 %all-to-all-done.chunks = f32[8,19,32,128]{3,2,1,0:T(8,128)} async-done(((f32[8,19,32,128]{3,2,1,0:T(8,128)}), f32[8,19,32,128]{3,2,1,0:T(8,128)}, u32[]{:S(2)}, u32[]{:S(2)}) %all-to-all-start) | async-done | bytes 2490400 | tf_op jit(solution)/shard_map/all_to_all | solution.py:758
  68.5 7.9 %all-to-all-start.1 = ((f32[8,2,8,32,128]{4,3,2,1,0:T(8,128)}), f32[8,2,8,32,128]{4,3,2,1,0:T(8,128)}, u32[]{:S(2)}, u32[]{:S(2)}) async-start(f32[8,2,8,32,128]{4,3,2,1,0:T(8,128)} %copy-done.15), calls=%async_computation.1 | async-start | bytes 4194304 | tf_op jit(solution)/shard_map/all_to_all | solution.py:758
  78.1 3.7 unpack.1
  85.4 7.7 %collective-permute-done.3.refs_3_ = f32[8,3,32,128]{3,2,1,0:T(8,128)S(1)} collective-permute-done((f32[8,3,32,128]{3,2,1,0:T(8,128)S(1)}, f32[8,3,32,128]{3,2,1,0:T(8,128)S(1)}, u32[]{:S(2)}, u32[]{:S(2)}) %collective-permute-start.3) | collective-permute-done | bytes 393248 | tf_op jit(solution)/shard_map/ppermute | solution.py:763
  93.1 9.2 %collective-permute-done.2.refs_2_ = f32[8,3,32,128]{3,2,1,0:T(8,128)S(1)} collective-permute-done((f32[8,3,32,128]{3,2,1,0:T(8,128)S(1)}, f32[8,3,32,128]{3,2,1,0:T(8,128)S(1)}, u32[]{:S(2)}, u32[]{:S(2)}) %collective-permute-start.2) | collective-permute-done | bytes 393248 | tf_op jit(solution)/shard_map/ppermute | solution.py:763
  103.8 2.8 collective-permute-start
  106.6 20.9 %all-to-all-done.1.chunks.refs_1_ = f32[8,2,8,32,128]{4,3,2,1,0:T(8,128)} async-done(((f32[8,2,8,32,128]{4,3,2,1,0:T(8,128)}), f32[8,2,8,32,128]{4,3,2,1,0:T(8,128)}, u32[]{:S(2)}, u32[]{:S(2)}) %all-to-all-start.1) | async-done | bytes 2097184 | tf_op jit(solution)/shard_map/all_to_all | solution.py:758
  127.6 5.7 %collective-permute-done.refs_0_.low_in.refs_3_ = f32[8,2,2,32,128]{4,3,2,1,0:T(8,128)S(1)} collective-permute-done((f32[8,2,2,32,128]{4,3,2,1,0:T(8,128)}, f32[8,2,2,32,128]{4,3,2,1,0:T(8,128)S(1)}, u32[]{:S(2)}, u32[]{:S(2)}) %collective-permute-start) | collective-permute-done | bytes 524320 | tf_op jit(solution)/shard_map/ppermute | solution.py:763
  142.1 7.0 %first_step.1.first.with_w.refs_6_ = f32[2,10,272,128]{3,2,1,0:T(8,128)S(1)} custom-call(f32[8,2,2,32,128]{4,3,2,1,0:T(8,128)S(1)} %collective-permute-done.refs_0_.low_in.refs_3_, f32[8,2,8,32,128]{4,3,2,1,0:T(8,128)} %after.3.main.refs_4_, f32[8,2,2,32,128]{4,3,2,1,0:T(8,128)} %collective-permute-done.4.refs_1_.high_in.refs_5_, ...), custom_call_target="tpu_custom_call" | custom-call | flops 1006632960 | bytes 7340032 | tf_op jit(solution)/shard_map/first_step/pallas_call | solution.py:48
  150.4 6.3 %second_step.2 = (f32[8,2,8,32,128]{4,3,2,1,0:T(8,128)S(1)}, f32[2,256,128]{2,1,0:T(8,128)S(1)}, f32[2,256,128]{2,1,0:T(8,128)S(1)}) custom-call(f32[2,10,272,128]{3,2,1,0:T(8,128)S(1)} %first_step.1.first.with_w.refs_6_, f32[2,10,272,128]{3,2,1,0:T(8,128)S(1)} %first_step.1.first.with_w.refs_6_, ...), custom_call_target="tpu_custom_call" | custom-call | flops 805306368 | bytes 11337728 | tf_op jit(solution)/shard_map/second_step/pallas_call | solution.py:48
  158.2 3.4 collective-permute-done.8.refs_3_
  165.3 6.1 %all-to-all-start.2 = ((f32[8,2,8,32,128]{4,3,2,1,0:T(8,128)}), f32[8,2,8,32,128]{4,3,2,1,0:T(8,128)}, u32[]{:S(2)}, u32[]{:S(2)}) async-start(f32[8,2,8,32,128]{4,3,2,1,0:T(8,128)} %copy-done.3), calls=%async_computation.2 | async-start | bytes 4194304 | tf_op jit(solution)/shard_map/all_to_all | solution.py:758
  176.4 7.6 %carried_step.1.first.refs_7_ = f32[2,10,272,128]{3,2,1,0:T(8,128)S(1)} custom-call(f32[8,2,2,32,128]{4,3,2,1,0:T(8,128)S(1)} %copy-done.29, f32[8,2,8,32,128]{4,3,2,1,0:T(8,128)} %all-to-all-done.1.chunks.refs_1_, f32[8,2,2,32,128]{4,3,2,1,0:T(8,128)S(1)} %copy-done.31, f32[8,2,2,32,128]{4,3,2,1,0:T(8,128)S(1)} %collective-permute-done.refs_0_.low_in.refs_3_, ...), custom_call_target="tpu_custom_call" | custom-call | flops 1006632960 | bytes 12058624 | tf_op jit(solution)/shard_map/carried_step/pallas_call | solution.py:48
  184.0 23.3 %collective-permute-done.9.refs_4_ = f32[8,2,6,32,128]{4,3,2,1,0:T(8,128)S(1)} collective-permute-done((f32[8,2,6,32,128]{4,3,2,1,0:T(8,128)}, f32[8,2,6,32,128]{4,3,2,1,0:T(8,128)S(1)}, u32[]{:S(2)}, u32[]{:S(2)}) %collective-permute-start.9) | collective-permute-done | bytes 1572896 | tf_op jit(solution)/shard_map/ppermute | solution.py:763
  207.3 5.4 %second_step.3 = (f32[8,2,8,32,128]{4,3,2,1,0:T(8,128)S(1)}, f32[2,256,128]{2,1,0:T(8,128)S(1)}, f32[2,256,128]{2,1,0:T(8,128)S(1)}) custom-call(f32[2,10,272,128]{3,2,1,0:T(8,128)S(1)} %carried_step.1.first.refs_7_, f32[2,10,272,128]{3,2,1,0:T(8,128)S(1)} %copy-done.1, f32[12,256,128]{2,1,0:T(8,128)S(1)} %to_frame.1.refs_1_.refs_2_.refs_0_.refs_7_.refs_8_, ...), custom_call_target="tpu_custom_call" | custom-call | flops 805306368 | bytes 13434880 | tf_op jit(solution)/shard_map/second_step/pallas_call | solution.py:48
  219.9 6.9 %collective-permute-done.13.refs_4_.refs_5_ = f32[2,256,128]{2,1,0:T(8,128)S(1)} collective-permute-done((f32[2,256,128]{2,1,0:T(8,128)S(1)}, f32[2,256,128]{2,1,0:T(8,128)S(1)}, u32[]{:S(2)}, u32[]{:S(2)}) %collective-permute-start.13) | collective-permute-done | bytes 262176 | tf_op jit(solution)/shard_map/ppermute | solution.py:763
  226.8 3.2 collective-permute-done.12.refs_3_.refs_4_
  232.9 4.6 %all-to-all-start.3 = ((f32[8,2,8,32,128]{4,3,2,1,0:T(8,128)}), f32[8,2,8,32,128]{4,3,2,1,0:T(8,128)}, u32[]{:S(2)}, u32[]{:S(2)}) async-start(f32[8,2,8,32,128]{4,3,2,1,0:T(8,128)} %copy-done.13), calls=%async_computation.3 | async-start | bytes 4194304 | tf_op jit(solution)/shard_map/all_to_all | solution.py:758
  245.3 11.0 %adjoint_step.1._ = f32[8,34,32,128]{3,2,1,0:T(8,128)S(1)} custom-call(f32[8,2,8,32,128]{4,3,2,1,0:T(8,128)S(1)} %copy-done.6, f32[8,2,8,32,128]{4,3,2,1,0:T(8,128)S(1)} %copy-done.14, f32[2,256,128]{2,1,0:T(8,128)S(1)} %collective-permute-done.10.refs_1_.refs_2_, f32[2,256,128]{2,1,0:T(8,128)S(1)} %collective-permute-done.11.refs_2_.refs_3_, ...), custom_call_target="tpu_custom_call" | custom-call | flops 3623878656 | bytes 14483456 | tf_op jit(solution)/shard_map/adjoint_step/pallas_call | solution.py:48
  258.5 24.2 %all-to-all-done.3.other = f32[8,2,8,32,128]{4,3,2,1,0:T(8,128)} async-done(((f32[8,2,8,32,128]{4,3,2,1,0:T(8,128)}), f32[8,2,8,32,128]{4,3,2,1,0:T(8,128)}, u32[]{:S(2)}, u32[]{:S(2)}) %all-to-all-start.3) | async-done | bytes 2097184 | tf_op jit(solution)/shard_map/all_to_all | solution.py:758
  282.6 7.8 %all-to-all-start.4 = ((f32[8,34,32,128]{3,2,1,0:T(8,128)}), f32[8,34,32,128]{3,2,1,0:T(8,128)}, u32[]{:S(2)}, u32[]{:S(2)}) async-start(f32[8,34,32,128]{3,2,1,0:T(8,128)} %copy-done.7), calls=%async_computation.4 | async-start | bytes 8912896 | tf_op jit(solution)/shard_map/all_to_all | solution.py:758
  290.4 2.2 collective-permute-start.16
  292.7 2.3 copy-done.8
  294.9 8.9 %to_planes.1 = (f32[8192,128]{1,0:T(8,128)}, f32[8,2,8,32,128]{4,3,2,1,0:T(8,128)S(1)}) custom-call(f32[8,2,8,32,128]{4,3,2,1,0:T(8,128)} %all-to-all-done.2.refs_5_.half, f32[8,2,8,32,128]{4,3,2,1,0:T(8,128)} %all-to-all-done.3.other, f32[8,34,32,128]{3,2,1,0:T(8,128)S(1)} %copy-done.8), custom_call_target="tpu_custom_call" | custom-call | bytes 8650752 | tf_op jit(solution)/shard_map/to_planes/pallas_call | solution.py:48
  304.1 2.8 collective-permute-start.15
  306.9 3.0 collective-permute-start.14
  309.9 79.8 %collective-permute-done.15.refs_2_ = f32[4,64,128]{2,1,0:T(8,128)S(1)} collective-permute-done((f32[4,64,128]{2,1,0:T(8,128)S(1)}, f32[4,64,128]{2,1,0:T(8,128)S(1)}, u32[]{:S(2)}, u32[]{:S(2)}) %collective-permute-start.15) | collective-permute-done | bytes 131104 | tf_op jit(solution)/shard_map/ppermute | solution.py:781
  398.8 12.7 %last_step.1 = f32[4,2048,128]{2,1,0:T(8,128)} custom-call(f32[8,8,32,128]{3,2,1,0:T(8,128)S(1)} %bitcast.12, f32[4,64,128]{2,1,0:T(8,128)S(1)} %collective-permute-done.14.refs_1_, f32[4,64,128]{2,1,0:T(8,128)S(1)} %collective-permute-done.15.refs_2_, f32[8,34,32,128]{3,2,1,0:T(8,128)} %all-to-all-done.4.refs_3_, f32[8,19,32,128]{3,2,1,0:T(8,128)S(1)} %copy-done.21, ...), custom_call_target="tpu_custom_call" | custom-call | flops 31457280 | bytes 14548992 | tf_op jit(solution)/shard_map/last_step/pallas_call | solution.py:48
  (122 shorter events, 64.4 us)
Async XLA Ops:
  8.8 5.8 %copy-start.34 = (f32[4,256,256]{2,1,0:T(8,128)S(1)}, f32[4,256,256]{2,1,0:T(8,128)}, u32[]{:S(2)}) copy-start(f32[4,256,256]{2,1,0:T(8,128)} %x_ref.1) | copy-start | bytes 3145732
  8.8 59.7 %all-to-all-start = ((f32[8,19,32,128]{3,2,1,0:T(8,128)}), f32[8,19,32,128]{3,2,1,0:T(8,128)}, u32[]{:S(2)}, u32[]{:S(2)}) async-start(f32[8,19,32,128]{3,2,1,0:T(8,128)} %copy-done.20), calls=%async_computation | async-start | bytes 4980736 | tf_op jit(solution)/shard_map/all_to_all | solution.py:758
  68.5 59.0 %all-to-all-start.1 = ((f32[8,2,8,32,128]{4,3,2,1,0:T(8,128)}), f32[8,2,8,32,128]{4,3,2,1,0:T(8,128)}, u32[]{:S(2)}, u32[]{:S(2)}) async-start(f32[8,2,8,32,128]{4,3,2,1,0:T(8,128)} %copy-done.15), calls=%async_computation.1 | async-start | bytes 4194304 | tf_op jit(solution)/shard_map/all_to_all | solution.py:758
  81.8 11.3 %collective-permute-start.3 = (f32[8,3,32,128]{3,2,1,0:T(8,128)S(1)}, f32[8,3,32,128]{3,2,1,0:T(8,128)S(1)}, u32[]{:S(2)}, u32[]{:S(2)}) collective-permute-start(f32[8,3,32,128]{3,2,1,0:T(8,128)S(1)} %get-tuple-element.31.refs_0_), channel_id=1, source_target_pairs={{0,8},{8,16},{16,24},{24,0},{1,9},{9,17},{17,25},{25,1},{2,10},{10... | collective-permute-start | bytes 1179656 | tf_op jit(solution)/shard_map/ppermute | solution.py:763
  83.0 19.3 %collective-permute-start.2 = (f32[8,3,32,128]{3,2,1,0:T(8,128)S(1)}, f32[8,3,32,128]{3,2,1,0:T(8,128)S(1)}, u32[]{:S(2)}, u32[]{:S(2)}) collective-permute-start(f32[8,3,32,128]{3,2,1,0:T(8,128)S(1)} %get-tuple-element.31.refs_0_), channel_id=1, source_target_pairs={{0,16},{8,24},{16,0},{24,8},{1,17},{9,25},{17,1},{25,9},{2,18},{10... | collective-permute-start | bytes 1179656 | tf_op jit(solution)/shard_map/ppermute | solution.py:763
  84.3 18.0 %collective-permute-start.1 = (f32[8,3,32,128]{3,2,1,0:T(8,128)S(1)}, f32[8,3,32,128]{3,2,1,0:T(8,128)S(1)}, u32[]{:S(2)}, u32[]{:S(2)}) collective-permute-start(f32[8,3,32,128]{3,2,1,0:T(8,128)S(1)} %get-tuple-element.31.refs_0_), channel_id=1, source_target_pairs={{0,24},{8,0},{16,8},{24,16},{1,25},{9,1},{17,9},{25,17},{2,26},{10... | collective-permute-start | bytes 1179656 | tf_op jit(solution)/shard_map/ppermute | solution.py:763
  103.3 47.1 %collective-permute-start.5 = (f32[8,2,8,32,128]{4,3,2,1,0:T(8,128)}, f32[8,2,8,32,128]{4,3,2,1,0:T(8,128)}, u32[]{:S(2)}, u32[]{:S(2)}) collective-permute-start(f32[8,2,8,32,128]{4,3,2,1,0:T(8,128)} %after.3.main.refs_4_), channel_id=1, source_target_pairs={{0,24},{8,0},{16,8},{24,16},{1,25},{9,1},{17,9},{25,17},{2,26},{10... | collective-permute-start | bytes 6291464 | tf_op jit(solution)/shard_map/ppermute | solution.py:763
  103.8 29.4 %collective-permute-start = (f32[8,2,2,32,128]{4,3,2,1,0:T(8,128)}, f32[8,2,2,32,128]{4,3,2,1,0:T(8,128)S(1)}, u32[]{:S(2)}, u32[]{:S(2)}) collective-permute-start(f32[8,2,2,32,128]{4,3,2,1,0:T(8,128)} %get-tuple-element.29), channel_id=1, source_target_pairs={{0,1},{1,2},{2,3},{3,4},{4,5},{5,6},{6,7},{7,0},{8,9},{9,10},{10,1... | collective-permute-start | bytes 1572872 | tf_op jit(solution)/shard_map/ppermute | solution.py:763
  106.6 28.8 %collective-permute-start.4 = (f32[8,2,2,32,128]{4,3,2,1,0:T(8,128)}, f32[8,2,2,32,128]{4,3,2,1,0:T(8,128)}, u32[]{:S(2)}, u32[]{:S(2)}) collective-permute-start(f32[8,2,2,32,128]{4,3,2,1,0:T(8,128)} %get-tuple-element.32), channel_id=1, source_target_pairs={{0,7},{1,0},{2,1},{3,2},{4,3},{5,4},{6,5},{7,6},{8,15},{9,8},{10,9... | collective-permute-start | bytes 1572872 | tf_op jit(solution)/shard_map/ppermute | solution.py:763
  136.6 21.6 %collective-permute-start.6 = (f32[8,2,2,32,128]{4,3,2,1,0:T(8,128)S(1)}, f32[8,2,2,32,128]{4,3,2,1,0:T(8,128)S(1)}, u32[]{:S(2)}, u32[]{:S(2)}) collective-permute-start(f32[8,2,2,32,128]{4,3,2,1,0:T(8,128)S(1)} %get-tuple-element.37), channel_id=1, source_target_pairs={{0,1},{1,2},{2,3},{3,4},{4,5},{5,6},{6,7},{7,0},{8,9},{9,10},{10,1... | collective-permute-start | bytes 1572872 | tf_op jit(solution)/shard_map/ppermute | solution.py:763
  136.9 21.3 %collective-permute-start.7 = (f32[8,2,2,32,128]{4,3,2,1,0:T(8,128)S(1)}, f32[8,2,2,32,128]{4,3,2,1,0:T(8,128)S(1)}, u32[]{:S(2)}, u32[]{:S(2)}) collective-permute-start(f32[8,2,2,32,128]{4,3,2,1,0:T(8,128)S(1)} %get-tuple-element.33._), channel_id=1, source_target_pairs={{0,7},{1,0},{2,1},{3,2},{4,3},{5,4},{6,5},{7,6},{8,15},{9,8},{10,9... | collective-permute-start | bytes 1572872 | tf_op jit(solution)/shard_map/ppermute | solution.py:763
  139.9 21.6 %collective-permute-start.8 = (f32[8,2,2,32,128]{4,3,2,1,0:T(8,128)S(1)}, f32[8,2,2,32,128]{4,3,2,1,0:T(8,128)S(1)}, u32[]{:S(2)}, u32[]{:S(2)}) collective-permute-start(f32[8,2,2,32,128]{4,3,2,1,0:T(8,128)S(1)} %get-tuple-element.34._), channel_id=1, source_target_pairs={{0,24},{8,0},{16,8},{24,16},{1,25},{9,1},{17,9},{25,17},{2,26},{10... | collective-permute-start | bytes 1572872 | tf_op jit(solution)/shard_map/ppermute | solution.py:763
  149.1 7.7 %copy-start = (f32[2,10,272,128]{3,2,1,0:T(8,128)}, f32[2,10,272,128]{3,2,1,0:T(8,128)S(1)}, u32[]{:S(2)}) copy-start(f32[2,10,272,128]{3,2,1,0:T(8,128)S(1)} %first_step.1.first.with_w.refs_6_) | copy-start | bytes 8355844
  165.3 64.6 %all-to-all-start.2 = ((f32[8,2,8,32,128]{4,3,2,1,0:T(8,128)}), f32[8,2,8,32,128]{4,3,2,1,0:T(8,128)}, u32[]{:S(2)}, u32[]{:S(2)}) async-start(f32[8,2,8,32,128]{4,3,2,1,0:T(8,128)} %copy-done.3), calls=%async_computation.2 | async-start | bytes 4194304 | tf_op jit(solution)/shard_map/all_to_all | solution.py:758
  171.4 35.9 %copy-start.1 = (f32[2,10,272,128]{3,2,1,0:T(8,128)S(1)}, f32[2,10,272,128]{3,2,1,0:T(8,128)}, u32[]{:S(2)}) copy-start(f32[2,10,272,128]{3,2,1,0:T(8,128)} %copy-done) | copy-start | bytes 8355844
  171.4 35.9 %collective-permute-start.9 = (f32[8,2,6,32,128]{4,3,2,1,0:T(8,128)}, f32[8,2,6,32,128]{4,3,2,1,0:T(8,128)S(1)}, u32[]{:S(2)}, u32[]{:S(2)}) collective-permute-start(f32[8,2,6,32,128]{4,3,2,1,0:T(8,128)} %copy-done.40), channel_id=1, source_target_pairs={{0,24},{8,0},{16,8},{24,16},{1,25},{9,1},{17,9},{25,17},{2,26},{10... | collective-permute-start | bytes 4718600 | tf_op jit(solution)/shard_map/ppermute | solution.py:763
  176.4 30.9 %copy-start.5 = (f32[8,2,8,32,128]{4,3,2,1,0:T(8,128)S(1)}, f32[8,2,8,32,128]{4,3,2,1,0:T(8,128)}, u32[]{:S(2)}) copy-start(f32[8,2,8,32,128]{4,3,2,1,0:T(8,128)} %copy-done.3) | copy-start | bytes 6291460
  176.4 30.9 %copy-start.27 = (f32[8,2,2,32,128]{4,3,2,1,0:T(8,128)S(1)}, f32[8,2,2,32,128]{4,3,2,1,0:T(8,128)}, u32[]{:S(2)}) copy-start(f32[8,2,2,32,128]{4,3,2,1,0:T(8,128)} %copy-done.26) | copy-start | bytes 1572868
  184.0 28.8 %copy-start.9 = (f32[2,10,272,128]{3,2,1,0:T(8,128)}, f32[2,10,272,128]{3,2,1,0:T(8,128)S(1)}, u32[]{:S(2)}) copy-start(f32[2,10,272,128]{3,2,1,0:T(8,128)S(1)} %carried_step.1.first.refs_7_) | copy-start | bytes 8355844
  184.0 32.3 %copy-start.44 = (f32[2,256,128]{2,1,0:T(8,128)S(1)}, f32[2,256,128]{2,1,0:T(8,128)}, u32[]{:S(2)}) copy-start(f32[2,256,128]{2,1,0:T(8,128)} %copy-done.43) | copy-start | bytes 786436
  184.0 34.0 %copy-start.42 = (f32[2,256,128]{2,1,0:T(8,128)S(1)}, f32[2,256,128]{2,1,0:T(8,128)}, u32[]{:S(2)}) copy-start(f32[2,256,128]{2,1,0:T(8,128)} %copy-done.41) | copy-start | bytes 786436
  214.1 5.7 %collective-permute-start.11 = (f32[2,256,128]{2,1,0:T(8,128)S(1)}, f32[2,256,128]{2,1,0:T(8,128)S(1)}, u32[]{:S(2)}, u32[]{:S(2)}) collective-permute-start(f32[2,256,128]{2,1,0:T(8,128)S(1)} %get-tuple-element.41), channel_id=1, source_target_pairs={{0,1},{1,2},{2,3},{3,4},{4,5},{5,6},{6,7},{7,0},{8,9},{9,10},{10,1... | collective-permute-start | bytes 786440 | tf_op jit(solution)/shard_map/ppermute | solution.py:763
  216.3 10.5 %collective-permute-start.13 = (f32[2,256,128]{2,1,0:T(8,128)S(1)}, f32[2,256,128]{2,1,0:T(8,128)S(1)}, u32[]{:S(2)}, u32[]{:S(2)}) collective-permute-start(f32[2,256,128]{2,1,0:T(8,128)S(1)} %get-tuple-element.43), channel_id=1, source_target_pairs={{0,7},{1,0},{2,1},{3,2},{4,3},{5,4},{6,5},{7,6},{8,15},{9,8},{10,9... | collective-permute-start | bytes 786440 | tf_op jit(solution)/shard_map/ppermute | solution.py:763
  216.3 10.5 %collective-permute-start.10 = (f32[2,256,128]{2,1,0:T(8,128)S(1)}, f32[2,256,128]{2,1,0:T(8,128)S(1)}, u32[]{:S(2)}, u32[]{:S(2)}) collective-permute-start(f32[2,256,128]{2,1,0:T(8,128)S(1)} %copy-done.44), channel_id=1, source_target_pairs={{0,1},{1,2},{2,3},{3,4},{4,5},{5,6},{6,7},{7,0},{8,9},{9,10},{10,1... | collective-permute-start | bytes 786440 | tf_op jit(solution)/shard_map/ppermute | solution.py:763
  218.0 11.9 %collective-permute-start.12 = (f32[2,256,128]{2,1,0:T(8,128)S(1)}, f32[2,256,128]{2,1,0:T(8,128)S(1)}, u32[]{:S(2)}, u32[]{:S(2)}) collective-permute-start(f32[2,256,128]{2,1,0:T(8,128)S(1)} %copy-done.42), channel_id=1, source_target_pairs={{0,7},{1,0},{2,1},{3,2},{4,3},{5,4},{6,5},{7,6},{8,15},{9,8},{10,9... | collective-permute-start | bytes 786440 | tf_op jit(solution)/shard_map/ppermute | solution.py:763
  232.9 49.7 %all-to-all-start.3 = ((f32[8,2,8,32,128]{4,3,2,1,0:T(8,128)}), f32[8,2,8,32,128]{4,3,2,1,0:T(8,128)}, u32[]{:S(2)}, u32[]{:S(2)}) async-start(f32[8,2,8,32,128]{4,3,2,1,0:T(8,128)} %copy-done.13), calls=%async_computation.3 | async-start | bytes 4194304 | tf_op jit(solution)/shard_map/all_to_all | solution.py:758
  282.6 109.7 %all-to-all-start.4 = ((f32[8,34,32,128]{3,2,1,0:T(8,128)}), f32[8,34,32,128]{3,2,1,0:T(8,128)}, u32[]{:S(2)}, u32[]{:S(2)}) async-start(f32[8,34,32,128]{3,2,1,0:T(8,128)} %copy-done.7), calls=%async_computation.4 | async-start | bytes 8912896 | tf_op jit(solution)/shard_map/all_to_all | solution.py:758
  290.4 99.3 %collective-permute-start.16 = (f32[8,2,8,32,128]{4,3,2,1,0:T(8,128)}, f32[8,2,8,32,128]{4,3,2,1,0:T(8,128)S(1)}, u32[]{:S(2)}, u32[]{:S(2)}) collective-permute-start(f32[8,2,8,32,128]{4,3,2,1,0:T(8,128)} %all-to-all-done.2.refs_5_.half), channel_id=1, source_target_pairs={{0,8},{8,16},{16,24},{24,0},{1,9},{9,17},{17,25},{25,1},{2,10},{10... | collective-permute-start | bytes 6291464 | tf_op jit(solution)/shard_map/ppermute | solution.py:763
  294.9 97.4 %copy-start.33 = (f32[64,32,128]{2,1,0:T(8,128)S(1)}, f32[64,32,128]{2,1,0:T(8,128)}, u32[]{:S(2)}) copy-start(f32[64,32,128]{2,1,0:T(8,128)} %copy-done.32) | copy-start | bytes 3145732
  303.8 87.2 %collective-permute-start.17 = (f32[8,2,8,32,128]{4,3,2,1,0:T(8,128)S(1)}, f32[8,2,8,32,128]{4,3,2,1,0:T(8,128)S(1)}, u32[]{:S(2)}, u32[]{:S(2)}) collective-permute-start(f32[8,2,8,32,128]{4,3,2,1,0:T(8,128)S(1)} %get-tuple-element.49), channel_id=1, source_target_pairs={{0,8},{8,16},{16,24},{24,0},{1,9},{9,17},{17,25},{25,1},{2,10},{10... | collective-permute-start | bytes 6291464 | tf_op jit(solution)/shard_map/ppermute | solution.py:763
  304.1 85.6 %collective-permute-start.15 = (f32[4,64,128]{2,1,0:T(8,128)S(1)}, f32[4,64,128]{2,1,0:T(8,128)S(1)}, u32[]{:S(2)}, u32[]{:S(2)}) collective-permute-start(f32[4,64,128]{2,1,0:T(8,128)S(1)} %get-tuple-element.50), channel_id=1, source_target_pairs={{1,0},{2,1},{3,2},{4,3},{5,4},{6,5},{7,6},{9,8},{10,9},{11,10},{12... | collective-permute-start | bytes 393224 | tf_op jit(solution)/shard_map/ppermute | solution.py:781
  306.9 82.8 %collective-permute-start.14 = (f32[4,64,128]{2,1,0:T(8,128)S(1)}, f32[4,64,128]{2,1,0:T(8,128)S(1)}, u32[]{:S(2)}, u32[]{:S(2)}) collective-permute-start(f32[4,64,128]{2,1,0:T(8,128)S(1)} %get-tuple-element.51), channel_id=1, source_target_pairs={{0,1},{1,2},{2,3},{3,4},{4,5},{5,6},{6,7},{8,9},{9,10},{10,11},{11... | collective-permute-start | bytes 393224 | tf_op jit(solution)/shard_map/ppermute | solution.py:780
  (36 other events, 56.2 us)

commit v12 on v9

--- a/solution.py
+++ b/solution.py
@@ -37,7 +37,7 @@
     return pltpu.SemaphoreType.DMA((count,))
 
 
-def call(kernel, ins, outs, scratch, flops, name, kind=f32, aliases=None):
+def call(kernel, ins, outs, scratch, flops, name, kind=f32, aliases=None, limit=vmem_bytes):
     moved = sum(4 * x.size for x, _ in ins)
     return pl.pallas_call(
         kernel,
@@ -46,7 +46,7 @@
         out_shape=tuple(jax.ShapeDtypeStruct(shape, kind) for shape, _ in outs),
         scratch_shapes=scratch,
         input_output_aliases=aliases or {},
-        compiler_params=pltpu.CompilerParams(vmem_limit_bytes=vmem_bytes),
+        compiler_params=pltpu.CompilerParams(vmem_limit_bytes=limit),
         cost_estimate=pl.CostEstimate(flops=flops, bytes_accessed=moved, transcendentals=0),
         name=name,
     )(*[x for x, _ in ins])
@@ -449,25 +449,27 @@
     )[0]
 
 
-def outer_kernel(chunks, _before, _after, low_rows, high_rows, *refs):
-    *again, sem = refs
+def outer_kernel(chunks, *refs):
+    *outs, sem = refs[-3:]
     block = chunks.shape[2]
     low, high = chunks.at[:, :, pl.ds(0, 2)], chunks.at[:, :, pl.ds(block - 2, 2)]
-    pairs = [(low, low_rows), (high, high_rows)]
-    pairs += [(chunks.at[:, :, span], part) for part, span in spans(again, 2)]
-    wait_all(start_all(pairs, sem))
-
-
-def outer_rows(chunks, later, pieces):
+    wait_all(start_all([(low, outs[0]), (high, outs[1])], sem))
+
+
+def pieces_kernel(chunks, _, *refs):
+    *outs, sem = refs
+    wait_all(start_all([(chunks.at[:, :, span], part) for part, span in spans(outs, 2)], sem))
+
+
+def row_parts(kernel, chunks, later, sizes, name):
     slabs, count, _, depth, width = chunks.shape
-    rows = [((slabs, count, size, depth, width), whole()) for size in (2, 2, *pieces)]
-    return call(
-        outer_kernel,
+    return call(
+        kernel,
         [(chunks, anywhere())] + [(x, anywhere()) for x in later],
-        rows,
-        [dmas(len(rows))],
+        [((slabs, count, size, depth, width), whole()) for size in sizes],
+        [dmas(len(sizes))],
         0,
-        "outer_rows",
+        name,
     )
 
 
@@ -580,8 +582,8 @@
 
 
 def last_kernel(*refs):
-    visc_in, edges_below, edges_above, chunks, *states, half, other, out = refs[:9]
-    pulled, state, prior, planes, coupling, ends, visc, sem = refs[9:]
+    visc, edges_below, edges_above, *states, half, other, chunks, out = refs[:9]
+    pulled, state, planes, coupling, ends, sem = refs[9:]
     slabs, block, depth, width = visc.shape
     rows, step = slabs * block, pulled.shape[3]
     main = pl.ds(pad, depth)
@@ -590,17 +592,15 @@
     def copy(source, target, which):
         return pltpu.make_async_copy(source, target, sem.at[which])
 
-    arrive = {"visc": copy(visc_in, visc, 0)}
+    arrive = {}
     arrive["ends"] = copy(chunks.at[:, pl.ds(fields * block, 2)], ends, 1)
     for f in range(fields):
         source = chunks.at[:, pl.ds(f * block, block)]
         arrive["pulled", f] = copy(source, pulled.at[f, :, :, main], 2 + f)
         source = states[f // 2].at[:, f % 2]
         arrive["state", f] = copy(source, state.at[f, :, :, main], 2 + fields + f)
-        source = (half, other)[f // 2].at[:, f % 2]
-        arrive["prior", f] = copy(source, prior.at[f], 2 + 2 * fields + f)
-    order = ["visc", "ends", ("state", W)]
-    order += [(which, f) for f in (U, V, T, W) for which in ("pulled", "state", "prior")]
+    order = ["ends", ("state", W)]
+    order += [(which, f) for f in (U, V, T, W) for which in ("pulled", "state")]
     for which in dict.fromkeys(order):
         arrive[which].start()
 
@@ -616,7 +616,7 @@
         base = f * rows * step
         state_rows[pl.ds(base + first, rows, stride=step), :] = edges_below[outside[f]]
         state_rows[pl.ds(base + last, rows, stride=step), :] = edges_above[outside[f]]
-    ready("visc", "ends")
+    ready("ends")
     for f in range(fields):
         for p in range(slabs):
             base, part = (f * rows + p * block) * step, pl.ds(f * block, block)
@@ -625,7 +625,7 @@
     ready(("state", W))
     leaving = []
     for f in (U, V, T, W):
-        ready(("pulled", f), ("state", f), ("prior", f))
+        ready(("pulled", f), ("state", f))
         if f == T:
             ready(("pulled", W))
         along_y = 0.5 * (visc[slabs - 1, block - 1] + visc[0, 0])
@@ -655,7 +655,8 @@
                     rate = rate + pulled[W, p, i, main]
                 else:
                     rate = rate + (coupling[p, i] - lost)
-                result = value + time_step * rate - prior[f, p, i]
+                prior = (half, other)[f // 2]
+                result = value + time_step * rate - prior[p, f % 2, i]
                 planes[f, pl.ds(p * block + i, depth, stride=rows), :] = result
             return south
 
@@ -674,21 +675,20 @@
     one = (slabs, block, depth, width)
     return call(
         last_kernel,
-        [(visc.reshape(one), anywhere()), (below, whole()), (above, whole())]
-        + [(x, anywhere()) for x in (chunks, *states, *priors)],
+        [(x, whole()) for x in (visc.reshape(one), below, above, *states, *priors)]
+        + [(chunks, anywhere())],
         [((fields, depth * rows, width), anywhere())],
         [
             padded,
             padded,
-            vmem(fields, *one),
             vmem(fields, depth * rows, width),
             vmem(*one),
             vmem(slabs, 2, depth, width),
-            vmem(*one),
-            dmas(2 + 3 * fields),
+            dmas(2 + 2 * fields),
         ],
         30 * fields * rows * depth * width,
         "last_step",
+        limit=36 * 1024 * 1024,
     )[0]
 
 
@@ -723,20 +723,20 @@
     above = lax.ppermute(ends[0], "slab", [(i, j) for j, i in forward])
 
     own, outer, targets, later = [], [], [], (visc_share, visc_share)
-    few = max(1, 3 * block // 8)
-    for part, pieces in ((main_half, (block,)), (main_other, (few, block - few))):
-        low_rows, high_rows, *again = outer_rows(part, later, pieces)
-        low_in = around(high_rows, "slab", 1)
-        high_in = around(low_rows, "slab", -1)
+    few = max(1, block // 4)
+    own, targets, later = [], [], (visc_share,)
+    for part, sizes in ((main_half, (block,)), (main_other, (few, block - few))):
+        low_rows, high_rows = row_parts(outer_kernel, part, later, (2, 2), "outer_rows")
+        low_in, high_in = around(high_rows, "slab", 1), around(low_rows, "slab", -1)
         own.append((low_in, part, high_in))
-        outer.append(low_rows)
-        targets.append([around(piece, "seg", -1) for piece in again])
+        parts = row_parts(pieces_kernel, part, (low_rows,), sizes, "pieces")
+        targets.append([around(piece, "seg", -1) for piece in parts])
         later = (low_in, high_in)
 
     mats = mat_high, mat_low
-    first_half = first_step(*own[0], outer[1], frame, *mats)
+    first_half = first_step(*own[0], frame, frame, *mats)
     out, low_edge, high_edge = second_step(
-        first_half, first_half, frame, *mats, W, targets[0], ()
+        first_half, first_half, frame, *mats, W, targets[0], (parts[0],)
     )
     out = after(out, (own[1][0], own[1][2], targets[1][0]))
     first_other = carried_step(own[1], own[0], out, frame, *mats)

time: 405 us -> 412 us (1.017)
  local copies, waits for them, and re-layouts: 10 us -> 17.4 us
    unnamed x46 -> x58, local copies, waits for them, and re-layouts: 10 us -> 17.4 us
    pallas_call x16 -> x18, Pallas kernels: 103 us -> 104 us  [call(): pl.pallas_call(kernel, in_specs=[spec for _, spec in ins], out_specs=tupl...]
where the time goes in v12:
time: 412 us; the launch traced here: 411 us
  waiting for transfers between devices  230 us (56%)
  Pallas kernels  104 us (25%)
  starting transfers between devices  58.6 us (14%)
  local copies, waits for them, and re-layouts  17.4 us (4%)
    pallas_call x18, Pallas kernels, call(): pl.pallas_call(kernel, in_specs=[spec for _, spec in ins], out_specs=tupl...  104 us
    ppermute x16, waiting for transfers between devices, around(): lax.ppermute(value, axis, [(i, (i + steps) % count) for i in range(count)])  97.3 us
    ppermute x1, waiting for transfers between devices, local(): above = lax.ppermute(ends[0], 'slab', [(i, j) for j, i in forward])  83.2 us
    all_to_all x6, waiting for transfers between devices, exchange(): lax.all_to_all(chunks, 'slab', split_axis=0, concat_axis=0, tiled=True)  49.8 us
    all_to_all x6, starting transfers between devices, exchange(): lax.all_to_all(chunks, 'slab', split_axis=0, concat_axis=0, tiled=True)  36.7 us
    unnamed x58, local copies, waits for them, and re-layouts  17.4 us
    ppermute x16, starting transfers between devices, around(): lax.ppermute(value, axis, [(i, (i + steps) % count) for i in range(count)])  16 us
  transfers between devices with their start and end apart: 24, of which 13 were waited for; matrix products, arithmetic and copies ran while one was open for 0% of the time, Pallas kernels for 21%

profile of v12, /device:TPU:9, one launch (start us, length us, event | category | flops | bytes accessed | tf_op | source)
XLA Modules:
  0.0 411.1 jit_solution(16529421087900332103)
XLA Ops:
  0.6 2.9 visc_chunks.1
  3.6 5.6 %all-to-all-start.1 = ((f32[8,3,32,128]{3,2,1,0:T(8,128)}), f32[8,3,32,128]{3,2,1,0:T(8,128)S(1)}, u32[]{:S(2)}, u32[]{:S(2)}) async-start(f32[8,3,32,128]{3,2,1,0:T(8,128)} %get-tuple-element.25.refs_0_), calls=%async_computation.1 | async-start | bytes 786432 | tf_op jit(solution)/shard_map/all_to_all | solution.py:696
  9.2 4.2 %to_chunks.2 = (f32[8,2,8,32,128]{4,3,2,1,0:T(8,128)}, f32[2,4,64,128]{3,2,1,0:T(8,128)}) custom-call(f32[4,2048,128]{2,1,0:T(8,128)} %bitcast.11, f32[8,3,32,128]{3,2,1,0:T(8,128)} %get-tuple-element.25.refs_0_), custom_call_target="tpu_custom_call" | custom-call | bytes 4587520 | tf_op jit(solution)/shard_map/to_chunks/pallas_call | solution.py:42
  13.4 5.3 %all-to-all-done.1.refs_0_ = f32[8,3,32,128]{3,2,1,0:T(8,128)S(1)} async-done(((f32[8,3,32,128]{3,2,1,0:T(8,128)}), f32[8,3,32,128]{3,2,1,0:T(8,128)S(1)}, u32[]{:S(2)}, u32[]{:S(2)}) %all-to-all-start.1) | async-done | bytes 393248 | tf_op jit(solution)/shard_map/all_to_all | solution.py:696
  18.7 6.6 %all-to-all-start = ((f32[8,2,8,32,128]{4,3,2,1,0:T(8,128)}), f32[8,2,8,32,128]{4,3,2,1,0:T(8,128)S(1)}, u32[]{:S(2)}, u32[]{:S(2)}) async-start(f32[8,2,8,32,128]{4,3,2,1,0:T(8,128)} %get-tuple-element.26.refs_3_), calls=%async_computation | async-start | bytes 4194304 | tf_op jit(solution)/shard_map/all_to_all | solution.py:696
  28.9 2.9 split.1
  31.8 4.8 %collective-permute-done.4.refs_3_ = f32[8,3,32,128]{3,2,1,0:T(8,128)S(1)} collective-permute-done((f32[8,3,32,128]{3,2,1,0:T(8,128)S(1)}, f32[8,3,32,128]{3,2,1,0:T(8,128)S(1)}, u32[]{:S(2)}, u32[]{:S(2)}) %collective-permute-start.4) | collective-permute-done | bytes 393248 | tf_op jit(solution)/shard_map/ppermute | solution.py:701
  36.6 9.1 %collective-permute-done.3.refs_2_ = f32[8,3,32,128]{3,2,1,0:T(8,128)S(1)} collective-permute-done((f32[8,3,32,128]{3,2,1,0:T(8,128)S(1)}, f32[8,3,32,128]{3,2,1,0:T(8,128)S(1)}, u32[]{:S(2)}, u32[]{:S(2)}) %collective-permute-start.3) | collective-permute-done | bytes 393248 | tf_op jit(solution)/shard_map/ppermute | solution.py:701
  47.1 2.8 to_frame.1._.refs_0_.refs_7_.refs_8_
  49.9 4.2 %to_chunks.3 = (f32[8,2,8,32,128]{4,3,2,1,0:T(8,128)}, f32[2,4,64,128]{3,2,1,0:T(8,128)}) custom-call(f32[4,2048,128]{2,1,0:T(8,128)} %bitcast.12, f32[12,256,128]{2,1,0:T(8,128)} %to_frame.1._.refs_0_.refs_7_.refs_8_, bf16[4,256,256]{2,1,0:T(8,128)(2,1)} %get-tuple-element.29.refs_1_.refs_8_), custom_call_target="tpu_custom_call" | custom-call | bytes 6815744 | tf_op jit(solution)/shard_map/to_chunks/pallas_call | solution.py:42
  54.1 16.7 %all-to-all-done.chunks.main.refs_4_ = f32[8,2,8,32,128]{4,3,2,1,0:T(8,128)S(1)} async-done(((f32[8,2,8,32,128]{4,3,2,1,0:T(8,128)}), f32[8,2,8,32,128]{4,3,2,1,0:T(8,128)S(1)}, u32[]{:S(2)}, u32[]{:S(2)}) %all-to-all-start) | async-done | bytes 2097184 | tf_op jit(solution)/shard_map/all_to_all | solution.py:696
  72.1 7.8 %all-to-all-start.2 = ((f32[8,2,8,32,128]{4,3,2,1,0:T(8,128)}), f32[8,2,8,32,128]{4,3,2,1,0:T(8,128)}, u32[]{:S(2)}, u32[]{:S(2)}) async-start(f32[8,2,8,32,128]{4,3,2,1,0:T(8,128)} %get-tuple-element.31.refs_4_), calls=%async_computation.2 | async-start | bytes 4194304 | tf_op jit(solution)/shard_map/all_to_all | solution.py:696
  82.1 3.0 pieces.2
  89.1 47.5 %collective-permute-done.low_in.refs_0_.refs_3_ = f32[8,2,2,32,128]{4,3,2,1,0:T(8,128)S(1)} collective-permute-done((f32[8,2,2,32,128]{4,3,2,1,0:T(8,128)S(1)}, f32[8,2,2,32,128]{4,3,2,1,0:T(8,128)S(1)}, u32[]{:S(2)}, u32[]{:S(2)}) %collective-permute-start) | collective-permute-done | bytes 524320 | tf_op jit(solution)/shard_map/ppermute | solution.py:701
  142.4 2.9 pieces.3
  147.5 9.1 %first_step.1.first.with_w.refs_6_ = f32[2,10,272,128]{3,2,1,0:T(8,128)} custom-call(f32[8,2,2,32,128]{4,3,2,1,0:T(8,128)} %copy-done.10, f32[8,2,8,32,128]{4,3,2,1,0:T(8,128)} %copy-done.7, f32[8,2,2,32,128]{4,3,2,1,0:T(8,128)} %copy-done.11, f32[12,256,128]{2,1,0:T(8,128)} %to_frame.1._.refs_0_.refs_7_.refs_8_, ...), custom_call_target="tpu_custom_call" | custom-call | flops 1006632960 | bytes 8388608 | tf_op jit(solution)/shard_map/first_step/pallas_call | solution.py:42
  157.9 9.3 %second_step.2 = (f32[8,2,8,32,128]{4,3,2,1,0:T(8,128)}, f32[2,256,128]{2,1,0:T(8,128)}, f32[2,256,128]{2,1,0:T(8,128)}) custom-call(f32[2,10,272,128]{3,2,1,0:T(8,128)} %first_step.1.first.with_w.refs_6_, f32[2,10,272,128]{3,2,1,0:T(8,128)} %first_step.1.first.with_w.refs_6_, f32[12,256,128]{2,1,0:T(8,128)} %to_frame.1._.refs_0_.refs_7_.refs_8_, ...), custom_call_target="tpu_custom_call" | custom-call | flops 805306368 | bytes 11862016 | tf_op jit(solution)/shard_map/second_step/pallas_call | solution.py:42
  168.4 4.9 %all-to-all-start.3 = ((f32[8,2,8,32,128]{4,3,2,1,0:T(8,128)}), f32[8,2,8,32,128]{4,3,2,1,0:T(8,128)S(1)}, u32[]{:S(2)}, u32[]{:S(2)}) async-start(f32[8,2,8,32,128]{4,3,2,1,0:T(8,128)} %after.2.refs_6_.refs_5_.refs_0_), calls=%async_computation.3 | async-start | bytes 4194304 | tf_op jit(solution)/shard_map/all_to_all | solution.py:696
  175.3 9.7 %carried_step.1.first.refs_7_ = f32[2,10,272,128]{3,2,1,0:T(8,128)} custom-call(f32[8,2,2,32,128]{4,3,2,1,0:T(8,128)} %copy-done.15, f32[8,2,8,32,128]{4,3,2,1,0:T(8,128)} %all-to-all-done.2.chunks.refs_1_, f32[8,2,2,32,128]{4,3,2,1,0:T(8,128)} %copy-done.16, f32[8,2,2,32,128]{4,3,2,1,0:T(8,128)} %copy-done.10, f32[8,2,8,32,128]{4,3,2,1,0:T(8,128)} %copy-done.7, ...), custom_call_target="tpu_custom_call" | custom-call | flops 1006632960 | bytes 12058624 | tf_op jit(solution)/shard_map/carried_step/pallas_call | solution.py:42
  185.0 24.1 %collective-permute-done.9.refs_4_ = f32[8,2,6,32,128]{4,3,2,1,0:T(8,128)S(1)} collective-permute-done((f32[8,2,6,32,128]{4,3,2,1,0:T(8,128)}, f32[8,2,6,32,128]{4,3,2,1,0:T(8,128)S(1)}, u32[]{:S(2)}, u32[]{:S(2)}) %collective-permute-start.9) | collective-permute-done | bytes 1572896 | tf_op jit(solution)/shard_map/ppermute | solution.py:701
  210.3 9.5 %second_step.3 = (f32[8,2,8,32,128]{4,3,2,1,0:T(8,128)}, f32[2,256,128]{2,1,0:T(8,128)}, f32[2,256,128]{2,1,0:T(8,128)}) custom-call(f32[2,10,272,128]{3,2,1,0:T(8,128)} %carried_step.1.first.refs_7_, f32[2,10,272,128]{3,2,1,0:T(8,128)} %first_step.1.first.with_w.refs_6_, f32[12,256,128]{2,1,0:T(8,128)} %to_frame.1._.refs_0_.refs_7_.refs_8_, ...), custom_call_target="tpu_custom_call" | custom-call | flops 805306368 | bytes 13434880 | tf_op jit(solution)/shard_map/second_step/pallas_call | solution.py:42
  222.2 2.3 collective-permute-done.10.refs_1_.refs_2_
  224.5 4.5 %collective-permute-done.12.refs_3_.refs_4_ = f32[2,256,128]{2,1,0:T(8,128)S(1)} collective-permute-done((f32[2,256,128]{2,1,0:T(8,128)S(1)}, f32[2,256,128]{2,1,0:T(8,128)S(1)}, u32[]{:S(2)}, u32[]{:S(2)}) %collective-permute-start.12) | collective-permute-done | bytes 262176 | tf_op jit(solution)/shard_map/ppermute | solution.py:701
  233.3 3.7 all-to-all-start.4
  237.0 17.4 %adjoint_step.1._ = f32[8,34,32,128]{3,2,1,0:T(8,128)} custom-call(f32[8,2,8,32,128]{4,3,2,1,0:T(8,128)} %after.2.refs_6_.refs_5_.refs_0_, f32[8,2,8,32,128]{4,3,2,1,0:T(8,128)} %after.3.refs_1_, f32[2,256,128]{2,1,0:T(8,128)} %copy-done.18, f32[2,256,128]{2,1,0:T(8,128)} %copy-done.20, f32[2,256,128]{2,1,0:T(8,128)} %copy-done.19, ...), custom_call_target="tpu_custom_call" | custom-call | flops 3623878656 | bytes 14483456 | tf_op jit(solution)/shard_map/adjoint_step/pallas_call | solution.py:42
  254.4 27.9 %all-to-all-done.4.other = f32[8,2,8,32,128]{4,3,2,1,0:T(8,128)S(1)} async-done(((f32[8,2,8,32,128]{4,3,2,1,0:T(8,128)}), f32[8,2,8,32,128]{4,3,2,1,0:T(8,128)S(1)}, u32[]{:S(2)}, u32[]{:S(2)}) %all-to-all-start.4) | async-done | bytes 2097184 | tf_op jit(solution)/shard_map/all_to_all | solution.py:696
  283.6 8.0 %all-to-all-start.5 = ((f32[8,34,32,128]{3,2,1,0:T(8,128)}), f32[8,34,32,128]{3,2,1,0:T(8,128)}, u32[]{:S(2)}, u32[]{:S(2)}) async-start(f32[8,34,32,128]{3,2,1,0:T(8,128)} %adjoint_step.1._), calls=%async_computation.5 | async-start | bytes 8912896 | tf_op jit(solution)/shard_map/all_to_all | solution.py:696
  291.7 8.8 %to_planes.1 = (f32[8192,128]{1,0:T(8,128)}, f32[8,2,8,32,128]{4,3,2,1,0:T(8,128)}) custom-call(f32[8,2,8,32,128]{4,3,2,1,0:T(8,128)} %copy-done.8, f32[8,2,8,32,128]{4,3,2,1,0:T(8,128)} %copy-done.9, f32[8,34,32,128]{3,2,1,0:T(8,128)} %adjoint_step.1._), custom_call_target="tpu_custom_call" | custom-call | bytes 8650752 | tf_op jit(solution)/shard_map/to_planes/pallas_call | solution.py:42
  301.8 2.8 collective-permute-start.15
  304.7 3.0 collective-permute-start.14
  307.7 83.2 %collective-permute-done.15.refs_2_ = f32[4,64,128]{2,1,0:T(8,128)S(1)} collective-permute-done((f32[4,64,128]{2,1,0:T(8,128)S(1)}, f32[4,64,128]{2,1,0:T(8,128)S(1)}, u32[]{:S(2)}, u32[]{:S(2)}) %collective-permute-start.15) | collective-permute-done | bytes 131104 | tf_op jit(solution)/shard_map/ppermute | solution.py:723
  398.3 12.6 %last_step.1 = f32[4,2048,128]{2,1,0:T(8,128)} custom-call(f32[8,8,32,128]{3,2,1,0:T(8,128)S(1)} %bitcast.10, f32[4,64,128]{2,1,0:T(8,128)S(1)} %collective-permute-done.14.refs_1_, f32[4,64,128]{2,1,0:T(8,128)S(1)} %collective-permute-done.15.refs_2_, f32[8,2,8,32,128]{4,3,2,1,0:T(8,128)S(1)} %copy-done, f32[8,2,8,32,128]{4,3,2,1,0:T(8,128)S(1)} %copy-done.1, ...), custom_call_target="tpu_custom_call" | custom-call | flops 31457280 | bytes 14155776 | tf_op jit(solution)/shard_map/last_step/pallas_call | solution.py:42
  (93 shorter events, 42.8 us)
Async XLA Ops:
  3.6 15.1 %all-to-all-start.1 = ((f32[8,3,32,128]{3,2,1,0:T(8,128)}), f32[8,3,32,128]{3,2,1,0:T(8,128)S(1)}, u32[]{:S(2)}, u32[]{:S(2)}) async-start(f32[8,3,32,128]{3,2,1,0:T(8,128)} %get-tuple-element.25.refs_0_), calls=%async_computation.1 | async-start | bytes 786432 | tf_op jit(solution)/shard_map/all_to_all | solution.py:696
  18.7 9.1 %copy-start.12 = (f32[8,3,32,128]{3,2,1,0:T(8,128)}, f32[8,3,32,128]{3,2,1,0:T(8,128)S(1)}, u32[]{:S(2)}) copy-start(f32[8,3,32,128]{3,2,1,0:T(8,128)S(1)} %all-to-all-done.1.refs_0_) | copy-start | bytes 1179652
  18.7 52.1 %all-to-all-start = ((f32[8,2,8,32,128]{4,3,2,1,0:T(8,128)}), f32[8,2,8,32,128]{4,3,2,1,0:T(8,128)S(1)}, u32[]{:S(2)}, u32[]{:S(2)}) async-start(f32[8,2,8,32,128]{4,3,2,1,0:T(8,128)} %get-tuple-element.26.refs_3_), calls=%async_computation | async-start | bytes 4194304 | tf_op jit(solution)/shard_map/all_to_all | solution.py:696
  25.3 11.3 %collective-permute-start.4 = (f32[8,3,32,128]{3,2,1,0:T(8,128)S(1)}, f32[8,3,32,128]{3,2,1,0:T(8,128)S(1)}, u32[]{:S(2)}, u32[]{:S(2)}) collective-permute-start(f32[8,3,32,128]{3,2,1,0:T(8,128)S(1)} %all-to-all-done.1.refs_0_), channel_id=1, source_target_pairs={{0,8},{8,16},{16,24},{24,0},{1,9},{9,17},{17,25},{25,1},{2,10},{10... | collective-permute-start | bytes 1179656 | tf_op jit(solution)/shard_map/ppermute | solution.py:701
  26.5 19.2 %collective-permute-start.3 = (f32[8,3,32,128]{3,2,1,0:T(8,128)S(1)}, f32[8,3,32,128]{3,2,1,0:T(8,128)S(1)}, u32[]{:S(2)}, u32[]{:S(2)}) collective-permute-start(f32[8,3,32,128]{3,2,1,0:T(8,128)S(1)} %all-to-all-done.1.refs_0_), channel_id=1, source_target_pairs={{0,16},{8,24},{16,0},{24,8},{1,17},{9,25},{17,1},{25,9},{2,18},{10... | collective-permute-start | bytes 1179656 | tf_op jit(solution)/shard_map/ppermute | solution.py:701
  27.7 17.9 %collective-permute-start.2 = (f32[8,3,32,128]{3,2,1,0:T(8,128)S(1)}, f32[8,3,32,128]{3,2,1,0:T(8,128)S(1)}, u32[]{:S(2)}, u32[]{:S(2)}) collective-permute-start(f32[8,3,32,128]{3,2,1,0:T(8,128)S(1)} %all-to-all-done.1.refs_0_), channel_id=1, source_target_pairs={{0,24},{8,0},{16,8},{24,16},{1,25},{9,1},{17,9},{25,17},{2,26},{10... | collective-permute-start | bytes 1179656 | tf_op jit(solution)/shard_map/ppermute | solution.py:701
  36.6 9.1 %copy-start.23 = (f32[8,3,32,128]{3,2,1,0:T(8,128)}, f32[8,3,32,128]{3,2,1,0:T(8,128)S(1)}, u32[]{:S(2)}) copy-start(f32[8,3,32,128]{3,2,1,0:T(8,128)S(1)} %collective-permute-done.4.refs_3_) | copy-start | bytes 1179652
  72.1 66.6 %all-to-all-start.2 = ((f32[8,2,8,32,128]{4,3,2,1,0:T(8,128)}), f32[8,2,8,32,128]{4,3,2,1,0:T(8,128)}, u32[]{:S(2)}, u32[]{:S(2)}) async-start(f32[8,2,8,32,128]{4,3,2,1,0:T(8,128)} %get-tuple-element.31.refs_4_), calls=%async_computation.2 | async-start | bytes 4194304 | tf_op jit(solution)/shard_map/all_to_all | solution.py:696
  82.1 7.0 %copy-start.22 = (f32[8,2,2,32,128]{4,3,2,1,0:T(8,128)S(1)}, f32[8,2,2,32,128]{4,3,2,1,0:T(8,128)}, u32[]{:S(2)}) copy-start(f32[8,2,2,32,128]{4,3,2,1,0:T(8,128)} %get-tuple-element.28._) | copy-start | bytes 1572868
  85.1 71.5 %collective-permute-start.5 = (f32[8,2,8,32,128]{4,3,2,1,0:T(8,128)}, f32[8,2,8,32,128]{4,3,2,1,0:T(8,128)S(1)}, u32[]{:S(2)}, u32[]{:S(2)}) collective-permute-start(f32[8,2,8,32,128]{4,3,2,1,0:T(8,128)} %pieces.2), channel_id=1, source_target_pairs={{0,24},{8,0},{16,8},{24,16},{1,25},{9,1},{17,9},{25,17},{2,26},{10... | collective-permute-start | bytes 6291464 | tf_op jit(solution)/shard_map/ppermute | solution.py:701
  87.3 49.2 %collective-permute-start = (f32[8,2,2,32,128]{4,3,2,1,0:T(8,128)S(1)}, f32[8,2,2,32,128]{4,3,2,1,0:T(8,128)S(1)}, u32[]{:S(2)}, u32[]{:S(2)}) collective-permute-start(f32[8,2,2,32,128]{4,3,2,1,0:T(8,128)S(1)} %copy-done.27), channel_id=1, source_target_pairs={{0,1},{1,2},{2,3},{3,4},{4,5},{5,6},{6,7},{7,0},{8,9},{9,10},{10,1... | collective-permute-start | bytes 1572872 | tf_op jit(solution)/shard_map/ppermute | solution.py:701
  89.1 49.7 %collective-permute-start.1 = (f32[8,2,2,32,128]{4,3,2,1,0:T(8,128)S(1)}, f32[8,2,2,32,128]{4,3,2,1,0:T(8,128)S(1)}, u32[]{:S(2)}, u32[]{:S(2)}) collective-permute-start(f32[8,2,2,32,128]{4,3,2,1,0:T(8,128)S(1)} %copy-done.22), channel_id=1, source_target_pairs={{0,7},{1,0},{2,1},{3,2},{4,3},{5,4},{6,5},{7,6},{8,15},{9,8},{10,9... | collective-permute-start | bytes 1572872 | tf_op jit(solution)/shard_map/ppermute | solution.py:701
  141.7 25.5 %collective-permute-start.6 = (f32[8,2,2,32,128]{4,3,2,1,0:T(8,128)}, f32[8,2,2,32,128]{4,3,2,1,0:T(8,128)S(1)}, u32[]{:S(2)}, u32[]{:S(2)}) collective-permute-start(f32[8,2,2,32,128]{4,3,2,1,0:T(8,128)} %get-tuple-element.35), channel_id=1, source_target_pairs={{0,1},{1,2},{2,3},{3,4},{4,5},{5,6},{6,7},{7,0},{8,9},{9,10},{10,1... | collective-permute-start | bytes 1572872 | tf_op jit(solution)/shard_map/ppermute | solution.py:701
  142.4 24.9 %collective-permute-start.7 = (f32[8,2,2,32,128]{4,3,2,1,0:T(8,128)}, f32[8,2,2,32,128]{4,3,2,1,0:T(8,128)S(1)}, u32[]{:S(2)}, u32[]{:S(2)}) collective-permute-start(f32[8,2,2,32,128]{4,3,2,1,0:T(8,128)} %get-tuple-element.32._), channel_id=1, source_target_pairs={{0,7},{1,0},{2,1},{3,2},{4,3},{5,4},{6,5},{7,6},{8,15},{9,8},{10,9... | collective-permute-start | bytes 1572872 | tf_op jit(solution)/shard_map/ppermute | solution.py:701
  145.3 22.0 %collective-permute-start.8 = (f32[8,2,2,32,128]{4,3,2,1,0:T(8,128)}, f32[8,2,2,32,128]{4,3,2,1,0:T(8,128)S(1)}, u32[]{:S(2)}, u32[]{:S(2)}) collective-permute-start(f32[8,2,2,32,128]{4,3,2,1,0:T(8,128)} %get-tuple-element.33.refs_4_), channel_id=1, source_target_pairs={{0,24},{8,0},{16,8},{24,16},{1,25},{9,1},{17,9},{25,17},{2,26},{10... | collective-permute-start | bytes 1572872 | tf_op jit(solution)/shard_map/ppermute | solution.py:701
  168.4 6.9 %copy-start.28 = (f32[2,256,128]{2,1,0:T(8,128)S(1)}, f32[2,256,128]{2,1,0:T(8,128)}, u32[]{:S(2)}) copy-start(f32[2,256,128]{2,1,0:T(8,128)} %get-tuple-element.40) | copy-start | bytes 786436
  168.4 63.4 %all-to-all-start.3 = ((f32[8,2,8,32,128]{4,3,2,1,0:T(8,128)}), f32[8,2,8,32,128]{4,3,2,1,0:T(8,128)S(1)}, u32[]{:S(2)}, u32[]{:S(2)}) async-start(f32[8,2,8,32,128]{4,3,2,1,0:T(8,128)} %after.2.refs_6_.refs_5_.refs_0_), calls=%async_computation.3 | async-start | bytes 4194304 | tf_op jit(solution)/shard_map/all_to_all | solution.py:696
  173.3 35.8 %collective-permute-start.9 = (f32[8,2,6,32,128]{4,3,2,1,0:T(8,128)}, f32[8,2,6,32,128]{4,3,2,1,0:T(8,128)S(1)}, u32[]{:S(2)}, u32[]{:S(2)}) collective-permute-start(f32[8,2,6,32,128]{4,3,2,1,0:T(8,128)} %get-tuple-element.36), channel_id=1, source_target_pairs={{0,24},{8,0},{16,8},{24,16},{1,25},{9,1},{17,9},{25,17},{2,26},{10... | collective-permute-start | bytes 4718600 | tf_op jit(solution)/shard_map/ppermute | solution.py:701
  173.6 50.9 %collective-permute-start.10 = (f32[2,256,128]{2,1,0:T(8,128)}, f32[2,256,128]{2,1,0:T(8,128)S(1)}, u32[]{:S(2)}, u32[]{:S(2)}) collective-permute-start(f32[2,256,128]{2,1,0:T(8,128)} %get-tuple-element.38), channel_id=1, source_target_pairs={{0,1},{1,2},{2,3},{3,4},{4,5},{5,6},{6,7},{7,0},{8,9},{9,10},{10,1... | collective-permute-start | bytes 786440 | tf_op jit(solution)/shard_map/ppermute | solution.py:701
  175.3 53.7 %collective-permute-start.12 = (f32[2,256,128]{2,1,0:T(8,128)S(1)}, f32[2,256,128]{2,1,0:T(8,128)S(1)}, u32[]{:S(2)}, u32[]{:S(2)}) collective-permute-start(f32[2,256,128]{2,1,0:T(8,128)S(1)} %copy-done.28), channel_id=1, source_target_pairs={{0,7},{1,0},{2,1},{3,2},{4,3},{5,4},{6,5},{7,6},{8,15},{9,8},{10,9... | collective-permute-start | bytes 786440 | tf_op jit(solution)/shard_map/ppermute | solution.py:701
  219.9 10.3 %collective-permute-start.11 = (f32[2,256,128]{2,1,0:T(8,128)}, f32[2,256,128]{2,1,0:T(8,128)S(1)}, u32[]{:S(2)}, u32[]{:S(2)}) collective-permute-start(f32[2,256,128]{2,1,0:T(8,128)} %get-tuple-element.39), channel_id=1, source_target_pairs={{0,1},{1,2},{2,3},{3,4},{4,5},{5,6},{6,7},{7,0},{8,9},{9,10},{10,1... | collective-permute-start | bytes 786440 | tf_op jit(solution)/shard_map/ppermute | solution.py:701
  222.2 9.7 %collective-permute-start.13 = (f32[2,256,128]{2,1,0:T(8,128)}, f32[2,256,128]{2,1,0:T(8,128)S(1)}, u32[]{:S(2)}, u32[]{:S(2)}) collective-permute-start(f32[2,256,128]{2,1,0:T(8,128)} %get-tuple-element.41), channel_id=1, source_target_pairs={{0,7},{1,0},{2,1},{3,2},{4,3},{5,4},{6,5},{7,6},{8,15},{9,8},{10,9... | collective-permute-start | bytes 786440 | tf_op jit(solution)/shard_map/ppermute | solution.py:701
  224.5 7.3 %copy-start.18 = (f32[2,256,128]{2,1,0:T(8,128)}, f32[2,256,128]{2,1,0:T(8,128)S(1)}, u32[]{:S(2)}) copy-start(f32[2,256,128]{2,1,0:T(8,128)S(1)} %collective-permute-done.10.refs_1_.refs_2_) | copy-start | bytes 786436
  233.3 49.0 %all-to-all-start.4 = ((f32[8,2,8,32,128]{4,3,2,1,0:T(8,128)}), f32[8,2,8,32,128]{4,3,2,1,0:T(8,128)S(1)}, u32[]{:S(2)}, u32[]{:S(2)}) async-start(f32[8,2,8,32,128]{4,3,2,1,0:T(8,128)} %after.3.refs_1_), calls=%async_computation.4 | async-start | bytes 4194304 | tf_op jit(solution)/shard_map/all_to_all | solution.py:696
  283.6 109.9 %all-to-all-start.5 = ((f32[8,34,32,128]{3,2,1,0:T(8,128)}), f32[8,34,32,128]{3,2,1,0:T(8,128)}, u32[]{:S(2)}, u32[]{:S(2)}) async-start(f32[8,34,32,128]{3,2,1,0:T(8,128)} %adjoint_step.1._), calls=%async_computation.5 | async-start | bytes 8912896 | tf_op jit(solution)/shard_map/all_to_all | solution.py:696
  291.6 10.2 %copy-start.26 = (f32[2,4,64,128]{3,2,1,0:T(8,128)S(1)}, f32[2,4,64,128]{3,2,1,0:T(8,128)}, u32[]{:S(2)}) copy-start(f32[2,4,64,128]{3,2,1,0:T(8,128)} %get-tuple-element.46) | copy-start | bytes 786436
  291.6 101.9 %copy-start = (f32[8,2,8,32,128]{4,3,2,1,0:T(8,128)S(1)}, f32[8,2,8,32,128]{4,3,2,1,0:T(8,128)}, u32[]{:S(2)}) copy-start(f32[8,2,8,32,128]{4,3,2,1,0:T(8,128)} %get-tuple-element.26.refs_3_) | copy-start | bytes 6291460
  291.6 101.9 %copy-start.6 = (f32[64,32,128]{2,1,0:T(8,128)S(1)}, f32[64,32,128]{2,1,0:T(8,128)}, u32[]{:S(2)}) copy-start(f32[64,32,128]{2,1,0:T(8,128)} %get-tuple-element.45) | copy-start | bytes 3145732
  291.6 99.3 %collective-permute-start.16 = (f32[8,2,8,32,128]{4,3,2,1,0:T(8,128)}, f32[8,2,8,32,128]{4,3,2,1,0:T(8,128)S(1)}, u32[]{:S(2)}, u32[]{:S(2)}) collective-permute-start(f32[8,2,8,32,128]{4,3,2,1,0:T(8,128)} %copy-done.8), channel_id=1, source_target_pairs={{0,8},{8,16},{16,24},{24,0},{1,9},{9,17},{17,25},{25,1},{2,10},{10... | collective-permute-start | bytes 6291464 | tf_op jit(solution)/shard_map/ppermute | solution.py:701
  300.5 91.7 %collective-permute-start.17 = (f32[8,2,8,32,128]{4,3,2,1,0:T(8,128)}, f32[8,2,8,32,128]{4,3,2,1,0:T(8,128)S(1)}, u32[]{:S(2)}, u32[]{:S(2)}) collective-permute-start(f32[8,2,8,32,128]{4,3,2,1,0:T(8,128)} %get-tuple-element.47), channel_id=1, source_target_pairs={{0,8},{8,16},{16,24},{24,0},{1,9},{9,17},{17,25},{25,1},{2,10},{10... | collective-permute-start | bytes 6291464 | tf_op jit(solution)/shard_map/ppermute | solution.py:701
  301.8 89.1 %collective-permute-start.15 = (f32[4,64,128]{2,1,0:T(8,128)S(1)}, f32[4,64,128]{2,1,0:T(8,128)S(1)}, u32[]{:S(2)}, u32[]{:S(2)}) collective-permute-start(f32[4,64,128]{2,1,0:T(8,128)S(1)} %get-tuple-element.48), channel_id=1, source_target_pairs={{1,0},{2,1},{3,2},{4,3},{5,4},{6,5},{7,6},{9,8},{10,9},{11,10},{12... | collective-permute-start | bytes 393224 | tf_op jit(solution)/shard_map/ppermute | solution.py:723
  304.7 86.2 %collective-permute-start.14 = (f32[4,64,128]{2,1,0:T(8,128)S(1)}, f32[4,64,128]{2,1,0:T(8,128)S(1)}, u32[]{:S(2)}, u32[]{:S(2)}) collective-permute-start(f32[4,64,128]{2,1,0:T(8,128)S(1)} %get-tuple-element.49), channel_id=1, source_target_pairs={{0,1},{1,2},{2,3},{3,4},{4,5},{5,6},{6,7},{8,9},{9,10},{10,11},{11... | collective-permute-start | bytes 393224 | tf_op jit(solution)/shard_map/ppermute | solution.py:722
  (21 other events, 31.8 us)

commit v13 on v9

--- a/solution.py
+++ b/solution.py
@@ -449,25 +449,29 @@
     )[0]
 
 
-def outer_kernel(chunks, _before, _after, low_rows, high_rows, *refs):
-    *again, sem = refs
+def outer_kernel(count, chunks, *refs):
+    *outs, sem = refs[-count - 1 :]
     block = chunks.shape[2]
     low, high = chunks.at[:, :, pl.ds(0, 2)], chunks.at[:, :, pl.ds(block - 2, 2)]
-    pairs = [(low, low_rows), (high, high_rows)]
-    pairs += [(chunks.at[:, :, span], part) for part, span in spans(again, 2)]
+    pairs = [(low, outs[0]), (high, outs[1])]
+    pairs += [(chunks.at[:, :, span], part) for part, span in spans(outs[2:], 2)]
     wait_all(start_all(pairs, sem))
 
 
-def outer_rows(chunks, later, pieces):
+def pieces_kernel(count, chunks, *refs):
+    *outs, sem = refs[-count - 1 :]
+    wait_all(start_all([(chunks.at[:, :, span], part) for part, span in spans(outs, 2)], sem))
+
+
+def row_parts(kernel, chunks, later, sizes, name):
     slabs, count, _, depth, width = chunks.shape
-    rows = [((slabs, count, size, depth, width), whole()) for size in (2, 2, *pieces)]
-    return call(
-        outer_kernel,
+    return call(
+        functools.partial(kernel, len(sizes)),
         [(chunks, anywhere())] + [(x, anywhere()) for x in later],
-        rows,
-        [dmas(len(rows))],
+        [((slabs, count, size, depth, width), whole()) for size in sizes],
+        [dmas(len(sizes))],
         0,
-        "outer_rows",
+        name,
     )
 
 
@@ -722,21 +726,23 @@
     below = lax.ppermute(ends[1], "slab", forward)
     above = lax.ppermute(ends[0], "slab", [(i, j) for j, i in forward])
 
-    own, outer, targets, later = [], [], [], (visc_share, visc_share)
-    few = max(1, 3 * block // 8)
-    for part, pieces in ((main_half, (block,)), (main_other, (few, block - few))):
-        low_rows, high_rows, *again = outer_rows(part, later, pieces)
-        low_in = around(high_rows, "slab", 1)
-        high_in = around(low_rows, "slab", -1)
-        own.append((low_in, part, high_in))
-        outer.append(low_rows)
-        targets.append([around(piece, "seg", -1) for piece in again])
-        later = (low_in, high_in)
-
     mats = mat_high, mat_low
-    first_half = first_step(*own[0], outer[1], frame, *mats)
+    low_rows, high_rows, again = row_parts(
+        outer_kernel, main_half, (visc_share,), (2, 2, block), "outer_rows"
+    )
+    own = [(around(high_rows, "slab", 1), main_half, around(low_rows, "slab", -1))]
+    target = around(again, "seg", -1)
+    first_half = first_step(*own[0], frame, frame, *mats)
+
+    later = (own[0][0], own[0][2], first_half)
+    low_rows, high_rows = row_parts(outer_kernel, main_other, later, (2, 2), "outer_rows")
+    own.append((around(high_rows, "slab", 1), main_other, around(low_rows, "slab", -1)))
+    few = max(1, block // 8)
+    parts = row_parts(pieces_kernel, main_other, (low_rows,), (few, block - few), "pieces")
+    targets = [[target], [around(part, "seg", -1) for part in parts]]
+
     out, low_edge, high_edge = second_step(
-        first_half, first_half, frame, *mats, W, targets[0], ()
+        first_half, first_half, frame, *mats, W, targets[0], (parts[0],)
     )
     out = after(out, (own[1][0], own[1][2], targets[1][0]))
     first_other = carried_step(own[1], own[0], out, frame, *mats)

time: 405 us -> 411 us (1.015)
  waiting for transfers between devices: 231 us -> 236 us
    pallas_call x16 -> x17, Pallas kernels: 103 us -> 104 us  [call(): pl.pallas_call(kernel, in_specs=[spec for _, spec in ins], out_specs=tupl...]
  transfers between devices with their start and end apart: 24 -> 24, of which waited for: 13 -> 11; matrix products, arithmetic and copies ran while one was open for 0% -> 0% of each run, Pallas kernels for 21% -> 21%
where the time goes in v13:
time: 411 us; the launch traced here: 410 us
  waiting for transfers between devices  236 us (57%)
  Pallas kernels  104 us (25%)
  starting transfers between devices  59.5 us (14%)
  local copies, waits for them, and re-layouts  10.1 us (2%)
    pallas_call x17, Pallas kernels, call(): pl.pallas_call(kernel, in_specs=[spec for _, spec in ins], out_specs=tupl...  104 us
    ppermute x16, waiting for transfers between devices, around(): lax.ppermute(value, axis, [(i, (i + steps) % count) for i in range(count)])  102 us
    ppermute x1, waiting for transfers between devices, local(): above = lax.ppermute(ends[0], 'slab', [(i, j) for j, i in forward])  83.2 us
    all_to_all x6, waiting for transfers between devices, exchange(): lax.all_to_all(chunks, 'slab', split_axis=0, concat_axis=0, tiled=True)  50.1 us
    all_to_all x6, starting transfers between devices, exchange(): lax.all_to_all(chunks, 'slab', split_axis=0, concat_axis=0, tiled=True)  37.3 us
    ppermute x16, starting transfers between devices, around(): lax.ppermute(value, axis, [(i, (i + steps) % count) for i in range(count)])  16.4 us
    unnamed x46, local copies, waits for them, and re-layouts  10 us
  transfers between devices with their start and end apart: 24, of which 11 were waited for; matrix products, arithmetic and copies ran while one was open for 0% of the time, Pallas kernels for 21%

profile of v13, /device:TPU:9, one launch (start us, length us, event | category | flops | bytes accessed | tf_op | source)
XLA Modules:
  0.0 410.5 jit_solution(4232669560171600479)
XLA Ops:
  0.6 2.9 visc_chunks.1
  3.6 5.6 %all-to-all-start.1 = ((f32[8,3,32,128]{3,2,1,0:T(8,128)}), f32[8,3,32,128]{3,2,1,0:T(8,128)S(1)}, u32[]{:S(2)}, u32[]{:S(2)}) async-start(f32[8,3,32,128]{3,2,1,0:T(8,128)} %get-tuple-element.26.refs_0_), calls=%async_computation.1 | async-start | bytes 786432 | tf_op jit(solution)/shard_map/all_to_all | solution.py:700
  9.2 4.2 %to_chunks.2 = (f32[8,2,8,32,128]{4,3,2,1,0:T(8,128)}, f32[2,4,64,128]{3,2,1,0:T(8,128)}) custom-call(f32[4,2048,128]{2,1,0:T(8,128)} %bitcast.10, f32[8,3,32,128]{3,2,1,0:T(8,128)} %get-tuple-element.26.refs_0_), custom_call_target="tpu_custom_call" | custom-call | bytes 4587520 | tf_op jit(solution)/shard_map/to_chunks/pallas_call | solution.py:42
  13.4 5.3 %all-to-all-done.1.refs_0_ = f32[8,3,32,128]{3,2,1,0:T(8,128)S(1)} async-done(((f32[8,3,32,128]{3,2,1,0:T(8,128)}), f32[8,3,32,128]{3,2,1,0:T(8,128)S(1)}, u32[]{:S(2)}, u32[]{:S(2)}) %all-to-all-start.1) | async-done | bytes 393248 | tf_op jit(solution)/shard_map/all_to_all | solution.py:700
  18.7 6.6 %all-to-all-start = ((f32[8,2,8,32,128]{4,3,2,1,0:T(8,128)}), f32[8,2,8,32,128]{4,3,2,1,0:T(8,128)S(1)}, u32[]{:S(2)}, u32[]{:S(2)}) async-start(f32[8,2,8,32,128]{4,3,2,1,0:T(8,128)} %get-tuple-element.27.refs_4_), calls=%async_computation | async-start | bytes 4194304 | tf_op jit(solution)/shard_map/all_to_all | solution.py:700
  28.9 2.9 split.1
  31.8 4.7 %collective-permute-done.4.refs_3_ = f32[8,3,32,128]{3,2,1,0:T(8,128)S(1)} collective-permute-done((f32[8,3,32,128]{3,2,1,0:T(8,128)S(1)}, f32[8,3,32,128]{3,2,1,0:T(8,128)S(1)}, u32[]{:S(2)}, u32[]{:S(2)}) %collective-permute-start.4) | collective-permute-done | bytes 393248 | tf_op jit(solution)/shard_map/ppermute | solution.py:705
  36.6 9.1 %collective-permute-done.3.refs_2_ = f32[8,3,32,128]{3,2,1,0:T(8,128)S(1)} collective-permute-done((f32[8,3,32,128]{3,2,1,0:T(8,128)S(1)}, f32[8,3,32,128]{3,2,1,0:T(8,128)S(1)}, u32[]{:S(2)}, u32[]{:S(2)}) %collective-permute-start.3) | collective-permute-done | bytes 393248 | tf_op jit(solution)/shard_map/ppermute | solution.py:705
  47.1 2.8 to_frame.1._.refs_0_.refs_7_.refs_8_
  49.9 4.2 %to_chunks.3 = (f32[8,2,8,32,128]{4,3,2,1,0:T(8,128)}, f32[2,4,64,128]{3,2,1,0:T(8,128)}) custom-call(f32[4,2048,128]{2,1,0:T(8,128)} %bitcast.11, f32[12,256,128]{2,1,0:T(8,128)} %to_frame.1._.refs_0_.refs_7_.refs_8_, bf16[4,256,256]{2,1,0:T(8,128)(2,1)} %get-tuple-element.30.refs_1_.refs_8_), custom_call_target="tpu_custom_call" | custom-call | bytes 6815744 | tf_op jit(solution)/shard_map/to_chunks/pallas_call | solution.py:42
  54.1 16.7 %all-to-all-done.chunks.main.refs_4_ = f32[8,2,8,32,128]{4,3,2,1,0:T(8,128)S(1)} async-done(((f32[8,2,8,32,128]{4,3,2,1,0:T(8,128)}), f32[8,2,8,32,128]{4,3,2,1,0:T(8,128)S(1)}, u32[]{:S(2)}, u32[]{:S(2)}) %all-to-all-start) | async-done | bytes 2097184 | tf_op jit(solution)/shard_map/all_to_all | solution.py:700
  72.1 7.8 %all-to-all-start.2 = ((f32[8,2,8,32,128]{4,3,2,1,0:T(8,128)}), f32[8,2,8,32,128]{4,3,2,1,0:T(8,128)}, u32[]{:S(2)}, u32[]{:S(2)}) async-start(f32[8,2,8,32,128]{4,3,2,1,0:T(8,128)} %get-tuple-element.33.refs_5_), calls=%async_computation.2 | async-start | bytes 4194304 | tf_op jit(solution)/shard_map/all_to_all | solution.py:700
  80.0 3.6 outer_rows.2
  87.5 49.2 %collective-permute-done.low_in.refs_0_.refs_3_ = f32[8,2,2,32,128]{4,3,2,1,0:T(8,128)S(1)} collective-permute-done((f32[8,2,2,32,128]{4,3,2,1,0:T(8,128)}, f32[8,2,2,32,128]{4,3,2,1,0:T(8,128)S(1)}, u32[]{:S(2)}, u32[]{:S(2)}) %collective-permute-start) | collective-permute-done | bytes 524320 | tf_op jit(solution)/shard_map/ppermute | solution.py:705
  139.3 9.1 %first_step.1.refs_2_.first.with_w.refs_6_ = f32[2,10,272,128]{3,2,1,0:T(8,128)} custom-call(f32[8,2,2,32,128]{4,3,2,1,0:T(8,128)} %copy-done.3, f32[8,2,8,32,128]{4,3,2,1,0:T(8,128)} %copy-done, f32[8,2,2,32,128]{4,3,2,1,0:T(8,128)} %copy-done.4, f32[12,256,128]{2,1,0:T(8,128)} %to_frame.1._.refs_0_.refs_7_.refs_8_, ...), custom_call_target="tpu_custom_call" | custom-call | flops 1006632960 | bytes 8388608 | tf_op jit(solution)/shard_map/first_step/pallas_call | solution.py:42
  151.5 3.0 pieces.1
  158.0 9.3 %second_step.2 = (f32[8,2,8,32,128]{4,3,2,1,0:T(8,128)}, f32[2,256,128]{2,1,0:T(8,128)}, f32[2,256,128]{2,1,0:T(8,128)}) custom-call(f32[2,10,272,128]{3,2,1,0:T(8,128)} %first_step.1.refs_2_.first.with_w.refs_6_, f32[2,10,272,128]{3,2,1,0:T(8,128)} %first_step.1.refs_2_.first.with_w.refs_6_, f32[12,256,128]{2,1,0:T(8,128)} %to_frame.1._.refs_0_.refs_7_.refs_8_, ...), custom_call_target="tpu_custom_call" | custom-call | flops 805306368 | bytes 11599872 | tf_op jit(solution)/shard_map/second_step/pallas_call | solution.py:42
  168.4 4.9 %all-to-all-start.3 = ((f32[8,2,8,32,128]{4,3,2,1,0:T(8,128)}), f32[8,2,8,32,128]{4,3,2,1,0:T(8,128)S(1)}, u32[]{:S(2)}, u32[]{:S(2)}) async-start(f32[8,2,8,32,128]{4,3,2,1,0:T(8,128)} %after.2.refs_6_.refs_5_.refs_0_), calls=%async_computation.3 | async-start | bytes 4194304 | tf_op jit(solution)/shard_map/all_to_all | solution.py:700
  175.3 9.7 %carried_step.1.first.refs_7_ = f32[2,10,272,128]{3,2,1,0:T(8,128)} custom-call(f32[8,2,2,32,128]{4,3,2,1,0:T(8,128)} %copy-done.8, f32[8,2,8,32,128]{4,3,2,1,0:T(8,128)} %all-to-all-done.2.chunks.refs_1_, f32[8,2,2,32,128]{4,3,2,1,0:T(8,128)} %copy-done.9, f32[8,2,2,32,128]{4,3,2,1,0:T(8,128)} %copy-done.3, f32[8,2,8,32,128]{4,3,2,1,0:T(8,128)} %copy-done, ...), custom_call_target="tpu_custom_call" | custom-call | flops 1006632960 | bytes 12058624 | tf_op jit(solution)/shard_map/carried_step/pallas_call | solution.py:42
  185.0 29.8 %collective-permute-done.9.refs_4_ = f32[8,2,7,32,128]{4,3,2,1,0:T(8,128)S(1)} collective-permute-done((f32[8,2,7,32,128]{4,3,2,1,0:T(8,128)}, f32[8,2,7,32,128]{4,3,2,1,0:T(8,128)S(1)}, u32[]{:S(2)}, u32[]{:S(2)}) %collective-permute-start.9) | collective-permute-done | bytes 1835040 | tf_op jit(solution)/shard_map/ppermute | solution.py:705
  216.0 9.6 %second_step.3 = (f32[8,2,8,32,128]{4,3,2,1,0:T(8,128)}, f32[2,256,128]{2,1,0:T(8,128)}, f32[2,256,128]{2,1,0:T(8,128)}) custom-call(f32[2,10,272,128]{3,2,1,0:T(8,128)} %carried_step.1.first.refs_7_, f32[2,10,272,128]{3,2,1,0:T(8,128)} %first_step.1.refs_2_.first.with_w.refs_6_, f32[12,256,128]{2,1,0:T(8,128)} %to_frame.1._.refs_0_.refs_7_.refs_8_, ...), custom_call_target="tpu_custom_call" | custom-call | flops 805306368 | bytes 13434880 | tf_op jit(solution)/shard_map/second_step/pallas_call | solution.py:42
  227.9 3.7 collective-permute-done.11.refs_2_.refs_3_
  231.7 4.0 collective-permute-done.13.refs_4_.refs_5_
  237.1 4.5 %all-to-all-start.4 = ((f32[8,2,8,32,128]{4,3,2,1,0:T(8,128)}), f32[8,2,8,32,128]{4,3,2,1,0:T(8,128)}, u32[]{:S(2)}, u32[]{:S(2)}) async-start(f32[8,2,8,32,128]{4,3,2,1,0:T(8,128)} %after.3.refs_1_), calls=%async_computation.4 | async-start | bytes 4194304 | tf_op jit(solution)/shard_map/all_to_all | solution.py:700
  241.5 17.4 %adjoint_step.1._ = f32[8,34,32,128]{3,2,1,0:T(8,128)} custom-call(f32[8,2,8,32,128]{4,3,2,1,0:T(8,128)} %after.2.refs_6_.refs_5_.refs_0_, f32[8,2,8,32,128]{4,3,2,1,0:T(8,128)} %after.3.refs_1_, f32[2,256,128]{2,1,0:T(8,128)} %copy-done.11, f32[2,256,128]{2,1,0:T(8,128)} %copy-done.13, f32[2,256,128]{2,1,0:T(8,128)} %copy-done.12, ...), custom_call_target="tpu_custom_call" | custom-call | flops 3623878656 | bytes 14483456 | tf_op jit(solution)/shard_map/adjoint_step/pallas_call | solution.py:42
  259.0 28.1 %all-to-all-done.4.other = f32[8,2,8,32,128]{4,3,2,1,0:T(8,128)} async-done(((f32[8,2,8,32,128]{4,3,2,1,0:T(8,128)}), f32[8,2,8,32,128]{4,3,2,1,0:T(8,128)}, u32[]{:S(2)}, u32[]{:S(2)}) %all-to-all-start.4) | async-done | bytes 2097184 | tf_op jit(solution)/shard_map/all_to_all | solution.py:700
  287.1 7.8 %all-to-all-start.5 = ((f32[8,34,32,128]{3,2,1,0:T(8,128)}), f32[8,34,32,128]{3,2,1,0:T(8,128)}, u32[]{:S(2)}, u32[]{:S(2)}) async-start(f32[8,34,32,128]{3,2,1,0:T(8,128)} %adjoint_step.1._), calls=%async_computation.5 | async-start | bytes 8912896 | tf_op jit(solution)/shard_map/all_to_all | solution.py:700
  295.1 8.6 %to_planes.1 = (f32[8192,128]{1,0:T(8,128)}, f32[8,2,8,32,128]{4,3,2,1,0:T(8,128)}) custom-call(f32[8,2,8,32,128]{4,3,2,1,0:T(8,128)} %copy-done.1, f32[8,2,8,32,128]{4,3,2,1,0:T(8,128)} %all-to-all-done.4.other, f32[8,34,32,128]{3,2,1,0:T(8,128)} %adjoint_step.1._), custom_call_target="tpu_custom_call" | custom-call | bytes 8650752 | tf_op jit(solution)/shard_map/to_planes/pallas_call | solution.py:42
  305.1 2.8 collective-permute-start.15
  307.9 3.0 collective-permute-start.14
  310.9 83.2 %collective-permute-done.15.refs_2_ = f32[4,64,128]{2,1,0:T(8,128)S(1)} collective-permute-done((f32[4,64,128]{2,1,0:T(8,128)S(1)}, f32[4,64,128]{2,1,0:T(8,128)S(1)}, u32[]{:S(2)}, u32[]{:S(2)}) %collective-permute-start.15) | collective-permute-done | bytes 131104 | tf_op jit(solution)/shard_map/ppermute | solution.py:727
  395.5 14.8 %last_step.1 = f32[4,2048,128]{2,1,0:T(8,128)} custom-call(f32[8,8,32,128]{3,2,1,0:T(8,128)} %bitcast.13, f32[4,64,128]{2,1,0:T(8,128)} %copy-done.21, f32[4,64,128]{2,1,0:T(8,128)} %copy-done.20, f32[8,34,32,128]{3,2,1,0:T(8,128)} %all-to-all-done.5.refs_3_, f32[8,2,8,32,128]{4,3,2,1,0:T(8,128)} %get-tuple-element.27.refs_4_, ...), custom_call_target="tpu_custom_call" | custom-call | flops 31457280 | bytes 14155776 | tf_op jit(solution)/shard_map/last_step/pallas_call | solution.py:42
  (80 shorter events, 30.5 us)
Async XLA Ops:
  3.6 15.1 %all-to-all-start.1 = ((f32[8,3,32,128]{3,2,1,0:T(8,128)}), f32[8,3,32,128]{3,2,1,0:T(8,128)S(1)}, u32[]{:S(2)}, u32[]{:S(2)}) async-start(f32[8,3,32,128]{3,2,1,0:T(8,128)} %get-tuple-element.26.refs_0_), calls=%async_computation.1 | async-start | bytes 786432 | tf_op jit(solution)/shard_map/all_to_all | solution.py:700
  18.7 9.1 %copy-start.5 = (f32[8,3,32,128]{3,2,1,0:T(8,128)}, f32[8,3,32,128]{3,2,1,0:T(8,128)S(1)}, u32[]{:S(2)}) copy-start(f32[8,3,32,128]{3,2,1,0:T(8,128)S(1)} %all-to-all-done.1.refs_0_) | copy-start | bytes 1179652
  18.7 52.1 %all-to-all-start = ((f32[8,2,8,32,128]{4,3,2,1,0:T(8,128)}), f32[8,2,8,32,128]{4,3,2,1,0:T(8,128)S(1)}, u32[]{:S(2)}, u32[]{:S(2)}) async-start(f32[8,2,8,32,128]{4,3,2,1,0:T(8,128)} %get-tuple-element.27.refs_4_), calls=%async_computation | async-start | bytes 4194304 | tf_op jit(solution)/shard_map/all_to_all | solution.py:700
  25.3 11.3 %collective-permute-start.4 = (f32[8,3,32,128]{3,2,1,0:T(8,128)S(1)}, f32[8,3,32,128]{3,2,1,0:T(8,128)S(1)}, u32[]{:S(2)}, u32[]{:S(2)}) collective-permute-start(f32[8,3,32,128]{3,2,1,0:T(8,128)S(1)} %all-to-all-done.1.refs_0_), channel_id=1, source_target_pairs={{0,8},{8,16},{16,24},{24,0},{1,9},{9,17},{17,25},{25,1},{2,10},{10... | collective-permute-start | bytes 1179656 | tf_op jit(solution)/shard_map/ppermute | solution.py:705
  26.5 19.2 %collective-permute-start.3 = (f32[8,3,32,128]{3,2,1,0:T(8,128)S(1)}, f32[8,3,32,128]{3,2,1,0:T(8,128)S(1)}, u32[]{:S(2)}, u32[]{:S(2)}) collective-permute-start(f32[8,3,32,128]{3,2,1,0:T(8,128)S(1)} %all-to-all-done.1.refs_0_), channel_id=1, source_target_pairs={{0,16},{8,24},{16,0},{24,8},{1,17},{9,25},{17,1},{25,9},{2,18},{10... | collective-permute-start | bytes 1179656 | tf_op jit(solution)/shard_map/ppermute | solution.py:705
  27.7 17.9 %collective-permute-start.2 = (f32[8,3,32,128]{3,2,1,0:T(8,128)S(1)}, f32[8,3,32,128]{3,2,1,0:T(8,128)S(1)}, u32[]{:S(2)}, u32[]{:S(2)}) collective-permute-start(f32[8,3,32,128]{3,2,1,0:T(8,128)S(1)} %all-to-all-done.1.refs_0_), channel_id=1, source_target_pairs={{0,24},{8,0},{16,8},{24,16},{1,25},{9,1},{17,9},{25,17},{2,26},{10... | collective-permute-start | bytes 1179656 | tf_op jit(solution)/shard_map/ppermute | solution.py:705
  36.6 9.1 %copy-start.16 = (f32[8,3,32,128]{3,2,1,0:T(8,128)}, f32[8,3,32,128]{3,2,1,0:T(8,128)S(1)}, u32[]{:S(2)}) copy-start(f32[8,3,32,128]{3,2,1,0:T(8,128)S(1)} %collective-permute-done.4.refs_3_) | copy-start | bytes 1179652
  72.1 76.3 %all-to-all-start.2 = ((f32[8,2,8,32,128]{4,3,2,1,0:T(8,128)}), f32[8,2,8,32,128]{4,3,2,1,0:T(8,128)}, u32[]{:S(2)}, u32[]{:S(2)}) async-start(f32[8,2,8,32,128]{4,3,2,1,0:T(8,128)} %get-tuple-element.33.refs_5_), calls=%async_computation.2 | async-start | bytes 4194304 | tf_op jit(solution)/shard_map/all_to_all | solution.py:700
  83.6 73.1 %collective-permute-start.5 = (f32[8,2,8,32,128]{4,3,2,1,0:T(8,128)}, f32[8,2,8,32,128]{4,3,2,1,0:T(8,128)S(1)}, u32[]{:S(2)}, u32[]{:S(2)}) collective-permute-start(f32[8,2,8,32,128]{4,3,2,1,0:T(8,128)} %get-tuple-element.32), channel_id=1, source_target_pairs={{0,24},{8,0},{16,8},{24,16},{1,25},{9,1},{17,9},{25,17},{2,26},{10... | collective-permute-start | bytes 6291464 | tf_op jit(solution)/shard_map/ppermute | solution.py:705
  85.8 50.9 %collective-permute-start = (f32[8,2,2,32,128]{4,3,2,1,0:T(8,128)}, f32[8,2,2,32,128]{4,3,2,1,0:T(8,128)S(1)}, u32[]{:S(2)}, u32[]{:S(2)}) collective-permute-start(f32[8,2,2,32,128]{4,3,2,1,0:T(8,128)} %get-tuple-element.28), channel_id=1, source_target_pairs={{0,1},{1,2},{2,3},{3,4},{4,5},{5,6},{6,7},{7,0},{8,9},{9,10},{10,1... | collective-permute-start | bytes 1572872 | tf_op jit(solution)/shard_map/ppermute | solution.py:705
  87.5 51.0 %collective-permute-start.1 = (f32[8,2,2,32,128]{4,3,2,1,0:T(8,128)}, f32[8,2,2,32,128]{4,3,2,1,0:T(8,128)S(1)}, u32[]{:S(2)}, u32[]{:S(2)}) collective-permute-start(f32[8,2,2,32,128]{4,3,2,1,0:T(8,128)} %get-tuple-element.29), channel_id=1, source_target_pairs={{0,7},{1,0},{2,1},{3,2},{4,3},{5,4},{6,5},{7,6},{8,15},{9,8},{10,9... | collective-permute-start | bytes 1572872 | tf_op jit(solution)/shard_map/ppermute | solution.py:705
  150.7 16.7 %collective-permute-start.6 = (f32[8,2,2,32,128]{4,3,2,1,0:T(8,128)}, f32[8,2,2,32,128]{4,3,2,1,0:T(8,128)S(1)}, u32[]{:S(2)}, u32[]{:S(2)}) collective-permute-start(f32[8,2,2,32,128]{4,3,2,1,0:T(8,128)} %get-tuple-element.37), channel_id=1, source_target_pairs={{0,1},{1,2},{2,3},{3,4},{4,5},{5,6},{6,7},{7,0},{8,9},{9,10},{10,1... | collective-permute-start | bytes 1572872 | tf_op jit(solution)/shard_map/ppermute | solution.py:705
  151.5 15.8 %collective-permute-start.7 = (f32[8,2,2,32,128]{4,3,2,1,0:T(8,128)}, f32[8,2,2,32,128]{4,3,2,1,0:T(8,128)S(1)}, u32[]{:S(2)}, u32[]{:S(2)}) collective-permute-start(f32[8,2,2,32,128]{4,3,2,1,0:T(8,128)} %get-tuple-element.34.refs_0_), channel_id=1, source_target_pairs={{0,7},{1,0},{2,1},{3,2},{4,3},{5,4},{6,5},{7,6},{8,15},{9,8},{10,9... | collective-permute-start | bytes 1572872 | tf_op jit(solution)/shard_map/ppermute | solution.py:705
  154.5 12.8 %collective-permute-start.8 = (f32[8,2,1,32,128]{4,3,2,1,0:T(8,128)}, f32[8,2,1,32,128]{4,3,2,1,0:T(8,128)S(1)}, u32[]{:S(2)}, u32[]{:S(2)}) collective-permute-start(f32[8,2,1,32,128]{4,3,2,1,0:T(8,128)} %get-tuple-element.35.refs_4_), channel_id=1, source_target_pairs={{0,24},{8,0},{16,8},{24,16},{1,25},{9,1},{17,9},{25,17},{2,26},{10... | collective-permute-start | bytes 786440 | tf_op jit(solution)/shard_map/ppermute | solution.py:705
  168.4 6.9 %copy-start.22 = (f32[2,256,128]{2,1,0:T(8,128)S(1)}, f32[2,256,128]{2,1,0:T(8,128)}, u32[]{:S(2)}) copy-start(f32[2,256,128]{2,1,0:T(8,128)} %get-tuple-element.42) | copy-start | bytes 786436
  168.4 67.3 %all-to-all-start.3 = ((f32[8,2,8,32,128]{4,3,2,1,0:T(8,128)}), f32[8,2,8,32,128]{4,3,2,1,0:T(8,128)S(1)}, u32[]{:S(2)}, u32[]{:S(2)}) async-start(f32[8,2,8,32,128]{4,3,2,1,0:T(8,128)} %after.2.refs_6_.refs_5_.refs_0_), calls=%async_computation.3 | async-start | bytes 4194304 | tf_op jit(solution)/shard_map/all_to_all | solution.py:700
  173.3 41.4 %collective-permute-start.9 = (f32[8,2,7,32,128]{4,3,2,1,0:T(8,128)}, f32[8,2,7,32,128]{4,3,2,1,0:T(8,128)S(1)}, u32[]{:S(2)}, u32[]{:S(2)}) collective-permute-start(f32[8,2,7,32,128]{4,3,2,1,0:T(8,128)} %get-tuple-element.38), channel_id=1, source_target_pairs={{0,24},{8,0},{16,8},{24,16},{1,25},{9,1},{17,9},{25,17},{2,26},{10... | collective-permute-start | bytes 5505032 | tf_op jit(solution)/shard_map/ppermute | solution.py:705
  173.6 54.3 %collective-permute-start.10 = (f32[2,256,128]{2,1,0:T(8,128)}, f32[2,256,128]{2,1,0:T(8,128)S(1)}, u32[]{:S(2)}, u32[]{:S(2)}) collective-permute-start(f32[2,256,128]{2,1,0:T(8,128)} %get-tuple-element.40), channel_id=1, source_target_pairs={{0,1},{1,2},{2,3},{3,4},{4,5},{5,6},{6,7},{7,0},{8,9},{9,10},{10,1... | collective-permute-start | bytes 786440 | tf_op jit(solution)/shard_map/ppermute | solution.py:705
  175.3 52.6 %collective-permute-start.12 = (f32[2,256,128]{2,1,0:T(8,128)S(1)}, f32[2,256,128]{2,1,0:T(8,128)S(1)}, u32[]{:S(2)}, u32[]{:S(2)}) collective-permute-start(f32[2,256,128]{2,1,0:T(8,128)S(1)} %copy-done.22), channel_id=1, source_target_pairs={{0,7},{1,0},{2,1},{3,2},{4,3},{5,4},{6,5},{7,6},{8,15},{9,8},{10,9... | collective-permute-start | bytes 786440 | tf_op jit(solution)/shard_map/ppermute | solution.py:705
  225.6 6.1 %collective-permute-start.11 = (f32[2,256,128]{2,1,0:T(8,128)}, f32[2,256,128]{2,1,0:T(8,128)S(1)}, u32[]{:S(2)}, u32[]{:S(2)}) collective-permute-start(f32[2,256,128]{2,1,0:T(8,128)} %get-tuple-element.41), channel_id=1, source_target_pairs={{0,1},{1,2},{2,3},{3,4},{4,5},{5,6},{6,7},{7,0},{8,9},{9,10},{10,1... | collective-permute-start | bytes 786440 | tf_op jit(solution)/shard_map/ppermute | solution.py:705
  227.9 7.8 %collective-permute-start.13 = (f32[2,256,128]{2,1,0:T(8,128)}, f32[2,256,128]{2,1,0:T(8,128)S(1)}, u32[]{:S(2)}, u32[]{:S(2)}) collective-permute-start(f32[2,256,128]{2,1,0:T(8,128)} %get-tuple-element.43), channel_id=1, source_target_pairs={{0,7},{1,0},{2,1},{3,2},{4,3},{5,4},{6,5},{7,6},{8,15},{9,8},{10,9... | collective-permute-start | bytes 786440 | tf_op jit(solution)/shard_map/ppermute | solution.py:705
  227.9 7.8 %copy-start.11 = (f32[2,256,128]{2,1,0:T(8,128)}, f32[2,256,128]{2,1,0:T(8,128)S(1)}, u32[]{:S(2)}) copy-start(f32[2,256,128]{2,1,0:T(8,128)S(1)} %collective-permute-done.10.refs_1_.refs_2_) | copy-start | bytes 786436
  227.9 7.7 %copy-start.12 = (f32[2,256,128]{2,1,0:T(8,128)}, f32[2,256,128]{2,1,0:T(8,128)S(1)}, u32[]{:S(2)}) copy-start(f32[2,256,128]{2,1,0:T(8,128)S(1)} %collective-permute-done.12.refs_3_.refs_4_) | copy-start | bytes 786436
  231.7 4.0 copy-start.13
  237.1 50.0 %all-to-all-start.4 = ((f32[8,2,8,32,128]{4,3,2,1,0:T(8,128)}), f32[8,2,8,32,128]{4,3,2,1,0:T(8,128)}, u32[]{:S(2)}, u32[]{:S(2)}) async-start(f32[8,2,8,32,128]{4,3,2,1,0:T(8,128)} %after.3.refs_1_), calls=%async_computation.4 | async-start | bytes 4194304 | tf_op jit(solution)/shard_map/all_to_all | solution.py:700
  259.0 35.9 %copy-start.2 = (f32[8,2,8,32,128]{4,3,2,1,0:T(8,128)S(1)}, f32[8,2,8,32,128]{4,3,2,1,0:T(8,128)}, u32[]{:S(2)}) copy-start(f32[8,2,8,32,128]{4,3,2,1,0:T(8,128)} %copy-done.1) | copy-start | bytes 6291460
  287.1 108.4 %all-to-all-start.5 = ((f32[8,34,32,128]{3,2,1,0:T(8,128)}), f32[8,34,32,128]{3,2,1,0:T(8,128)}, u32[]{:S(2)}, u32[]{:S(2)}) async-start(f32[8,34,32,128]{3,2,1,0:T(8,128)} %adjoint_step.1._), calls=%async_computation.5 | async-start | bytes 8912896 | tf_op jit(solution)/shard_map/all_to_all | solution.py:700
  294.9 10.2 %copy-start.19 = (f32[2,4,64,128]{3,2,1,0:T(8,128)S(1)}, f32[2,4,64,128]{3,2,1,0:T(8,128)}, u32[]{:S(2)}) copy-start(f32[2,4,64,128]{3,2,1,0:T(8,128)} %get-tuple-element.48) | copy-start | bytes 786436
  294.9 99.3 %collective-permute-start.16 = (f32[8,2,8,32,128]{4,3,2,1,0:T(8,128)S(1)}, f32[8,2,8,32,128]{4,3,2,1,0:T(8,128)S(1)}, u32[]{:S(2)}, u32[]{:S(2)}) collective-permute-start(f32[8,2,8,32,128]{4,3,2,1,0:T(8,128)S(1)} %copy-done.2), channel_id=1, source_target_pairs={{0,8},{8,16},{16,24},{24,0},{1,9},{9,17},{17,25},{25,1},{2,10},{10... | collective-permute-start | bytes 6291464 | tf_op jit(solution)/shard_map/ppermute | solution.py:705
  303.8 91.7 %collective-permute-start.17 = (f32[8,2,8,32,128]{4,3,2,1,0:T(8,128)}, f32[8,2,8,32,128]{4,3,2,1,0:T(8,128)}, u32[]{:S(2)}, u32[]{:S(2)}) collective-permute-start(f32[8,2,8,32,128]{4,3,2,1,0:T(8,128)} %get-tuple-element.49), channel_id=1, source_target_pairs={{0,8},{8,16},{16,24},{24,0},{1,9},{9,17},{17,25},{25,1},{2,10},{10... | collective-permute-start | bytes 6291464 | tf_op jit(solution)/shard_map/ppermute | solution.py:705
  305.1 89.1 %collective-permute-start.15 = (f32[4,64,128]{2,1,0:T(8,128)S(1)}, f32[4,64,128]{2,1,0:T(8,128)S(1)}, u32[]{:S(2)}, u32[]{:S(2)}) collective-permute-start(f32[4,64,128]{2,1,0:T(8,128)S(1)} %get-tuple-element.50), channel_id=1, source_target_pairs={{1,0},{2,1},{3,2},{4,3},{5,4},{6,5},{7,6},{9,8},{10,9},{11,10},{12... | collective-permute-start | bytes 393224 | tf_op jit(solution)/shard_map/ppermute | solution.py:727
  307.9 86.2 %collective-permute-start.14 = (f32[4,64,128]{2,1,0:T(8,128)S(1)}, f32[4,64,128]{2,1,0:T(8,128)S(1)}, u32[]{:S(2)}, u32[]{:S(2)}) collective-permute-start(f32[4,64,128]{2,1,0:T(8,128)S(1)} %get-tuple-element.51), channel_id=1, source_target_pairs={{0,1},{1,2},{2,3},{3,4},{4,5},{5,6},{6,7},{8,9},{9,10},{10,11},{11... | collective-permute-start | bytes 393224 | tf_op jit(solution)/shard_map/ppermute | solution.py:726
  (15 other events, 16.8 us)

commit v14 on v9

--- a/solution.py
+++ b/solution.py
@@ -326,36 +326,6 @@
     return finish
 
 
-def first_kernel(low_in, main, high_in, _, *refs):
-    sources, (first, state, *scratch, sem) = refs[:3], refs[3:]
-    slabs, _, block, depth, _ = main.shape
-    pairs = constants(W, sources, scratch)
-    for p in range(slabs):
-        pairs += [(a.at[p], b) for a, b in rows_of(low_in, main, high_in, p, state)]
-    copies = start_all(pairs, sem)
-    clear_pads(state)
-    clear_pads(first)
-    wait_all(copies)
-    finish = first_finish(first, slabs * depth)
-    advance_rows(state, state.at[W], 0, True, scratch, block + 2, finish)
-
-
-def first_step(low_in, main, high_in, later, frame, mat_high, mat_low):
-    slabs, _, block, depth, width = main.shape
-    order = slabs * depth
-    volume = 2 * (block + 2) * order * width
-    return call(
-        first_kernel,
-        [(x, anywhere()) for x in (low_in, main, high_in, later, frame, mat_high, mat_low)],
-        [((2, block + 2, order + 2 * pad, width), whole())],
-        [vmem(2, block + 4, order + 2 * pad, width)]
-        + two_scratch(frame)
-        + [dmas(3 * slabs + 3)],
-        6 * order * volume,
-        "first_step",
-    )[0]
-
-
 def carried_kernel(*refs):
     low_in, main, high_in, low_w, main_w, high_w, _ = refs[:7]
     sources, (first, state, speeds, *scratch, sem) = refs[7:10], refs[10:]
@@ -430,6 +400,54 @@
         + [vmem(2, block, order, width), dmas(2 * slabs + 5)],
         6 * order * 2 * block * order * width,
         "second_step",
+    )
+
+
+def two_steps_kernel(low_in, main, high_in, target, _, *refs):
+    sources, (first, out, low_edge, high_edge), refs = refs[:3], refs[3:7], refs[7:]
+    state, *scratch, held, sem = refs
+    slabs, _, block, depth, _ = main.shape
+    pairs = constants(W, sources, scratch)
+    places = [held.at[:, :, pl.ds(p * depth, depth)] for p in range(slabs)]
+    for p in range(slabs):
+        pairs += [(a.at[p], b) for a, b in rows_of(low_in, main, high_in, p, state)]
+        pairs.append((target.at[p], places[p]))
+    copies = start_all(pairs, sem)
+    clear_pads(state)
+    clear_pads(first)
+    wait_all(copies)
+    finish = first_finish(first, slabs * depth)
+    advance_rows(state, state.at[W], 0, True, scratch, block + 2, finish)
+
+    def subtract(f, row, piece):
+        held[f, row] = piece - held[f, row]
+
+    advance_rows(first, first.at[W], 1, True, scratch, block, subtract)
+    copies = start_all([(places[p], out.at[p]) for p in range(slabs)], sem)
+    low_edge[...] = held[:, 0]
+    high_edge[...] = held[:, block - 1]
+    wait_all(copies)
+
+
+def two_steps(low_in, main, high_in, target, later, frame, mat_high, mat_low):
+    slabs, _, block, depth, width = main.shape
+    order = slabs * depth
+    volume = 2 * (block + 1) * order * width
+    operands = (low_in, main, high_in, target, later, frame, mat_high, mat_low)
+    return call(
+        two_steps_kernel,
+        [(x, anywhere()) for x in operands],
+        [
+            ((2, block + 2, order + 2 * pad, width), whole()),
+            (main.shape, anywhere()),
+            ((2, order, width), whole()),
+            ((2, order, width), whole()),
+        ],
+        [vmem(2, block + 4, order + 2 * pad, width)]
+        + two_scratch(frame)
+        + [vmem(2, block, order, width), dmas(4 * slabs + 3)],
+        12 * order * volume,
+        "two_steps",
     )
 
 
@@ -734,9 +752,8 @@
         later = (low_in, high_in)
 
     mats = mat_high, mat_low
-    first_half = first_step(*own[0], outer[1], frame, *mats)
-    out, low_edge, high_edge = second_step(
-        first_half, first_half, frame, *mats, W, targets[0], ()
+    first_half, out, low_edge, high_edge = two_steps(
+        *own[0], targets[0][0], outer[1], frame, *mats
     )
     out = after(out, (own[1][0], own[1][2], targets[1][0]))
     first_other = carried_step(own[1], own[0], out, frame, *mats)

time: 405 us -> 402 us (level)
    pallas_call x16 -> x15, Pallas kernels: 103 us -> 99.7 us  [call(): pl.pallas_call(kernel, in_specs=[spec for _, spec in ins], out_specs=tupl...]
  transfers between devices with their start and end apart: 24 -> 24, of which waited for: 13 -> 13; matrix products, arithmetic and copies ran while one was open for 0% -> 0% of each run, Pallas kernels for 21% -> 20%
where the time goes in v14:
time: 402 us
  waiting for transfers between devices  231 us (57%)
  Pallas kernels  99.7 us (25%)
  starting transfers between devices  59.4 us (15%)
  local copies, waits for them, and re-layouts  10 us (2%)
    pallas_call x15, Pallas kernels, call(): pl.pallas_call(kernel, in_specs=[spec for _, spec in ins], out_specs=tupl...  99.7 us
    ppermute x16, waiting for transfers between devices, around(): lax.ppermute(value, axis, [(i, (i + steps) % count) for i in range(count)])  99 us
    ppermute x1, waiting for transfers between devices, local(): above = lax.ppermute(ends[0], 'slab', [(i, j) for j, i in forward])  83.2 us
    all_to_all x6, waiting for transfers between devices, exchange(): lax.all_to_all(chunks, 'slab', split_axis=0, concat_axis=0, tiled=True)  49 us
    all_to_all x6, starting transfers between devices, exchange(): lax.all_to_all(chunks, 'slab', split_axis=0, concat_axis=0, tiled=True)  37.3 us
    ppermute x16, starting transfers between devices, around(): lax.ppermute(value, axis, [(i, (i + steps) % count) for i in range(count)])  16.3 us
    unnamed x46, local copies, waits for them, and re-layouts  10 us
  transfers between devices with their start and end apart: 24, of which 13 were waited for; matrix products, arithmetic and copies ran while one was open for 0% of the time, Pallas kernels for 20%

profile of v14, /device:TPU:9, one launch (start us, length us, event | category | flops | bytes accessed | tf_op | source)
XLA Modules:
  0.0 401.5 jit_solution(7496263149715849683)
XLA Ops:
  0.6 2.9 visc_chunks.1
  3.6 5.6 %all-to-all-start.1 = ((f32[8,3,32,128]{3,2,1,0:T(8,128)}), f32[8,3,32,128]{3,2,1,0:T(8,128)S(1)}, u32[]{:S(2)}, u32[]{:S(2)}) async-start(f32[8,3,32,128]{3,2,1,0:T(8,128)} %get-tuple-element.27.refs_0_), calls=%async_computation.1 | async-start | bytes 786432 | tf_op jit(solution)/shard_map/all_to_all | solution.py:714
  9.2 4.2 %to_chunks.2 = (f32[8,2,8,32,128]{4,3,2,1,0:T(8,128)}, f32[2,4,64,128]{3,2,1,0:T(8,128)}) custom-call(f32[4,2048,128]{2,1,0:T(8,128)} %bitcast.10, f32[8,3,32,128]{3,2,1,0:T(8,128)} %get-tuple-element.27.refs_0_), custom_call_target="tpu_custom_call" | custom-call | bytes 4587520 | tf_op jit(solution)/shard_map/to_chunks/pallas_call | solution.py:42
  13.4 5.3 %all-to-all-done.1._before._after.refs_0_ = f32[8,3,32,128]{3,2,1,0:T(8,128)S(1)} async-done(((f32[8,3,32,128]{3,2,1,0:T(8,128)}), f32[8,3,32,128]{3,2,1,0:T(8,128)S(1)}, u32[]{:S(2)}, u32[]{:S(2)}) %all-to-all-start.1) | async-done | bytes 393248 | tf_op jit(solution)/shard_map/all_to_all | solution.py:714
  18.7 6.6 %all-to-all-start = ((f32[8,2,8,32,128]{4,3,2,1,0:T(8,128)}), f32[8,2,8,32,128]{4,3,2,1,0:T(8,128)S(1)}, u32[]{:S(2)}, u32[]{:S(2)}) async-start(f32[8,2,8,32,128]{4,3,2,1,0:T(8,128)} %get-tuple-element.28.refs_4_), calls=%async_computation | async-start | bytes 4194304 | tf_op jit(solution)/shard_map/all_to_all | solution.py:714
  28.9 2.9 split.1
  31.8 4.8 %collective-permute-done.5.refs_3_ = f32[8,3,32,128]{3,2,1,0:T(8,128)S(1)} collective-permute-done((f32[8,3,32,128]{3,2,1,0:T(8,128)S(1)}, f32[8,3,32,128]{3,2,1,0:T(8,128)S(1)}, u32[]{:S(2)}, u32[]{:S(2)}) %collective-permute-start.5) | collective-permute-done | bytes 393248 | tf_op jit(solution)/shard_map/ppermute | solution.py:719
  36.6 9.1 %collective-permute-done.4.refs_2_ = f32[8,3,32,128]{3,2,1,0:T(8,128)S(1)} collective-permute-done((f32[8,3,32,128]{3,2,1,0:T(8,128)S(1)}, f32[8,3,32,128]{3,2,1,0:T(8,128)S(1)}, u32[]{:S(2)}, u32[]{:S(2)}) %collective-permute-start.4) | collective-permute-done | bytes 393248 | tf_op jit(solution)/shard_map/ppermute | solution.py:719
  47.1 2.8 to_frame.1.refs_0_.refs_7_.refs_8_
  49.9 4.2 %to_chunks.3 = (f32[8,2,8,32,128]{4,3,2,1,0:T(8,128)}, f32[2,4,64,128]{3,2,1,0:T(8,128)}) custom-call(f32[4,2048,128]{2,1,0:T(8,128)} %bitcast.11, f32[12,256,128]{2,1,0:T(8,128)} %to_frame.1.refs_0_.refs_7_.refs_8_, bf16[4,256,256]{2,1,0:T(8,128)(2,1)} %get-tuple-element.32.refs_1_.refs_8_), custom_call_target="tpu_custom_call" | custom-call | bytes 6815744 | tf_op jit(solution)/shard_map/to_chunks/pallas_call | solution.py:42
  54.2 16.6 %all-to-all-done.chunks.main.refs_4_ = f32[8,2,8,32,128]{4,3,2,1,0:T(8,128)S(1)} async-done(((f32[8,2,8,32,128]{4,3,2,1,0:T(8,128)}), f32[8,2,8,32,128]{4,3,2,1,0:T(8,128)S(1)}, u32[]{:S(2)}, u32[]{:S(2)}) %all-to-all-start) | async-done | bytes 2097184 | tf_op jit(solution)/shard_map/all_to_all | solution.py:714
  72.1 7.8 %all-to-all-start.2 = ((f32[8,2,8,32,128]{4,3,2,1,0:T(8,128)}), f32[8,2,8,32,128]{4,3,2,1,0:T(8,128)}, u32[]{:S(2)}, u32[]{:S(2)}) async-start(f32[8,2,8,32,128]{4,3,2,1,0:T(8,128)} %get-tuple-element.33.refs_5_), calls=%async_computation.2 | async-start | bytes 4194304 | tf_op jit(solution)/shard_map/all_to_all | solution.py:714
  80.0 3.6 outer_rows.2
  83.6 2.2 collective-permute-start.2
  87.5 49.2 %collective-permute-done._before.low_in.refs_3_ = f32[8,2,2,32,128]{4,3,2,1,0:T(8,128)S(1)} collective-permute-done((f32[8,2,2,32,128]{4,3,2,1,0:T(8,128)}, f32[8,2,2,32,128]{4,3,2,1,0:T(8,128)S(1)}, u32[]{:S(2)}, u32[]{:S(2)}) %collective-permute-start) | collective-permute-done | bytes 524320 | tf_op jit(solution)/shard_map/ppermute | solution.py:719
  139.6 3.6 outer_rows.3
  147.6 15.3 %two_steps.1 = (f32[2,10,272,128]{3,2,1,0:T(8,128)}, f32[8,2,8,32,128]{4,3,2,1,0:T(8,128)}, f32[2,256,128]{2,1,0:T(8,128)}, f32[2,256,128]{2,1,0:T(8,128)}) custom-call(f32[8,2,2,32,128]{4,3,2,1,0:T(8,128)} %copy-done.4, f32[8,2,8,32,128]{4,3,2,1,0:T(8,128)} %copy-done, f32[8,2,2,32,128]{4,3,2,1,0:T(8,128)} %copy-done.5, f32[8,2,8,32,128]{4,3,2,1,0:T(8,128)} %copy-done.8, ...), custom_call_target="tpu_custom_call" | custom-call | flops 1811939328 | bytes 9437184 | tf_op jit(solution)/shard_map/two_steps/pallas_call | solution.py:42
  164.1 4.6 %all-to-all-start.3 = ((f32[8,2,8,32,128]{4,3,2,1,0:T(8,128)}), f32[8,2,8,32,128]{4,3,2,1,0:T(8,128)S(1)}, u32[]{:S(2)}, u32[]{:S(2)}) async-start(f32[8,2,8,32,128]{4,3,2,1,0:T(8,128)} %after.2.refs_6_.refs_5_.refs_0_), calls=%async_computation.3 | async-start | bytes 4194304 | tf_op jit(solution)/shard_map/all_to_all | solution.py:714
  170.7 9.7 %carried_step.1.first.refs_7_ = f32[2,10,272,128]{3,2,1,0:T(8,128)} custom-call(f32[8,2,2,32,128]{4,3,2,1,0:T(8,128)} %copy-done.9, f32[8,2,8,32,128]{4,3,2,1,0:T(8,128)} %all-to-all-done.2.chunks.refs_1_, f32[8,2,2,32,128]{4,3,2,1,0:T(8,128)} %copy-done.10, f32[8,2,2,32,128]{4,3,2,1,0:T(8,128)} %copy-done.4, f32[8,2,8,32,128]{4,3,2,1,0:T(8,128)} %copy-done, ...), custom_call_target="tpu_custom_call" | custom-call | flops 1006632960 | bytes 12058624 | tf_op jit(solution)/shard_map/carried_step/pallas_call | solution.py:42
  180.5 18.5 %collective-permute-done.9.refs_4_ = f32[8,2,5,32,128]{4,3,2,1,0:T(8,128)S(1)} collective-permute-done((f32[8,2,5,32,128]{4,3,2,1,0:T(8,128)}, f32[8,2,5,32,128]{4,3,2,1,0:T(8,128)S(1)}, u32[]{:S(2)}, u32[]{:S(2)}) %collective-permute-start.9) | collective-permute-done | bytes 1310752 | tf_op jit(solution)/shard_map/ppermute | solution.py:719
  200.0 9.6 %second_step.1 = (f32[8,2,8,32,128]{4,3,2,1,0:T(8,128)}, f32[2,256,128]{2,1,0:T(8,128)}, f32[2,256,128]{2,1,0:T(8,128)}) custom-call(f32[2,10,272,128]{3,2,1,0:T(8,128)} %carried_step.1.first.refs_7_, f32[2,10,272,128]{3,2,1,0:T(8,128)} %get-tuple-element.39.with_w.refs_6_, f32[12,256,128]{2,1,0:T(8,128)} %to_frame.1.refs_0_.refs_7_.refs_8_, ...), custom_call_target="tpu_custom_call" | custom-call | flops 805306368 | bytes 13434880 | tf_op jit(solution)/shard_map/second_step/pallas_call | solution.py:42
  209.6 2.3 collective-permute-start.11
  211.9 10.9 %collective-permute-done.10.refs_1_.refs_2_ = f32[2,256,128]{2,1,0:T(8,128)S(1)} collective-permute-done((f32[2,256,128]{2,1,0:T(8,128)}, f32[2,256,128]{2,1,0:T(8,128)S(1)}, u32[]{:S(2)}, u32[]{:S(2)}) %collective-permute-start.10) | collective-permute-done | bytes 262176 | tf_op jit(solution)/shard_map/ppermute | solution.py:719
  228.8 4.5 %all-to-all-start.4 = ((f32[8,2,8,32,128]{4,3,2,1,0:T(8,128)}), f32[8,2,8,32,128]{4,3,2,1,0:T(8,128)}, u32[]{:S(2)}, u32[]{:S(2)}) async-start(f32[8,2,8,32,128]{4,3,2,1,0:T(8,128)} %after.3.refs_1_), calls=%async_computation.4 | async-start | bytes 4194304 | tf_op jit(solution)/shard_map/all_to_all | solution.py:714
  233.2 17.4 %adjoint_step.1._ = f32[8,34,32,128]{3,2,1,0:T(8,128)} custom-call(f32[8,2,8,32,128]{4,3,2,1,0:T(8,128)} %after.2.refs_6_.refs_5_.refs_0_, f32[8,2,8,32,128]{4,3,2,1,0:T(8,128)} %after.3.refs_1_, f32[2,256,128]{2,1,0:T(8,128)} %copy-done.12, f32[2,256,128]{2,1,0:T(8,128)} %copy-done.14, f32[2,256,128]{2,1,0:T(8,128)} %copy-done.13, ...), custom_call_target="tpu_custom_call" | custom-call | flops 3623878656 | bytes 14483456 | tf_op jit(solution)/shard_map/adjoint_step/pallas_call | solution.py:42
  250.7 27.2 %all-to-all-done.4.other = f32[8,2,8,32,128]{4,3,2,1,0:T(8,128)} async-done(((f32[8,2,8,32,128]{4,3,2,1,0:T(8,128)}), f32[8,2,8,32,128]{4,3,2,1,0:T(8,128)}, u32[]{:S(2)}, u32[]{:S(2)}) %all-to-all-start.4) | async-done | bytes 2097184 | tf_op jit(solution)/shard_map/all_to_all | solution.py:714
  277.8 8.1 %all-to-all-start.5 = ((f32[8,34,32,128]{3,2,1,0:T(8,128)}), f32[8,34,32,128]{3,2,1,0:T(8,128)}, u32[]{:S(2)}, u32[]{:S(2)}) async-start(f32[8,34,32,128]{3,2,1,0:T(8,128)} %adjoint_step.1._), calls=%async_computation.5 | async-start | bytes 8912896 | tf_op jit(solution)/shard_map/all_to_all | solution.py:714
  286.0 8.7 %to_planes.1 = (f32[8192,128]{1,0:T(8,128)}, f32[8,2,8,32,128]{4,3,2,1,0:T(8,128)}) custom-call(f32[8,2,8,32,128]{4,3,2,1,0:T(8,128)} %copy-done.1, f32[8,2,8,32,128]{4,3,2,1,0:T(8,128)} %all-to-all-done.4.other, f32[8,34,32,128]{3,2,1,0:T(8,128)} %adjoint_step.1._), custom_call_target="tpu_custom_call" | custom-call | bytes 8650752 | tf_op jit(solution)/shard_map/to_planes/pallas_call | solution.py:42
  296.1 2.8 collective-permute-start.15
  298.9 3.0 collective-permute-start.14
  302.0 83.2 %collective-permute-done.15.refs_2_ = f32[4,64,128]{2,1,0:T(8,128)S(1)} collective-permute-done((f32[4,64,128]{2,1,0:T(8,128)S(1)}, f32[4,64,128]{2,1,0:T(8,128)S(1)}, u32[]{:S(2)}, u32[]{:S(2)}) %collective-permute-start.15) | collective-permute-done | bytes 131104 | tf_op jit(solution)/shard_map/ppermute | solution.py:741
  386.6 14.8 %last_step.1 = f32[4,2048,128]{2,1,0:T(8,128)} custom-call(f32[8,8,32,128]{3,2,1,0:T(8,128)} %bitcast.13, f32[4,64,128]{2,1,0:T(8,128)} %copy-done.21, f32[4,64,128]{2,1,0:T(8,128)} %copy-done.20, f32[8,34,32,128]{3,2,1,0:T(8,128)} %all-to-all-done.5.refs_3_, f32[8,2,8,32,128]{4,3,2,1,0:T(8,128)} %get-tuple-element.28.refs_4_, ...), custom_call_target="tpu_custom_call" | custom-call | flops 31457280 | bytes 14155776 | tf_op jit(solution)/shard_map/last_step/pallas_call | solution.py:42
  (78 shorter events, 28.4 us)
Async XLA Ops:
  3.6 15.1 %all-to-all-start.1 = ((f32[8,3,32,128]{3,2,1,0:T(8,128)}), f32[8,3,32,128]{3,2,1,0:T(8,128)S(1)}, u32[]{:S(2)}, u32[]{:S(2)}) async-start(f32[8,3,32,128]{3,2,1,0:T(8,128)} %get-tuple-element.27.refs_0_), calls=%async_computation.1 | async-start | bytes 786432 | tf_op jit(solution)/shard_map/all_to_all | solution.py:714
  18.7 9.1 %copy-start.3 = (f32[8,3,32,128]{3,2,1,0:T(8,128)}, f32[8,3,32,128]{3,2,1,0:T(8,128)S(1)}, u32[]{:S(2)}) copy-start(f32[8,3,32,128]{3,2,1,0:T(8,128)S(1)} %all-to-all-done.1._before._after.refs_0_) | copy-start | bytes 1179652
  18.7 52.1 %all-to-all-start = ((f32[8,2,8,32,128]{4,3,2,1,0:T(8,128)}), f32[8,2,8,32,128]{4,3,2,1,0:T(8,128)S(1)}, u32[]{:S(2)}, u32[]{:S(2)}) async-start(f32[8,2,8,32,128]{4,3,2,1,0:T(8,128)} %get-tuple-element.28.refs_4_), calls=%async_computation | async-start | bytes 4194304 | tf_op jit(solution)/shard_map/all_to_all | solution.py:714
  25.3 11.3 %collective-permute-start.5 = (f32[8,3,32,128]{3,2,1,0:T(8,128)S(1)}, f32[8,3,32,128]{3,2,1,0:T(8,128)S(1)}, u32[]{:S(2)}, u32[]{:S(2)}) collective-permute-start(f32[8,3,32,128]{3,2,1,0:T(8,128)S(1)} %all-to-all-done.1._before._after.refs_0_), channel_id=1, source_target_pairs={{0,8},{8,16},{16,24},{24,0},{1,9},{9,17},{17,25},{25,1},{2,10},{10... | collective-permute-start | bytes 1179656 | tf_op jit(solution)/shard_map/ppermute | solution.py:719
  26.5 19.2 %collective-permute-start.4 = (f32[8,3,32,128]{3,2,1,0:T(8,128)S(1)}, f32[8,3,32,128]{3,2,1,0:T(8,128)S(1)}, u32[]{:S(2)}, u32[]{:S(2)}) collective-permute-start(f32[8,3,32,128]{3,2,1,0:T(8,128)S(1)} %all-to-all-done.1._before._after.refs_0_), channel_id=1, source_target_pairs={{0,16},{8,24},{16,0},{24,8},{1,17},{9,25},{17,1},{25,9},{2,18},{10... | collective-permute-start | bytes 1179656 | tf_op jit(solution)/shard_map/ppermute | solution.py:719
  27.7 17.9 %collective-permute-start.3 = (f32[8,3,32,128]{3,2,1,0:T(8,128)S(1)}, f32[8,3,32,128]{3,2,1,0:T(8,128)S(1)}, u32[]{:S(2)}, u32[]{:S(2)}) collective-permute-start(f32[8,3,32,128]{3,2,1,0:T(8,128)S(1)} %all-to-all-done.1._before._after.refs_0_), channel_id=1, source_target_pairs={{0,24},{8,0},{16,8},{24,16},{1,25},{9,1},{17,9},{25,17},{2,26},{10... | collective-permute-start | bytes 1179656 | tf_op jit(solution)/shard_map/ppermute | solution.py:719
  36.6 9.1 %copy-start.16 = (f32[8,3,32,128]{3,2,1,0:T(8,128)}, f32[8,3,32,128]{3,2,1,0:T(8,128)S(1)}, u32[]{:S(2)}) copy-start(f32[8,3,32,128]{3,2,1,0:T(8,128)S(1)} %collective-permute-done.5.refs_3_) | copy-start | bytes 1179652
  72.1 66.7 %all-to-all-start.2 = ((f32[8,2,8,32,128]{4,3,2,1,0:T(8,128)}), f32[8,2,8,32,128]{4,3,2,1,0:T(8,128)}, u32[]{:S(2)}, u32[]{:S(2)}) async-start(f32[8,2,8,32,128]{4,3,2,1,0:T(8,128)} %get-tuple-element.33.refs_5_), calls=%async_computation.2 | async-start | bytes 4194304 | tf_op jit(solution)/shard_map/all_to_all | solution.py:714
  83.6 62.6 %collective-permute-start.2 = (f32[8,2,8,32,128]{4,3,2,1,0:T(8,128)}, f32[8,2,8,32,128]{4,3,2,1,0:T(8,128)S(1)}, u32[]{:S(2)}, u32[]{:S(2)}) collective-permute-start(f32[8,2,8,32,128]{4,3,2,1,0:T(8,128)} %get-tuple-element.31), channel_id=1, source_target_pairs={{0,24},{8,0},{16,8},{24,16},{1,25},{9,1},{17,9},{25,17},{2,26},{10... | collective-permute-start | bytes 6291464 | tf_op jit(solution)/shard_map/ppermute | solution.py:719
  85.8 50.9 %collective-permute-start = (f32[8,2,2,32,128]{4,3,2,1,0:T(8,128)}, f32[8,2,2,32,128]{4,3,2,1,0:T(8,128)S(1)}, u32[]{:S(2)}, u32[]{:S(2)}) collective-permute-start(f32[8,2,2,32,128]{4,3,2,1,0:T(8,128)} %get-tuple-element.29), channel_id=1, source_target_pairs={{0,1},{1,2},{2,3},{3,4},{4,5},{5,6},{6,7},{7,0},{8,9},{9,10},{10,1... | collective-permute-start | bytes 1572872 | tf_op jit(solution)/shard_map/ppermute | solution.py:719
  87.5 51.3 %collective-permute-start.1 = (f32[8,2,2,32,128]{4,3,2,1,0:T(8,128)}, f32[8,2,2,32,128]{4,3,2,1,0:T(8,128)S(1)}, u32[]{:S(2)}, u32[]{:S(2)}) collective-permute-start(f32[8,2,2,32,128]{4,3,2,1,0:T(8,128)} %get-tuple-element.30), channel_id=1, source_target_pairs={{0,7},{1,0},{2,1},{3,2},{4,3},{5,4},{6,5},{7,6},{8,15},{9,8},{10,9... | collective-permute-start | bytes 1572872 | tf_op jit(solution)/shard_map/ppermute | solution.py:719
  136.8 2.0 copy-start.4
  143.2 19.7 %collective-permute-start.8 = (f32[8,2,3,32,128]{4,3,2,1,0:T(8,128)}, f32[8,2,3,32,128]{4,3,2,1,0:T(8,128)S(1)}, u32[]{:S(2)}, u32[]{:S(2)}) collective-permute-start(f32[8,2,3,32,128]{4,3,2,1,0:T(8,128)} %get-tuple-element.38), channel_id=1, source_target_pairs={{0,24},{8,0},{16,8},{24,16},{1,25},{9,1},{17,9},{25,17},{2,26},{10... | collective-permute-start | bytes 2359304 | tf_op jit(solution)/shard_map/ppermute | solution.py:719
  145.1 17.8 %collective-permute-start.6 = (f32[8,2,2,32,128]{4,3,2,1,0:T(8,128)}, f32[8,2,2,32,128]{4,3,2,1,0:T(8,128)S(1)}, u32[]{:S(2)}, u32[]{:S(2)}) collective-permute-start(f32[8,2,2,32,128]{4,3,2,1,0:T(8,128)} %get-tuple-element.37), channel_id=1, source_target_pairs={{0,1},{1,2},{2,3},{3,4},{4,5},{5,6},{6,7},{7,0},{8,9},{9,10},{10,1... | collective-permute-start | bytes 1572872 | tf_op jit(solution)/shard_map/ppermute | solution.py:719
  146.2 16.7 %collective-permute-start.7 = (f32[8,2,2,32,128]{4,3,2,1,0:T(8,128)}, f32[8,2,2,32,128]{4,3,2,1,0:T(8,128)S(1)}, u32[]{:S(2)}, u32[]{:S(2)}) collective-permute-start(f32[8,2,2,32,128]{4,3,2,1,0:T(8,128)} %get-tuple-element.34._), channel_id=1, source_target_pairs={{0,7},{1,0},{2,1},{3,2},{4,3},{5,4},{6,5},{7,6},{8,15},{9,8},{10,9... | collective-permute-start | bytes 1572872 | tf_op jit(solution)/shard_map/ppermute | solution.py:719
  164.1 6.6 %copy-start.22 = (f32[2,256,128]{2,1,0:T(8,128)S(1)}, f32[2,256,128]{2,1,0:T(8,128)}, u32[]{:S(2)}) copy-start(f32[2,256,128]{2,1,0:T(8,128)} %get-tuple-element.44) | copy-start | bytes 786436
  164.1 63.2 %all-to-all-start.3 = ((f32[8,2,8,32,128]{4,3,2,1,0:T(8,128)}), f32[8,2,8,32,128]{4,3,2,1,0:T(8,128)S(1)}, u32[]{:S(2)}, u32[]{:S(2)}) async-start(f32[8,2,8,32,128]{4,3,2,1,0:T(8,128)} %after.2.refs_6_.refs_5_.refs_0_), calls=%async_computation.3 | async-start | bytes 4194304 | tf_op jit(solution)/shard_map/all_to_all | solution.py:714
  168.8 30.2 %collective-permute-start.9 = (f32[8,2,5,32,128]{4,3,2,1,0:T(8,128)}, f32[8,2,5,32,128]{4,3,2,1,0:T(8,128)S(1)}, u32[]{:S(2)}, u32[]{:S(2)}) collective-permute-start(f32[8,2,5,32,128]{4,3,2,1,0:T(8,128)} %get-tuple-element.40), channel_id=1, source_target_pairs={{0,24},{8,0},{16,8},{24,16},{1,25},{9,1},{17,9},{25,17},{2,26},{10... | collective-permute-start | bytes 3932168 | tf_op jit(solution)/shard_map/ppermute | solution.py:719
  169.0 53.8 %collective-permute-start.10 = (f32[2,256,128]{2,1,0:T(8,128)}, f32[2,256,128]{2,1,0:T(8,128)S(1)}, u32[]{:S(2)}, u32[]{:S(2)}) collective-permute-start(f32[2,256,128]{2,1,0:T(8,128)} %get-tuple-element.42), channel_id=1, source_target_pairs={{0,1},{1,2},{2,3},{3,4},{4,5},{5,6},{6,7},{7,0},{8,9},{9,10},{10,1... | collective-permute-start | bytes 786440 | tf_op jit(solution)/shard_map/ppermute | solution.py:719
  170.7 53.8 %collective-permute-start.12 = (f32[2,256,128]{2,1,0:T(8,128)S(1)}, f32[2,256,128]{2,1,0:T(8,128)S(1)}, u32[]{:S(2)}, u32[]{:S(2)}) collective-permute-start(f32[2,256,128]{2,1,0:T(8,128)S(1)} %copy-done.22), channel_id=1, source_target_pairs={{0,7},{1,0},{2,1},{3,2},{4,3},{5,4},{6,5},{7,6},{8,15},{9,8},{10,9... | collective-permute-start | bytes 786440 | tf_op jit(solution)/shard_map/ppermute | solution.py:719
  209.6 16.0 %collective-permute-start.11 = (f32[2,256,128]{2,1,0:T(8,128)}, f32[2,256,128]{2,1,0:T(8,128)S(1)}, u32[]{:S(2)}, u32[]{:S(2)}) collective-permute-start(f32[2,256,128]{2,1,0:T(8,128)} %get-tuple-element.43), channel_id=1, source_target_pairs={{0,1},{1,2},{2,3},{3,4},{4,5},{5,6},{6,7},{7,0},{8,9},{9,10},{10,1... | collective-permute-start | bytes 786440 | tf_op jit(solution)/shard_map/ppermute | solution.py:719
  211.9 15.4 %collective-permute-start.13 = (f32[2,256,128]{2,1,0:T(8,128)}, f32[2,256,128]{2,1,0:T(8,128)S(1)}, u32[]{:S(2)}, u32[]{:S(2)}) collective-permute-start(f32[2,256,128]{2,1,0:T(8,128)} %get-tuple-element.45), channel_id=1, source_target_pairs={{0,7},{1,0},{2,1},{3,2},{4,3},{5,4},{6,5},{7,6},{8,15},{9,8},{10,9... | collective-permute-start | bytes 786440 | tf_op jit(solution)/shard_map/ppermute | solution.py:719
  222.8 4.5 %copy-start.12 = (f32[2,256,128]{2,1,0:T(8,128)}, f32[2,256,128]{2,1,0:T(8,128)S(1)}, u32[]{:S(2)}) copy-start(f32[2,256,128]{2,1,0:T(8,128)S(1)} %collective-permute-done.10.refs_1_.refs_2_) | copy-start | bytes 786436
  224.5 2.8 copy-start.13
  228.8 49.1 %all-to-all-start.4 = ((f32[8,2,8,32,128]{4,3,2,1,0:T(8,128)}), f32[8,2,8,32,128]{4,3,2,1,0:T(8,128)}, u32[]{:S(2)}, u32[]{:S(2)}) async-start(f32[8,2,8,32,128]{4,3,2,1,0:T(8,128)} %after.3.refs_1_), calls=%async_computation.4 | async-start | bytes 4194304 | tf_op jit(solution)/shard_map/all_to_all | solution.py:714
  250.7 35.2 %copy-start.2 = (f32[8,2,8,32,128]{4,3,2,1,0:T(8,128)S(1)}, f32[8,2,8,32,128]{4,3,2,1,0:T(8,128)}, u32[]{:S(2)}) copy-start(f32[8,2,8,32,128]{4,3,2,1,0:T(8,128)} %copy-done.1) | copy-start | bytes 6291460
  277.8 108.7 %all-to-all-start.5 = ((f32[8,34,32,128]{3,2,1,0:T(8,128)}), f32[8,34,32,128]{3,2,1,0:T(8,128)}, u32[]{:S(2)}, u32[]{:S(2)}) async-start(f32[8,34,32,128]{3,2,1,0:T(8,128)} %adjoint_step.1._), calls=%async_computation.5 | async-start | bytes 8912896 | tf_op jit(solution)/shard_map/all_to_all | solution.py:714
  285.9 10.2 %copy-start.19 = (f32[2,4,64,128]{3,2,1,0:T(8,128)S(1)}, f32[2,4,64,128]{3,2,1,0:T(8,128)}, u32[]{:S(2)}) copy-start(f32[2,4,64,128]{3,2,1,0:T(8,128)} %get-tuple-element.50) | copy-start | bytes 786436
  285.9 99.3 %collective-permute-start.16 = (f32[8,2,8,32,128]{4,3,2,1,0:T(8,128)S(1)}, f32[8,2,8,32,128]{4,3,2,1,0:T(8,128)S(1)}, u32[]{:S(2)}, u32[]{:S(2)}) collective-permute-start(f32[8,2,8,32,128]{4,3,2,1,0:T(8,128)S(1)} %copy-done.2), channel_id=1, source_target_pairs={{0,8},{8,16},{16,24},{24,0},{1,9},{9,17},{17,25},{25,1},{2,10},{10... | collective-permute-start | bytes 6291464 | tf_op jit(solution)/shard_map/ppermute | solution.py:719
  294.7 91.9 %collective-permute-start.17 = (f32[8,2,8,32,128]{4,3,2,1,0:T(8,128)}, f32[8,2,8,32,128]{4,3,2,1,0:T(8,128)}, u32[]{:S(2)}, u32[]{:S(2)}) collective-permute-start(f32[8,2,8,32,128]{4,3,2,1,0:T(8,128)} %get-tuple-element.51), channel_id=1, source_target_pairs={{0,8},{8,16},{16,24},{24,0},{1,9},{9,17},{17,25},{25,1},{2,10},{10... | collective-permute-start | bytes 6291464 | tf_op jit(solution)/shard_map/ppermute | solution.py:719
  296.1 89.1 %collective-permute-start.15 = (f32[4,64,128]{2,1,0:T(8,128)S(1)}, f32[4,64,128]{2,1,0:T(8,128)S(1)}, u32[]{:S(2)}, u32[]{:S(2)}) collective-permute-start(f32[4,64,128]{2,1,0:T(8,128)S(1)} %get-tuple-element.52), channel_id=1, source_target_pairs={{1,0},{2,1},{3,2},{4,3},{5,4},{6,5},{7,6},{9,8},{10,9},{11,10},{12... | collective-permute-start | bytes 393224 | tf_op jit(solution)/shard_map/ppermute | solution.py:741
  298.9 86.2 %collective-permute-start.14 = (f32[4,64,128]{2,1,0:T(8,128)S(1)}, f32[4,64,128]{2,1,0:T(8,128)S(1)}, u32[]{:S(2)}, u32[]{:S(2)}) collective-permute-start(f32[4,64,128]{2,1,0:T(8,128)S(1)} %get-tuple-element.53), channel_id=1, source_target_pairs={{0,1},{1,2},{2,3},{3,4},{4,5},{5,6},{6,7},{8,9},{9,10},{10,11},{11... | collective-permute-start | bytes 393224 | tf_op jit(solution)/shard_map/ppermute | solution.py:740
  (15 other events, 17.0 us)

commit v15 on v14

--- a/solution.py
+++ b/solution.py
@@ -433,10 +433,11 @@
     slabs, _, block, depth, width = main.shape
     order = slabs * depth
     volume = 2 * (block + 1) * order * width
-    operands = (low_in, main, high_in, target, later, frame, mat_high, mat_low)
+    operands = [(x, anywhere()) for x in (low_in, main, high_in)] + [(target, whole())]
+    operands += [(x, anywhere()) for x in (later, frame, mat_high, mat_low)]
     return call(
         two_steps_kernel,
-        [(x, anywhere()) for x in operands],
+        operands,
         [
             ((2, block + 2, order + 2 * pad, width), whole()),
             (main.shape, anywhere()),

time: 402 us -> 403 us (level)
  transfers between devices with their start and end apart: 24 -> 24, of which waited for: 13 -> 13; matrix products, arithmetic and copies ran while one was open for 0% -> 0% of each run, Pallas kernels for 20% -> 21%
where the time goes in v15:
time: 403 us
  waiting for transfers between devices  231 us (57%)
  Pallas kernels  101 us (25%)
  starting transfers between devices  59.4 us (15%)
  local copies, waits for them, and re-layouts  10 us (2%)
    pallas_call x15, Pallas kernels, call(): pl.pallas_call(kernel, in_specs=[spec for _, spec in ins], out_specs=tupl...  101 us
    ppermute x16, waiting for transfers between devices, around(): lax.ppermute(value, axis, [(i, (i + steps) % count) for i in range(count)])  99 us
    ppermute x1, waiting for transfers between devices, local(): above = lax.ppermute(ends[0], 'slab', [(i, j) for j, i in forward])  83.2 us
    all_to_all x6, waiting for transfers between devices, exchange(): lax.all_to_all(chunks, 'slab', split_axis=0, concat_axis=0, tiled=True)  49 us
    all_to_all x6, starting transfers between devices, exchange(): lax.all_to_all(chunks, 'slab', split_axis=0, concat_axis=0, tiled=True)  37.3 us
    ppermute x16, starting transfers between devices, around(): lax.ppermute(value, axis, [(i, (i + steps) % count) for i in range(count)])  16.3 us
    unnamed x46, local copies, waits for them, and re-layouts  10 us
  transfers between devices with their start and end apart: 24, of which 13 were waited for; matrix products, arithmetic and copies ran while one was open for 0% of the time, Pallas kernels for 21%

profile of v15, /device:TPU:9, one launch (start us, length us, event | category | flops | bytes accessed | tf_op | source)
XLA Modules:
  0.0 402.5 jit_solution(16054027028895698956)
XLA Ops:
  0.6 2.9 visc_chunks.1
  3.6 5.6 %all-to-all-start.1 = ((f32[8,3,32,128]{3,2,1,0:T(8,128)}), f32[8,3,32,128]{3,2,1,0:T(8,128)S(1)}, u32[]{:S(2)}, u32[]{:S(2)}) async-start(f32[8,3,32,128]{3,2,1,0:T(8,128)} %get-tuple-element.27.refs_0_), calls=%async_computation.1 | async-start | bytes 786432 | tf_op jit(solution)/shard_map/all_to_all | solution.py:715
  9.2 4.2 %to_chunks.2 = (f32[8,2,8,32,128]{4,3,2,1,0:T(8,128)}, f32[2,4,64,128]{3,2,1,0:T(8,128)}) custom-call(f32[4,2048,128]{2,1,0:T(8,128)} %bitcast.10, f32[8,3,32,128]{3,2,1,0:T(8,128)} %get-tuple-element.27.refs_0_), custom_call_target="tpu_custom_call" | custom-call | bytes 4587520 | tf_op jit(solution)/shard_map/to_chunks/pallas_call | solution.py:42
  13.4 5.3 %all-to-all-done.1._before._after.refs_0_ = f32[8,3,32,128]{3,2,1,0:T(8,128)S(1)} async-done(((f32[8,3,32,128]{3,2,1,0:T(8,128)}), f32[8,3,32,128]{3,2,1,0:T(8,128)S(1)}, u32[]{:S(2)}, u32[]{:S(2)}) %all-to-all-start.1) | async-done | bytes 393248 | tf_op jit(solution)/shard_map/all_to_all | solution.py:715
  18.7 6.6 %all-to-all-start = ((f32[8,2,8,32,128]{4,3,2,1,0:T(8,128)}), f32[8,2,8,32,128]{4,3,2,1,0:T(8,128)S(1)}, u32[]{:S(2)}, u32[]{:S(2)}) async-start(f32[8,2,8,32,128]{4,3,2,1,0:T(8,128)} %get-tuple-element.28.refs_4_), calls=%async_computation | async-start | bytes 4194304 | tf_op jit(solution)/shard_map/all_to_all | solution.py:715
  28.9 2.9 split.1
  31.8 4.8 %collective-permute-done.5.refs_3_ = f32[8,3,32,128]{3,2,1,0:T(8,128)S(1)} collective-permute-done((f32[8,3,32,128]{3,2,1,0:T(8,128)S(1)}, f32[8,3,32,128]{3,2,1,0:T(8,128)S(1)}, u32[]{:S(2)}, u32[]{:S(2)}) %collective-permute-start.5) | collective-permute-done | bytes 393248 | tf_op jit(solution)/shard_map/ppermute | solution.py:720
  36.6 9.1 %collective-permute-done.4.refs_2_ = f32[8,3,32,128]{3,2,1,0:T(8,128)S(1)} collective-permute-done((f32[8,3,32,128]{3,2,1,0:T(8,128)S(1)}, f32[8,3,32,128]{3,2,1,0:T(8,128)S(1)}, u32[]{:S(2)}, u32[]{:S(2)}) %collective-permute-start.4) | collective-permute-done | bytes 393248 | tf_op jit(solution)/shard_map/ppermute | solution.py:720
  47.1 2.8 to_frame.1.refs_0_.refs_7_.refs_8_
  49.9 4.2 %to_chunks.3 = (f32[8,2,8,32,128]{4,3,2,1,0:T(8,128)}, f32[2,4,64,128]{3,2,1,0:T(8,128)}) custom-call(f32[4,2048,128]{2,1,0:T(8,128)} %bitcast.11, f32[12,256,128]{2,1,0:T(8,128)} %to_frame.1.refs_0_.refs_7_.refs_8_, bf16[4,256,256]{2,1,0:T(8,128)(2,1)} %get-tuple-element.32.refs_1_.refs_8_), custom_call_target="tpu_custom_call" | custom-call | bytes 6815744 | tf_op jit(solution)/shard_map/to_chunks/pallas_call | solution.py:42
  54.2 16.6 %all-to-all-done.chunks.main.refs_4_ = f32[8,2,8,32,128]{4,3,2,1,0:T(8,128)S(1)} async-done(((f32[8,2,8,32,128]{4,3,2,1,0:T(8,128)}), f32[8,2,8,32,128]{4,3,2,1,0:T(8,128)S(1)}, u32[]{:S(2)}, u32[]{:S(2)}) %all-to-all-start) | async-done | bytes 2097184 | tf_op jit(solution)/shard_map/all_to_all | solution.py:715
  72.1 7.8 %all-to-all-start.2 = ((f32[8,2,8,32,128]{4,3,2,1,0:T(8,128)}), f32[8,2,8,32,128]{4,3,2,1,0:T(8,128)}, u32[]{:S(2)}, u32[]{:S(2)}) async-start(f32[8,2,8,32,128]{4,3,2,1,0:T(8,128)} %get-tuple-element.33.refs_5_), calls=%async_computation.2 | async-start | bytes 4194304 | tf_op jit(solution)/shard_map/all_to_all | solution.py:715
  80.0 3.6 outer_rows.2
  83.6 2.2 collective-permute-start.2
  87.5 49.2 %collective-permute-done._before.low_in.refs_3_ = f32[8,2,2,32,128]{4,3,2,1,0:T(8,128)S(1)} collective-permute-done((f32[8,2,2,32,128]{4,3,2,1,0:T(8,128)}, f32[8,2,2,32,128]{4,3,2,1,0:T(8,128)S(1)}, u32[]{:S(2)}, u32[]{:S(2)}) %collective-permute-start) | collective-permute-done | bytes 524320 | tf_op jit(solution)/shard_map/ppermute | solution.py:720
  139.6 3.6 outer_rows.3
  147.6 16.3 %two_steps.1 = (f32[2,10,272,128]{3,2,1,0:T(8,128)}, f32[8,2,8,32,128]{4,3,2,1,0:T(8,128)}, f32[2,256,128]{2,1,0:T(8,128)}, f32[2,256,128]{2,1,0:T(8,128)}) custom-call(f32[8,2,2,32,128]{4,3,2,1,0:T(8,128)} %copy-done.4, f32[8,2,8,32,128]{4,3,2,1,0:T(8,128)} %copy-done, f32[8,2,2,32,128]{4,3,2,1,0:T(8,128)} %copy-done.5, f32[8,2,8,32,128]{4,3,2,1,0:T(8,128)} %copy-done.8, ...), custom_call_target="tpu_custom_call" | custom-call | flops 1811939328 | bytes 9437184 | tf_op jit(solution)/shard_map/two_steps/pallas_call | solution.py:42
  165.1 4.6 %all-to-all-start.3 = ((f32[8,2,8,32,128]{4,3,2,1,0:T(8,128)}), f32[8,2,8,32,128]{4,3,2,1,0:T(8,128)S(1)}, u32[]{:S(2)}, u32[]{:S(2)}) async-start(f32[8,2,8,32,128]{4,3,2,1,0:T(8,128)} %after.2.refs_6_.refs_5_.refs_0_), calls=%async_computation.3 | async-start | bytes 4194304 | tf_op jit(solution)/shard_map/all_to_all | solution.py:715
  171.7 9.7 %carried_step.1.first.refs_7_ = f32[2,10,272,128]{3,2,1,0:T(8,128)} custom-call(f32[8,2,2,32,128]{4,3,2,1,0:T(8,128)} %copy-done.9, f32[8,2,8,32,128]{4,3,2,1,0:T(8,128)} %all-to-all-done.2.chunks.refs_1_, f32[8,2,2,32,128]{4,3,2,1,0:T(8,128)} %copy-done.10, f32[8,2,2,32,128]{4,3,2,1,0:T(8,128)} %copy-done.4, f32[8,2,8,32,128]{4,3,2,1,0:T(8,128)} %copy-done, ...), custom_call_target="tpu_custom_call" | custom-call | flops 1006632960 | bytes 12058624 | tf_op jit(solution)/shard_map/carried_step/pallas_call | solution.py:42
  181.5 18.5 %collective-permute-done.9.refs_4_ = f32[8,2,5,32,128]{4,3,2,1,0:T(8,128)S(1)} collective-permute-done((f32[8,2,5,32,128]{4,3,2,1,0:T(8,128)}, f32[8,2,5,32,128]{4,3,2,1,0:T(8,128)S(1)}, u32[]{:S(2)}, u32[]{:S(2)}) %collective-permute-start.9) | collective-permute-done | bytes 1310752 | tf_op jit(solution)/shard_map/ppermute | solution.py:720
  201.0 9.6 %second_step.1 = (f32[8,2,8,32,128]{4,3,2,1,0:T(8,128)}, f32[2,256,128]{2,1,0:T(8,128)}, f32[2,256,128]{2,1,0:T(8,128)}) custom-call(f32[2,10,272,128]{3,2,1,0:T(8,128)} %carried_step.1.first.refs_7_, f32[2,10,272,128]{3,2,1,0:T(8,128)} %get-tuple-element.39.with_w.refs_6_, f32[12,256,128]{2,1,0:T(8,128)} %to_frame.1.refs_0_.refs_7_.refs_8_, ...), custom_call_target="tpu_custom_call" | custom-call | flops 805306368 | bytes 13434880 | tf_op jit(solution)/shard_map/second_step/pallas_call | solution.py:42
  210.6 2.3 collective-permute-start.11
  212.9 10.9 %collective-permute-done.10.refs_1_.refs_2_ = f32[2,256,128]{2,1,0:T(8,128)S(1)} collective-permute-done((f32[2,256,128]{2,1,0:T(8,128)}, f32[2,256,128]{2,1,0:T(8,128)S(1)}, u32[]{:S(2)}, u32[]{:S(2)}) %collective-permute-start.10) | collective-permute-done | bytes 262176 | tf_op jit(solution)/shard_map/ppermute | solution.py:720
  229.8 4.5 %all-to-all-start.4 = ((f32[8,2,8,32,128]{4,3,2,1,0:T(8,128)}), f32[8,2,8,32,128]{4,3,2,1,0:T(8,128)}, u32[]{:S(2)}, u32[]{:S(2)}) async-start(f32[8,2,8,32,128]{4,3,2,1,0:T(8,128)} %after.3.refs_1_), calls=%async_computation.4 | async-start | bytes 4194304 | tf_op jit(solution)/shard_map/all_to_all | solution.py:715
  234.2 17.4 %adjoint_step.1._ = f32[8,34,32,128]{3,2,1,0:T(8,128)} custom-call(f32[8,2,8,32,128]{4,3,2,1,0:T(8,128)} %after.2.refs_6_.refs_5_.refs_0_, f32[8,2,8,32,128]{4,3,2,1,0:T(8,128)} %after.3.refs_1_, f32[2,256,128]{2,1,0:T(8,128)} %copy-done.12, f32[2,256,128]{2,1,0:T(8,128)} %copy-done.14, f32[2,256,128]{2,1,0:T(8,128)} %copy-done.13, ...), custom_call_target="tpu_custom_call" | custom-call | flops 3623878656 | bytes 14483456 | tf_op jit(solution)/shard_map/adjoint_step/pallas_call | solution.py:42
  251.7 27.2 %all-to-all-done.4.other = f32[8,2,8,32,128]{4,3,2,1,0:T(8,128)} async-done(((f32[8,2,8,32,128]{4,3,2,1,0:T(8,128)}), f32[8,2,8,32,128]{4,3,2,1,0:T(8,128)}, u32[]{:S(2)}, u32[]{:S(2)}) %all-to-all-start.4) | async-done | bytes 2097184 | tf_op jit(solution)/shard_map/all_to_all | solution.py:715
  278.8 8.1 %all-to-all-start.5 = ((f32[8,34,32,128]{3,2,1,0:T(8,128)}), f32[8,34,32,128]{3,2,1,0:T(8,128)}, u32[]{:S(2)}, u32[]{:S(2)}) async-start(f32[8,34,32,128]{3,2,1,0:T(8,128)} %adjoint_step.1._), calls=%async_computation.5 | async-start | bytes 8912896 | tf_op jit(solution)/shard_map/all_to_all | solution.py:715
  287.0 8.7 %to_planes.1 = (f32[8192,128]{1,0:T(8,128)}, f32[8,2,8,32,128]{4,3,2,1,0:T(8,128)}) custom-call(f32[8,2,8,32,128]{4,3,2,1,0:T(8,128)} %copy-done.1, f32[8,2,8,32,128]{4,3,2,1,0:T(8,128)} %all-to-all-done.4.other, f32[8,34,32,128]{3,2,1,0:T(8,128)} %adjoint_step.1._), custom_call_target="tpu_custom_call" | custom-call | bytes 8650752 | tf_op jit(solution)/shard_map/to_planes/pallas_call | solution.py:42
  297.1 2.8 collective-permute-start.15
  299.9 3.0 collective-permute-start.14
  303.0 83.2 %collective-permute-done.15.refs_2_ = f32[4,64,128]{2,1,0:T(8,128)S(1)} collective-permute-done((f32[4,64,128]{2,1,0:T(8,128)S(1)}, f32[4,64,128]{2,1,0:T(8,128)S(1)}, u32[]{:S(2)}, u32[]{:S(2)}) %collective-permute-start.15) | collective-permute-done | bytes 131104 | tf_op jit(solution)/shard_map/ppermute | solution.py:742
  387.6 14.8 %last_step.1 = f32[4,2048,128]{2,1,0:T(8,128)} custom-call(f32[8,8,32,128]{3,2,1,0:T(8,128)} %bitcast.13, f32[4,64,128]{2,1,0:T(8,128)} %copy-done.21, f32[4,64,128]{2,1,0:T(8,128)} %copy-done.20, f32[8,34,32,128]{3,2,1,0:T(8,128)} %all-to-all-done.5.refs_3_, f32[8,2,8,32,128]{4,3,2,1,0:T(8,128)} %get-tuple-element.28.refs_4_, ...), custom_call_target="tpu_custom_call" | custom-call | flops 31457280 | bytes 14155776 | tf_op jit(solution)/shard_map/last_step/pallas_call | solution.py:42
  (78 shorter events, 28.4 us)
Async XLA Ops:
  3.6 15.1 %all-to-all-start.1 = ((f32[8,3,32,128]{3,2,1,0:T(8,128)}), f32[8,3,32,128]{3,2,1,0:T(8,128)S(1)}, u32[]{:S(2)}, u32[]{:S(2)}) async-start(f32[8,3,32,128]{3,2,1,0:T(8,128)} %get-tuple-element.27.refs_0_), calls=%async_computation.1 | async-start | bytes 786432 | tf_op jit(solution)/shard_map/all_to_all | solution.py:715
  18.7 9.1 %copy-start.3 = (f32[8,3,32,128]{3,2,1,0:T(8,128)}, f32[8,3,32,128]{3,2,1,0:T(8,128)S(1)}, u32[]{:S(2)}) copy-start(f32[8,3,32,128]{3,2,1,0:T(8,128)S(1)} %all-to-all-done.1._before._after.refs_0_) | copy-start | bytes 1179652
  18.7 52.1 %all-to-all-start = ((f32[8,2,8,32,128]{4,3,2,1,0:T(8,128)}), f32[8,2,8,32,128]{4,3,2,1,0:T(8,128)S(1)}, u32[]{:S(2)}, u32[]{:S(2)}) async-start(f32[8,2,8,32,128]{4,3,2,1,0:T(8,128)} %get-tuple-element.28.refs_4_), calls=%async_computation | async-start | bytes 4194304 | tf_op jit(solution)/shard_map/all_to_all | solution.py:715
  25.3 11.3 %collective-permute-start.5 = (f32[8,3,32,128]{3,2,1,0:T(8,128)S(1)}, f32[8,3,32,128]{3,2,1,0:T(8,128)S(1)}, u32[]{:S(2)}, u32[]{:S(2)}) collective-permute-start(f32[8,3,32,128]{3,2,1,0:T(8,128)S(1)} %all-to-all-done.1._before._after.refs_0_), channel_id=1, source_target_pairs={{0,8},{8,16},{16,24},{24,0},{1,9},{9,17},{17,25},{25,1},{2,10},{10... | collective-permute-start | bytes 1179656 | tf_op jit(solution)/shard_map/ppermute | solution.py:720
  26.5 19.2 %collective-permute-start.4 = (f32[8,3,32,128]{3,2,1,0:T(8,128)S(1)}, f32[8,3,32,128]{3,2,1,0:T(8,128)S(1)}, u32[]{:S(2)}, u32[]{:S(2)}) collective-permute-start(f32[8,3,32,128]{3,2,1,0:T(8,128)S(1)} %all-to-all-done.1._before._after.refs_0_), channel_id=1, source_target_pairs={{0,16},{8,24},{16,0},{24,8},{1,17},{9,25},{17,1},{25,9},{2,18},{10... | collective-permute-start | bytes 1179656 | tf_op jit(solution)/shard_map/ppermute | solution.py:720
  27.7 17.9 %collective-permute-start.3 = (f32[8,3,32,128]{3,2,1,0:T(8,128)S(1)}, f32[8,3,32,128]{3,2,1,0:T(8,128)S(1)}, u32[]{:S(2)}, u32[]{:S(2)}) collective-permute-start(f32[8,3,32,128]{3,2,1,0:T(8,128)S(1)} %all-to-all-done.1._before._after.refs_0_), channel_id=1, source_target_pairs={{0,24},{8,0},{16,8},{24,16},{1,25},{9,1},{17,9},{25,17},{2,26},{10... | collective-permute-start | bytes 1179656 | tf_op jit(solution)/shard_map/ppermute | solution.py:720
  36.6 9.1 %copy-start.16 = (f32[8,3,32,128]{3,2,1,0:T(8,128)}, f32[8,3,32,128]{3,2,1,0:T(8,128)S(1)}, u32[]{:S(2)}) copy-start(f32[8,3,32,128]{3,2,1,0:T(8,128)S(1)} %collective-permute-done.5.refs_3_) | copy-start | bytes 1179652
  72.1 66.7 %all-to-all-start.2 = ((f32[8,2,8,32,128]{4,3,2,1,0:T(8,128)}), f32[8,2,8,32,128]{4,3,2,1,0:T(8,128)}, u32[]{:S(2)}, u32[]{:S(2)}) async-start(f32[8,2,8,32,128]{4,3,2,1,0:T(8,128)} %get-tuple-element.33.refs_5_), calls=%async_computation.2 | async-start | bytes 4194304 | tf_op jit(solution)/shard_map/all_to_all | solution.py:715
  83.6 62.6 %collective-permute-start.2 = (f32[8,2,8,32,128]{4,3,2,1,0:T(8,128)}, f32[8,2,8,32,128]{4,3,2,1,0:T(8,128)S(1)}, u32[]{:S(2)}, u32[]{:S(2)}) collective-permute-start(f32[8,2,8,32,128]{4,3,2,1,0:T(8,128)} %get-tuple-element.31), channel_id=1, source_target_pairs={{0,24},{8,0},{16,8},{24,16},{1,25},{9,1},{17,9},{25,17},{2,26},{10... | collective-permute-start | bytes 6291464 | tf_op jit(solution)/shard_map/ppermute | solution.py:720
  85.8 50.9 %collective-permute-start = (f32[8,2,2,32,128]{4,3,2,1,0:T(8,128)}, f32[8,2,2,32,128]{4,3,2,1,0:T(8,128)S(1)}, u32[]{:S(2)}, u32[]{:S(2)}) collective-permute-start(f32[8,2,2,32,128]{4,3,2,1,0:T(8,128)} %get-tuple-element.29), channel_id=1, source_target_pairs={{0,1},{1,2},{2,3},{3,4},{4,5},{5,6},{6,7},{7,0},{8,9},{9,10},{10,1... | collective-permute-start | bytes 1572872 | tf_op jit(solution)/shard_map/ppermute | solution.py:720
  87.5 51.3 %collective-permute-start.1 = (f32[8,2,2,32,128]{4,3,2,1,0:T(8,128)}, f32[8,2,2,32,128]{4,3,2,1,0:T(8,128)S(1)}, u32[]{:S(2)}, u32[]{:S(2)}) collective-permute-start(f32[8,2,2,32,128]{4,3,2,1,0:T(8,128)} %get-tuple-element.30), channel_id=1, source_target_pairs={{0,7},{1,0},{2,1},{3,2},{4,3},{5,4},{6,5},{7,6},{8,15},{9,8},{10,9... | collective-permute-start | bytes 1572872 | tf_op jit(solution)/shard_map/ppermute | solution.py:720
  136.8 2.0 copy-start.4
  143.2 20.7 %collective-permute-start.8 = (f32[8,2,3,32,128]{4,3,2,1,0:T(8,128)}, f32[8,2,3,32,128]{4,3,2,1,0:T(8,128)S(1)}, u32[]{:S(2)}, u32[]{:S(2)}) collective-permute-start(f32[8,2,3,32,128]{4,3,2,1,0:T(8,128)} %get-tuple-element.38), channel_id=1, source_target_pairs={{0,24},{8,0},{16,8},{24,16},{1,25},{9,1},{17,9},{25,17},{2,26},{10... | collective-permute-start | bytes 2359304 | tf_op jit(solution)/shard_map/ppermute | solution.py:720
  145.1 18.8 %collective-permute-start.6 = (f32[8,2,2,32,128]{4,3,2,1,0:T(8,128)}, f32[8,2,2,32,128]{4,3,2,1,0:T(8,128)S(1)}, u32[]{:S(2)}, u32[]{:S(2)}) collective-permute-start(f32[8,2,2,32,128]{4,3,2,1,0:T(8,128)} %get-tuple-element.37), channel_id=1, source_target_pairs={{0,1},{1,2},{2,3},{3,4},{4,5},{5,6},{6,7},{7,0},{8,9},{9,10},{10,1... | collective-permute-start | bytes 1572872 | tf_op jit(solution)/shard_map/ppermute | solution.py:720
  146.2 17.7 %collective-permute-start.7 = (f32[8,2,2,32,128]{4,3,2,1,0:T(8,128)}, f32[8,2,2,32,128]{4,3,2,1,0:T(8,128)S(1)}, u32[]{:S(2)}, u32[]{:S(2)}) collective-permute-start(f32[8,2,2,32,128]{4,3,2,1,0:T(8,128)} %get-tuple-element.34._), channel_id=1, source_target_pairs={{0,7},{1,0},{2,1},{3,2},{4,3},{5,4},{6,5},{7,6},{8,15},{9,8},{10,9... | collective-permute-start | bytes 1572872 | tf_op jit(solution)/shard_map/ppermute | solution.py:720
  165.1 6.6 %copy-start.22 = (f32[2,256,128]{2,1,0:T(8,128)S(1)}, f32[2,256,128]{2,1,0:T(8,128)}, u32[]{:S(2)}) copy-start(f32[2,256,128]{2,1,0:T(8,128)} %get-tuple-element.44) | copy-start | bytes 786436
  165.1 63.2 %all-to-all-start.3 = ((f32[8,2,8,32,128]{4,3,2,1,0:T(8,128)}), f32[8,2,8,32,128]{4,3,2,1,0:T(8,128)S(1)}, u32[]{:S(2)}, u32[]{:S(2)}) async-start(f32[8,2,8,32,128]{4,3,2,1,0:T(8,128)} %after.2.refs_6_.refs_5_.refs_0_), calls=%async_computation.3 | async-start | bytes 4194304 | tf_op jit(solution)/shard_map/all_to_all | solution.py:715
  169.8 30.2 %collective-permute-start.9 = (f32[8,2,5,32,128]{4,3,2,1,0:T(8,128)}, f32[8,2,5,32,128]{4,3,2,1,0:T(8,128)S(1)}, u32[]{:S(2)}, u32[]{:S(2)}) collective-permute-start(f32[8,2,5,32,128]{4,3,2,1,0:T(8,128)} %get-tuple-element.40), channel_id=1, source_target_pairs={{0,24},{8,0},{16,8},{24,16},{1,25},{9,1},{17,9},{25,17},{2,26},{10... | collective-permute-start | bytes 3932168 | tf_op jit(solution)/shard_map/ppermute | solution.py:720
  170.0 53.8 %collective-permute-start.10 = (f32[2,256,128]{2,1,0:T(8,128)}, f32[2,256,128]{2,1,0:T(8,128)S(1)}, u32[]{:S(2)}, u32[]{:S(2)}) collective-permute-start(f32[2,256,128]{2,1,0:T(8,128)} %get-tuple-element.42), channel_id=1, source_target_pairs={{0,1},{1,2},{2,3},{3,4},{4,5},{5,6},{6,7},{7,0},{8,9},{9,10},{10,1... | collective-permute-start | bytes 786440 | tf_op jit(solution)/shard_map/ppermute | solution.py:720
  171.7 53.8 %collective-permute-start.12 = (f32[2,256,128]{2,1,0:T(8,128)S(1)}, f32[2,256,128]{2,1,0:T(8,128)S(1)}, u32[]{:S(2)}, u32[]{:S(2)}) collective-permute-start(f32[2,256,128]{2,1,0:T(8,128)S(1)} %copy-done.22), channel_id=1, source_target_pairs={{0,7},{1,0},{2,1},{3,2},{4,3},{5,4},{6,5},{7,6},{8,15},{9,8},{10,9... | collective-permute-start | bytes 786440 | tf_op jit(solution)/shard_map/ppermute | solution.py:720
  210.6 16.0 %collective-permute-start.11 = (f32[2,256,128]{2,1,0:T(8,128)}, f32[2,256,128]{2,1,0:T(8,128)S(1)}, u32[]{:S(2)}, u32[]{:S(2)}) collective-permute-start(f32[2,256,128]{2,1,0:T(8,128)} %get-tuple-element.43), channel_id=1, source_target_pairs={{0,1},{1,2},{2,3},{3,4},{4,5},{5,6},{6,7},{7,0},{8,9},{9,10},{10,1... | collective-permute-start | bytes 786440 | tf_op jit(solution)/shard_map/ppermute | solution.py:720
  212.9 15.4 %collective-permute-start.13 = (f32[2,256,128]{2,1,0:T(8,128)}, f32[2,256,128]{2,1,0:T(8,128)S(1)}, u32[]{:S(2)}, u32[]{:S(2)}) collective-permute-start(f32[2,256,128]{2,1,0:T(8,128)} %get-tuple-element.45), channel_id=1, source_target_pairs={{0,7},{1,0},{2,1},{3,2},{4,3},{5,4},{6,5},{7,6},{8,15},{9,8},{10,9... | collective-permute-start | bytes 786440 | tf_op jit(solution)/shard_map/ppermute | solution.py:720
  223.8 4.5 %copy-start.12 = (f32[2,256,128]{2,1,0:T(8,128)}, f32[2,256,128]{2,1,0:T(8,128)S(1)}, u32[]{:S(2)}) copy-start(f32[2,256,128]{2,1,0:T(8,128)S(1)} %collective-permute-done.10.refs_1_.refs_2_) | copy-start | bytes 786436
  225.5 2.8 copy-start.13
  229.8 49.1 %all-to-all-start.4 = ((f32[8,2,8,32,128]{4,3,2,1,0:T(8,128)}), f32[8,2,8,32,128]{4,3,2,1,0:T(8,128)}, u32[]{:S(2)}, u32[]{:S(2)}) async-start(f32[8,2,8,32,128]{4,3,2,1,0:T(8,128)} %after.3.refs_1_), calls=%async_computation.4 | async-start | bytes 4194304 | tf_op jit(solution)/shard_map/all_to_all | solution.py:715
  251.7 35.2 %copy-start.2 = (f32[8,2,8,32,128]{4,3,2,1,0:T(8,128)S(1)}, f32[8,2,8,32,128]{4,3,2,1,0:T(8,128)}, u32[]{:S(2)}) copy-start(f32[8,2,8,32,128]{4,3,2,1,0:T(8,128)} %copy-done.1) | copy-start | bytes 6291460
  278.8 108.7 %all-to-all-start.5 = ((f32[8,34,32,128]{3,2,1,0:T(8,128)}), f32[8,34,32,128]{3,2,1,0:T(8,128)}, u32[]{:S(2)}, u32[]{:S(2)}) async-start(f32[8,34,32,128]{3,2,1,0:T(8,128)} %adjoint_step.1._), calls=%async_computation.5 | async-start | bytes 8912896 | tf_op jit(solution)/shard_map/all_to_all | solution.py:715
  286.9 10.2 %copy-start.19 = (f32[2,4,64,128]{3,2,1,0:T(8,128)S(1)}, f32[2,4,64,128]{3,2,1,0:T(8,128)}, u32[]{:S(2)}) copy-start(f32[2,4,64,128]{3,2,1,0:T(8,128)} %get-tuple-element.50) | copy-start | bytes 786436
  286.9 99.3 %collective-permute-start.16 = (f32[8,2,8,32,128]{4,3,2,1,0:T(8,128)S(1)}, f32[8,2,8,32,128]{4,3,2,1,0:T(8,128)S(1)}, u32[]{:S(2)}, u32[]{:S(2)}) collective-permute-start(f32[8,2,8,32,128]{4,3,2,1,0:T(8,128)S(1)} %copy-done.2), channel_id=1, source_target_pairs={{0,8},{8,16},{16,24},{24,0},{1,9},{9,17},{17,25},{25,1},{2,10},{10... | collective-permute-start | bytes 6291464 | tf_op jit(solution)/shard_map/ppermute | solution.py:720
  295.7 91.9 %collective-permute-start.17 = (f32[8,2,8,32,128]{4,3,2,1,0:T(8,128)}, f32[8,2,8,32,128]{4,3,2,1,0:T(8,128)}, u32[]{:S(2)}, u32[]{:S(2)}) collective-permute-start(f32[8,2,8,32,128]{4,3,2,1,0:T(8,128)} %get-tuple-element.51), channel_id=1, source_target_pairs={{0,8},{8,16},{16,24},{24,0},{1,9},{9,17},{17,25},{25,1},{2,10},{10... | collective-permute-start | bytes 6291464 | tf_op jit(solution)/shard_map/ppermute | solution.py:720
  297.1 89.1 %collective-permute-start.15 = (f32[4,64,128]{2,1,0:T(8,128)S(1)}, f32[4,64,128]{2,1,0:T(8,128)S(1)}, u32[]{:S(2)}, u32[]{:S(2)}) collective-permute-start(f32[4,64,128]{2,1,0:T(8,128)S(1)} %get-tuple-element.52), channel_id=1, source_target_pairs={{1,0},{2,1},{3,2},{4,3},{5,4},{6,5},{7,6},{9,8},{10,9},{11,10},{12... | collective-permute-start | bytes 393224 | tf_op jit(solution)/shard_map/ppermute | solution.py:742
  299.9 86.2 %collective-permute-start.14 = (f32[4,64,128]{2,1,0:T(8,128)S(1)}, f32[4,64,128]{2,1,0:T(8,128)S(1)}, u32[]{:S(2)}, u32[]{:S(2)}) collective-permute-start(f32[4,64,128]{2,1,0:T(8,128)S(1)} %get-tuple-element.53), channel_id=1, source_target_pairs={{0,1},{1,2},{2,3},{3,4},{4,5},{5,6},{6,7},{8,9},{9,10},{10,11},{11... | collective-permute-start | bytes 393224 | tf_op jit(solution)/shard_map/ppermute | solution.py:741
  (15 other events, 17.0 us)
